TPU v7x, 128 devices: a whole 4x4x4 slice. The times are simulated.
128 devices in a mesh: group: 8 (over z, core), local: 16 (over y, x).
Axes of the slice: x: 4, y: 4, z: 4, core: 2. Of those that a mesh axis runs over, the one named last changes fastest.
Arguments:
- tokens: bfloat16 [512, 7168], P('local'), may hold values from -6 to 6
- cotangent: bfloat16 [512, 7168], P('local'), may hold values from -6 to 6
- gate_logits: float32 [512, 24], P('local'), may hold values from -8 to 8
- route_slot: int32 [512, 8], P('local'), may hold values from 0 to 31, all different within a row; in each aligned block of 32 rows (0 to 31, 32 to 63, ...) at most 16 rows name the same one
- slot_expert: int32 [32], replicated, may hold values from 0 to 23, as said below
- w_gate: bfloat16 [32, 7168, 1024], P('local', None, 'group')
- w_up: bfloat16 [32, 7168, 1024], P('local', None, 'group')
- w_down: bfloat16 [32, 1024, 7168], P('local', 'group'), as said below
Outputs:
- mixed: bfloat16 [512, 7168], P('local', 'group')
- grad_tokens: bfloat16 [512, 7168], P('local', 'group')
- grad_logits: float32 [512, 24], P('local')
- grad_gate: bfloat16 [32, 7168, 1024], P('local', None, 'group')
- grad_up: bfloat16 [32, 7168, 1024], P('local', None, 'group')
- grad_down: bfloat16 [32, 1024, 7168], P('local', 'group')
Inputs may be any that keep to these rules, and one draw needn't show every extreme that they name: `route_slot`: each token names 8 different slots. Of the 32 tokens of one index of local, at most 16 name one slot, a bound that some block reaches of them. `slot_expert`: the even slots hold 16 different experts, the odd slots the remaining ones, each on two odd slots: slot 2i + 1 and slot 2j + 1 hold the same expert where j = i plus or minus half the size of local (the one that stays in range). Every expert is held. `w_down`: two odd slots that hold the same expert have equal weights; entries have standard deviation 1024 ** -0.5.
All inputs are finite; a program needn't handle non-finite values.
Results may differ from a plain program's by a relative error of at most 0.019.
Values may be sent and summed in bfloat16 or wider, within the bound.
No kernel may reach another device: no remote copies, remote signals or barrier semaphores. Data moves between devices by JAX's collectives and lax.ppermute only.
A program may use at most 192 MiB of HBM per device.

v0:
```python
import jax
import jax.numpy as jnp
from jax import lax
from jax.sharding import PartitionSpec as P

ROUTE_SCALE = 2.5
CONTRACT_ONE = (((1,), (1,)), ((), ()))
CONTRACT_ZERO = (((0,), (0,)), ((), ()))


def swapped(block, axis, apart):
    count = lax.axis_size(axis)
    route = []
    for low in range(count):
        high = low | 1 << apart
        if high != low and high < count:
            route += [(low, high), (high, low)]
    return lax.ppermute(block, axis, route)


def gate_weights(logits, expert_ids, experts):
    match = expert_ids[:, :, None] == jnp.arange(experts, dtype=jnp.int32)[None, None, :]
    picked = jnp.sum(jnp.where(match, logits[:, None, :], 0.0), axis=2)
    sig = jax.nn.sigmoid(picked)
    return ROUTE_SCALE * sig / jnp.sum(sig, axis=1, keepdims=True)


def activations(rows_x, rows_g, w_g, w_u, w_d):
    first = jnp.dot(rows_x, w_g, preferred_element_type=jnp.float32)
    second = jnp.dot(rows_x, w_u, preferred_element_type=jnp.float32)
    sig = jax.nn.sigmoid(first)
    silu = first * sig
    hidden = (silu * second).astype(jnp.bfloat16)
    back = lax.dot_general(rows_g, w_d, CONTRACT_ONE, preferred_element_type=jnp.float32)
    d_first = (back * second * sig * (1.0 + first * (1.0 - sig))).astype(jnp.bfloat16)
    d_second = (back * silu).astype(jnp.bfloat16)
    return (hidden, d_first, d_second)


def weight_grads(rows_x, rows_g, hidden, d_first, d_second):
    own_gate = lax.dot_general(rows_x, d_first, CONTRACT_ZERO, preferred_element_type=jnp.float32)
    own_up = lax.dot_general(rows_x, d_second, CONTRACT_ZERO, preferred_element_type=jnp.float32)
    own_down = lax.dot_general(hidden, rows_g, CONTRACT_ZERO, preferred_element_type=jnp.float32)
    return (
        own_gate.astype(jnp.bfloat16),
        own_up.astype(jnp.bfloat16),
        own_down.astype(jnp.bfloat16),
    )


def slot_pass(rows_x, rows_g, w_g, w_u, w_d):
    hidden, d_first, d_second = activations(rows_x, rows_g, w_g, w_u, w_d)
    out_rows = jnp.dot(hidden, w_d, preferred_element_type=jnp.float32).astype(jnp.bfloat16)
    both = lax.dot_general(d_first, w_g, CONTRACT_ONE, preferred_element_type=jnp.float32)
    both = both + lax.dot_general(d_second, w_u, CONTRACT_ONE, preferred_element_type=jnp.float32)
    grad_rows = both.astype(jnp.bfloat16)
    return (out_rows, grad_rows, weight_grads(rows_x, rows_g, hidden, d_first, d_second))


def per_device(tokens, cotangent, gate_logits, route_slot, slot_expert, w_gate, w_up, w_down):
    tok = tokens.shape[0]
    width = tokens.shape[1]
    top = route_slot.shape[1]
    slots = slot_expert.shape[0]
    experts = gate_logits.shape[1]
    lines = lax.axis_size("local")
    cap = top * tok // lines
    match_slot = route_slot[:, :, None] == jnp.arange(slots, dtype=jnp.int32)[None, None, :]
    expert_ids = jnp.sum(jnp.where(match_slot, slot_expert[None, None, :], 0), axis=2)
    weights, pull_back = jax.vjp(lambda lg: gate_weights(lg, expert_ids, experts), gate_logits)
    scaled = (weights[:, :, None] * cotangent.astype(jnp.float32)[:, None, :]).astype(jnp.bfloat16)
    flat = route_slot.reshape(-1)
    onehot = (flat[:, None] == jnp.arange(slots, dtype=jnp.int32)[None, :]).astype(jnp.int32)
    rank = jnp.sum((jnp.cumsum(onehot, axis=0) - onehot) * onehot, axis=1)
    target = flat * cap + rank
    placer = (jnp.arange(slots * cap, dtype=jnp.int32)[:, None] == target[None, :]).astype(
        jnp.bfloat16
    )
    token_placer = jnp.sum(placer.reshape(slots * cap, tok, top), axis=2)
    x_buffer = jnp.dot(token_placer, tokens, preferred_element_type=jnp.float32).astype(
        jnp.bfloat16
    )
    g_buffer = jnp.dot(
        placer, scaled.reshape(tok * top, width), preferred_element_type=jnp.float32
    ).astype(jnp.bfloat16)
    x_buffer = x_buffer.reshape(lines, 2 * cap, width)
    g_buffer = g_buffer.reshape(lines, 2 * cap, width)
    got_x, got_g = (
        lax.all_to_all(x_buffer, "local", split_axis=0, concat_axis=0, tiled=True),
        lax.all_to_all(g_buffer, "local", split_axis=0, concat_axis=0, tiled=True),
    )
    got_x = got_x.reshape(lines, 2, cap, width)
    got_g = got_g.reshape(lines, 2, cap, width)
    rows_cold_x = got_x[:, 0].reshape(lines * cap, width)
    rows_cold_g = got_g[:, 0].reshape(lines * cap, width)
    rows_hot_x = got_x[:, 1].reshape(lines * cap, width)
    rows_hot_g = got_g[:, 1].reshape(lines * cap, width)
    out_cold, dx_cold, grads_cold = slot_pass(
        rows_cold_x, rows_cold_g, w_gate[0], w_up[0], w_down[0]
    )
    out_hot, dx_hot, grads_hot = slot_pass(rows_hot_x, rows_hot_g, w_gate[1], w_up[1], w_down[1])
    outs_back = jnp.stack(
        [out_cold.reshape(lines, cap, width), out_hot.reshape(lines, cap, width)], axis=1
    )
    dxs_back = jnp.stack(
        [dx_cold.reshape(lines, cap, width), dx_hot.reshape(lines, cap, width)], axis=1
    )
    outs_back = outs_back.reshape(lines, 2 * cap, width)
    dxs_back = dxs_back.reshape(lines, 2 * cap, width)
    home_out, home_dx = (
        lax.all_to_all(outs_back, "local", split_axis=0, concat_axis=0, tiled=True),
        lax.all_to_all(dxs_back, "local", split_axis=0, concat_axis=0, tiled=True),
    )
    home_out = home_out.reshape(slots * cap, width)
    home_dx = home_dx.reshape(slots * cap, width)
    gathered = lax.dot_general(placer, home_out, CONTRACT_ZERO, preferred_element_type=jnp.float32)
    gathered = gathered.reshape(tok, top, width)
    partial_out = jnp.sum(weights[:, :, None] * gathered, axis=1)
    partial_dx = lax.dot_general(
        token_placer, home_dx, CONTRACT_ZERO, preferred_element_type=jnp.float32
    )
    partial_dots = jnp.sum(cotangent.astype(jnp.float32)[:, None, :] * gathered, axis=2)
    mixed, grad_tokens = (
        lax.psum_scatter(
            partial_out.astype(jnp.bfloat16), "group", scatter_dimension=1, tiled=True
        ).astype(jnp.float32),
        lax.psum_scatter(
            partial_dx.astype(jnp.bfloat16), "group", scatter_dimension=1, tiled=True
        ).astype(jnp.float32),
    )
    gate_dots = lax.psum(partial_dots, "group")
    grad_logits = pull_back(gate_dots)[0]
    partner_bit = lax.axis_size("local").bit_length() - 2
    other = swapped((grads_hot[0], grads_hot[1], grads_hot[2]), "local", partner_bit)
    joined = [
        (mine.astype(jnp.float32) + theirs.astype(jnp.float32)).astype(jnp.bfloat16)
        for mine, theirs in zip(grads_hot, other)
    ]
    grad_gate = jnp.stack([grads_cold[0], joined[0]], axis=0)
    grad_up = jnp.stack([grads_cold[1], joined[1]], axis=0)
    grad_down = jnp.stack([grads_cold[2], joined[2]], axis=0)
    return (
        mixed.astype(jnp.bfloat16),
        grad_tokens.astype(jnp.bfloat16),
        grad_logits,
        grad_gate,
        grad_up,
        grad_down,
    )


def solution(mesh):
    return jax.shard_map(
        per_device,
        mesh=mesh,
        in_specs=(
            P("local", None),
            P("local", None),
            P("local", None),
            P("local", None),
            P(),
            P("local", None, "group"),
            P("local", None, "group"),
            P("local", "group", None),
        ),
        out_specs=(
            P("local", "group"),
            P("local", "group"),
            P("local", None),
            P("local", None, "group"),
            P("local", None, "group"),
            P("local", "group", None),
        ),
        check_vma=False,
    )
```

profile of v0, /device:TPU:0, one launch (start us, length us, event | category | flops | bytes accessed | tf_op | source)
XLA Modules:
  0.0 620.1 jit_solution(16297483419287537097)
XLA Ops:
  9.5 5.0 convolution_convert_fusion.1
  14.5 7.3 %all-to-all-start = ((bf16[16,32,7168]{2,1,0:T(8,128)(2,1)}), bf16[16,32,7168]{2,1,0:T(8,128)(2,1)}, u32[]{:S(2)}, u32[]{:S(2)}) async-start(bf16[16,32,7168]{2,1,0:T(8,128)(2,1)} %bitcast.142), calls=%async_computation | async-start | bytes 14680064 | tf_op jit(solution)/shard_map/all_to_all | solution.py:89
  22.9 5.2 convolution_convert_fusion
  28.1 102.3 %all-to-all-done = bf16[16,32,7168]{2,1,0:T(8,128)(2,1)} async-done(((bf16[16,32,7168]{2,1,0:T(8,128)(2,1)}), bf16[16,32,7168]{2,1,0:T(8,128)(2,1)}, u32[]{:S(2)}, u32[]{:S(2)}) %all-to-all-start) | async-done | bytes 7340064 | tf_op jit(solution)/shard_map/all_to_all | solution.py:89
  130.5 5.8 all-to-all-start.2
  136.3 3.8 fusion.60
  148.3 94.5 %all-to-all-done.2 = bf16[16,32,7168]{2,1,0:T(8,128)(2,1)} async-done(((bf16[16,32,7168]{2,1,0:T(8,128)(2,1)}), bf16[16,32,7168]{2,1,0:T(8,128)(2,1)}, u32[]{:S(2)}, u32[]{:S(2)}) %all-to-all-start.2) | async-done | bytes 7340064 | tf_op jit(solution)/shard_map/all_to_all | solution.py:90
  242.8 3.8 fusion.59
  258.0 3.8 pad_maximum_fusion.1
  261.8 4.9 all-to-all-start.3
  266.7 4.2 convolution_convert_fusion.4
  294.9 77.8 %all-to-all-done.3 = bf16[16,32,7168]{2,1,0:T(8,128)(2,1)} async-done(((bf16[16,32,7168]{2,1,0:T(8,128)(2,1)}), bf16[16,32,7168]{2,1,0:T(8,128)(2,1)}, u32[]{:S(2)}, u32[]{:S(2)}) %all-to-all-start.3) | async-done | bytes 7340064 | tf_op jit(solution)/shard_map/all_to_all | solution.py:112
  372.7 10.7 %all-to-all-start.1 = ((bf16[16,32,7168]{2,1,0:T(8,128)(2,1)}), bf16[16,32,7168]{2,1,0:T(8,128)(2,1)}, u32[]{:S(2)}, u32[]{:S(2)}) async-start(bf16[16,32,7168]{2,1,0:T(8,128)(2,1)} %bitcast.144), calls=%async_computation.1 | async-start | bytes 14680064 | tf_op jit(solution)/shard_map/all_to_all | solution.py:111
  383.8 58.0 %collective-permute-done.2 = bf16[128,7168]{1,0:T(8,128)(2,1)} collective-permute-done((bf16[128,7168]{1,0:T(8,128)(2,1)}, bf16[128,7168]{1,0:T(8,128)(2,1)}, u32[]{:S(2)}, u32[]{:S(2)}) %collective-permute-start.2) | collective-permute-done | bytes 1835040 | tf_op jit(solution)/shard_map/ppermute | solution.py:18
  446.5 44.4 %collective-permute-done.1 = bf16[7168,128]{1,0:T(8,128)(2,1)} collective-permute-done((bf16[7168,128]{1,0:T(8,128)(2,1)}, bf16[7168,128]{1,0:T(8,128)(2,1)}, u32[]{:S(2)}, u32[]{:S(2)}) %collective-permute-start.1) | collective-permute-done | bytes 1835040 | tf_op jit(solution)/shard_map/ppermute | solution.py:18
  490.9 3.7 fusion.10
  494.6 35.5 %collective-permute-done = bf16[7168,128]{1,0:T(8,128)(2,1)} collective-permute-done((bf16[7168,128]{1,0:T(8,128)(2,1)S(1)}, bf16[7168,128]{1,0:T(8,128)(2,1)}, u32[]{:S(2)}, u32[]{:S(2)}) %collective-permute-start) | collective-permute-done | bytes 1835040 | tf_op jit(solution)/shard_map/ppermute | solution.py:18
  533.4 4.5 convolution_convert_fusion.10
  539.8 3.7 pad_maximum_fusion.3
  543.5 4.1 all-to-all-done.1
  547.5 7.9 %multiply_reduce_fusion = (f32[32,8]{1,0:T(8,128)S(1)}, bf16[32,7168]{1,0:T(8,128)(2,1)S(1)}) fusion(f32[32,7168]{1,0:T(8,128)S(1)} %convert_element_type.121, f32[32,8]{1,0:T(8,128)S(1)} %copy.51, bf16[512,7168,1]{1,0,2:T(8,128)(2,1)} %bitcast.18, s32[256]{0:T(256)S(1)} %multiply_add_fusion.1), kind=kOutput, calls=%fused_computation.22 | convolution fusion | flops 1886289664 | bytes 8719360 | tf_op jit(solution)/shard_map/dot_general | solution.py:116
  557.4 3.7 pad_maximum_fusion.2
  561.2 14.0 %psum.7 = f32[32,8]{0,1:T(8,128)S(1)} all-reduce(f32[32,8]{0,1:T(8,128)S(1)} %copy.61), channel_id=1, replica_groups=mesh['group'=8,'local'=16] {'group'}, use_global_device_ids=true, to_apply=%region_11.12 | all-reduce | flops 256 | bytes 2048 | tf_op jit(solution)/shard_map/psum | solution.py:131
  578.8 32.8 %reduce-scatter.7.cloned.1.call-done = bf16[896,32]{1,0:T(8,128)(2,1)} async-done(((bf16[7168,32]{1,0:T(8,128)(2,1)}), bf16[896,32]{1,0:T(8,128)(2,1)}) %reduce-scatter.7.cloned.1.call-update) | async-done | bytes 57360
  (102 shorter events, 64.2 us)
Async XLA Ops:
  14.5 7.3 %copy-start.20 = (s32[32]{0:T(128)S(1)}, s32[32]{0:T(128)}, u32[]{:S(2)}) copy-start(s32[32]{0:T(128)} %param.12) | copy-start | bytes 388
  14.5 8.1 %copy-start.19 = (f32[32,24]{0,1:T(8,128)S(1)}, f32[32,24]{0,1:T(8,128)}, u32[]{:S(2)}) copy-start(f32[32,24]{0,1:T(8,128)} %param.10) | copy-start | bytes 9220
  14.5 8.3 %copy-start.18 = (bf16[32,7168]{1,0:T(8,128)(2,1)S(1)}, bf16[32,7168]{1,0:T(8,128)(2,1)}, u32[]{:S(2)}) copy-start(bf16[32,7168]{1,0:T(8,128)(2,1)} %param.9) | copy-start | bytes 1376260
  14.5 116.0 %all-to-all-start = ((bf16[16,32,7168]{2,1,0:T(8,128)(2,1)}), bf16[16,32,7168]{2,1,0:T(8,128)(2,1)}, u32[]{:S(2)}, u32[]{:S(2)}) async-start(bf16[16,32,7168]{2,1,0:T(8,128)(2,1)} %bitcast.142), calls=%async_computation | async-start | bytes 14680064 | tf_op jit(solution)/shard_map/all_to_all | solution.py:89
  130.5 112.4 %all-to-all-start.2 = ((bf16[16,32,7168]{2,1,0:T(8,128)(2,1)}), bf16[16,32,7168]{2,1,0:T(8,128)(2,1)}, u32[]{:S(2)}, u32[]{:S(2)}) async-start(bf16[16,32,7168]{2,1,0:T(8,128)(2,1)} %bitcast.143), calls=%async_computation.2 | async-start | bytes 14680064 | tf_op jit(solution)/shard_map/all_to_all | solution.py:90
  136.3 4.2 copy-start.12
  140.1 5.9 copy-start.4
  140.1 7.0 %copy-start.2 = (bf16[16,1,16,7168]{3,2,1,0:T(8,128)(2,1)}, bf16[16,1,16,7168]{3,2,1,0:T(8,128)(2,1)S(1)}, u32[]{:S(2)}) copy-start(bf16[16,1,16,7168]{3,2,1,0:T(8,128)(2,1)S(1)} %get-tuple-element.10) | copy-start | bytes 11010052
  140.1 4.8 copy-start.14
  242.8 4.2 copy-start.16
  246.6 5.9 copy-start.6
  246.6 5.9 copy-start.8
  246.6 4.8 copy-start.15
  261.8 111.0 %all-to-all-start.3 = ((bf16[16,32,7168]{2,1,0:T(8,128)(2,1)}), bf16[16,32,7168]{2,1,0:T(8,128)(2,1)}, u32[]{:S(2)}, u32[]{:S(2)}) async-start(bf16[16,32,7168]{2,1,0:T(8,128)(2,1)} %bitcast.145), calls=%async_computation.3 | async-start | bytes 14680064 | tf_op jit(solution)/shard_map/all_to_all | solution.py:112
  266.6 7.6 %copy-start.3 = (bf16[16,1,16,7168]{3,2,1,0:T(8,128)(2,1)S(1)}, bf16[16,1,16,7168]{3,2,1,0:T(8,128)(2,1)}, u32[]{:S(2)}) copy-start(bf16[16,1,16,7168]{3,2,1,0:T(8,128)(2,1)} %copy-done.2) | copy-start | bytes 11010052
  270.9 170.9 %collective-permute-start.2 = (bf16[128,7168]{1,0:T(8,128)(2,1)}, bf16[128,7168]{1,0:T(8,128)(2,1)}, u32[]{:S(2)}, u32[]{:S(2)}) collective-permute-start(bf16[128,7168]{1,0:T(8,128)(2,1)} %convolution_convert_fusion.4), channel_id=1, source_target_pairs={{0,8},{8,0},{1,9},{9,1},{2,10},{10,2},{3,11},{11,3},{4,12},{12,4},... | collective-permute-start | bytes 5505032 | tf_op jit(solution)/shard_map/ppermute | solution.py:18
  282.7 6.3 %copy-start.17 = (bf16[2,128,7168]{2,1,0:T(8,128)(2,1)S(1)}, bf16[2,128,7168]{2,1,0:T(8,128)(2,1)}, u32[]{:S(2)}) copy-start(bf16[2,128,7168]{2,1,0:T(8,128)(2,1)} %param.15) | copy-start | bytes 11010052
  285.5 205.4 %collective-permute-start.1 = (bf16[7168,128]{1,0:T(8,128)(2,1)}, bf16[7168,128]{1,0:T(8,128)(2,1)}, u32[]{:S(2)}, u32[]{:S(2)}) collective-permute-start(bf16[7168,128]{1,0:T(8,128)(2,1)} %convolution_convert_fusion.6), channel_id=1, source_target_pairs={{0,8},{8,0},{1,9},{9,1},{2,10},{10,2},{3,11},{11,3},{4,12},{12,4},... | collective-permute-start | bytes 5505032 | tf_op jit(solution)/shard_map/ppermute | solution.py:18
  285.6 244.5 %collective-permute-start = (bf16[7168,128]{1,0:T(8,128)(2,1)S(1)}, bf16[7168,128]{1,0:T(8,128)(2,1)}, u32[]{:S(2)}, u32[]{:S(2)}) collective-permute-start(bf16[7168,128]{1,0:T(8,128)(2,1)S(1)} %convolution_convert_fusion.8), channel_id=1, source_target_pairs={{0,8},{8,0},{1,9},{9,1},{2,10},{10,2},{3,11},{11,3},{4,12},{12,4},... | collective-permute-start | bytes 5505032 | tf_op jit(solution)/shard_map/ppermute | solution.py:18
  372.7 174.8 %all-to-all-start.1 = ((bf16[16,32,7168]{2,1,0:T(8,128)(2,1)}), bf16[16,32,7168]{2,1,0:T(8,128)(2,1)}, u32[]{:S(2)}, u32[]{:S(2)}) async-start(bf16[16,32,7168]{2,1,0:T(8,128)(2,1)} %bitcast.144), calls=%async_computation.1 | async-start | bytes 14680064 | tf_op jit(solution)/shard_map/all_to_all | solution.py:111
  383.5 193.7 %reduce-scatter.9.cloned.1.call-start = ((), (), s32[]{:S(2)}) async-start(), calls=%async_computation.7 | async-start | bytes 2064384
  383.8 60.5 %copy-start.11 = (bf16[1,128,7168]{2,1,0:T(8,128)(2,1)S(1)}, bf16[1,128,7168]{2,1,0:T(8,128)(2,1)}, u32[]{:S(2)}) copy-start(bf16[1,128,7168]{2,1,0:T(8,128)(2,1)} %fusion.4) | copy-start | bytes 5505028
  539.6 72.0 %reduce-scatter.7.cloned.1.call-start = ((), (), s32[]{:S(2)}) async-start(), calls=%async_computation.6 | async-start | bytes 2064384
  557.4 55.9 %copy-start.1 = (bf16[32,7168]{1,0:T(8,128)(2,1)S(1)}, bf16[32,7168]{1,0:T(8,128)(2,1)}, u32[]{:S(2)}) copy-start(bf16[32,7168]{1,0:T(8,128)(2,1)} %param.8) | copy-start | bytes 1376260
  (6 other events, 12.6 us)
Sparse Core Ops, SparseCore 0:
  539.7 37.4 reduce-scatter.8
  579.6 31.9 reduce-scatter.6
where the time goes:
time: 621 us; the launch traced here: 620 us
  waiting for transfers between devices  451 us (73%)
  matrix products  50.6 us (8%)
  starting transfers between devices  36 us (6%)
  other arithmetic  29 us (5%)
  local copies, waits for them, and re-layouts  25.2 us (4%)
  between operations  14.5 us (2%)
  blocking collectives  14 us (2%)
    ppermute x3, waiting for transfers between devices, swapped(): return lax.ppermute(block, axis, route)  138 us
    all_to_all x1, waiting for transfers between devices, per_device(): lax.all_to_all(x_buffer, 'local', split_axis=0, concat_axis=0, tiled=True)  102 us
    all_to_all x1, waiting for transfers between devices, per_device(): lax.all_to_all(g_buffer, 'local', split_axis=0, concat_axis=0, tiled=True)  94.5 us
    all_to_all x1, waiting for transfers between devices, per_device(): lax.all_to_all(dxs_back, 'local', split_axis=0, concat_axis=0, tiled=True)  77.8 us
    unnamed x4, waiting for transfers between devices  34.1 us
    unnamed x47, local copies, waits for them, and re-layouts  17 us
    psum x1, blocking collectives, per_device(): gate_dots = lax.psum(partial_dots, 'group')  14 us
  transfers between devices with their start and end apart: 9, of which 9 were waited for; matrix products, arithmetic and copies ran while one was open for 12% of the time, Pallas kernels for 0%

commit v1 on v0

v1 whole, which is shorter than its diff:
```python
import functools

import jax
import jax.numpy as jnp
from jax import lax
from jax.experimental import pallas as pl
from jax.experimental.pallas import tpu as pltpu
from jax.sharding import Mesh
from jax.sharding import PartitionSpec as P

ROUTE_SCALE = 2.5
NZ, NC, NY, NX = 4, 2, 4, 4
AXES = ("z", "c", "y", "x")
STEPS = 4
BF, F32 = jnp.bfloat16, jnp.float32
NT = (((1,), (1,)), ((), ()))
TN = (((0,), (0,)), ((), ()))
RING = (0, 1, 3, 2)


def moves(step):
    pairs = []
    for z in range(NZ):
        for c in range(NC):
            for y in range(NY):
                for x in range(NX):
                    z2, c2, y2, x2 = step(z, c, y, x)
                    source = ((z * NC + c) * NY + y) * NX + x
                    target = ((z2 % NZ * NC + c2 % NC) * NY + y2 % NY) * NX + x2 % NX
                    pairs.append((source, target))
    return pairs


def outer(by):
    return moves(lambda z, c, y, x: (z, c, y + by, x) if c == 0 else (z, c, y, x + by))


def inner(by):
    return moves(lambda z, c, y, x: (z, c, y, x + by) if c == 0 else (z, c, y + by, x))


def along_z(by):
    return moves(lambda z, c, y, x: (z + by, c, y, x))


def other_core():
    return moves(lambda z, c, y, x: (z, c + 1, y, x))


def send(value, pairs):
    return lax.ppermute(value, AXES, pairs)


def places(swapped):
    found = []
    for out in range(4):
        for inn in range(4):
            a, b = (inn, out) if swapped else (out, inn)
            found.append((2 * a + b // 2, 64 * (b % 2)))
    return found


def rows_of(refs, swapped, second, tok):
    parts = []
    for piece, row in places(swapped):
        row = row + (tok if second else 0)
        parts.append(refs[piece][row : row + tok, :])
    return jnp.concatenate(parts, axis=0)


def two(ref):
    return jnp.concatenate([ref[0, 0, 0], ref[1, 0, 0]], axis=1)


def partial_sums(swapped, rows, wg, wu, wd):
    tok = rows_of(rows, swapped, False, 32)
    cot = rows_of(rows, swapped, True, 32)
    first = jnp.dot(tok, two(wg), preferred_element_type=F32)
    second = jnp.dot(tok, two(wu), preferred_element_type=F32)
    down = wd[...].reshape(-1, wd.shape[-1])
    back = lax.dot_general(cot, down, NT, preferred_element_type=F32)
    return first, second, back


def own_half_kernel(sel, *refs):
    rows, (wg, wu, wd) = refs[:8], refs[8:11]
    sums = refs[11:14]
    parts = partial_sums(False, rows, wg, wu, wd)

    @pl.when(pl.program_id(0) == 0)
    def _():
        for ref, part in zip(sums, parts):
            ref[...] = part

    @pl.when(pl.program_id(0) > 0)
    def _():
        for ref, part in zip(sums, parts):
            ref[...] += part


def other_half_kernel(sel, *refs):
    rows, (wg, wu, wd) = refs[:8], refs[8:11]
    start, gains = refs[11:14], refs[14]
    h_out, d1_out, d2_out, h_grad, d1_grad, d2_grad, dots = refs[15:22]
    sums = refs[22:25]
    parts = partial_sums(True, rows, wg, wu, wd)

    @pl.when(pl.program_id(0) == 0)
    def _():
        for ref, before, part in zip(sums, start, parts):
            ref[...] = before[...] + part

    @pl.when(pl.program_id(0) > 0)
    def _():
        for ref, part in zip(sums, parts):
            ref[...] += part

    @pl.when(pl.program_id(0) == STEPS - 1)
    def _():
        lane = lax.broadcasted_iota(jnp.int32, dots.shape, 1)
        total = jnp.zeros(dots.shape, F32)
        for slot in range(2):
            units = slice(128 * slot, 128 * slot + 128)
            first, second, back = (ref[:, units] for ref in sums)
            mine = gains[:, slot : slot + 1]
            both = gains[:, 2 * slot : 2 * slot + 1]
            sig = jax.nn.sigmoid(first)
            silu = first * sig
            hidden = silu * second
            total = jnp.where(lane == slot, jnp.sum(hidden * back, axis=1, keepdims=True), total)
            d_first = back * second * sig * (1.0 + first * (1.0 - sig))
            d_second = back * silu
            h_out[:, units] = (hidden * mine).astype(BF)
            d1_out[:, units] = (d_first * mine).astype(BF)
            d2_out[:, units] = (d_second * mine).astype(BF)
            h_grad[:, units] = (hidden * both).astype(BF)
            d1_grad[:, units] = (d_first * both).astype(BF)
            d2_grad[:, units] = (d_second * both).astype(BF)
        dots[...] = total


def results_kernel(swapped, sel, hid, d1, d2, wg, wu, wd, *pieces):
    down = wd[...].reshape(-1, wd.shape[-1])
    out = jnp.dot(hid[...], down, preferred_element_type=F32)
    grad = lax.dot_general(d1[...], two(wg), NT, preferred_element_type=F32)
    grad += lax.dot_general(d2[...], two(wu), NT, preferred_element_type=F32)
    for block, (piece, row) in enumerate(places(swapped)):
        here = slice(32 * block, 32 * block + 32)
        pieces[piece][row : row + 32, :] = out[here].astype(BF)
        pieces[piece][row + 32 : row + 64, :] = grad[here].astype(BF)


def grads_kernel(sel, *refs):
    own, other = refs[:8], refs[8:16]
    hid, d1, d2 = refs[16:19]
    grad_gate, grad_up, grad_down = refs[19:22]

    def form(rows, swapped):
        tok = rows_of(rows, swapped, False, 32)
        cot = rows_of(rows, swapped, True, 32)
        gate = lax.dot_general(tok, d1[...], TN, preferred_element_type=F32).astype(BF)
        up = lax.dot_general(tok, d2[...], TN, preferred_element_type=F32).astype(BF)
        down = lax.dot_general(hid[...], cot, TN, preferred_element_type=F32).astype(BF)
        for slot in range(2):
            units = slice(128 * slot, 128 * slot + 128)
            grad_gate[slot, 0, 0] = gate[:, units]
            grad_up[slot, 0, 0] = up[:, units]
            grad_down[slot] = down[units]

    @pl.when(pl.program_id(0) == 0)
    def _():
        form(own, False)

    @pl.when(pl.program_id(0) == 1)
    def _():
        form(other, True)


def whole(shape):
    return pl.BlockSpec(shape, lambda *_: (0,) * len(shape))


def weight_specs(width):
    up_spec = pl.BlockSpec((2, 1, 1, width, 128), lambda k, sel: (0, k, sel[0], 0, 0))
    down_spec = pl.BlockSpec((2, 128, width), lambda k, sel: (0, 0, 2 * k + sel[0]))
    return [up_spec, up_spec, down_spec]


def params():
    return pltpu.CompilerParams(vmem_limit_bytes=48 * 2**20)


def own_half(sel, rows, weights):
    width = rows[0].shape[1] // STEPS
    row_spec = pl.BlockSpec((128, width), lambda k, sel: (0, k))
    return pl.pallas_call(
        own_half_kernel,
        grid_spec=pltpu.PrefetchScalarGridSpec(
            num_scalar_prefetch=1,
            grid=(STEPS,),
            in_specs=[row_spec] * 8 + weight_specs(width),
            out_specs=[whole((512, 256))] * 3,
        ),
        out_shape=[jax.ShapeDtypeStruct((512, 256), F32)] * 3,
        compiler_params=params(),
        cost_estimate=pl.CostEstimate(
            flops=2 * 512 * 768 * width * STEPS, bytes_accessed=13 * 2**20, transcendentals=0
        ),
        name="own_half",
    )(sel, *rows, *weights)


def other_half(sel, rows, weights, sums, gains):
    width = rows[0].shape[1] // STEPS
    row_spec = pl.BlockSpec((128, width), lambda k, sel: (0, k))
    return pl.pallas_call(
        other_half_kernel,
        grid_spec=pltpu.PrefetchScalarGridSpec(
            num_scalar_prefetch=1,
            grid=(STEPS,),
            in_specs=[row_spec] * 8
            + weight_specs(width)
            + [whole((512, 256))] * 3
            + [whole((512, 128))],
            out_specs=[whole((512, 256))] * 6 + [whole((512, 128))],
            scratch_shapes=[pltpu.VMEM((512, 256), F32)] * 3,
        ),
        out_shape=[jax.ShapeDtypeStruct((512, 256), BF)] * 6
        + [jax.ShapeDtypeStruct((512, 128), F32)],
        compiler_params=params(),
        cost_estimate=pl.CostEstimate(
            flops=2 * 512 * 768 * width * STEPS, bytes_accessed=15 * 2**20, transcendentals=512 * 256
        ),
        name="other_half",
    )(sel, *rows, *weights, *sums, gains)


def results(swapped, sel, hid, d1, d2, weights, half):
    width = half // STEPS
    return pl.pallas_call(
        functools.partial(results_kernel, swapped),
        grid_spec=pltpu.PrefetchScalarGridSpec(
            num_scalar_prefetch=1,
            grid=(STEPS,),
            in_specs=[whole((512, 256))] * 3 + weight_specs(width),
            out_specs=[pl.BlockSpec((128, width), lambda k, sel: (0, k))] * 8,
        ),
        out_shape=[jax.ShapeDtypeStruct((128, half), BF)] * 8,
        compiler_params=params(),
        cost_estimate=pl.CostEstimate(
            flops=2 * 512 * 768 * half, bytes_accessed=14 * 2**20, transcendentals=0
        ),
        name="results_other" if swapped else "results_own",
    )(sel, hid, d1, d2, *weights)


def weight_grads(core, own, other, hid, d1, d2):
    half = own[0].shape[1]
    width = half // STEPS
    place = lambda p, k, sel: (0, k, sel[p], 0, 0)
    up_spec = pl.BlockSpec((2, 1, 1, width, 128), place)
    down_spec = pl.BlockSpec((2, 128, width), lambda p, k, sel: (0, 0, 2 * k + sel[p]))
    first_rows = pl.BlockSpec((128, width), lambda p, k, sel: (0, jnp.where(p == 0, k, STEPS - 1)))
    last_rows = pl.BlockSpec((128, width), lambda p, k, sel: (0, jnp.where(p == 0, 0, k)))
    up_shape = jax.ShapeDtypeStruct((2, STEPS, 2, width, 128), BF)
    return pl.pallas_call(
        grads_kernel,
        grid_spec=pltpu.PrefetchScalarGridSpec(
            num_scalar_prefetch=1,
            grid=(2, STEPS),
            in_specs=[first_rows] * 8 + [last_rows] * 8 + [whole((512, 256))] * 3,
            out_specs=[up_spec, up_spec, down_spec],
        ),
        out_shape=[up_shape, up_shape, jax.ShapeDtypeStruct((2, 128, 2 * half), BF)],
        compiler_params=params(),
        cost_estimate=pl.CostEstimate(
            flops=4 * 512 * 768 * half, bytes_accessed=26 * 2**20, transcendentals=0
        ),
        name="weight_grads",
    )(jnp.stack([core, 1 - core]), *own, *other, hid, d1, d2)


def gate_weights(logits, slot_expert, chosen):
    experts = logits.shape[1]
    held = jnp.arange(experts, dtype=jnp.int32)[:, None] == slot_expert[None, :]
    picked = jnp.sum(jnp.where(held[None], logits[:, :, None], 0.0), axis=1)
    sig = jnp.where(chosen, jax.nn.sigmoid(picked), 0.0)
    return ROUTE_SCALE * sig / jnp.sum(sig, axis=1, keepdims=True)


def add(*values):
    total = values[0].astype(F32)
    for value in values[1:]:
        total = total + value.astype(F32)
    return total.astype(BF)


def per_device(tokens, cotangent, gate_logits, route_slot, slot_expert, w_gate, w_up, w_down):
    tok, wide = tokens.shape
    half = wide // 2
    width = half // STEPS
    slots = slot_expert.shape[0]
    z, core, y, x = (lax.axis_index(a) for a in AXES)
    line = y * NX + x
    own_sel, other_sel = core[None], (1 - core)[None]
    weights = (
        w_gate.reshape(2, STEPS, 2, width, 128),
        w_up.reshape(2, STEPS, 2, width, 128),
        w_down,
    )

    def mine(rows):
        return jnp.where(
            core == 0, rows.reshape(tok, STEPS, 2, width)[:, :, 0], rows.reshape(tok, STEPS, 2, width)[:, :, 1]
        ).reshape(tok, half)

    own = jnp.concatenate([mine(tokens), mine(cotangent)], axis=0)
    minus, plus, far = send(own, inner(1)), send(own, inner(-1)), send(own, inner(2))
    a = jnp.concatenate([own, plus], axis=0)
    b = jnp.concatenate([minus, far], axis=0)
    a_minus, b_plus = send(a, outer(1)), send(b, outer(-1))
    b_minus, a_plus = send(b, outer(1)), send(a, outer(-1))
    a_far, b_far = send(a_minus, outer(1)), send(b_plus, outer(-1))
    rows = [a, b, a_plus, b_plus, a_minus, b_minus, a_far, b_far]
    rows_other = [send(piece, other_core()) for piece in rows]

    chosen = jnp.any(
        route_slot[:, :, None] == jnp.arange(slots, dtype=jnp.int32)[None, None, :], axis=1
    )
    gate, pull_back = jax.vjp(lambda lg: gate_weights(lg, slot_expert, chosen), gate_logits)
    all_gates = lax.all_gather(gate, ("y", "x"), tiled=False).reshape(NY * NX, tok, slots)
    ring = jnp.array(RING, jnp.int32)
    out_y = ((y + ring) % NY)[:, None] * NX + ((x + ring) % NX)[None, :]
    out_x = ((y + ring) % NY)[None, :] * NX + ((x + ring) % NX)[:, None]
    order = jnp.where(core == 0, out_y, out_x).reshape(-1)
    pick_line = order[:, None] == jnp.arange(NY * NX, dtype=jnp.int32)[None, :]
    columns = jnp.stack([2 * line, 2 * line + 1, 2 * (line ^ (NY * NX // 2)) + 1])
    pick_slot = jnp.arange(slots, dtype=jnp.int32)[:, None] == columns[None, :]
    cols = jnp.sum(jnp.where(pick_slot[None, None], all_gates[..., None], 0.0), axis=2)
    cols = jnp.sum(jnp.where(pick_line[:, :, None, None], cols[None], 0.0), axis=1)
    cols = cols.reshape(NY * NX * tok, 3)
    gains = jnp.stack([cols[:, 0], cols[:, 1], cols[:, 1] + cols[:, 2]], axis=1)
    gains = jnp.pad(gains, ((0, 0), (0, 125)))

    sums = own_half(own_sel, rows, weights)
    h_out, d1_out, d2_out, h_grad, d1_grad, d2_grad, dots = other_half(
        other_sel, rows_other, weights, sums, gains
    )

    away = results(True, other_sel, h_out, d1_out, d2_out, weights, half)
    here = results(False, own_sel, h_out, d1_out, d2_out, weights, half)
    got = [None] * 8
    for piece in (6, 7, 3, 4, 2, 5, 0, 1):
        got[piece] = send(away[piece], other_core())
    part = [None] * 8
    for piece in (6, 7, 3, 4):
        part[piece] = add(here[piece], got[piece])
    from_a, from_b = send(part[6], outer(1)), send(part[7], outer(-1))
    b_early, a_early = send(part[3], outer(1)), send(part[4], outer(-1))
    a_late = send(add(here[2], got[2], from_a), outer(1))
    b_late = send(add(here[5], got[5], from_b), outer(-1))

    def final(piece, early, late):
        f = here[piece].astype(F32) + got[piece].astype(F32)
        return f + early.astype(F32) + late.astype(F32)

    sum_a, sum_b = final(0, a_early, a_late), final(1, b_early, b_late)
    keep = sum_a[:64]
    to_plus, to_minus, to_far = (v.astype(BF) for v in (sum_a[64:], sum_b[:64], sum_b[64:]))
    total = add(
        keep, send(to_plus, inner(1)), send(to_minus, inner(-1)), send(to_far, inner(2))
    )

    def block_for(by):
        return lax.dynamic_slice(total, (0, (z + by) % NZ * width), (64, width))

    last = add(
        block_for(0),
        send(block_for(1), along_z(1)),
        send(block_for(3), along_z(-1)),
        send(block_for(2), along_z(2)),
    )
    mixed, grad_tokens = last[:tok], last[tok:]

    grads = weight_grads(core, rows, rows_other, h_grad, d1_grad, d2_grad)

    dots = dots[:, :2].reshape(NY * NX, tok, 2)
    home = jnp.sum(jnp.where(pick_line[:, :, None, None], dots[:, None], 0.0), axis=0)
    home = lax.all_to_all(home, ("y", "x"), split_axis=0, concat_axis=0, tiled=True)
    home = jnp.transpose(home, (1, 0, 2)).reshape(tok, slots)
    home = lax.psum(home, ("z", "c"))
    grad_logits = pull_back(home)[0]
    return (
        mixed,
        grad_tokens,
        grad_logits,
        grads[0].reshape(w_gate.shape),
        grads[1].reshape(w_up.shape),
        grads[2],
    )


def solution(mesh):
    split = Mesh(mesh.devices.reshape(NZ, NC, NY, NX), AXES)
    local, group = ("y", "x"), ("z", "c")
    return jax.shard_map(
        per_device,
        mesh=split,
        in_specs=(
            P(local, None),
            P(local, None),
            P(local, None),
            P(local, None),
            P(),
            P(local, None, group),
            P(local, None, group),
            P(local, group, None),
        ),
        out_specs=(
            P(local, group),
            P(local, group),
            P(local, None),
            P(local, None, group),
            P(local, None, group),
            P(local, group, None),
        ),
        check_vma=False,
    )
```

time: 621 us -> 237 us (0.38)
  waiting for transfers between devices: 451 us -> 59.4 us
  matrix products: 50.6 us -> 0 us
  blocking collectives: 14 us -> 61.8 us
  Pallas kernels: 0 us -> 45.2 us
  other arithmetic: 29 us -> 12.5 us
  between operations: 14.5 us -> 1.33 us
  local copies, waits for them, and re-layouts: 25.2 us -> 14.4 us
    all_to_all x4 -> x1, waiting for transfers between devices: 279 us -> 0.01 us  [per_device(): lax.all_to_all(home, ('y', 'x'), split_axis=0, concat_axis=0, tiled=True)]
    ppermute x3 -> x37, waiting for transfers between devices: 138 us -> 59.4 us  [send(): return lax.ppermute(value, AXES, pairs)]
    dot_general x22 -> x0, matrix products: 50.6 us -> none  [the longest x1 7.95 us: per_device(): lax.dot_general(placer, home_out, CONTRACT_ZERO, preferred_element_type=j...]
    pallas_call x0 -> x5, Pallas kernels: none -> 45.2 us  [the longest x1 15.1 us: weight_grads(): pl.pallas_call(grads_kernel, grid_spec=pltpu.PrefetchScalarGridSpec(num_s...]
    all_gather x0 -> x1, blocking collectives: none -> 37.1 us  [per_device(): lax.all_gather(gate, ('y', 'x'), tiled=False).reshape(NY * NX, tok, slots)]
    unnamed x4 -> x0, waiting for transfers between devices: 34.1 us -> none
    ppermute x3 -> x37, starting transfers between devices: 6.91 us -> 37.2 us  [send(): return lax.ppermute(value, AXES, pairs)]
    another operation x10 -> x4, other arithmetic: 27.2 us -> 1.79 us  [the longest x2 7.41 us: per_device(): grad_up = jnp.stack([grads_cold[1], joined[1]], axis=0)]
  transfers between devices with their start and end apart: 9 -> 38, of which waited for: 9 -> 10; matrix products, arithmetic and copies ran while one was open for 12% -> 5% of each run, Pallas kernels for 0% -> 13%
where the time goes in v1:
time: 237 us; the launch traced here: 235 us
  blocking collectives  61.8 us (26%)
  waiting for transfers between devices  59.4 us (25%)
  Pallas kernels  45.2 us (19%)
  starting transfers between devices  40.6 us (17%)
  local copies, waits for them, and re-layouts  14.4 us (6%)
  other arithmetic  12.5 us (5%)
    ppermute x37, waiting for transfers between devices, send(): return lax.ppermute(value, AXES, pairs)  59.4 us
    ppermute x37, starting transfers between devices, send(): return lax.ppermute(value, AXES, pairs)  37.2 us
    all_gather x1, blocking collectives, per_device(): lax.all_gather(gate, ('y', 'x'), tiled=False).reshape(NY * NX, tok, slots)  37.1 us
    psum x1, blocking collectives, per_device(): home = lax.psum(home, ('z', 'c'))  24.6 us
    pallas_call x1, Pallas kernels, weight_grads(): pl.pallas_call(grads_kernel, grid_spec=pltpu.PrefetchScalarGridSpec(num_s...  15.1 us
    pallas_call x2, Pallas kernels, results(): pl.pallas_call(functools.partial(results_kernel, swapped), grid_spec=pltp...  14.5 us
    unnamed x73, local copies, waits for them, and re-layouts  9.3 us
    pallas_call x1, Pallas kernels, other_half(): pl.pallas_call(other_half_kernel, grid_spec=pltpu.PrefetchScalarGridSpec(...  8.19 us
  transfers between devices with their start and end apart: 38, of which 10 were waited for; matrix products, arithmetic and copies ran while one was open for 5% of the time, Pallas kernels for 13%

profile of v1, /device:TPU:0, one launch (start us, length us, event | category | flops | bytes accessed | tf_op | source)
XLA Modules:
  0.0 235.2 jit_solution(2000192159587193699)
XLA Ops:
  5.9 2.7 %collective-permute-start.3 = (bf16[64,3584]{1,0:T(8,128)(2,1)S(1)}, bf16[64,3584]{1,0:T(8,128)(2,1)S(1)}, u32[]{:S(2)}, u32[]{:S(2)}) collective-permute-start(bf16[64,3584]{1,0:T(8,128)(2,1)S(1)} %get-tuple-element.91), channel_id=1, source_target_pairs={{0,2},{1,3},{2,0},{3,1},{4,6},{5,7},{6,4},{7,5},{8,10},{9,11},{10,... | collective-permute-start | bytes 1376264 | tf_op jit(solution)/shard_map/ppermute | solution.py:51
  10.1 4.0 %collective-permute-done.2 = bf16[64,3584]{1,0:T(8,128)(2,1)S(1)} collective-permute-done((bf16[64,3584]{1,0:T(8,128)(2,1)S(1)}, bf16[64,3584]{1,0:T(8,128)(2,1)S(1)}, u32[]{:S(2)}, u32[]{:S(2)}) %collective-permute-start.2) | collective-permute-done | bytes 458784 | tf_op jit(solution)/shard_map/ppermute | solution.py:51
  14.1 5.9 %collective-permute-done.3 = bf16[64,3584]{1,0:T(8,128)(2,1)S(1)} collective-permute-done((bf16[64,3584]{1,0:T(8,128)(2,1)S(1)}, bf16[64,3584]{1,0:T(8,128)(2,1)S(1)}, u32[]{:S(2)}, u32[]{:S(2)}) %collective-permute-start.3) | collective-permute-done | bytes 458784 | tf_op jit(solution)/shard_map/ppermute | solution.py:51
  20.1 3.1 %collective-permute-start.7 = (bf16[128,3584]{1,0:T(8,128)(2,1)S(1)}, bf16[128,3584]{1,0:T(8,128)(2,1)}, u32[]{:S(2)}, u32[]{:S(2)}) collective-permute-start(bf16[128,3584]{1,0:T(8,128)(2,1)S(1)} %constant_dynamic-update-slice_fusion.5.refs_1_), channel_id=1, source_target_pairs={{0,12},{1,13},{2,14},{3,15},{4,0},{5,1},{6,2},{7,3},{8,4},{9,5},{1... | collective-permute-start | bytes 2752520 | tf_op jit(solution)/shard_map/ppermute | solution.py:51
  24.4 3.2 %collective-permute-start.5 = (bf16[128,3584]{1,0:T(8,128)(2,1)S(1)}, bf16[128,3584]{1,0:T(8,128)(2,1)}, u32[]{:S(2)}, u32[]{:S(2)}) collective-permute-start(bf16[128,3584]{1,0:T(8,128)(2,1)S(1)} %constant_dynamic-update-slice_fusion.2.refs_0_), channel_id=1, source_target_pairs={{0,12},{1,13},{2,14},{3,15},{4,0},{5,1},{6,2},{7,3},{8,4},{9,5},{1... | collective-permute-start | bytes 2752520 | tf_op jit(solution)/shard_map/ppermute | solution.py:51
  28.3 37.1 %all_gather.4 = f32[16,32,32]{2,1,0:T(8,128)S(1)} all-gather(f32[1,32,32]{2,1,0:T(8,128)S(1)} %bitcast_divide_fusion), channel_id=1, replica_groups=mesh['z'=4,'c'=2,'y'=4,'x'=4] {'y','x'}, dimensions={0}, use_global_device_ids=true | all-gather | bytes 69632 | tf_op jit(solution)/shard_map/all_gather | solution.py:331
  70.2 9.4 %collective-permute-done.15.refs_7_ = bf16[128,3584]{1,0:T(8,128)(2,1)} collective-permute-done((bf16[128,3584]{1,0:T(8,128)(2,1)}, bf16[128,3584]{1,0:T(8,128)(2,1)}, u32[]{:S(2)}, u32[]{:S(2)}) %collective-permute-start.15) | collective-permute-done | bytes 917536 | tf_op jit(solution)/shard_map/ppermute | solution.py:51
  79.7 3.5 %collective-permute-done.13.refs_6_ = bf16[128,3584]{1,0:T(8,128)(2,1)} collective-permute-done((bf16[128,3584]{1,0:T(8,128)(2,1)}, bf16[128,3584]{1,0:T(8,128)(2,1)}, u32[]{:S(2)}, u32[]{:S(2)}) %collective-permute-start.13) | collective-permute-done | bytes 917536 | tf_op jit(solution)/shard_map/ppermute | solution.py:51
  84.6 7.4 %own_half.1 = (f32[512,256]{1,0:T(8,128)S(1)}, f32[512,256]{1,0:T(8,128)S(1)}, f32[512,256]{1,0:T(8,128)S(1)}) custom-call(s32[1]{0:T(128)} %bitcast.sel, bf16[128,3584]{1,0:T(8,128)(2,1)S(1)} %constant_dynamic-update-slice_fusion.2.refs_0_, bf16[128,3584]{1,0:T(8,128)(2,1)S(1)} %constant_dynamic-update-slice_fusion.5.refs_1_, ...), custom_call_target="tpu_custom_call" | custom-call | flops 2818572288 | bytes 13631488 | tf_op jit(solution)/shard_map/own_half/pallas_call | solution.py:196
  92.1 8.2 %other_half.1 = (bf16[512,256]{1,0:T(8,128)(2,1)S(1)}, bf16[512,256]{1,0:T(8,128)(2,1)S(1)}, bf16[512,256]{1,0:T(8,128)(2,1)S(1)}, bf16[512,256]{1,0:T(8,128)(2,...) custom-call(s32[1]{0:T(128)} %bitcast.1.sel, ...), custom_call_target="tpu_custom_call" | custom-call | flops 2818572288 | bytes 15728640 | tf_op jit(solution)/shard_map/other_half/pallas_call | solution.py:216
  103.1 7.2 %results_other.1 = (bf16[128,3584]{1,0:T(8,128)(2,1)S(1)}, bf16[128,3584]{1,0:T(8,128)(2,1)S(1)}, bf16[128,3584]{1,0:T(8,128)(2,1)S(1)}, bf16[128,3584]{1,0:T(8,...) custom-call(s32[1]{0:T(128)} %bitcast.1.sel, ...), custom_call_target="tpu_custom_call" | custom-call | flops 2818572288 | bytes 14680064 | tf_op jit(solution)/shard_map/results_other/pallas_call | solution.py:240
  116.2 3.5 %all-to-all-start = ((f32[16,32,2]{1,2,0:T(2,128)}), f32[16,32,2]{1,2,0:T(2,128)S(1)}, u32[]{:S(2)}, u32[]{:S(2)}) async-start(f32[16,32,2]{1,2,0:T(2,128)} %copy.73), calls=%async_computation | async-start | bytes 32768 | tf_op jit(solution)/shard_map/all_to_all | solution.py:389
  119.8 7.3 %results_own.1 = (bf16[128,3584]{1,0:T(8,128)(2,1)S(1)}, bf16[128,3584]{1,0:T(8,128)(2,1)S(1)}, bf16[128,3584]{1,0:T(8,128)(2,1)S(1)}, bf16[128,3584]{1,0:T(8,12...) custom-call(s32[1]{0:T(128)} %bitcast.sel, ...), custom_call_target="tpu_custom_call" | custom-call | flops 2818572288 | bytes 14680064 | tf_op jit(solution)/shard_map/results_own/pallas_call | solution.py:240
  132.5 3.0 %collective-permute-start.30 = (bf16[128,3584]{1,0:T(8,128)(2,1)S(1)}, bf16[128,3584]{1,0:T(8,128)(2,1)S(1)}, u32[]{:S(2)}, u32[]{:S(2)}) collective-permute-start(bf16[128,3584]{1,0:T(8,128)(2,1)S(1)} %add_convert_fusion.2), channel_id=1, source_target_pairs={{0,12},{1,13},{2,14},{3,15},{4,0},{5,1},{6,2},{7,3},{8,4},{9,5},{1... | collective-permute-start | bytes 2752520 | tf_op jit(solution)/shard_map/ppermute | solution.py:51
  135.8 10.6 %collective-permute-done.30 = bf16[128,3584]{1,0:T(8,128)(2,1)S(1)} collective-permute-done((bf16[128,3584]{1,0:T(8,128)(2,1)S(1)}, bf16[128,3584]{1,0:T(8,128)(2,1)S(1)}, u32[]{:S(2)}, u32[]{:S(2)}) %collective-permute-start.30) | collective-permute-done | bytes 917536 | tf_op jit(solution)/shard_map/ppermute | solution.py:51
  149.1 2.6 %collective-permute-start.19 = (bf16[128,3584]{1,0:T(8,128)(2,1)S(1)}, bf16[128,3584]{1,0:T(8,128)(2,1)S(1)}, u32[]{:S(2)}, u32[]{:S(2)}) collective-permute-start(bf16[128,3584]{1,0:T(8,128)(2,1)S(1)} %add_convert_fusion.6), channel_id=1, source_target_pairs={{0,12},{1,13},{2,14},{3,15},{4,0},{5,1},{6,2},{7,3},{8,4},{9,5},{1... | collective-permute-start | bytes 2752520 | tf_op jit(solution)/shard_map/ppermute | solution.py:51
  151.7 9.8 %collective-permute-done.22 = bf16[128,3584]{1,0:T(8,128)(2,1)S(1)} collective-permute-done((bf16[128,3584]{1,0:T(8,128)(2,1)S(1)}, bf16[128,3584]{1,0:T(8,128)(2,1)S(1)}, u32[]{:S(2)}, u32[]{:S(2)}) %collective-permute-start.22) | collective-permute-done | bytes 917536 | tf_op jit(solution)/shard_map/ppermute | solution.py:51
  164.1 10.7 %collective-permute-done.31 = bf16[128,3584]{1,0:T(8,128)(2,1)S(1)} collective-permute-done((bf16[128,3584]{1,0:T(8,128)(2,1)S(1)}, bf16[128,3584]{1,0:T(8,128)(2,1)S(1)}, u32[]{:S(2)}, u32[]{:S(2)}) %collective-permute-start.31) | collective-permute-done | bytes 917536 | tf_op jit(solution)/shard_map/ppermute | solution.py:51
  176.6 2.8 %collective-permute-start.32 = (bf16[64,3584]{1,0:T(8,128)(2,1)S(1)}, bf16[64,3584]{1,0:T(8,128)(2,1)}, u32[]{:S(2)}, u32[]{:S(2)}) collective-permute-start(bf16[64,3584]{1,0:T(8,128)(2,1)S(1)} %get-tuple-element.82), channel_id=1, source_target_pairs={{0,3},{1,0},{2,1},{3,2},{4,7},{5,4},{6,5},{7,6},{8,11},{9,8},{10,9... | collective-permute-start | bytes 1376264 | tf_op jit(solution)/shard_map/ppermute | solution.py:51
  182.9 15.1 %weight_grads.1 = (bf16[2,4,2,896,128]{4,3,2,1,0:T(8,128)(2,1)}, bf16[2,4,2,896,128]{4,3,2,1,0:T(8,128)(2,1)}, bf16[2,128,7168]{2,1,0:T(8,128)(2,1)}) custom-call(s32[2]{0:T(128)S(1)} %pad_add_fusion.1.sel, bf16[128,3584]{1,0:T(8,128)(2,1)S(1)} %constant_dynamic-update-slice_fusion.2.refs_0_, ...), custom_call_target="tpu_custom_call" | custom-call | flops 5637144576 | bytes 27262976 | tf_op jit(solution)/shard_map/weight_grads/pallas_call | solution.py:266
  198.1 24.6 %psum.7 = f32[32,32]{1,0:T(8,128)S(1)} all-reduce(f32[32,32]{1,0:T(8,128)S(1)} %copy.74), channel_id=1, replica_groups=mesh['z'=4,'c'=2,'y'=4,'x'=4] {'z','c'}, use_global_device_ids=true, to_apply=%region_6.7 | all-reduce | flops 1024 | bytes 8192 | tf_op jit(solution)/shard_map/psum | solution.py:391
  225.0 3.2 %collective-permute-start.35 = (bf16[64,896]{1,0:T(8,128)(2,1)S(1)}, bf16[64,896]{1,0:T(8,128)(2,1)S(1)}, u32[]{:S(2)}, u32[]{:S(2)}) collective-permute-start(bf16[64,896]{1,0:T(8,128)(2,1)S(1)} %get-tuple-element.86), channel_id=1, source_target_pairs={{0,96},{1,97},{2,98},{3,99},{4,100},{5,101},{6,102},{7,103},{8,104... | collective-permute-start | bytes 344072 | tf_op jit(solution)/shard_map/ppermute | solution.py:51
  229.1 2.4 %collective-permute-done.34 = bf16[64,896]{1,0:T(8,128)(2,1)S(1)} collective-permute-done((bf16[64,896]{1,0:T(8,128)(2,1)S(1)}, bf16[64,896]{1,0:T(8,128)(2,1)S(1)}, u32[]{:S(2)}, u32[]{:S(2)}) %collective-permute-start.34) | collective-permute-done | bytes 114720 | tf_op jit(solution)/shard_map/ppermute | solution.py:51
  231.8 2.7 %collective-permute-done.36 = bf16[64,896]{1,0:T(8,128)(2,1)S(1)} collective-permute-done((bf16[64,896]{1,0:T(8,128)(2,1)S(1)}, bf16[64,896]{1,0:T(8,128)(2,1)S(1)}, u32[]{:S(2)}, u32[]{:S(2)}) %collective-permute-start.36) | collective-permute-done | bytes 114720 | tf_op jit(solution)/shard_map/ppermute | solution.py:51
  (185 shorter events, 44.0 us)
Async XLA Ops:
  5.9 14.1 %collective-permute-start.3 = (bf16[64,3584]{1,0:T(8,128)(2,1)S(1)}, bf16[64,3584]{1,0:T(8,128)(2,1)S(1)}, u32[]{:S(2)}, u32[]{:S(2)}) collective-permute-start(bf16[64,3584]{1,0:T(8,128)(2,1)S(1)} %get-tuple-element.91), channel_id=1, source_target_pairs={{0,2},{1,3},{2,0},{3,1},{4,6},{5,7},{6,4},{7,5},{8,10},{9,11},{10,... | collective-permute-start | bytes 1376264 | tf_op jit(solution)/shard_map/ppermute | solution.py:51
  8.7 14.5 %collective-permute-start = (bf16[64,3584]{1,0:T(8,128)(2,1)S(1)}, bf16[64,3584]{1,0:T(8,128)(2,1)S(1)}, u32[]{:S(2)}, u32[]{:S(2)}) collective-permute-start(bf16[64,3584]{1,0:T(8,128)(2,1)S(1)} %get-tuple-element.91), channel_id=1, source_target_pairs={{0,3},{1,0},{2,1},{3,2},{4,7},{5,4},{6,5},{7,6},{8,11},{9,8},{10,9... | collective-permute-start | bytes 1376264 | tf_op jit(solution)/shard_map/ppermute | solution.py:51
  20.1 45.4 %collective-permute-start.7 = (bf16[128,3584]{1,0:T(8,128)(2,1)S(1)}, bf16[128,3584]{1,0:T(8,128)(2,1)}, u32[]{:S(2)}, u32[]{:S(2)}) collective-permute-start(bf16[128,3584]{1,0:T(8,128)(2,1)S(1)} %constant_dynamic-update-slice_fusion.5.refs_1_), channel_id=1, source_target_pairs={{0,12},{1,13},{2,14},{3,15},{4,0},{5,1},{6,2},{7,3},{8,4},{9,5},{1... | collective-permute-start | bytes 2752520 | tf_op jit(solution)/shard_map/ppermute | solution.py:51
  23.2 42.8 %collective-permute-start.9 = (bf16[128,3584]{1,0:T(8,128)(2,1)S(1)}, bf16[128,3584]{1,0:T(8,128)(2,1)}, u32[]{:S(2)}, u32[]{:S(2)}) collective-permute-start(bf16[128,3584]{1,0:T(8,128)(2,1)S(1)} %constant_dynamic-update-slice_fusion.2.refs_0_), channel_id=1, source_target_pairs={{0,4},{1,5},{2,6},{3,7},{4,8},{5,9},{6,10},{7,11},{8,12},{9,13},{1... | collective-permute-start | bytes 2752520 | tf_op jit(solution)/shard_map/ppermute | solution.py:51
  24.3 43.9 %collective-permute-start.11 = (bf16[128,3584]{1,0:T(8,128)(2,1)S(1)}, bf16[128,3584]{1,0:T(8,128)(2,1)}, u32[]{:S(2)}, u32[]{:S(2)}) collective-permute-start(bf16[128,3584]{1,0:T(8,128)(2,1)S(1)} %constant_dynamic-update-slice_fusion.5.refs_1_), channel_id=1, source_target_pairs={{0,4},{1,5},{2,6},{3,7},{4,8},{5,9},{6,10},{7,11},{8,12},{9,13},{1... | collective-permute-start | bytes 2752520 | tf_op jit(solution)/shard_map/ppermute | solution.py:51
  24.4 43.8 %collective-permute-start.5 = (bf16[128,3584]{1,0:T(8,128)(2,1)S(1)}, bf16[128,3584]{1,0:T(8,128)(2,1)}, u32[]{:S(2)}, u32[]{:S(2)}) collective-permute-start(bf16[128,3584]{1,0:T(8,128)(2,1)S(1)} %constant_dynamic-update-slice_fusion.2.refs_0_), channel_id=1, source_target_pairs={{0,12},{1,13},{2,14},{3,15},{4,0},{5,1},{6,2},{7,3},{8,4},{9,5},{1... | collective-permute-start | bytes 2752520 | tf_op jit(solution)/shard_map/ppermute | solution.py:51
  68.2 15.0 %collective-permute-start.8 = (bf16[128,3584]{1,0:T(8,128)(2,1)}, bf16[128,3584]{1,0:T(8,128)(2,1)}, u32[]{:S(2)}, u32[]{:S(2)}) collective-permute-start(bf16[128,3584]{1,0:T(8,128)(2,1)} %collective-permute-done.7.refs_3_), channel_id=1, source_target_pairs={{0,16},{1,17},{2,18},{3,19},{4,20},{5,21},{6,22},{7,23},{8,24},{9,... | collective-permute-start | bytes 2752520 | tf_op jit(solution)/shard_map/ppermute | solution.py:51
  68.2 15.0 %collective-permute-start.13 = (bf16[128,3584]{1,0:T(8,128)(2,1)}, bf16[128,3584]{1,0:T(8,128)(2,1)}, u32[]{:S(2)}, u32[]{:S(2)}) collective-permute-start(bf16[128,3584]{1,0:T(8,128)(2,1)} %collective-permute-done.9.refs_4_), channel_id=1, source_target_pairs={{0,4},{1,5},{2,6},{3,7},{4,8},{5,9},{6,10},{7,11},{8,12},{9,13},{1... | collective-permute-start | bytes 2752520 | tf_op jit(solution)/shard_map/ppermute | solution.py:51
  68.9 23.1 %collective-permute-start.10 = (bf16[128,3584]{1,0:T(8,128)(2,1)}, bf16[128,3584]{1,0:T(8,128)(2,1)}, u32[]{:S(2)}, u32[]{:S(2)}) collective-permute-start(bf16[128,3584]{1,0:T(8,128)(2,1)} %collective-permute-done.9.refs_4_), channel_id=1, source_target_pairs={{0,16},{1,17},{2,18},{3,19},{4,20},{5,21},{6,22},{7,23},{8,24},{9,... | collective-permute-start | bytes 2752520 | tf_op jit(solution)/shard_map/ppermute | solution.py:51
  70.1 21.9 %collective-permute-start.12 = (bf16[128,3584]{1,0:T(8,128)(2,1)}, bf16[128,3584]{1,0:T(8,128)(2,1)}, u32[]{:S(2)}, u32[]{:S(2)}) collective-permute-start(bf16[128,3584]{1,0:T(8,128)(2,1)} %collective-permute-done.11.refs_5_), channel_id=1, source_target_pairs={{0,16},{1,17},{2,18},{3,19},{4,20},{5,21},{6,22},{7,23},{8,24},{9,... | collective-permute-start | bytes 2752520 | tf_op jit(solution)/shard_map/ppermute | solution.py:51
  114.2 14.8 %collective-permute-start.29 = (bf16[128,3584]{1,0:T(8,128)(2,1)}, bf16[128,3584]{1,0:T(8,128)(2,1)}, u32[]{:S(2)}, u32[]{:S(2)}) collective-permute-start(bf16[128,3584]{1,0:T(8,128)(2,1)} %get-tuple-element.56), channel_id=1, source_target_pairs={{0,16},{1,17},{2,18},{3,19},{4,20},{5,21},{6,22},{7,23},{8,24},{9,... | collective-permute-start | bytes 2752520 | tf_op jit(solution)/shard_map/ppermute | solution.py:51
  114.7 21.0 %collective-permute-start.28 = (bf16[128,3584]{1,0:T(8,128)(2,1)}, bf16[128,3584]{1,0:T(8,128)(2,1)}, u32[]{:S(2)}, u32[]{:S(2)}) collective-permute-start(bf16[128,3584]{1,0:T(8,128)(2,1)} %get-tuple-element.54), channel_id=1, source_target_pairs={{0,16},{1,17},{2,18},{3,19},{4,20},{5,21},{6,22},{7,23},{8,24},{9,... | collective-permute-start | bytes 2752520 | tf_op jit(solution)/shard_map/ppermute | solution.py:51
  114.8 49.0 %collective-permute-start.25 = (bf16[128,3584]{1,0:T(8,128)(2,1)}, bf16[128,3584]{1,0:T(8,128)(2,1)}, u32[]{:S(2)}, u32[]{:S(2)}) collective-permute-start(bf16[128,3584]{1,0:T(8,128)(2,1)} %copy-done.5), channel_id=1, source_target_pairs={{0,16},{1,17},{2,18},{3,19},{4,20},{5,21},{6,22},{7,23},{8,24},{9,... | collective-permute-start | bytes 2752520 | tf_op jit(solution)/shard_map/ppermute | solution.py:51
  115.2 15.4 %collective-permute-start.18 = (bf16[128,3584]{1,0:T(8,128)(2,1)}, bf16[128,3584]{1,0:T(8,128)(2,1)}, u32[]{:S(2)}, u32[]{:S(2)}) collective-permute-start(bf16[128,3584]{1,0:T(8,128)(2,1)} %copy-done.8), channel_id=1, source_target_pairs={{0,16},{1,17},{2,18},{3,19},{4,20},{5,21},{6,22},{7,23},{8,24},{9,... | collective-permute-start | bytes 2752520 | tf_op jit(solution)/shard_map/ppermute | solution.py:51
  116.2 81.8 %all-to-all-start = ((f32[16,32,2]{1,2,0:T(2,128)}), f32[16,32,2]{1,2,0:T(2,128)S(1)}, u32[]{:S(2)}, u32[]{:S(2)}) async-start(f32[16,32,2]{1,2,0:T(2,128)} %copy.73), calls=%async_computation | async-start | bytes 32768 | tf_op jit(solution)/shard_map/all_to_all | solution.py:389
  129.0 20.1 %collective-permute-start.20 = (bf16[128,3584]{1,0:T(8,128)(2,1)S(1)}, bf16[128,3584]{1,0:T(8,128)(2,1)S(1)}, u32[]{:S(2)}, u32[]{:S(2)}) collective-permute-start(bf16[128,3584]{1,0:T(8,128)(2,1)S(1)} %copy-done.7), channel_id=1, source_target_pairs={{0,16},{1,17},{2,18},{3,19},{4,20},{5,21},{6,22},{7,23},{8,24},{9,... | collective-permute-start | bytes 2752520 | tf_op jit(solution)/shard_map/ppermute | solution.py:51
  130.7 49.5 %collective-permute-start.17 = (bf16[128,3584]{1,0:T(8,128)(2,1)S(1)}, bf16[128,3584]{1,0:T(8,128)(2,1)S(1)}, u32[]{:S(2)}, u32[]{:S(2)}) collective-permute-start(bf16[128,3584]{1,0:T(8,128)(2,1)S(1)} %copy-done.4), channel_id=1, source_target_pairs={{0,16},{1,17},{2,18},{3,19},{4,20},{5,21},{6,22},{7,23},{8,24},{9,... | collective-permute-start | bytes 2752520 | tf_op jit(solution)/shard_map/ppermute | solution.py:51
  135.7 28.4 %collective-permute-start.27 = (bf16[128,3584]{1,0:T(8,128)(2,1)S(1)}, bf16[128,3584]{1,0:T(8,128)(2,1)S(1)}, u32[]{:S(2)}, u32[]{:S(2)}) collective-permute-start(bf16[128,3584]{1,0:T(8,128)(2,1)S(1)} %add_convert_fusion.3), channel_id=1, source_target_pairs={{0,4},{1,5},{2,6},{3,7},{4,8},{5,9},{6,10},{7,11},{8,12},{9,13},{1... | collective-permute-start | bytes 2752520 | tf_op jit(solution)/shard_map/ppermute | solution.py:51
  146.4 15.1 %collective-permute-start.22 = (bf16[128,3584]{1,0:T(8,128)(2,1)S(1)}, bf16[128,3584]{1,0:T(8,128)(2,1)S(1)}, u32[]{:S(2)}, u32[]{:S(2)}) collective-permute-start(bf16[128,3584]{1,0:T(8,128)(2,1)S(1)} %add_convert_fusion.5), channel_id=1, source_target_pairs={{0,4},{1,5},{2,6},{3,7},{4,8},{5,9},{6,10},{7,11},{8,12},{9,13},{1... | collective-permute-start | bytes 2752520 | tf_op jit(solution)/shard_map/ppermute | solution.py:51
  149.1 31.0 %collective-permute-start.19 = (bf16[128,3584]{1,0:T(8,128)(2,1)S(1)}, bf16[128,3584]{1,0:T(8,128)(2,1)S(1)}, u32[]{:S(2)}, u32[]{:S(2)}) collective-permute-start(bf16[128,3584]{1,0:T(8,128)(2,1)S(1)} %add_convert_fusion.6), channel_id=1, source_target_pairs={{0,12},{1,13},{2,14},{3,15},{4,0},{5,1},{6,2},{7,3},{8,4},{9,5},{1... | collective-permute-start | bytes 2752520 | tf_op jit(solution)/shard_map/ppermute | solution.py:51
  163.8 16.3 %collective-permute-start.23 = (bf16[128,3584]{1,0:T(8,128)(2,1)S(1)}, bf16[128,3584]{1,0:T(8,128)(2,1)S(1)}, u32[]{:S(2)}, u32[]{:S(2)}) collective-permute-start(bf16[128,3584]{1,0:T(8,128)(2,1)S(1)} %add_convert_fusion.4), channel_id=1, source_target_pairs={{0,4},{1,5},{2,6},{3,7},{4,8},{5,9},{6,10},{7,11},{8,12},{9,13},{1... | collective-permute-start | bytes 2752520 | tf_op jit(solution)/shard_map/ppermute | solution.py:51
  176.6 46.5 %collective-permute-start.32 = (bf16[64,3584]{1,0:T(8,128)(2,1)S(1)}, bf16[64,3584]{1,0:T(8,128)(2,1)}, u32[]{:S(2)}, u32[]{:S(2)}) collective-permute-start(bf16[64,3584]{1,0:T(8,128)(2,1)S(1)} %get-tuple-element.82), channel_id=1, source_target_pairs={{0,3},{1,0},{2,1},{3,2},{4,7},{5,4},{6,5},{7,6},{8,11},{9,8},{10,9... | collective-permute-start | bytes 1376264 | tf_op jit(solution)/shard_map/ppermute | solution.py:51
  179.3 43.7 %collective-permute-start.33 = (bf16[64,3584]{1,0:T(8,128)(2,1)S(1)}, bf16[64,3584]{1,0:T(8,128)(2,1)}, u32[]{:S(2)}, u32[]{:S(2)}) collective-permute-start(bf16[64,3584]{1,0:T(8,128)(2,1)S(1)} %get-tuple-element.83), channel_id=1, source_target_pairs={{0,2},{1,3},{2,0},{3,1},{4,6},{5,7},{6,4},{7,5},{8,10},{9,11},{10,... | collective-permute-start | bytes 1376264 | tf_op jit(solution)/shard_map/ppermute | solution.py:51
  182.0 41.1 %collective-permute-start.24 = (bf16[64,3584]{1,0:T(8,128)(2,1)S(1)}, bf16[64,3584]{1,0:T(8,128)(2,1)}, u32[]{:S(2)}, u32[]{:S(2)}) collective-permute-start(bf16[64,3584]{1,0:T(8,128)(2,1)S(1)} %slice.84), channel_id=1, source_target_pairs={{0,1},{1,2},{2,3},{3,0},{4,5},{5,6},{6,7},{7,4},{8,9},{9,10},{10,1... | collective-permute-start | bytes 1376264 | tf_op jit(solution)/shard_map/ppermute | solution.py:51
  (47 other events, 595.9 us)

commit v2 on v1

v2 whole, which is shorter than its diff:
```python
import functools

import jax
import jax.numpy as jnp
from jax import lax
from jax.experimental import pallas as pl
from jax.experimental.pallas import tpu as pltpu
from jax.sharding import Mesh
from jax.sharding import PartitionSpec as P

ROUTE_SCALE = 2.5
NZ, NC, NY, NX = 4, 2, 4, 4
AXES = ("z", "c", "y", "x")
STEPS = 4
BF, F32 = jnp.bfloat16, jnp.float32
NT = (((1,), (1,)), ((), ()))
TN = (((0,), (0,)), ((), ()))
RING = (0, 1, 3, 2)


def moves(step):
    pairs = []
    for z in range(NZ):
        for c in range(NC):
            for y in range(NY):
                for x in range(NX):
                    z2, c2, y2, x2 = step(z, c, y, x)
                    source = ((z * NC + c) * NY + y) * NX + x
                    target = ((z2 % NZ * NC + c2 % NC) * NY + y2 % NY) * NX + x2 % NX
                    pairs.append((source, target))
    return pairs


def outer(by):
    return moves(lambda z, c, y, x: (z, c, y + by, x) if c == 0 else (z, c, y, x + by))


def inner(by):
    return moves(lambda z, c, y, x: (z, c, y, x + by) if c == 0 else (z, c, y + by, x))


def along_z(by):
    return moves(lambda z, c, y, x: (z + by, c, y, x))


def other_core():
    return moves(lambda z, c, y, x: (z, c + 1, y, x))


def send(value, pairs):
    return lax.ppermute(value, AXES, pairs)


def joined(parts, axis=0):
    return jnp.concatenate(parts, axis=axis)


def rows_of(refs, blocks, second, first_piece=0):
    parts = []
    for outer_at, inner_at in blocks:
        row = 64 * (inner_at % 2) + (32 if second else 0)
        parts.append(refs[2 * outer_at + inner_at // 2 - first_piece][row : row + 32, :])
    return joined(parts)


def turned(blocks):
    return [(b, a) for a, b in blocks]


ALL = [(a, b) for a in range(4) for b in range(4)]
NEAR_OWN = [(a, b) for a in range(3) for b in range(4)]
FAR_OWN = [(3, b) for b in range(4)]
NEAR_OTHER = [(a, b) for a in range(4) for b in range(3)]
FAR_OTHER = [(a, 3) for a in range(4)]


def up_block(ref, k, half):
    return joined([ref[0, k, half], ref[1, k, half]], axis=1)


def down_block(ref, k, half, width):
    at = pl.multiple_of((2 * k + half) * width, 128)
    return ref[:, :, pl.ds(at, width)].reshape(-1, width)


def products(tok, cot, k, half, wg, wu, wd):
    first = jnp.dot(tok, up_block(wg, k, half), preferred_element_type=F32)
    second = jnp.dot(tok, up_block(wu, k, half), preferred_element_type=F32)
    down = down_block(wd, k, half, tok.shape[1])
    back = lax.dot_general(cot, down, NT, preferred_element_type=F32)
    return first, second, back


def pack_kernel(sel, tok, cot, packed):
    rows = tok.shape[0]
    packed[:rows] = tok[...]
    packed[rows:] = cot[...]


def pack_weights_kernel(sel, wg, wu, wd, wall, sems):
    away = sel[1]
    copies = []

    def copy(source, target):
        copies.append(pltpu.make_async_copy(source, target, sems.at[len(copies)]))
        copies[-1].start()

    for base, ref in ((0, wg), (56, wu)):
        for slot in range(2):
            for k in range(STEPS):
                copy(ref.at[slot, k, away], wall.at[pl.ds(base + (slot * STEPS + k) * 7, 7)])
    for k in range(STEPS):
        for q in range(7):
            at = pl.multiple_of((2 * k + away) * 896 + q * 128, 128)
            for slot in range(2):
                copy(wd.at[slot, :, pl.ds(at, 128)], wall.at[112 + 2 * (7 * k + q) + slot])
    for one in copies:
        one.wait()


def near_kernel(sel, *refs):
    own, other, (wg, wu, wd) = refs[:6], refs[6:12], refs[12:15]
    sums = refs[15:18]
    k = pl.program_id(0)
    a = products(
        rows_of(own, NEAR_OWN, False), rows_of(own, NEAR_OWN, True), k, sel[0], wg, wu, wd
    )
    there = turned(NEAR_OTHER)
    b = products(rows_of(other, there, False), rows_of(other, there, True), k, sel[1], wg, wu, wd)

    @pl.when(k == 0)
    def _():
        for ref in sums:
            ref[...] = jnp.zeros_like(ref)

    for ref, one, two in zip(sums, a, b):
        ref[:384] += one
        for out in range(4):
            ref[128 * out : 128 * out + 96] += two[96 * out : 96 * out + 96]


def far_kernel(sel, *refs):
    own, other, (wg, wu, wd) = refs[:2], refs[2:4], refs[4:7]
    start, gains = refs[7:10], refs[10]
    acts, acts_grad, dots = refs[11:14]
    sums = refs[14:17]
    width = own[0].shape[1] // STEPS
    a, b = None, None
    for k in range(STEPS):
        cols = pl.ds(k * width, width)
        mine = [ref.at[:, cols] for ref in own]
        there = [ref.at[:, cols] for ref in other]
        blocks = turned(FAR_OTHER)
        a_k = products(
            rows_of(mine, FAR_OWN, False, 6), rows_of(mine, FAR_OWN, True, 6), k, sel[0], wg, wu, wd
        )
        b_k = products(
            rows_of(there, blocks, False, 6), rows_of(there, blocks, True, 6), k, sel[1], wg, wu, wd
        )
        a = a_k if a is None else [u + v for u, v in zip(a, a_k)]
        b = b_k if b is None else [u + v for u, v in zip(b, b_k)]
    for ref, before, one, two in zip(sums, start, a, b):
        ref[...] = before[...]
        ref[384:] += one
        for out in range(4):
            ref[128 * out + 96 : 128 * out + 128] += two[32 * out : 32 * out + 32]
    lane = lax.broadcasted_iota(jnp.int32, dots.shape, 1)
    total = jnp.zeros(dots.shape, F32)
    for slot in range(2):
        units = slice(128 * slot, 128 * slot + 128)
        first, second, back = (ref[:, units] for ref in sums)
        mine = gains[:, slot : slot + 1]
        both = gains[:, 2 * slot : 2 * slot + 1]
        sig = jax.nn.sigmoid(first)
        silu = first * sig
        hidden = silu * second
        total = jnp.where(lane == slot, jnp.sum(hidden * back, axis=1, keepdims=True), total)
        d_first = back * second * sig * (1.0 + first * (1.0 - sig))
        d_second = back * silu
        for at, value in ((0, hidden), (256, d_first), (512, d_second)):
            units = slice(at + 128 * slot, at + 128 * slot + 128)
            acts[:, units] = (value * mine).astype(BF)
            acts_grad[:, units] = (value * both).astype(BF)
    dots[...] = total


def results_kernel(pieces, sel, acts, acts_other, wg, wu, wd, wall, *outs):
    half = sel[0]
    blocks = [(p // 2, 2 * (p % 2) + b) for p in pieces for b in range(2)]
    own = joined([acts[32 * (4 * a + b) : 32 * (4 * a + b) + 32, :] for a, b in blocks])
    other = joined([acts_other[32 * (4 * b + a) : 32 * (4 * b + a) + 32, :] for a, b in blocks])
    hidden = joined([own[:, :256], other[:, :256]], axis=1)
    grads = joined([own[:, 256:], other[:, 256:]], axis=1)
    width = outs[0].shape[1] // STEPS
    for k in range(STEPS):
        cols = slice(k * width, k * width + width)
        down = joined([wall[112 + 2 * (7 * k + q) : 114 + 2 * (7 * k + q)].reshape(256, 128) for q in range(7)], axis=1)
        down = joined([down_block(wd, k, half, width), down])
        up = [up_block(wg, k, half), up_block(wu, k, half)]
        for base in (0, 56):
            for slot in range(2):
                at = base + (slot * STEPS + k) * 7
                up.append(wall[at : at + 7].reshape(width, 128))
        out = jnp.dot(hidden, down, preferred_element_type=F32)
        grad = lax.dot_general(grads, joined(up, axis=1), NT, preferred_element_type=F32)
        for block in range(len(blocks)):
            here = slice(32 * block, 32 * block + 32)
            row = 64 * (block % 2)
            outs[block // 2][row : row + 32, cols] = out[here].astype(BF)
            outs[block // 2][row + 32 : row + 64, cols] = grad[here].astype(BF)


def grads_kernel(swapped, sel, *refs):
    rows, acts = refs[:8], refs[8]
    grad_gate, grad_up, grad_down = refs[-3:]
    blocks = turned(ALL) if swapped else ALL
    tok, cot = rows_of(rows, blocks, False), rows_of(rows, blocks, True)
    hid, d1, d2 = acts[:, :256], acts[:, 256:512], acts[:, 512:]
    gate = lax.dot_general(tok, d1, TN, preferred_element_type=F32).astype(BF)
    up = lax.dot_general(tok, d2, TN, preferred_element_type=F32).astype(BF)
    down = lax.dot_general(hid, cot, TN, preferred_element_type=F32).astype(BF)
    for slot in range(2):
        units = slice(128 * slot, 128 * slot + 128)
        grad_gate[slot, 0, 0] = gate[:, units]
        grad_up[slot, 0, 0] = up[:, units]
        grad_down[slot] = down[units]


VM = pl.BlockSpec(memory_space=pltpu.VMEM)
SM = pl.BlockSpec(memory_space=pltpu.SMEM)
HB = pl.BlockSpec(memory_space=pl.ANY)


def whole(shape):
    return pl.BlockSpec(shape, lambda *_: (0,) * len(shape))


def params(mib):
    return pltpu.CompilerParams(vmem_limit_bytes=mib * 2**20)


def cost(flops, mib):
    return pl.CostEstimate(flops=int(flops), bytes_accessed=int(mib * 2**20), transcendentals=0)


def shape(dims, dtype=BF):
    return jax.ShapeDtypeStruct(dims, dtype)


def pack(sel, tokens, cotangent):
    tok, wide = tokens.shape
    half = wide // 2
    width = half // STEPS
    spec = pl.BlockSpec((tok, width), lambda k, sel: (0, 2 * k + sel[0]))
    return pl.pallas_call(
        pack_kernel,
        grid_spec=pltpu.PrefetchScalarGridSpec(
            num_scalar_prefetch=1,
            grid=(STEPS,),
            in_specs=[spec, spec],
            out_specs=pl.BlockSpec((2 * tok, width), lambda k, sel: (0, k)),
        ),
        out_shape=shape((2 * tok, half)),
        compiler_params=params(4),
        cost_estimate=cost(0, 2),
        name="pack",
    )(sel, tokens, cotangent)


def pack_weights(sel, w_gate, w_up, w_down):
    views = [w.reshape(2, STEPS, 2, 7, 128, 128) for w in (w_gate, w_up)]
    return pl.pallas_call(
        pack_weights_kernel,
        in_specs=[SM, HB, HB, HB],
        out_specs=HB,
        out_shape=shape((168, 128, 128)),
        scratch_shapes=[pltpu.SemaphoreType.DMA((72,))],
        compiler_params=params(1),
        cost_estimate=cost(0, 11),
        name="pack_weights",
    )(sel, *views, w_down)


def near_sums(sel, own, other, weights):
    width = own[0].shape[1] // STEPS
    row_spec = pl.BlockSpec((128, width), lambda k, sel: (0, k))
    return pl.pallas_call(
        near_kernel,
        grid_spec=pltpu.PrefetchScalarGridSpec(
            num_scalar_prefetch=1,
            grid=(STEPS,),
            in_specs=[row_spec] * 12 + [VM] * 3,
            out_specs=[whole((512, 256))] * 3,
        ),
        out_shape=[shape((512, 256), F32)] * 3,
        compiler_params=params(20),
        cost_estimate=cost(4 * 384 * 768 * width * STEPS, 12),
        name="near_sums",
    )(sel, *own, *other, *weights)


def activations(sel, own, other, weights, sums, gains):
    return pl.pallas_call(
        far_kernel,
        in_specs=[SM] + [VM] * 11,
        out_specs=[VM] * 3,
        out_shape=[shape((512, 768)), shape((512, 768)), shape((512, 128), F32)],
        scratch_shapes=[pltpu.VMEM((512, 256), F32)] * 3,
        compiler_params=params(12),
        cost_estimate=cost(4 * 128 * 768 * own[0].shape[1], 12),
        name="activations",
    )(sel, *own, *other, *weights, *sums, gains)


def results(pieces, sel, acts, acts_other, weights, wall, half):
    return pl.pallas_call(
        functools.partial(results_kernel, pieces),
        in_specs=[SM] + [VM] * 6,
        out_specs=[VM] * len(pieces),
        out_shape=[shape((128, half))] * len(pieces),
        compiler_params=params(12),
        cost_estimate=cost(2 * 32 * 2 * len(pieces) * 1536 * half, 12),
        name="results",
    )(sel, acts, acts_other, *weights, wall)


def weight_grads(swapped, sel, rows, acts, before):
    half = rows[0].shape[1]
    width = half // STEPS
    at = 1 if swapped else 0
    up_spec = pl.BlockSpec((2, 1, 1, width, 128), lambda k, sel: (0, k, sel[at], 0, 0))
    down_spec = pl.BlockSpec((2, 128, width), lambda k, sel: (0, 0, 2 * k + sel[at]))
    row_spec = pl.BlockSpec((128, width), lambda k, sel: (0, k))
    up_shape = shape((2, STEPS, 2, width, 128))
    return pl.pallas_call(
        functools.partial(grads_kernel, swapped),
        grid_spec=pltpu.PrefetchScalarGridSpec(
            num_scalar_prefetch=1,
            grid=(STEPS,),
            in_specs=[row_spec] * 8 + [whole((512, 768))] + [HB] * len(before),
            out_specs=[up_spec, up_spec, down_spec],
        ),
        out_shape=[up_shape, up_shape, shape((2, 128, 2 * half))],
        input_output_aliases={10 + i: i for i in range(len(before))},
        compiler_params=params(20),
        cost_estimate=cost(2 * 512 * 768 * half, 13),
        name="weight_grads",
    )(sel, *rows, acts, *before)


def gate_weights(logits, slot_expert, chosen):
    experts = logits.shape[1]
    held = jnp.arange(experts, dtype=jnp.int32)[:, None] == slot_expert[None, :]
    picked = jnp.sum(jnp.where(held[None], logits[:, :, None], 0.0), axis=1)
    sig = jnp.where(chosen, jax.nn.sigmoid(picked), 0.0)
    return ROUTE_SCALE * sig / jnp.sum(sig, axis=1, keepdims=True)


def add(*values):
    total = values[0].astype(F32)
    for value in values[1:]:
        total = total + value.astype(F32)
    return total.astype(BF)


def per_device(tokens, cotangent, gate_logits, route_slot, slot_expert, w_gate, w_up, w_down):
    tok, wide = tokens.shape
    half = wide // 2
    width = half // STEPS
    slots = slot_expert.shape[0]
    z, core, y, x = (lax.axis_index(a) for a in AXES)
    sel = jnp.stack([core, 1 - core])
    weights = (
        w_gate.reshape(2, STEPS, 2, width, 128),
        w_up.reshape(2, STEPS, 2, width, 128),
        w_down,
    )

    own = pack(sel, tokens, cotangent)
    minus, plus, far = send(own, inner(1)), send(own, inner(-1)), send(own, inner(2))
    a = jnp.concatenate([own, plus], axis=0)
    b = jnp.concatenate([minus, far], axis=0)
    a_minus, b_plus = send(a, outer(1)), send(b, outer(-1))
    b_minus, a_plus = send(b, outer(1)), send(a, outer(-1))
    a_far, b_far = send(a_minus, outer(1)), send(b_plus, outer(-1))
    rows = [a, b, a_plus, b_plus, a_minus, b_minus, a_far, b_far]
    rows_other = [send(piece, other_core()) for piece in rows]
    wall = send(pack_weights(sel, w_gate, w_up, w_down), other_core())

    chosen = jnp.any(
        route_slot[:, :, None] == jnp.arange(slots, dtype=jnp.int32)[None, None, :], axis=1
    )
    gate, pull_back = jax.vjp(lambda lg: gate_weights(lg, slot_expert, chosen), gate_logits)
    lines = jnp.arange(NY * NX, dtype=jnp.int32)
    columns = jnp.stack([2 * lines, 2 * lines + 1, 2 * (lines ^ (NY * NX // 2)) + 1], axis=1)
    pick_slot = columns[:, :, None] == jnp.arange(slots, dtype=jnp.int32)[None, None, :]
    cols = jnp.sum(jnp.where(pick_slot[:, None], gate[None, :, None, :], 0.0), axis=3)
    cols = lax.all_to_all(cols, ("y", "x"), split_axis=0, concat_axis=0, tiled=True)
    ring = jnp.array(RING, jnp.int32)
    out_y = ((y + ring) % NY)[:, None] * NX + ((x + ring) % NX)[None, :]
    out_x = ((y + ring) % NY)[None, :] * NX + ((x + ring) % NX)[:, None]
    order = jnp.where(core == 0, out_y, out_x).reshape(-1)
    pick_line = order[:, None] == lines[None, :]
    cols = jnp.sum(jnp.where(pick_line[:, :, None, None], cols[None], 0.0), axis=1)
    cols = cols.reshape(NY * NX * tok, 3)
    gains = jnp.stack([cols[:, 0], cols[:, 1], cols[:, 1] + cols[:, 2]], axis=1)
    gains = jnp.pad(gains, ((0, 0), (0, 125)))

    sums = near_sums(sel, rows[:6], rows_other[:6], weights)
    acts, acts_grad, dots = activations(sel, rows[6:], rows_other[6:], weights, sums, gains)
    acts_other = send(acts, other_core())
    grads = weight_grads(False, sel, rows, acts_grad, [])
    acts_other, grads = lax.optimization_barrier((acts_other, grads))

    part = [None] * 8
    part[6], part[7], part[3], part[4] = results(
        (6, 7, 3, 4), sel, acts, acts_other, weights, wall, half
    )
    part[0], part[1], part[2], part[5] = results(
        (0, 1, 2, 5), sel, acts, acts_other, weights, wall, half
    )
    part[0], grads, dots = lax.optimization_barrier((part[0], grads, dots))
    from_a, from_b = send(part[6], outer(1)), send(part[7], outer(-1))
    b_early, a_early = send(part[3], outer(1)), send(part[4], outer(-1))
    a_late = send(add(part[2], from_a), outer(1))
    b_late = send(add(part[5], from_b), outer(-1))

    def final(piece, early, late):
        return part[piece].astype(F32) + early.astype(F32) + late.astype(F32)

    grads = weight_grads(True, sel, rows_other, acts_grad, grads)
    (a_late, b_late), grads = lax.optimization_barrier(((a_late, b_late), grads))
    sum_a, sum_b = final(0, a_early, a_late), final(1, b_early, b_late)
    keep = sum_a[:64]
    to_plus, to_minus, to_far = (v.astype(BF) for v in (sum_a[64:], sum_b[:64], sum_b[64:]))
    total = add(
        keep, send(to_plus, inner(1)), send(to_minus, inner(-1)), send(to_far, inner(2))
    )

    def block_for(by):
        return lax.dynamic_slice(total, (0, (z + by) % NZ * width), (64, width))

    last = add(
        block_for(0),
        send(block_for(1), along_z(1)),
        send(block_for(3), along_z(-1)),
        send(block_for(2), along_z(2)),
    )
    mixed, grad_tokens = last[:tok], last[tok:]

    dots = dots[:, :2].reshape(NY * NX, tok, 2)
    home = jnp.sum(jnp.where(pick_line[:, :, None, None], dots[:, None], 0.0), axis=0)
    home = lax.all_to_all(home, ("y", "x"), split_axis=0, concat_axis=0, tiled=True)
    home = jnp.transpose(home, (1, 0, 2)).reshape(tok, slots)
    home = home + send(home, other_core())
    home = home + send(home, along_z(1)) + send(home, along_z(-1)) + send(home, along_z(2))
    grad_logits = pull_back(home)[0]
    return (
        mixed,
        grad_tokens,
        grad_logits,
        grads[0].reshape(w_gate.shape),
        grads[1].reshape(w_up.shape),
        grads[2],
    )


def solution(mesh):
    split = Mesh(mesh.devices.reshape(NZ, NC, NY, NX), AXES)
    local, group = ("y", "x"), ("z", "c")
    return jax.shard_map(
        per_device,
        mesh=split,
        in_specs=(
            P(local, None),
            P(local, None),
            P(local, None),
            P(local, None),
            P(),
            P(local, None, group),
            P(local, None, group),
            P(local, group, None),
        ),
        out_specs=(
            P(local, group),
            P(local, group),
            P(local, None),
            P(local, None, group),
            P(local, None, group),
            P(local, group, None),
        ),
        check_vma=False,
    )
```

time: 237 us -> 191 us (0.81)
  blocking collectives: 61.8 us -> 0 us
  starting transfers between devices: 40.6 us -> 53.5 us
  local copies, waits for them, and re-layouts: 14.4 us -> 25.5 us
  waiting for transfers between devices: 59.4 us -> 51.2 us
  Pallas kernels: 45.2 us -> 47.8 us
    all_gather x1 -> x0, blocking collectives: 37.1 us -> none  [per_device(): lax.all_gather(gate, ('y', 'x'), tiled=False).reshape(NY * NX, tok, slots)]
    psum x1 -> x0, blocking collectives: 24.6 us -> none  [per_device(): home = lax.psum(home, ('z', 'c'))]
    ppermute x37 -> x35, waiting for transfers between devices: 59.4 us -> 42.1 us  [send(): return lax.ppermute(value, AXES, pairs)]
    unnamed x73 -> x58, local copies, waits for them, and re-layouts: 9.3 us -> 19.7 us
    all_to_all x1, waiting for transfers between devices: 0.01 us -> 7.89 us  [per_device(): lax.all_to_all(home, ('y', 'x'), split_axis=0, concat_axis=0, tiled=True)]
    ppermute x37 -> x35, starting transfers between devices: 37.2 us -> 43.1 us  [send(): return lax.ppermute(value, AXES, pairs)]
    convert_element_type x8 -> x4, other arithmetic: 8.11 us -> 3.87 us  [add(): return total.astype(BF)]
    all_to_all x0 -> x1, starting transfers between devices: none -> 3.98 us  [per_device(): lax.all_to_all(cols, ('y', 'x'), split_axis=0, concat_axis=0, tiled=True)]
  transfers between devices with their start and end apart: 38 -> 37, of which waited for: 10 -> 15; matrix products, arithmetic and copies ran while one was open for 5% -> 8% of each run, Pallas kernels for 13% -> 21%
where the time goes in v2:
time: 191 us; the launch traced here: 190 us
  starting transfers between devices  53.5 us (28%)
  waiting for transfers between devices  51.2 us (27%)
  Pallas kernels  47.8 us (25%)
  local copies, waits for them, and re-layouts  25.5 us (13%)
  other arithmetic  10.8 us (6%)
    ppermute x35, starting transfers between devices, send(): return lax.ppermute(value, AXES, pairs)  43.1 us
    ppermute x35, waiting for transfers between devices, send(): return lax.ppermute(value, AXES, pairs)  42.1 us
    unnamed x58, local copies, waits for them, and re-layouts  19.7 us
    pallas_call x2, Pallas kernels, weight_grads(): pl.pallas_call(functools.partial(grads_kernel, swapped), grid_spec=pltpu....  16.3 us
    pallas_call x2, Pallas kernels, results(): pl.pallas_call(functools.partial(results_kernel, pieces), in_specs=[SM] +...  13.1 us
    pallas_call x1, Pallas kernels, near_sums(): pl.pallas_call(near_kernel, grid_spec=pltpu.PrefetchScalarGridSpec(num_sc...  8.93 us
    all_to_all x1, waiting for transfers between devices, per_device(): lax.all_to_all(home, ('y', 'x'), split_axis=0, concat_axis=0, tiled=True)  7.89 us
    all_to_all x1, starting transfers between devices, per_device(): lax.all_to_all(home, ('y', 'x'), split_axis=0, concat_axis=0, tiled=True)  6.41 us
  transfers between devices with their start and end apart: 37, of which 15 were waited for; matrix products, arithmetic and copies ran while one was open for 8% of the time, Pallas kernels for 21%

profile of v2, /device:TPU:0, one launch (start us, length us, event | category | flops | bytes accessed | tf_op | source)
XLA Modules:
  0.0 189.9 jit_solution(12730839906112150876)
XLA Ops:
  3.6 2.9 %collective-permute-start = (bf16[64,3584]{1,0:T(8,128)(2,1)S(1)}, bf16[64,3584]{1,0:T(8,128)(2,1)S(1)}, u32[]{:S(2)}, u32[]{:S(2)}) collective-permute-start(bf16[64,3584]{1,0:T(8,128)(2,1)S(1)} %pack.1), channel_id=1, source_target_pairs={{0,3},{1,0},{2,1},{3,2},{4,7},{5,4},{6,5},{7,6},{8,11},{9,8},{10,9... | collective-permute-start | bytes 1376264 | tf_op jit(solution)/shard_map/ppermute | solution.py:51
  14.3 3.6 %pack_weights.1 = bf16[168,128,128]{2,1,0:T(8,128)(2,1)} custom-call(s32[2]{0:T(128)S(1)} %pad_add_fusion.1.sel, bf16[2,4,2,7,128,128]{5,4,3,2,1,0:T(8,128)(2,1)S(1)} %bitcast.15, bf16[2,4,2,7,128,128]{5,4,3,2,1,0:T(8,128)(2,1)S(1)} %bitcast.20, bf16[2,128,7168]{2,1,0:T(8,128)(2,1)S(1)} %copy-done.6), custom_call_target="tpu_custom_call" | custom-call | bytes 11534336 | tf_op jit(solution)/shard_map/pack_weights/pallas_call | solution.py:272
  18.7 3.0 %collective-permute-start.9 = (bf16[128,3584]{1,0:T(8,128)(2,1)S(1)}, bf16[128,3584]{1,0:T(8,128)(2,1)S(1)}, u32[]{:S(2)}, u32[]{:S(2)}) collective-permute-start(bf16[128,3584]{1,0:T(8,128)(2,1)S(1)} %pad_maximum_fusion.refs_0_), channel_id=1, source_target_pairs={{0,12},{1,13},{2,14},{3,15},{4,0},{5,1},{6,2},{7,3},{8,4},{9,5},{1... | collective-permute-start | bytes 2752520 | tf_op jit(solution)/shard_map/ppermute | solution.py:51
  24.6 3.4 %collective-permute-done.11.refs_6_.refs_0_ = bf16[128,3584]{1,0:T(8,128)(2,1)S(1)} collective-permute-done((bf16[128,3584]{1,0:T(8,128)(2,1)S(1)}, bf16[128,3584]{1,0:T(8,128)(2,1)S(1)}, u32[]{:S(2)}, u32[]{:S(2)}) %collective-permute-start.11) | collective-permute-done | bytes 917536 | tf_op jit(solution)/shard_map/ppermute | solution.py:51
  29.6 3.1 %collective-permute-done.9.refs_2_ = bf16[128,3584]{1,0:T(8,128)(2,1)S(1)} collective-permute-done((bf16[128,3584]{1,0:T(8,128)(2,1)S(1)}, bf16[128,3584]{1,0:T(8,128)(2,1)S(1)}, u32[]{:S(2)}, u32[]{:S(2)}) %collective-permute-start.9) | collective-permute-done | bytes 917536 | tf_op jit(solution)/shard_map/ppermute | solution.py:51
  33.6 3.7 %collective-permute-start.5 = (bf16[128,3584]{1,0:T(8,128)(2,1)}, bf16[128,3584]{1,0:T(8,128)(2,1)}, u32[]{:S(2)}, u32[]{:S(2)}) collective-permute-start(bf16[128,3584]{1,0:T(8,128)(2,1)} %constant_dynamic-update-slice_fusion.refs_1_), channel_id=1, source_target_pairs={{0,12},{1,13},{2,14},{3,15},{4,0},{5,1},{6,2},{7,3},{8,4},{9,5},{1... | collective-permute-start | bytes 2752520 | tf_op jit(solution)/shard_map/ppermute | solution.py:51
  38.4 7.8 %collective-permute-done.10.refs_5_ = bf16[128,3584]{1,0:T(8,128)(2,1)} collective-permute-done((bf16[128,3584]{1,0:T(8,128)(2,1)}, bf16[128,3584]{1,0:T(8,128)(2,1)}, u32[]{:S(2)}, u32[]{:S(2)}) %collective-permute-start.10) | collective-permute-done | bytes 917536 | tf_op jit(solution)/shard_map/ppermute | solution.py:51
  48.5 3.7 %collective-permute-start.6 = (bf16[128,3584]{1,0:T(8,128)(2,1)}, bf16[128,3584]{1,0:T(8,128)(2,1)}, u32[]{:S(2)}, u32[]{:S(2)}) collective-permute-start(bf16[128,3584]{1,0:T(8,128)(2,1)} %collective-permute-done.5.refs_3_), channel_id=1, source_target_pairs={{0,12},{1,13},{2,14},{3,15},{4,0},{5,1},{6,2},{7,3},{8,4},{9,5},{1... | collective-permute-start | bytes 2752520 | tf_op jit(solution)/shard_map/ppermute | solution.py:51
  53.5 4.0 %all-to-all-start = ((f32[16,32,3]{1,2,0:T(4,128)}), f32[16,32,3]{1,2,0:T(4,128)S(1)}, u32[]{:S(2)}, u32[]{:S(2)}) async-start(f32[16,32,3]{1,2,0:T(4,128)} %select_reduce_fusion), calls=%async_computation | async-start | bytes 65536 | tf_op jit(solution)/shard_map/all_to_all | solution.py:398
  58.2 3.0 %collective-permute-done.2.refs_0_.refs_6_ = bf16[128,3584]{1,0:T(8,128)(2,1)} collective-permute-done((bf16[128,3584]{1,0:T(8,128)(2,1)}, bf16[128,3584]{1,0:T(8,128)(2,1)}, u32[]{:S(2)}, u32[]{:S(2)}) %collective-permute-start.2) | collective-permute-done | bytes 917536 | tf_op jit(solution)/shard_map/ppermute | solution.py:51
  72.9 8.9 %near_sums.1 = (f32[512,256]{1,0:T(8,128)S(1)}, f32[512,256]{1,0:T(8,128)S(1)}, f32[512,256]{1,0:T(8,128)S(1)}) custom-call(s32[2]{0:T(128)S(1)} %pad_add_fusion.1.sel, bf16[128,3584]{1,0:T(8,128)(2,1)S(1)} %pad_maximum_fusion.refs_0_, bf16[128,3584]{1,0:T(8,128)(2,1)} %constant_dynamic-update-slice_fusion.refs_1_, bf16[128,3584]{1,0:T(8,128)(2,1)S(1)} %copy-done.10, ...), custom_call_target="tpu_custom_call" | custom-call | flops 4227858432 | bytes 12582912 | tf_op jit(solution)/shard_map/near_sums/pallas_call | solution.py:287
  81.8 5.0 %activations.1 = (bf16[512,768]{1,0:T(8,128)(2,1)S(1)}, bf16[512,768]{1,0:T(8,128)(2,1)S(1)}, f32[512,128]{1,0:T(8,128)S(1)}) custom-call(s32[2]{0:T(128)S(1)} %pad_add_fusion.1.sel, bf16[128,3584]{1,0:T(8,128)(2,1)} %collective-permute-done.2.refs_0_.refs_6_, bf16[128,3584]{1,0:T(8,128)(2,1)} %collective-permute-done.6.refs_1_.refs_7_, ...), custom_call_target="tpu_custom_call" | custom-call | flops 1409286144 | bytes 12582912 | tf_op jit(solution)/shard_map/activations/pallas_call | solution.py:303
  87.5 8.3 %weight_grads.2 = (bf16[2,4,2,896,128]{4,3,2,1,0:T(8,128)(2,1)}, bf16[2,4,2,896,128]{4,3,2,1,0:T(8,128)(2,1)}, bf16[2,128,7168]{2,1,0:T(8,128)(2,1)}) custom-call(s32[2]{0:T(128)S(1)} %pad_add_fusion.1.sel, bf16[128,3584]{1,0:T(8,128)(2,1)S(1)} %pad_maximum_fusion.refs_0_, bf16[128,3584]{1,0:T(8,128)(2,1)} %constant_dynamic-update-slice_fusion.refs_1_, ...), custom_call_target="tpu_custom_call" | custom-call | flops 2818572288 | bytes 13631488 | tf_op jit(solution)/shard_map/weight_grads/pallas_call | solution.py:335
  95.9 7.1 %results.3 = (bf16[128,3584]{1,0:T(8,128)(2,1)S(1)}, bf16[128,3584]{1,0:T(8,128)(2,1)S(1)}, bf16[128,3584]{1,0:T(8,128)(2,1)}, bf16[128,3584]{1,0:T(8,128)(2,1)S(1)}) custom-call(s32[2]{0:T(128)S(1)} %pad_add_fusion.1.sel, bf16[512,768]{1,0:T(8,128)(2,1)S(1)} %get-tuple-element.43.acts, bf16[512,768]{1,0:T(8,128)(2,1)S(1)} %collective-permute-done.17.acts_other, ...), custom_call_target="tpu_custom_call" | custom-call | flops 2818572288 | bytes 12582912 | tf_op jit(solution)/shard_map/results/pallas_call | solution.py:316
  107.1 6.1 %results.2 = (bf16[128,3584]{1,0:T(8,128)(2,1)S(1)}, bf16[128,3584]{1,0:T(8,128)(2,1)S(1)}, bf16[128,3584]{1,0:T(8,128)(2,1)S(1)}, bf16[128,3584]{1,0:T(8,128)(2,1)S(1)}) custom-call(s32[2]{0:T(128)S(1)} %pad_add_fusion.1.sel, bf16[512,768]{1,0:T(8,128)(2,1)S(1)} %get-tuple-element.43.acts, bf16[512,768]{1,0:T(8,128)(2,1)S(1)} %collective-permute-done.17.acts_other, ...), custom_call_target="tpu_custom_call" | custom-call | flops 2818572288 | bytes 12582912 | tf_op jit(solution)/shard_map/results/pallas_call | solution.py:316
  113.2 5.3 %collective-permute-done.20 = bf16[128,3584]{1,0:T(8,128)(2,1)S(1)} collective-permute-done((bf16[128,3584]{1,0:T(8,128)(2,1)S(1)}, bf16[128,3584]{1,0:T(8,128)(2,1)S(1)}, u32[]{:S(2)}, u32[]{:S(2)}) %collective-permute-start.20) | collective-permute-done | bytes 917536 | tf_op jit(solution)/shard_map/ppermute | solution.py:51
  120.8 3.2 %collective-permute-start.23 = (bf16[128,3584]{1,0:T(8,128)(2,1)}, bf16[128,3584]{1,0:T(8,128)(2,1)}, u32[]{:S(2)}, u32[]{:S(2)}) collective-permute-start(bf16[128,3584]{1,0:T(8,128)(2,1)} %add_convert_fusion.1), channel_id=1, source_target_pairs={{0,12},{1,13},{2,14},{3,15},{4,0},{5,1},{6,2},{7,3},{8,4},{9,5},{1... | collective-permute-start | bytes 2752520 | tf_op jit(solution)/shard_map/ppermute | solution.py:51
  127.2 6.4 %all-to-all-start.1 = ((f32[16,32,2]{1,2,0:T(2,128)}), f32[16,32,2]{1,2,0:T(2,128)}, u32[]{:S(2)}, u32[]{:S(2)}) async-start(f32[16,32,2]{1,2,0:T(2,128)} %copy.59), calls=%async_computation.1 | async-start | bytes 32768 | tf_op jit(solution)/shard_map/all_to_all | solution.py:453
  133.6 3.1 %collective-permute-start.19 = (bf16[128,3584]{1,0:T(8,128)(2,1)}, bf16[128,3584]{1,0:T(8,128)(2,1)}, u32[]{:S(2)}, u32[]{:S(2)}) collective-permute-start(bf16[128,3584]{1,0:T(8,128)(2,1)} %copy-done.17), channel_id=1, source_target_pairs={{0,12},{1,13},{2,14},{3,15},{4,0},{5,1},{6,2},{7,3},{8,4},{9,5},{1... | collective-permute-start | bytes 2752520 | tf_op jit(solution)/shard_map/ppermute | solution.py:51
  136.7 7.9 %all-to-all-done.1 = f32[16,32,2]{1,2,0:T(2,128)} async-done(((f32[16,32,2]{1,2,0:T(2,128)}), f32[16,32,2]{1,2,0:T(2,128)}, u32[]{:S(2)}, u32[]{:S(2)}) %all-to-all-start.1) | async-done | bytes 4128 | tf_op jit(solution)/shard_map/all_to_all | solution.py:453
  146.3 8.0 %weight_grads.3 = (bf16[2,4,2,896,128]{4,3,2,1,0:T(8,128)(2,1)}, bf16[2,4,2,896,128]{4,3,2,1,0:T(8,128)(2,1)}, bf16[2,128,7168]{2,1,0:T(8,128)(2,1)}) custom-call(s32[2]{0:T(128)S(1)} %pad_add_fusion.1.sel, bf16[128,3584]{1,0:T(8,128)(2,1)S(1)} %collective-permute-done.11.refs_6_.refs_0_, ...), custom_call_target="tpu_custom_call", output_to_operand_aliasing={{0}: (10, {}), {1}: (11, {}), {2}: (12, {})} | custom-call | flops 2818572288 | bytes 13631488 | tf_op jit(solution)/shard_map/weight_grads/pallas_call | solution.py:335
  154.4 4.0 %collective-permute-start.34 = (f32[32,32]{1,0:T(8,128)S(1)}, f32[32,32]{1,0:T(8,128)S(1)}, u32[]{:S(2)}, u32[]{:S(2)}) collective-permute-start(f32[32,32]{1,0:T(8,128)S(1)} %add.220), channel_id=1, source_target_pairs={{0,64},{1,65},{2,66},{3,67},{4,68},{5,69},{6,70},{7,71},{8,72},{9,... | collective-permute-start | bytes 12296 | tf_op jit(solution)/shard_map/ppermute | solution.py:51
  168.2 5.8 %collective-permute-done.24 = bf16[64,3584]{1,0:T(8,128)(2,1)} collective-permute-done((bf16[64,3584]{1,0:T(8,128)(2,1)S(1)}, bf16[64,3584]{1,0:T(8,128)(2,1)}, u32[]{:S(2)}, u32[]{:S(2)}) %collective-permute-start.24) | collective-permute-done | bytes 458784 | tf_op jit(solution)/shard_map/ppermute | solution.py:51
  174.1 4.4 %collective-permute-done.26 = bf16[64,3584]{1,0:T(8,128)(2,1)} collective-permute-done((bf16[64,3584]{1,0:T(8,128)(2,1)S(1)}, bf16[64,3584]{1,0:T(8,128)(2,1)}, u32[]{:S(2)}, u32[]{:S(2)}) %collective-permute-start.26) | collective-permute-done | bytes 458784 | tf_op jit(solution)/shard_map/ppermute | solution.py:51
  (163 shorter events, 67.1 us)
Async XLA Ops:
  3.6 14.5 %collective-permute-start = (bf16[64,3584]{1,0:T(8,128)(2,1)S(1)}, bf16[64,3584]{1,0:T(8,128)(2,1)S(1)}, u32[]{:S(2)}, u32[]{:S(2)}) collective-permute-start(bf16[64,3584]{1,0:T(8,128)(2,1)S(1)} %pack.1), channel_id=1, source_target_pairs={{0,3},{1,0},{2,1},{3,2},{4,7},{5,4},{6,5},{7,6},{8,11},{9,8},{10,9... | collective-permute-start | bytes 1376264 | tf_op jit(solution)/shard_map/ppermute | solution.py:51
  6.5 17.3 %collective-permute-start.4 = (bf16[64,3584]{1,0:T(8,128)(2,1)S(1)}, bf16[64,3584]{1,0:T(8,128)(2,1)S(1)}, u32[]{:S(2)}, u32[]{:S(2)}) collective-permute-start(bf16[64,3584]{1,0:T(8,128)(2,1)S(1)} %pack.1), channel_id=1, source_target_pairs={{0,2},{1,3},{2,0},{3,1},{4,6},{5,7},{6,4},{7,5},{8,10},{9,11},{10,... | collective-permute-start | bytes 1376264 | tf_op jit(solution)/shard_map/ppermute | solution.py:51
  7.3 14.4 %collective-permute-start.3 = (bf16[64,3584]{1,0:T(8,128)(2,1)S(1)}, bf16[64,3584]{1,0:T(8,128)(2,1)S(1)}, u32[]{:S(2)}, u32[]{:S(2)}) collective-permute-start(bf16[64,3584]{1,0:T(8,128)(2,1)S(1)} %pack.1), channel_id=1, source_target_pairs={{0,1},{1,2},{2,3},{3,0},{4,5},{5,6},{6,7},{7,4},{8,9},{9,10},{10,1... | collective-permute-start | bytes 1376264 | tf_op jit(solution)/shard_map/ppermute | solution.py:51
  18.0 77.9 %collective-permute-start.18 = (bf16[168,128,128]{2,1,0:T(8,128)(2,1)}, bf16[168,128,128]{2,1,0:T(8,128)(2,1)}, u32[]{:S(2)}, u32[]{:S(2)}) collective-permute-start(bf16[168,128,128]{2,1,0:T(8,128)(2,1)} %pack_weights.1), channel_id=1, source_target_pairs={{0,16},{1,17},{2,18},{3,19},{4,20},{5,21},{6,22},{7,23},{8,24},{9,... | collective-permute-start | bytes 16515080 | tf_op jit(solution)/shard_map/ppermute | solution.py:51
  18.7 13.9 %collective-permute-start.9 = (bf16[128,3584]{1,0:T(8,128)(2,1)S(1)}, bf16[128,3584]{1,0:T(8,128)(2,1)S(1)}, u32[]{:S(2)}, u32[]{:S(2)}) collective-permute-start(bf16[128,3584]{1,0:T(8,128)(2,1)S(1)} %pad_maximum_fusion.refs_0_), channel_id=1, source_target_pairs={{0,12},{1,13},{2,14},{3,15},{4,0},{5,1},{6,2},{7,3},{8,4},{9,5},{1... | collective-permute-start | bytes 2752520 | tf_op jit(solution)/shard_map/ppermute | solution.py:51
  21.7 15.8 %collective-permute-start.1 = (bf16[128,3584]{1,0:T(8,128)(2,1)S(1)}, bf16[128,3584]{1,0:T(8,128)(2,1)}, u32[]{:S(2)}, u32[]{:S(2)}) collective-permute-start(bf16[128,3584]{1,0:T(8,128)(2,1)S(1)} %pad_maximum_fusion.refs_0_), channel_id=1, source_target_pairs={{0,4},{1,5},{2,6},{3,7},{4,8},{5,9},{6,10},{7,11},{8,12},{9,13},{1... | collective-permute-start | bytes 2752520 | tf_op jit(solution)/shard_map/ppermute | solution.py:51
  24.6 13.1 %collective-permute-start.12 = (bf16[128,3584]{1,0:T(8,128)(2,1)}, bf16[128,3584]{1,0:T(8,128)(2,1)S(1)}, u32[]{:S(2)}, u32[]{:S(2)}) collective-permute-start(bf16[128,3584]{1,0:T(8,128)(2,1)} %constant_dynamic-update-slice_fusion.refs_1_), channel_id=1, source_target_pairs={{0,16},{1,17},{2,18},{3,19},{4,20},{5,21},{6,22},{7,23},{8,24},{9,... | collective-permute-start | bytes 2752520 | tf_op jit(solution)/shard_map/ppermute | solution.py:51
  28.0 18.3 %collective-permute-start.10 = (bf16[128,3584]{1,0:T(8,128)(2,1)}, bf16[128,3584]{1,0:T(8,128)(2,1)}, u32[]{:S(2)}, u32[]{:S(2)}) collective-permute-start(bf16[128,3584]{1,0:T(8,128)(2,1)} %constant_dynamic-update-slice_fusion.refs_1_), channel_id=1, source_target_pairs={{0,4},{1,5},{2,6},{3,7},{4,8},{5,9},{6,10},{7,11},{8,12},{9,13},{1... | collective-permute-start | bytes 2752520 | tf_op jit(solution)/shard_map/ppermute | solution.py:51
  33.6 14.9 %collective-permute-start.5 = (bf16[128,3584]{1,0:T(8,128)(2,1)}, bf16[128,3584]{1,0:T(8,128)(2,1)}, u32[]{:S(2)}, u32[]{:S(2)}) collective-permute-start(bf16[128,3584]{1,0:T(8,128)(2,1)} %constant_dynamic-update-slice_fusion.refs_1_), channel_id=1, source_target_pairs={{0,12},{1,13},{2,14},{3,15},{4,0},{5,1},{6,2},{7,3},{8,4},{9,5},{1... | collective-permute-start | bytes 2752520 | tf_op jit(solution)/shard_map/ppermute | solution.py:51
  37.6 19.9 %collective-permute-start.13 = (bf16[128,3584]{1,0:T(8,128)(2,1)}, bf16[128,3584]{1,0:T(8,128)(2,1)}, u32[]{:S(2)}, u32[]{:S(2)}) collective-permute-start(bf16[128,3584]{1,0:T(8,128)(2,1)} %copy-done.9), channel_id=1, source_target_pairs={{0,16},{1,17},{2,18},{3,19},{4,20},{5,21},{6,22},{7,23},{8,24},{9,... | collective-permute-start | bytes 2752520 | tf_op jit(solution)/shard_map/ppermute | solution.py:51
  37.7 19.9 %collective-permute-start.15 = (bf16[128,3584]{1,0:T(8,128)(2,1)}, bf16[128,3584]{1,0:T(8,128)(2,1)}, u32[]{:S(2)}, u32[]{:S(2)}) collective-permute-start(bf16[128,3584]{1,0:T(8,128)(2,1)} %collective-permute-done.1.refs_4_), channel_id=1, source_target_pairs={{0,16},{1,17},{2,18},{3,19},{4,20},{5,21},{6,22},{7,23},{8,24},{9,... | collective-permute-start | bytes 2752520 | tf_op jit(solution)/shard_map/ppermute | solution.py:51
  46.3 15.0 %collective-permute-start.2 = (bf16[128,3584]{1,0:T(8,128)(2,1)}, bf16[128,3584]{1,0:T(8,128)(2,1)}, u32[]{:S(2)}, u32[]{:S(2)}) collective-permute-start(bf16[128,3584]{1,0:T(8,128)(2,1)} %collective-permute-done.1.refs_4_), channel_id=1, source_target_pairs={{0,4},{1,5},{2,6},{3,7},{4,8},{5,9},{6,10},{7,11},{8,12},{9,13},{1... | collective-permute-start | bytes 2752520 | tf_op jit(solution)/shard_map/ppermute | solution.py:51
  48.5 15.3 %collective-permute-start.6 = (bf16[128,3584]{1,0:T(8,128)(2,1)}, bf16[128,3584]{1,0:T(8,128)(2,1)}, u32[]{:S(2)}, u32[]{:S(2)}) collective-permute-start(bf16[128,3584]{1,0:T(8,128)(2,1)} %collective-permute-done.5.refs_3_), channel_id=1, source_target_pairs={{0,12},{1,13},{2,14},{3,15},{4,0},{5,1},{6,2},{7,3},{8,4},{9,5},{1... | collective-permute-start | bytes 2752520 | tf_op jit(solution)/shard_map/ppermute | solution.py:51
  61.2 20.6 %collective-permute-start.7 = (bf16[128,3584]{1,0:T(8,128)(2,1)}, bf16[128,3584]{1,0:T(8,128)(2,1)}, u32[]{:S(2)}, u32[]{:S(2)}) collective-permute-start(bf16[128,3584]{1,0:T(8,128)(2,1)} %collective-permute-done.2.refs_0_.refs_6_), channel_id=1, source_target_pairs={{0,16},{1,17},{2,18},{3,19},{4,20},{5,21},{6,22},{7,23},{8,24},{9,... | collective-permute-start | bytes 2752520 | tf_op jit(solution)/shard_map/ppermute | solution.py:51
  63.8 18.0 %collective-permute-start.8 = (bf16[128,3584]{1,0:T(8,128)(2,1)}, bf16[128,3584]{1,0:T(8,128)(2,1)}, u32[]{:S(2)}, u32[]{:S(2)}) collective-permute-start(bf16[128,3584]{1,0:T(8,128)(2,1)} %collective-permute-done.6.refs_1_.refs_7_), channel_id=1, source_target_pairs={{0,16},{1,17},{2,18},{3,19},{4,20},{5,21},{6,22},{7,23},{8,24},{9,... | collective-permute-start | bytes 2752520 | tf_op jit(solution)/shard_map/ppermute | solution.py:51
  103.9 14.6 %collective-permute-start.20 = (bf16[128,3584]{1,0:T(8,128)(2,1)S(1)}, bf16[128,3584]{1,0:T(8,128)(2,1)S(1)}, u32[]{:S(2)}, u32[]{:S(2)}) collective-permute-start(bf16[128,3584]{1,0:T(8,128)(2,1)S(1)} %get-tuple-element.57), channel_id=1, source_target_pairs={{0,4},{1,5},{2,6},{3,7},{4,8},{5,9},{6,10},{7,11},{8,12},{9,13},{1... | collective-permute-start | bytes 2752520 | tf_op jit(solution)/shard_map/ppermute | solution.py:51
  104.4 15.2 %collective-permute-start.22 = (bf16[128,3584]{1,0:T(8,128)(2,1)S(1)}, bf16[128,3584]{1,0:T(8,128)(2,1)S(1)}, u32[]{:S(2)}, u32[]{:S(2)}) collective-permute-start(bf16[128,3584]{1,0:T(8,128)(2,1)S(1)} %get-tuple-element.59), channel_id=1, source_target_pairs={{0,12},{1,13},{2,14},{3,15},{4,0},{5,1},{6,2},{7,3},{8,4},{9,5},{1... | collective-permute-start | bytes 2752520 | tf_op jit(solution)/shard_map/ppermute | solution.py:51
  119.6 38.7 %collective-permute-start.21 = (bf16[128,3584]{1,0:T(8,128)(2,1)}, bf16[128,3584]{1,0:T(8,128)(2,1)}, u32[]{:S(2)}, u32[]{:S(2)}) collective-permute-start(bf16[128,3584]{1,0:T(8,128)(2,1)} %add_convert_fusion.2), channel_id=1, source_target_pairs={{0,4},{1,5},{2,6},{3,7},{4,8},{5,9},{6,10},{7,11},{8,12},{9,13},{1... | collective-permute-start | bytes 2752520 | tf_op jit(solution)/shard_map/ppermute | solution.py:51
  120.8 38.3 %collective-permute-start.23 = (bf16[128,3584]{1,0:T(8,128)(2,1)}, bf16[128,3584]{1,0:T(8,128)(2,1)}, u32[]{:S(2)}, u32[]{:S(2)}) collective-permute-start(bf16[128,3584]{1,0:T(8,128)(2,1)} %add_convert_fusion.1), channel_id=1, source_target_pairs={{0,12},{1,13},{2,14},{3,15},{4,0},{5,1},{6,2},{7,3},{8,4},{9,5},{1... | collective-permute-start | bytes 2752520 | tf_op jit(solution)/shard_map/ppermute | solution.py:51
  124.0 36.4 %collective-permute-start.25 = (bf16[128,3584]{1,0:T(8,128)(2,1)}, bf16[128,3584]{1,0:T(8,128)(2,1)}, u32[]{:S(2)}, u32[]{:S(2)}) collective-permute-start(bf16[128,3584]{1,0:T(8,128)(2,1)} %get-tuple-element.68), channel_id=1, source_target_pairs={{0,4},{1,5},{2,6},{3,7},{4,8},{5,9},{6,10},{7,11},{8,12},{9,13},{1... | collective-permute-start | bytes 2752520 | tf_op jit(solution)/shard_map/ppermute | solution.py:51
  127.2 17.4 %all-to-all-start.1 = ((f32[16,32,2]{1,2,0:T(2,128)}), f32[16,32,2]{1,2,0:T(2,128)}, u32[]{:S(2)}, u32[]{:S(2)}) async-start(f32[16,32,2]{1,2,0:T(2,128)} %copy.59), calls=%async_computation.1 | async-start | bytes 32768 | tf_op jit(solution)/shard_map/all_to_all | solution.py:453
  133.6 28.7 %collective-permute-start.19 = (bf16[128,3584]{1,0:T(8,128)(2,1)}, bf16[128,3584]{1,0:T(8,128)(2,1)}, u32[]{:S(2)}, u32[]{:S(2)}) collective-permute-start(bf16[128,3584]{1,0:T(8,128)(2,1)} %copy-done.17), channel_id=1, source_target_pairs={{0,12},{1,13},{2,14},{3,15},{4,0},{5,1},{6,2},{7,3},{8,4},{9,5},{1... | collective-permute-start | bytes 2752520 | tf_op jit(solution)/shard_map/ppermute | solution.py:51
  154.4 13.1 %collective-permute-start.34 = (f32[32,32]{1,0:T(8,128)S(1)}, f32[32,32]{1,0:T(8,128)S(1)}, u32[]{:S(2)}, u32[]{:S(2)}) collective-permute-start(f32[32,32]{1,0:T(8,128)S(1)} %add.220), channel_id=1, source_target_pairs={{0,64},{1,65},{2,66},{3,67},{4,68},{5,69},{6,70},{7,71},{8,72},{9,... | collective-permute-start | bytes 12296 | tf_op jit(solution)/shard_map/ppermute | solution.py:51
  165.7 12.8 %collective-permute-start.26 = (bf16[64,3584]{1,0:T(8,128)(2,1)S(1)}, bf16[64,3584]{1,0:T(8,128)(2,1)}, u32[]{:S(2)}, u32[]{:S(2)}) collective-permute-start(bf16[64,3584]{1,0:T(8,128)(2,1)S(1)} %get-tuple-element.94), channel_id=1, source_target_pairs={{0,3},{1,0},{2,1},{3,2},{4,7},{5,4},{6,5},{7,6},{8,11},{9,8},{10,9... | collective-permute-start | bytes 1376264 | tf_op jit(solution)/shard_map/ppermute | solution.py:51
  (40 other events, 305.5 us)

commit v3 on v2

v3 whole, which is shorter than its diff:
```python
import functools

import jax
import jax.numpy as jnp
from jax import lax
from jax.experimental import pallas as pl
from jax.experimental.pallas import tpu as pltpu
from jax.sharding import Mesh
from jax.sharding import PartitionSpec as P

ROUTE_SCALE = 2.5
NZ, NC, NY, NX = 4, 2, 4, 4
AXES = ("z", "c", "y", "x")
STEPS = 4
BF, F32 = jnp.bfloat16, jnp.float32
NT = (((1,), (1,)), ((), ()))
TN = (((0,), (0,)), ((), ()))
RING = (0, 1, 3, 2)


def moves(step):
    pairs = []
    for z in range(NZ):
        for c in range(NC):
            for y in range(NY):
                for x in range(NX):
                    z2, c2, y2, x2 = step(z, c, y, x)
                    source = ((z * NC + c) * NY + y) * NX + x
                    target = ((z2 % NZ * NC + c2 % NC) * NY + y2 % NY) * NX + x2 % NX
                    pairs.append((source, target))
    return pairs


def outer(by):
    return moves(lambda z, c, y, x: (z, c, y + by, x) if c == 0 else (z, c, y, x + by))


def inner(by):
    return moves(lambda z, c, y, x: (z, c, y, x + by) if c == 0 else (z, c, y + by, x))


def along_z(by):
    return moves(lambda z, c, y, x: (z + by, c, y, x))


def other_core():
    return moves(lambda z, c, y, x: (z, c + 1, y, x))


def send(value, pairs):
    return lax.ppermute(value, AXES, pairs)


def joined(parts, axis=0):
    return jnp.concatenate(parts, axis=axis)


def rows_of(refs, blocks, second):
    parts = []
    for outer_at, inner_at in blocks:
        ref, row = refs[outer_at] if outer_at < 3 else refs[-2 + inner_at // 2], 64 * inner_at
        if outer_at == 3:
            row = 64 * (inner_at % 2)
        if second:
            row += 32
        parts.append(ref[row : row + 32, :])
    return joined(parts)


def turned(blocks):
    return [(b, a) for a, b in blocks]


ALL = [(a, b) for a in range(4) for b in range(4)]
NEAR_OWN = [(a, b) for a in range(3) for b in range(4)]
FAR_OWN = [(3, b) for b in range(4)]
NEAR_OTHER = [(a, b) for a in range(4) for b in range(3)]
FAR_OTHER = [(a, 3) for a in range(4)]


def pair(first, second):
    return joined([first, second], axis=1)


def weight_block(wg, wu, wd):
    gate, up = (pair(ref[0, 0, 0], ref[1, 0, 0]) for ref in (wg, wu))
    return gate, up, wd[...].reshape(-1, wd.shape[2])


def products(tok, cot, gate, up, down):
    first = jnp.dot(tok, gate, preferred_element_type=F32)
    second = jnp.dot(tok, up, preferred_element_type=F32)
    back = lax.dot_general(cot, down, NT, preferred_element_type=F32)
    return first, second, back


def pack_kernel(sel, tok, cot, packed, sems):
    rows, width = tok.shape[0], tok.shape[1] // (2 * STEPS)
    copies = []
    for k in range(STEPS):
        at = pl.multiple_of((2 * k + sel[0]) * width, 128)
        for base, ref in enumerate((tok, cot)):
            target = packed.at[pl.ds(base * rows, rows), pl.ds(k * width, width)]
            copies.append(pltpu.make_async_copy(ref.at[:, pl.ds(at, width)], target, sems.at[len(copies)]))
            copies[-1].start()
    for one in copies:
        one.wait()


def pack_weights_kernel(sel, wg, wu, wd, wall, sems):
    away = sel[1]
    copies = []

    def copy(source, target):
        copies.append(pltpu.make_async_copy(source, target, sems.at[len(copies)]))
        copies[-1].start()

    for k in range(STEPS):
        for base, ref in ((0, wg), (14, wu)):
            for slot in range(2):
                copy(ref.at[slot, k, away], wall.at[k, pl.ds(base + 7 * slot, 7)])
        for q in range(7):
            at = pl.multiple_of((2 * k + away) * 896 + q * 128, 128)
            for slot in range(2):
                copy(wd.at[slot, :, pl.ds(at, 128)], wall.at[k, 28 + 2 * q + slot])
    for one in copies:
        one.wait()


def accumulate(sums, own, other, mine, theirs, own_blocks, other_blocks):
    there = turned(other_blocks)
    a = products(
        rows_of(own, own_blocks, False), rows_of(own, own_blocks, True), *weight_block(*mine)
    )
    b = products(rows_of(other, there, False), rows_of(other, there, True), *weight_block(*theirs))
    for ref, one, two in zip(sums, a, b):
        for blocks, value in ((own_blocks, one), (other_blocks, two)):
            for outer_at in sorted({o for o, _ in blocks}):
                inners = [i for o, i in blocks if o == outer_at]
                low = 32 * blocks.index((outer_at, inners[0]))
                to = 32 * (4 * outer_at + inners[0])
                ref[to : to + 32 * len(inners)] += value[low : low + 32 * len(inners)]


def near_kernel(sel, *refs):
    own, other, mine, theirs, sums = refs[:3], refs[3:6], refs[6:9], refs[9:12], refs[12:15]

    @pl.when(pl.program_id(0) == 0)
    def _():
        for ref in sums:
            ref[...] = jnp.zeros_like(ref)

    accumulate(sums, own, other, mine, theirs, NEAR_OWN, NEAR_OTHER)


def thirds(value):
    high = value.astype(BF).astype(F32)
    middle = (value - high).astype(BF).astype(F32)
    return high, middle, value - high - middle


def far_kernel(sel, *refs):
    own, other, mine, theirs = refs[:2], refs[2:4], refs[4:7], refs[7:10]
    start, gains = refs[10:13], refs[13]
    acts, acts_grad = refs[14:16]
    sums = refs[16:19]

    @pl.when(pl.program_id(0) == 0)
    def _():
        for ref, before in zip(sums, start):
            ref[...] = before[...]

    accumulate(sums, own, other, mine, theirs, FAR_OWN, FAR_OTHER)

    @pl.when(pl.program_id(0) == STEPS - 1)
    def _():
        finish(sums, gains, acts, acts_grad)


def finish(sums, gains, acts, acts_grad):
    lane = lax.broadcasted_iota(jnp.int32, (512, 128), 1)
    dots = jnp.zeros((512, 128), F32)
    for slot in range(2):
        units = slice(128 * slot, 128 * slot + 128)
        first, second, back = (ref[:, units] for ref in sums)
        mine = gains[:, slot : slot + 1]
        both = gains[:, 2 * slot : 2 * slot + 1]
        sig = jax.nn.sigmoid(first)
        silu = first * sig
        hidden = silu * second
        for at, part in enumerate(thirds(jnp.sum(hidden * back, axis=1, keepdims=True))):
            dots = jnp.where(lane == 2 * at + slot, part, dots)
        d_first = back * second * sig * (1.0 + first * (1.0 - sig))
        d_second = back * silu
        for at, value in ((0, hidden), (256, d_first), (512, d_second)):
            units = slice(at + 128 * slot, at + 128 * slot + 128)
            acts[:, units] = (value * mine).astype(BF)
            acts_grad[:, units] = (value * both).astype(BF)
    acts[:, 768:] = dots.astype(BF)


def results_kernel(pieces, sel, acts, acts_other, wg, wu, wd, wall, *outs):
    blocks = [(p // 2, 2 * (p % 2) + b) for group in pieces for p in group for b in range(2)]
    places = [(at, 64 * row) for at, group in enumerate(pieces) for row in range(2 * len(group))]
    own = joined([acts[32 * (4 * a + b) : 32 * (4 * a + b) + 32, :] for a, b in blocks])
    other = joined([acts_other[32 * (4 * b + a) : 32 * (4 * b + a) + 32, :] for a, b in blocks])
    hidden = pair(own[:, :256], other[:, :256])
    grads = pair(own[:, 256:768], other[:, 256:768])
    total = outs[0].shape[1] - 128
    width = total // STEPS
    k = pl.program_id(0)

    @pl.when(k == STEPS - 1)
    def _():
        lane = lax.broadcasted_iota(jnp.int32, (own.shape[0], 128), 1)
        dots = jnp.zeros((own.shape[0], 128), F32)
        last = own[:, 768:].astype(F32) + other[:, 768:].astype(F32)
        for slot in range(2):
            mine = jnp.sum(jnp.where((lane < 6) & (lane % 2 == slot), last, 0.0), axis=1, keepdims=True)
            for at, part in enumerate(thirds(mine)):
                dots = jnp.where(lane == 32 * at + 2 * sel[2] + slot, part, dots)
        for block, (at, row) in enumerate(places):
            outs[at][row : row + 32, total:] = dots[32 * block : 32 * block + 32].astype(BF)
            outs[at][row + 32 : row + 64, total:] = jnp.zeros((32, 128), BF)

    tiles = [
        joined([wall[0, 28 + 2 * q : 30 + 2 * q].reshape(256, 128) for q in range(7)], axis=1)
    ]
    gate, up, down = weight_block(wg, wu, wd)
    down = joined([down, *tiles])
    ups = [gate, up] + [wall[0, at : at + 7].reshape(width, 128) for at in (0, 7, 14, 21)]
    out = jnp.dot(hidden, down, preferred_element_type=F32)
    grad = lax.dot_general(grads, joined(ups, axis=1), NT, preferred_element_type=F32)
    cols = pl.ds(pl.multiple_of(k * width, 128), width)
    for block, (at, row) in enumerate(places):
        here = slice(32 * block, 32 * block + 32)
        outs[at][row : row + 32, cols] = out[here].astype(BF)
        outs[at][row + 32 : row + 64, cols] = grad[here].astype(BF)


def grads_kernel(swapped, sel, *refs):
    rows, acts = refs[:5], refs[5]
    grad_gate, grad_up, grad_down = refs[-3:]
    blocks = turned(ALL) if swapped else ALL
    tok, cot = rows_of(rows, blocks, False), rows_of(rows, blocks, True)
    hid, d1, d2 = acts[:, :256], acts[:, 256:512], acts[:, 512:768]
    gate = lax.dot_general(tok, d1, TN, preferred_element_type=F32).astype(BF)
    up = lax.dot_general(tok, d2, TN, preferred_element_type=F32).astype(BF)
    down = lax.dot_general(hid, cot, TN, preferred_element_type=F32).astype(BF)
    for slot in range(2):
        units = slice(128 * slot, 128 * slot + 128)
        grad_gate[slot, 0, 0] = gate[:, units]
        grad_up[slot, 0, 0] = up[:, units]
        grad_down[slot] = down[units]


VM = pl.BlockSpec(memory_space=pltpu.VMEM)
SM = pl.BlockSpec(memory_space=pltpu.SMEM)
HB = pl.BlockSpec(memory_space=pltpu.HBM)


def whole(shape):
    return pl.BlockSpec(shape, lambda *_: (0,) * len(shape))


def params(mib):
    return pltpu.CompilerParams(vmem_limit_bytes=mib * 2**20)


def cost(flops, mib):
    return pl.CostEstimate(flops=int(flops), bytes_accessed=int(mib * 2**20), transcendentals=0)


def shape(dims, dtype=BF):
    return jax.ShapeDtypeStruct(dims, dtype)


def pack(sel, tokens, cotangent):
    return pl.pallas_call(
        pack_kernel,
        in_specs=[SM, HB, HB],
        out_specs=HB,
        out_shape=shape((2 * tokens.shape[0], tokens.shape[1] // 2)),
        scratch_shapes=[pltpu.SemaphoreType.DMA((2 * STEPS,))],
        compiler_params=params(60),
        cost_estimate=cost(0, 2),
        name="pack",
    )(sel, tokens, cotangent)


def pack_weights(sel, w_gate, w_up, w_down):
    views = [w.reshape(2, STEPS, 2, 7, 128, 128) for w in (w_gate, w_up)]
    return pl.pallas_call(
        pack_weights_kernel,
        in_specs=[SM, HB, HB, HB],
        out_specs=HB,
        out_shape=shape((STEPS, 42, 128, 128)),
        scratch_shapes=[pltpu.SemaphoreType.DMA((72,))],
        compiler_params=params(60),
        cost_estimate=cost(0, 11),
        name="pack_weights",
    )(sel, *views, w_down)


def weight_specs(width, which):
    up_spec = pl.BlockSpec((2, 1, 1, width, 128), lambda k, sel: (0, k, sel[which], 0, 0))
    down_spec = pl.BlockSpec((2, 128, width), lambda k, sel: (0, 0, 2 * k + sel[which]))
    return [up_spec, up_spec, down_spec]


def row_specs(rows, width, first=0):
    return [pl.BlockSpec((r.shape[0], width), lambda k, sel: (0, first + k)) for r in rows]


def near_sums(sel, own, other, weights):
    width = own[0].shape[1] // STEPS
    return pl.pallas_call(
        near_kernel,
        grid_spec=pltpu.PrefetchScalarGridSpec(
            num_scalar_prefetch=1,
            grid=(STEPS,),
            in_specs=row_specs(own + other, width) + weight_specs(width, 0) + weight_specs(width, 1),
            out_specs=[whole((512, 256))] * 3,
        ),
        out_shape=[shape((512, 256), F32)] * 3,
        compiler_params=params(58),
        cost_estimate=cost(4 * 384 * 768 * width * STEPS, 22),
        name="near_sums",
    )(sel, *own, *other, *weights, *weights)


def activations(sel, own, other, weights, sums, gains):
    width = own[0].shape[1] // STEPS
    return pl.pallas_call(
        far_kernel,
        grid_spec=pltpu.PrefetchScalarGridSpec(
            num_scalar_prefetch=1,
            grid=(STEPS,),
            in_specs=row_specs(own + other, width)
            + weight_specs(width, 0)
            + weight_specs(width, 1)
            + [whole((512, 256))] * 3
            + [whole((512, 128))],
            out_specs=[whole((512, 896)), whole((512, 768))],
            scratch_shapes=[pltpu.VMEM((512, 256), F32)] * 3,
        ),
        out_shape=[shape((512, 896)), shape((512, 768))],
        compiler_params=params(58),
        cost_estimate=cost(4 * 128 * 768 * own[0].shape[1], 15),
        name="activations",
    )(sel, *own, *other, *weights, *weights, *sums, gains)


def results(pieces, sel, acts, acts_other, weights, wall, half):
    width = half // STEPS
    sizes = [128 * len(group) for group in pieces]
    return pl.pallas_call(
        functools.partial(results_kernel, pieces),
        grid_spec=pltpu.PrefetchScalarGridSpec(
            num_scalar_prefetch=1,
            grid=(STEPS,),
            in_specs=[whole((512, 896))] * 2
            + weight_specs(width, 0)
            + [pl.BlockSpec((1, 42, 128, 128), lambda k, sel: (k, 0, 0, 0))],
            out_specs=[VM] * len(sizes),
        ),
        out_shape=[shape((size, half + 128)) for size in sizes],
        compiler_params=params(60 - sum(sizes) // 128),
        cost_estimate=cost(sum(sizes) * 1536 * half, 12 + sum(sizes) // 128),
        name="results",
    )(sel, acts, acts_other, *weights, wall)


def weight_grads(swapped, first, count, sel, rows, acts, before):
    half = rows[0].shape[1]
    width = half // STEPS
    at = 1 if swapped else 0
    up_spec = pl.BlockSpec((2, 1, 1, width, 128), lambda k, sel: (0, first + k, sel[at], 0, 0))
    down_spec = pl.BlockSpec((2, 128, width), lambda k, sel: (0, 0, 2 * (first + k) + sel[at]))
    up_shape = shape((2, STEPS, 2, width, 128))
    return pl.pallas_call(
        functools.partial(grads_kernel, swapped),
        grid_spec=pltpu.PrefetchScalarGridSpec(
            num_scalar_prefetch=1,
            grid=(count,),
            in_specs=row_specs(rows, width, first) + [whole((512, 768))] + [HB] * len(before),
            out_specs=[up_spec, up_spec, down_spec],
        ),
        out_shape=[up_shape, up_shape, shape((2, 128, 2 * half))],
        input_output_aliases={2 + len(rows) + i: i for i in range(len(before))},
        compiler_params=params(56),
        cost_estimate=cost(2 * 512 * 768 * width * count, 3.5 * count),
        name="weight_grads",
    )(sel, *rows, acts, *before)


def gate_weights(logits, slot_expert, chosen):
    experts = logits.shape[1]
    held = jnp.arange(experts, dtype=jnp.int32)[:, None] == slot_expert[None, :]
    picked = jnp.sum(jnp.where(held[None], logits[:, :, None], 0.0), axis=1)
    sig = jnp.where(chosen, jax.nn.sigmoid(picked), 0.0)
    return ROUTE_SCALE * sig / jnp.sum(sig, axis=1, keepdims=True)


def add(*values):
    total = values[0].astype(F32)
    for value in values[1:]:
        total = total + value.astype(F32)
    return total.astype(BF)


def per_device(tokens, cotangent, gate_logits, route_slot, slot_expert, w_gate, w_up, w_down):
    tok, wide = tokens.shape
    half = wide // 2
    width = half // STEPS
    slots = slot_expert.shape[0]
    z, core, y, x = (lax.axis_index(a) for a in AXES)
    sel = jnp.stack([core, 1 - core, y * NX + x])
    weights = (
        w_gate.reshape(2, STEPS, 2, width, 128),
        w_up.reshape(2, STEPS, 2, width, 128),
        w_down,
    )
    own = pack(sel, tokens, cotangent)
    minus, plus, far = send(own, inner(1)), send(own, inner(-1)), send(own, inner(2))
    chosen = jnp.any(
        route_slot[:, :, None] == jnp.arange(slots, dtype=jnp.int32)[None, None, :], axis=1
    )
    gate, pull_back = jax.vjp(lambda lg: gate_weights(lg, slot_expert, chosen), gate_logits)
    lines = jnp.arange(NY * NX, dtype=jnp.int32)
    columns = jnp.stack([2 * lines, 2 * lines + 1, 2 * (lines ^ (NY * NX // 2)) + 1], axis=1)
    pick_slot = columns[:, :, None] == jnp.arange(slots, dtype=jnp.int32)[None, None, :]
    cols = jnp.sum(jnp.where(pick_slot[:, None], gate[None, :, None, :], 0.0), axis=3)
    stack = joined([own, plus, minus, far])
    stack, cols = lax.optimization_barrier((stack, cols))
    from_minus, from_plus = send(stack, outer(1)), send(stack, outer(-1))
    a_far, b_far = send(from_minus[:128], outer(1)), send(from_plus[128:], outer(-1))
    rows = [stack, from_plus, from_minus, a_far, b_far]
    rows_other = [send(piece, other_core()) for piece in rows]
    wall = send(pack_weights(sel, w_gate, w_up, w_down), other_core())

    cols = lax.all_to_all(cols, ("y", "x"), split_axis=0, concat_axis=0, tiled=True)
    ring = jnp.array(RING, jnp.int32)
    out_y = ((y + ring) % NY)[:, None] * NX + ((x + ring) % NX)[None, :]
    out_x = ((y + ring) % NY)[None, :] * NX + ((x + ring) % NX)[:, None]
    order = jnp.where(core == 0, out_y, out_x).reshape(-1)
    pick_line = order[:, None] == lines[None, :]
    cols = jnp.sum(jnp.where(pick_line[:, :, None, None], cols[None], 0.0), axis=1)
    cols = cols.reshape(NY * NX * tok, 3)
    gains = jnp.stack([cols[:, 0], cols[:, 1], cols[:, 1] + cols[:, 2]], axis=1)
    gains = jnp.pad(gains, ((0, 0), (0, 125)))

    sums = near_sums(sel, rows[:3], rows_other[:3], weights)
    acts, acts_grad = activations(sel, rows[3:], rows_other[3:], weights, sums, gains)
    acts_other = send(acts, other_core())
    grads = weight_grads(False, 0, 2, sel, rows, acts_grad, [])
    acts_other, grads = lax.optimization_barrier((acts_other, grads))

    far_a, far_b = results(((6,), (7,)), sel, acts, acts_other, weights, wall, half)
    own_a, own_b, to_plus, to_minus = results(
        ((0,), (1,), (2, 3), (5, 4)), sel, acts, acts_other, weights, wall, half
    )
    own_a, grads = lax.optimization_barrier((own_a, grads))
    from_a, from_b = send(far_a, outer(1)), send(far_b, outer(-1))
    to_plus = lax.dynamic_update_slice(to_plus, add(to_plus[:128], from_a), (0, 0))
    to_minus = lax.dynamic_update_slice(to_minus, add(to_minus[:128], from_b), (0, 0))
    got_p, got_m = send(to_plus, outer(1)), send(to_minus, outer(-1))
    grads = weight_grads(False, 2, 2, sel, rows, acts_grad, grads)
    grads = weight_grads(True, 0, 4, sel, rows_other, acts_grad, grads)
    (got_p, got_m), grads = lax.optimization_barrier(((got_p, got_m), grads))
    keep = (own_a[:64], got_p[:64], got_m[128:192])
    to_plus = add(own_a[64:], got_p[64:128], got_m[192:])
    to_minus = add(own_b[:64], got_p[128:192], got_m[:64])
    to_far = add(own_b[64:], got_p[192:], got_m[64:128])
    total = add(
        *keep, send(to_plus, inner(1)), send(to_minus, inner(-1)), send(to_far, inner(2))
    )

    def block_for(by):
        block = lax.dynamic_slice(total, (0, (z + by) % NZ * width), (2 * tok, width))
        return joined([block, total[:, half:]], axis=1)

    last = block_for(0).astype(F32)
    for by in (1, 3, 2):
        last = last + send(block_for(by), along_z(by)).astype(F32)
    mixed, grad_tokens = last[:tok, :width].astype(BF), last[tok:, :width].astype(BF)
    home = sum(last[:tok, width + at : width + at + slots] for at in (0, slots, 2 * slots))
    grad_logits = pull_back(home)[0]
    return (
        mixed,
        grad_tokens,
        grad_logits,
        grads[0].reshape(w_gate.shape),
        grads[1].reshape(w_up.shape),
        grads[2],
    )


def solution(mesh):
    split = Mesh(mesh.devices.reshape(NZ, NC, NY, NX), AXES)
    local, group = ("y", "x"), ("z", "c")
    return jax.shard_map(
        per_device,
        mesh=split,
        in_specs=(
            P(local, None),
            P(local, None),
            P(local, None),
            P(local, None),
            P(),
            P(local, None, group),
            P(local, None, group),
            P(local, group, None),
        ),
        out_specs=(
            P(local, group),
            P(local, group),
            P(local, None),
            P(local, None, group),
            P(local, None, group),
            P(local, group, None),
        ),
        check_vma=False,
    )
```

time: 191 us -> 360 us (1.88)
  Pallas kernels: 47.8 us -> 249 us
  starting transfers between devices: 53.5 us -> 32.5 us
  local copies, waits for them, and re-layouts: 25.5 us -> 9.29 us
  waiting for transfers between devices: 51.2 us -> 57.3 us
    pallas_call x1, Pallas kernels: 3.63 us -> 169 us  [pack_weights(): pl.pallas_call(pack_weights_kernel, in_specs=[SM, HB, HB, HB], out_specs=...]
    pallas_call x4, Pallas kernels: 18.9 us -> 47.1 us  [the longest x2 21.1 us: results(): pl.pallas_call(functools.partial(results_kernel, pieces), grid_spec=pltpu...]
    unnamed x58 -> x29, local copies, waits for them, and re-layouts: 19.7 us -> 3.11 us
    ppermute x35 -> x24, waiting for transfers between devices: 42.1 us -> 57.3 us  [send(): return lax.ppermute(value, AXES, pairs)]
    ppermute x35 -> x24, starting transfers between devices: 43.1 us -> 29 us  [send(): return lax.ppermute(value, AXES, pairs)]
    all_to_all x1 -> x0, waiting for transfers between devices: 7.89 us -> none  [per_device(): lax.all_to_all(home, ('y', 'x'), split_axis=0, concat_axis=0, tiled=True)]
    all_to_all x1 -> x0, starting transfers between devices: 6.41 us -> none  [per_device(): lax.all_to_all(home, ('y', 'x'), split_axis=0, concat_axis=0, tiled=True)]
    pallas_call x2 -> x3, Pallas kernels: 16.3 us -> 20.8 us  [weight_grads(): pl.pallas_call(functools.partial(grads_kernel, swapped), grid_spec=pltpu....]
  transfers between devices with their start and end apart: 37 -> 25, of which waited for: 15 -> 11; matrix products, arithmetic and copies ran while one was open for 8% -> 3% of each run, Pallas kernels for 21% -> 62%
where the time goes in v3:
time: 360 us; the launch traced here: 359 us
  Pallas kernels  249 us (69%)
  waiting for transfers between devices  57.3 us (16%)
  starting transfers between devices  32.5 us (9%)
  other arithmetic  10.5 us (3%)
  local copies, waits for them, and re-layouts  9.29 us (3%)
    pallas_call x1, Pallas kernels, pack_weights(): pl.pallas_call(pack_weights_kernel, in_specs=[SM, HB, HB, HB], out_specs=...  169 us
    ppermute x24, waiting for transfers between devices, send(): return lax.ppermute(value, AXES, pairs)  57.3 us
    ppermute x24, starting transfers between devices, send(): return lax.ppermute(value, AXES, pairs)  29 us
    pallas_call x2, Pallas kernels, results(): pl.pallas_call(functools.partial(results_kernel, pieces), grid_spec=pltpu...  21.1 us
    pallas_call x3, Pallas kernels, weight_grads(): pl.pallas_call(functools.partial(grads_kernel, swapped), grid_spec=pltpu....  20.8 us
    pallas_call x1, Pallas kernels, pack(): pl.pallas_call(pack_kernel, in_specs=[SM, HB, HB], out_specs=HB, out_shap...  15.7 us
    pallas_call x1, Pallas kernels, near_sums(): pl.pallas_call(near_kernel, grid_spec=pltpu.PrefetchScalarGridSpec(num_sc...  11.6 us
    pallas_call x1, Pallas kernels, activations(): pl.pallas_call(far_kernel, grid_spec=pltpu.PrefetchScalarGridSpec(num_sca...  10.2 us
  transfers between devices with their start and end apart: 25, of which 11 were waited for; matrix products, arithmetic and copies ran while one was open for 3% of the time, Pallas kernels for 62%

profile of v3, /device:TPU:0, one launch (start us, length us, event | category | flops | bytes accessed | tf_op | source)
XLA Modules:
  0.0 359.3 jit_solution(9243607246833918078)
XLA Ops:
  1.3 15.7 %pack.1 = bf16[64,3584]{1,0:T(8,128)(2,1)} custom-call(s32[3]{0:T(128)} %pad_add_fusion.1.sel, bf16[32,7168]{1,0:T(8,128)(2,1)} %tok.1, bf16[32,7168]{1,0:T(8,128)(2,1)} %cot.1), custom_call_target="tpu_custom_call" | custom-call | bytes 2097152 | tf_op jit(solution)/shard_map/pack/pallas_call | solution.py:279
  17.0 3.2 collective-permute-start.2
  20.8 2.6 collective-permute-start
  23.5 169.3 %pack_weights.1 = bf16[4,42,128,128]{3,2,1,0:T(8,128)(2,1)} custom-call(s32[3]{0:T(128)} %pad_add_fusion.1.sel, bf16[2,4,2,7,128,128]{5,4,3,2,1,0:T(8,128)(2,1)} %bitcast.11, bf16[2,4,2,7,128,128]{5,4,3,2,1,0:T(8,128)(2,1)} %bitcast.18, bf16[2,128,7168]{2,1,0:T(8,128)(2,1)} %wd.5), custom_call_target="tpu_custom_call" | custom-call | bytes 11534336 | tf_op jit(solution)/shard_map/pack_weights/pallas_call | solution.py:293
  195.9 3.1 collective-permute-start.5
  199.0 20.7 %collective-permute-done.5.refs_1_ = bf16[256,3584]{1,0:T(8,128)(2,1)} collective-permute-done((bf16[256,3584]{1,0:T(8,128)(2,1)S(1)}, bf16[256,3584]{1,0:T(8,128)(2,1)}, u32[]{:S(2)}, u32[]{:S(2)}) %collective-permute-start.5) | collective-permute-done | bytes 1835040 | tf_op jit(solution)/shard_map/ppermute | solution.py:51
  219.8 3.8 %collective-permute-done.3.refs_2_ = bf16[256,3584]{1,0:T(8,128)(2,1)} collective-permute-done((bf16[256,3584]{1,0:T(8,128)(2,1)S(1)}, bf16[256,3584]{1,0:T(8,128)(2,1)}, u32[]{:S(2)}, u32[]{:S(2)}) %collective-permute-start.3) | collective-permute-done | bytes 1835040 | tf_op jit(solution)/shard_map/ppermute | solution.py:51
  229.2 3.2 collective-permute-start.6
  232.6 3.5 all-to-all-start
  236.1 4.5 %collective-permute-done.4.refs_0_.refs_3_ = bf16[128,3584]{1,0:T(8,128)(2,1)S(1)} collective-permute-done((bf16[128,3584]{1,0:T(8,128)(2,1)}, bf16[128,3584]{1,0:T(8,128)(2,1)S(1)}, u32[]{:S(2)}, u32[]{:S(2)}) %collective-permute-start.4) | collective-permute-done | bytes 917536 | tf_op jit(solution)/shard_map/ppermute | solution.py:51
  240.6 3.4 collective-permute-done.6.refs_1_.refs_4_
  245.3 11.6 %near_sums.1 = (f32[512,256]{1,0:T(8,128)}, f32[512,256]{1,0:T(8,128)}, f32[512,256]{1,0:T(8,128)}) custom-call(s32[3]{0:T(128)} %pad_add_fusion.1.sel, bf16[256,3584]{1,0:T(8,128)(2,1)} %copy-done, bf16[256,3584]{1,0:T(8,128)(2,1)} %collective-permute-done.5.refs_1_, bf16[256,3584]{1,0:T(8,128)(2,1)} %collective-permute-done.3.refs_2_, ...), custom_call_target="tpu_custom_call" | custom-call | flops 4227858432 | bytes 23068672 | tf_op jit(solution)/shard_map/near_sums/pallas_call | solution.py:317
  256.9 10.2 %activations.1 = (bf16[512,896]{1,0:T(8,128)(2,1)}, bf16[512,768]{1,0:T(8,128)(2,1)}) custom-call(s32[3]{0:T(128)} %pad_add_fusion.1.sel, bf16[128,3584]{1,0:T(8,128)(2,1)} %copy-done.1, bf16[128,3584]{1,0:T(8,128)(2,1)} %collective-permute-done.6.refs_1_.refs_4_, bf16[128,3584]{1,0:T(8,128)(2,1)} %collective-permute-done.7.refs_2_.refs_3_, ...), custom_call_target="tpu_custom_call" | custom-call | flops 1409286144 | bytes 15728640 | tf_op jit(solution)/shard_map/activations/pallas_call | solution.py:334
  267.7 5.8 %weight_grads.3 = (bf16[2,4,2,896,128]{4,3,2,1,0:T(8,128)(2,1)}, bf16[2,4,2,896,128]{4,3,2,1,0:T(8,128)(2,1)}, bf16[2,128,7168]{2,1,0:T(8,128)(2,1)}) custom-call(s32[3]{0:T(128)} %pad_add_fusion.1.sel, bf16[256,3584]{1,0:T(8,128)(2,1)} %copy-done, bf16[256,3584]{1,0:T(8,128)(2,1)} %collective-permute-done.5.refs_1_, ...), custom_call_target="tpu_custom_call" | custom-call | flops 1409286144 | bytes 7340032 | tf_op jit(solution)/shard_map/weight_grads/pallas_call | solution.py:381
  274.5 9.2 %results.3 = (bf16[128,3712]{1,0:T(8,128)(2,1)}, bf16[128,3712]{1,0:T(8,128)(2,1)}) custom-call(s32[3]{0:T(128)} %pad_add_fusion.1.sel, bf16[512,896]{1,0:T(8,128)(2,1)} %get-tuple-element.46.acts, bf16[512,896]{1,0:T(8,128)(2,1)} %copy-done.3, bf16[2,4,2,896,128]{4,3,2,1,0:T(8,128)(2,1)} %bitcast.16, bf16[2,4,2,896,128]{4,3,2,1,0:T(8,128)(2,1)} %bitcast.23, ...), custom_call_target="tpu_custom_call" | custom-call | flops 1409286144 | bytes 14680064 | tf_op jit(solution)/shard_map/results/pallas_call | solution.py:357
  284.3 3.3 collective-permute-start.16
  287.6 11.9 %results.2 = (bf16[128,3712]{1,0:T(8,128)(2,1)}, bf16[128,3712]{1,0:T(8,128)(2,1)}, bf16[256,3712]{1,0:T(8,128)(2,1)}, bf16[256,3712]{1,0:T(8,128)(2,1)}) custom-call(s32[3]{0:T(128)} %pad_add_fusion.1.sel, bf16[512,896]{1,0:T(8,128)(2,1)} %get-tuple-element.46.acts, bf16[512,896]{1,0:T(8,128)(2,1)} %copy-done.3, bf16[2,4,2,896,128]{4,3,2,1,0:T(8,128)(2,1)} %bitcast.17, ...), custom_call_target="tpu_custom_call" | custom-call | flops 4227858432 | bytes 18874368 | tf_op jit(solution)/shard_map/results/pallas_call | solution.py:357
  302.4 3.3 collective-permute-start.17
  305.7 5.8 %weight_grads.4 = (bf16[2,4,2,896,128]{4,3,2,1,0:T(8,128)(2,1)}, bf16[2,4,2,896,128]{4,3,2,1,0:T(8,128)(2,1)}, bf16[2,128,7168]{2,1,0:T(8,128)(2,1)}) custom-call(s32[3]{0:T(128)} %pad_add_fusion.1.sel, bf16[256,3584]{1,0:T(8,128)(2,1)} %copy-done, ...), custom_call_target="tpu_custom_call", output_to_operand_aliasing={{0}: (7, {}), {1}: (8, {}), {2}: (9, {})} | custom-call | flops 1409286144 | bytes 7340032 | tf_op jit(solution)/shard_map/weight_grads/pallas_call | solution.py:381
  311.6 9.1 %weight_grads.5 = (bf16[2,4,2,896,128]{4,3,2,1,0:T(8,128)(2,1)}, bf16[2,4,2,896,128]{4,3,2,1,0:T(8,128)(2,1)}, bf16[2,128,7168]{2,1,0:T(8,128)(2,1)}) custom-call(s32[3]{0:T(128)} %pad_add_fusion.1.sel, bf16[256,3584]{1,0:T(8,128)(2,1)} %copy-done.2, ...), custom_call_target="tpu_custom_call", output_to_operand_aliasing={{0}: (7, {}), {1}: (8, {}), {2}: (9, {})} | custom-call | flops 2818572288 | bytes 14680064 | tf_op jit(solution)/shard_map/weight_grads/pallas_call | solution.py:381
  320.7 6.8 %collective-permute-done.15 = bf16[256,3712]{1,0:T(8,128)(2,1)S(1)} collective-permute-done((bf16[256,3712]{1,0:T(8,128)(2,1)}, bf16[256,3712]{1,0:T(8,128)(2,1)S(1)}, u32[]{:S(2)}, u32[]{:S(2)}) %collective-permute-start.15) | collective-permute-done | bytes 1900576 | tf_op jit(solution)/shard_map/ppermute | solution.py:51
  331.6 8.1 %collective-permute-done.20 = bf16[64,3712]{1,0:T(8,128)(2,1)S(1)} collective-permute-done((bf16[64,3712]{1,0:T(8,128)(2,1)}, bf16[64,3712]{1,0:T(8,128)(2,1)S(1)}, u32[]{:S(2)}, u32[]{:S(2)}) %collective-permute-start.20) | collective-permute-done | bytes 475168 | tf_op jit(solution)/shard_map/ppermute | solution.py:51
  339.7 4.0 %collective-permute-done.19 = bf16[64,3712]{1,0:T(8,128)(2,1)} collective-permute-done((bf16[64,3712]{1,0:T(8,128)(2,1)}, bf16[64,3712]{1,0:T(8,128)(2,1)}, u32[]{:S(2)}, u32[]{:S(2)}) %collective-permute-start.19) | collective-permute-done | bytes 475168 | tf_op jit(solution)/shard_map/ppermute | solution.py:51
  346.6 4.0 %collective-permute-start.23 = (bf16[64,1024]{1,0:T(8,128)(2,1)S(1)}, bf16[64,1024]{1,0:T(8,128)(2,1)S(1)}, u32[]{:S(2)}, u32[]{:S(2)}) collective-permute-start(bf16[64,1024]{1,0:T(8,128)(2,1)S(1)} %get-tuple-element.101), channel_id=1, source_target_pairs={{0,64},{1,65},{2,66},{3,67},{4,68},{5,69},{6,70},{7,71},{8,72},{9,... | collective-permute-start | bytes 393224 | tf_op jit(solution)/shard_map/ppermute | solution.py:51
  (106 shorter events, 32.2 us)
Async XLA Ops:
  17.0 177.7 %collective-permute-start.2 = (bf16[64,3584]{1,0:T(8,128)(2,1)}, bf16[64,3584]{1,0:T(8,128)(2,1)S(1)}, u32[]{:S(2)}, u32[]{:S(2)}) collective-permute-start(bf16[64,3584]{1,0:T(8,128)(2,1)} %pack.1), channel_id=1, source_target_pairs={{0,2},{1,3},{2,0},{3,1},{4,6},{5,7},{6,4},{7,5},{8,10},{9,11},{10,... | collective-permute-start | bytes 1376264 | tf_op jit(solution)/shard_map/ppermute | solution.py:51
  20.2 174.5 %collective-permute-start.1 = (bf16[64,3584]{1,0:T(8,128)(2,1)}, bf16[64,3584]{1,0:T(8,128)(2,1)S(1)}, u32[]{:S(2)}, u32[]{:S(2)}) collective-permute-start(bf16[64,3584]{1,0:T(8,128)(2,1)} %pack.1), channel_id=1, source_target_pairs={{0,1},{1,2},{2,3},{3,0},{4,5},{5,6},{6,7},{7,4},{8,9},{9,10},{10,1... | collective-permute-start | bytes 1376264 | tf_op jit(solution)/shard_map/ppermute | solution.py:51
  20.8 173.9 %collective-permute-start = (bf16[64,3584]{1,0:T(8,128)(2,1)}, bf16[64,3584]{1,0:T(8,128)(2,1)}, u32[]{:S(2)}, u32[]{:S(2)}) collective-permute-start(bf16[64,3584]{1,0:T(8,128)(2,1)} %pack.1), channel_id=1, source_target_pairs={{0,3},{1,0},{2,1},{3,2},{4,7},{5,4},{6,5},{7,6},{8,11},{9,8},{10,9... | collective-permute-start | bytes 1376264 | tf_op jit(solution)/shard_map/ppermute | solution.py:51
  192.8 80.8 %collective-permute-start.13 = (bf16[4,42,128,128]{3,2,1,0:T(8,128)(2,1)}, bf16[4,42,128,128]{3,2,1,0:T(8,128)(2,1)}, u32[]{:S(2)}, u32[]{:S(2)}) collective-permute-start(bf16[4,42,128,128]{3,2,1,0:T(8,128)(2,1)} %pack_weights.1), channel_id=1, source_target_pairs={{0,16},{1,17},{2,18},{3,19},{4,20},{5,21},{6,22},{7,23},{8,24},{9,... | collective-permute-start | bytes 16515080 | tf_op jit(solution)/shard_map/ppermute | solution.py:51
  195.9 23.8 %collective-permute-start.5 = (bf16[256,3584]{1,0:T(8,128)(2,1)S(1)}, bf16[256,3584]{1,0:T(8,128)(2,1)}, u32[]{:S(2)}, u32[]{:S(2)}) collective-permute-start(bf16[256,3584]{1,0:T(8,128)(2,1)S(1)} %pad_maximum_fusion.refs_0_), channel_id=1, source_target_pairs={{0,12},{1,13},{2,14},{3,15},{4,0},{5,1},{6,2},{7,3},{8,4},{9,5},{1... | collective-permute-start | bytes 5505032 | tf_op jit(solution)/shard_map/ppermute | solution.py:51
  199.0 24.5 %collective-permute-start.3 = (bf16[256,3584]{1,0:T(8,128)(2,1)S(1)}, bf16[256,3584]{1,0:T(8,128)(2,1)}, u32[]{:S(2)}, u32[]{:S(2)}) collective-permute-start(bf16[256,3584]{1,0:T(8,128)(2,1)S(1)} %pad_maximum_fusion.refs_0_), channel_id=1, source_target_pairs={{0,4},{1,5},{2,6},{3,7},{4,8},{5,9},{6,10},{7,11},{8,12},{9,13},{1... | collective-permute-start | bytes 5505032 | tf_op jit(solution)/shard_map/ppermute | solution.py:51
  199.0 28.9 %collective-permute-start.9 = (bf16[256,3584]{1,0:T(8,128)(2,1)S(1)}, bf16[256,3584]{1,0:T(8,128)(2,1)S(1)}, u32[]{:S(2)}, u32[]{:S(2)}) collective-permute-start(bf16[256,3584]{1,0:T(8,128)(2,1)S(1)} %pad_maximum_fusion.refs_0_), channel_id=1, source_target_pairs={{0,16},{1,17},{2,18},{3,19},{4,20},{5,21},{6,22},{7,23},{8,24},{9,... | collective-permute-start | bytes 5505032 | tf_op jit(solution)/shard_map/ppermute | solution.py:51
  219.7 25.5 %collective-permute-start.10 = (bf16[256,3584]{1,0:T(8,128)(2,1)}, bf16[256,3584]{1,0:T(8,128)(2,1)}, u32[]{:S(2)}, u32[]{:S(2)}) collective-permute-start(bf16[256,3584]{1,0:T(8,128)(2,1)} %collective-permute-done.5.refs_1_), channel_id=1, source_target_pairs={{0,16},{1,17},{2,18},{3,19},{4,20},{5,21},{6,22},{7,23},{8,24},{9,... | collective-permute-start | bytes 5505032 | tf_op jit(solution)/shard_map/ppermute | solution.py:51
  223.5 21.8 %collective-permute-start.11 = (bf16[256,3584]{1,0:T(8,128)(2,1)}, bf16[256,3584]{1,0:T(8,128)(2,1)}, u32[]{:S(2)}, u32[]{:S(2)}) collective-permute-start(bf16[256,3584]{1,0:T(8,128)(2,1)} %collective-permute-done.3.refs_2_), channel_id=1, source_target_pairs={{0,16},{1,17},{2,18},{3,19},{4,20},{5,21},{6,22},{7,23},{8,24},{9,... | collective-permute-start | bytes 5505032 | tf_op jit(solution)/shard_map/ppermute | solution.py:51
  225.7 14.9 %collective-permute-start.4 = (bf16[128,3584]{1,0:T(8,128)(2,1)}, bf16[128,3584]{1,0:T(8,128)(2,1)S(1)}, u32[]{:S(2)}, u32[]{:S(2)}) collective-permute-start(bf16[128,3584]{1,0:T(8,128)(2,1)} %slice.107), channel_id=1, source_target_pairs={{0,4},{1,5},{2,6},{3,7},{4,8},{5,9},{6,10},{7,11},{8,12},{9,13},{1... | collective-permute-start | bytes 2752520 | tf_op jit(solution)/shard_map/ppermute | solution.py:51
  229.2 14.8 %collective-permute-start.6 = (bf16[128,3584]{1,0:T(8,128)(2,1)}, bf16[128,3584]{1,0:T(8,128)(2,1)}, u32[]{:S(2)}, u32[]{:S(2)}) collective-permute-start(bf16[128,3584]{1,0:T(8,128)(2,1)} %slice.108), channel_id=1, source_target_pairs={{0,12},{1,13},{2,14},{3,15},{4,0},{5,1},{6,2},{7,3},{8,4},{9,5},{1... | collective-permute-start | bytes 2752520 | tf_op jit(solution)/shard_map/ppermute | solution.py:51
  232.6 11.5 %all-to-all-start = ((f32[16,32,3]{1,2,0:T(4,128)}), f32[16,32,3]{1,2,0:T(4,128)S(1)}, u32[]{:S(2)}, u32[]{:S(2)}) async-start(f32[16,32,3]{1,2,0:T(4,128)} %select_reduce_fusion), calls=%async_computation | async-start | bytes 65536 | tf_op jit(solution)/shard_map/all_to_all | solution.py:442
  240.6 16.3 %collective-permute-start.7 = (bf16[128,3584]{1,0:T(8,128)(2,1)S(1)}, bf16[128,3584]{1,0:T(8,128)(2,1)}, u32[]{:S(2)}, u32[]{:S(2)}) collective-permute-start(bf16[128,3584]{1,0:T(8,128)(2,1)S(1)} %collective-permute-done.4.refs_0_.refs_3_), channel_id=1, source_target_pairs={{0,16},{1,17},{2,18},{3,19},{4,20},{5,21},{6,22},{7,23},{8,24},{9,... | collective-permute-start | bytes 2752520 | tf_op jit(solution)/shard_map/ppermute | solution.py:51
  244.0 12.9 %collective-permute-start.8 = (bf16[128,3584]{1,0:T(8,128)(2,1)}, bf16[128,3584]{1,0:T(8,128)(2,1)}, u32[]{:S(2)}, u32[]{:S(2)}) collective-permute-start(bf16[128,3584]{1,0:T(8,128)(2,1)} %collective-permute-done.6.refs_1_.refs_4_), channel_id=1, source_target_pairs={{0,16},{1,17},{2,18},{3,19},{4,20},{5,21},{6,22},{7,23},{8,24},{9,... | collective-permute-start | bytes 2752520 | tf_op jit(solution)/shard_map/ppermute | solution.py:51
  267.1 6.4 %collective-permute-start.12 = (bf16[512,896]{1,0:T(8,128)(2,1)}, bf16[512,896]{1,0:T(8,128)(2,1)S(1)}, u32[]{:S(2)}, u32[]{:S(2)}) collective-permute-start(bf16[512,896]{1,0:T(8,128)(2,1)} %get-tuple-element.46.acts), channel_id=1, source_target_pairs={{0,16},{1,17},{2,18},{3,19},{4,20},{5,21},{6,22},{7,23},{8,24},{9,... | collective-permute-start | bytes 2752520 | tf_op jit(solution)/shard_map/ppermute | solution.py:51
  283.6 15.9 %collective-permute-start.14 = (bf16[128,3712]{1,0:T(8,128)(2,1)}, bf16[128,3712]{1,0:T(8,128)(2,1)S(1)}, u32[]{:S(2)}, u32[]{:S(2)}) collective-permute-start(bf16[128,3712]{1,0:T(8,128)(2,1)} %get-tuple-element.58), channel_id=1, source_target_pairs={{0,4},{1,5},{2,6},{3,7},{4,8},{5,9},{6,10},{7,11},{8,12},{9,13},{1... | collective-permute-start | bytes 2850824 | tf_op jit(solution)/shard_map/ppermute | solution.py:51
  284.3 17.9 %collective-permute-start.16 = (bf16[128,3712]{1,0:T(8,128)(2,1)}, bf16[128,3712]{1,0:T(8,128)(2,1)S(1)}, u32[]{:S(2)}, u32[]{:S(2)}) collective-permute-start(bf16[128,3712]{1,0:T(8,128)(2,1)} %get-tuple-element.60), channel_id=1, source_target_pairs={{0,12},{1,13},{2,14},{3,15},{4,0},{5,1},{6,2},{7,3},{8,4},{9,5},{1... | collective-permute-start | bytes 2850824 | tf_op jit(solution)/shard_map/ppermute | solution.py:51
  302.1 25.3 %collective-permute-start.15 = (bf16[256,3712]{1,0:T(8,128)(2,1)}, bf16[256,3712]{1,0:T(8,128)(2,1)S(1)}, u32[]{:S(2)}, u32[]{:S(2)}) collective-permute-start(bf16[256,3712]{1,0:T(8,128)(2,1)} %fusion), channel_id=1, source_target_pairs={{0,4},{1,5},{2,6},{3,7},{4,8},{5,9},{6,10},{7,11},{8,12},{9,13},{1... | collective-permute-start | bytes 5701640 | tf_op jit(solution)/shard_map/ppermute | solution.py:51
  302.4 25.0 %collective-permute-start.17 = (bf16[256,3712]{1,0:T(8,128)(2,1)S(1)}, bf16[256,3712]{1,0:T(8,128)(2,1)S(1)}, u32[]{:S(2)}, u32[]{:S(2)}) collective-permute-start(bf16[256,3712]{1,0:T(8,128)(2,1)S(1)} %fusion.1), channel_id=1, source_target_pairs={{0,12},{1,13},{2,14},{3,15},{4,0},{5,1},{6,2},{7,3},{8,4},{9,5},{1... | collective-permute-start | bytes 5701640 | tf_op jit(solution)/shard_map/ppermute | solution.py:51
  329.2 10.5 %collective-permute-start.20 = (bf16[64,3712]{1,0:T(8,128)(2,1)}, bf16[64,3712]{1,0:T(8,128)(2,1)S(1)}, u32[]{:S(2)}, u32[]{:S(2)}) collective-permute-start(bf16[64,3712]{1,0:T(8,128)(2,1)} %get-tuple-element.91), channel_id=1, source_target_pairs={{0,2},{1,3},{2,0},{3,1},{4,6},{5,7},{6,4},{7,5},{8,10},{9,11},{10,... | collective-permute-start | bytes 1425416 | tf_op jit(solution)/shard_map/ppermute | solution.py:51
  329.2 14.4 %collective-permute-start.19 = (bf16[64,3712]{1,0:T(8,128)(2,1)}, bf16[64,3712]{1,0:T(8,128)(2,1)}, u32[]{:S(2)}, u32[]{:S(2)}) collective-permute-start(bf16[64,3712]{1,0:T(8,128)(2,1)} %get-tuple-element.90), channel_id=1, source_target_pairs={{0,3},{1,0},{2,1},{3,2},{4,7},{5,4},{6,5},{7,6},{8,11},{9,8},{10,9... | collective-permute-start | bytes 1425416 | tf_op jit(solution)/shard_map/ppermute | solution.py:51
  331.2 13.5 %collective-permute-start.18 = (bf16[64,3712]{1,0:T(8,128)(2,1)}, bf16[64,3712]{1,0:T(8,128)(2,1)}, u32[]{:S(2)}, u32[]{:S(2)}) collective-permute-start(bf16[64,3712]{1,0:T(8,128)(2,1)} %get-tuple-element.92), channel_id=1, source_target_pairs={{0,1},{1,2},{2,3},{3,0},{4,5},{5,6},{6,7},{7,4},{8,9},{9,10},{10,1... | collective-permute-start | bytes 1425416 | tf_op jit(solution)/shard_map/ppermute | solution.py:51
  346.6 8.4 %collective-permute-start.23 = (bf16[64,1024]{1,0:T(8,128)(2,1)S(1)}, bf16[64,1024]{1,0:T(8,128)(2,1)S(1)}, u32[]{:S(2)}, u32[]{:S(2)}) collective-permute-start(bf16[64,1024]{1,0:T(8,128)(2,1)S(1)} %get-tuple-element.101), channel_id=1, source_target_pairs={{0,64},{1,65},{2,66},{3,67},{4,68},{5,69},{6,70},{7,71},{8,72},{9,... | collective-permute-start | bytes 393224 | tf_op jit(solution)/shard_map/ppermute | solution.py:51
  351.2 6.2 %collective-permute-start.21 = (bf16[64,1024]{1,0:T(8,128)(2,1)S(1)}, bf16[64,1024]{1,0:T(8,128)(2,1)S(1)}, u32[]{:S(2)}, u32[]{:S(2)}) collective-permute-start(bf16[64,1024]{1,0:T(8,128)(2,1)S(1)} %get-tuple-element.99), channel_id=1, source_target_pairs={{0,32},{1,33},{2,34},{3,35},{4,36},{5,37},{6,38},{7,39},{8,40},{9,... | collective-permute-start | bytes 393224 | tf_op jit(solution)/shard_map/ppermute | solution.py:51
  (14 other events, 824.9 us)

commit v4 on v3

--- a/solution.py
+++ b/solution.py
@@ -58,12 +58,8 @@
 def rows_of(refs, blocks, second):
     parts = []
     for outer_at, inner_at in blocks:
-        ref, row = refs[outer_at] if outer_at < 3 else refs[-2 + inner_at // 2], 64 * inner_at
-        if outer_at == 3:
-            row = 64 * (inner_at % 2)
-        if second:
-            row += 32
-        parts.append(ref[row : row + 32, :])
+        row = 64 * (inner_at % 2) + (32 if second else 0)
+        parts.append(refs[2 * outer_at + inner_at // 2][row : row + 32, :])
     return joined(parts)
 
 
@@ -87,6 +83,15 @@
     return gate, up, wd[...].reshape(-1, wd.shape[2])
 
 
+def up_block(ref, k, half):
+    return pair(ref[0, k, half], ref[1, k, half])
+
+
+def down_block(ref, k, half, width):
+    at = pl.multiple_of((2 * k + half) * width, 128)
+    return ref[:, :, pl.ds(at, width)].reshape(-1, width)
+
+
 def products(tok, cot, gate, up, down):
     first = jnp.dot(tok, gate, preferred_element_type=F32)
     second = jnp.dot(tok, up, preferred_element_type=F32)
@@ -94,63 +99,55 @@
     return first, second, back
 
 
-def pack_kernel(sel, tok, cot, packed, sems):
-    rows, width = tok.shape[0], tok.shape[1] // (2 * STEPS)
-    copies = []
-    for k in range(STEPS):
-        at = pl.multiple_of((2 * k + sel[0]) * width, 128)
-        for base, ref in enumerate((tok, cot)):
-            target = packed.at[pl.ds(base * rows, rows), pl.ds(k * width, width)]
-            copies.append(pltpu.make_async_copy(ref.at[:, pl.ds(at, width)], target, sems.at[len(copies)]))
-            copies[-1].start()
-    for one in copies:
-        one.wait()
-
-
-def pack_weights_kernel(sel, wg, wu, wd, wall, sems):
-    away = sel[1]
-    copies = []
-
-    def copy(source, target):
-        copies.append(pltpu.make_async_copy(source, target, sems.at[len(copies)]))
-        copies[-1].start()
-
-    for k in range(STEPS):
-        for base, ref in ((0, wg), (14, wu)):
-            for slot in range(2):
-                copy(ref.at[slot, k, away], wall.at[k, pl.ds(base + 7 * slot, 7)])
-        for q in range(7):
-            at = pl.multiple_of((2 * k + away) * 896 + q * 128, 128)
-            for slot in range(2):
-                copy(wd.at[slot, :, pl.ds(at, 128)], wall.at[k, 28 + 2 * q + slot])
-    for one in copies:
-        one.wait()
-
-
-def accumulate(sums, own, other, mine, theirs, own_blocks, other_blocks):
-    there = turned(other_blocks)
-    a = products(
-        rows_of(own, own_blocks, False), rows_of(own, own_blocks, True), *weight_block(*mine)
-    )
-    b = products(rows_of(other, there, False), rows_of(other, there, True), *weight_block(*theirs))
-    for ref, one, two in zip(sums, a, b):
-        for blocks, value in ((own_blocks, one), (other_blocks, two)):
-            for outer_at in sorted({o for o, _ in blocks}):
-                inners = [i for o, i in blocks if o == outer_at]
-                low = 32 * blocks.index((outer_at, inners[0]))
-                to = 32 * (4 * outer_at + inners[0])
-                ref[to : to + 32 * len(inners)] += value[low : low + 32 * len(inners)]
+def pack_kernel(sel, tok, cot, packed):
+    rows = tok.shape[0]
+    packed[:rows] = tok[...]
+    packed[rows:] = cot[...]
+
+
+def pack_weights_kernel(sel, wg, wu, wd, wall):
+    for base, ref in ((0, wg), (14, wu)):
+        for slot in range(2):
+            at = base + 7 * slot
+            wall[0, at : at + 7] = ref[slot, 0, 0].reshape(7, 128, 128)
+    for q in range(7):
+        wall[0, 28 + 2 * q : 30 + 2 * q] = wd[:, :, 128 * q : 128 * q + 128]
+
+
+def multiply(sums, rows, weights, blocks, swapped):
+    where = turned(blocks) if swapped else blocks
+    parts = products(
+        rows_of(rows, where, False), rows_of(rows, where, True), *weight_block(*weights)
+    )
+    for ref, part in zip(sums, parts):
+        for outer_at in sorted({o for o, _ in blocks}):
+            inners = [i for o, i in blocks if o == outer_at]
+            low = 32 * blocks.index((outer_at, inners[0]))
+            to = 32 * (4 * outer_at + inners[0])
+            ref[to : to + 32 * len(inners)] += part[low : low + 32 * len(inners)]
 
 
 def near_kernel(sel, *refs):
-    own, other, mine, theirs, sums = refs[:3], refs[3:6], refs[6:9], refs[9:12], refs[12:15]
+    own, other, mine, theirs, sums = refs[:6], refs[6:12], refs[12:15], refs[15:18], refs[18:21]
 
     @pl.when(pl.program_id(0) == 0)
     def _():
         for ref in sums:
             ref[...] = jnp.zeros_like(ref)
 
-    accumulate(sums, own, other, mine, theirs, NEAR_OWN, NEAR_OTHER)
+    multiply(sums, own, mine, NEAR_OWN, False)
+    multiply(sums, other, theirs, NEAR_OTHER, True)
+
+
+def far_own_kernel(sel, *refs):
+    own, mine, start, sums = dict(zip((6, 7), refs)), refs[2:5], refs[5:8], refs[8:11]
+
+    @pl.when(pl.program_id(0) == 0)
+    def _():
+        for ref, before in zip(sums, start):
+            ref[...] = before[...]
+
+    multiply(sums, own, mine, FAR_OWN, False)
 
 
 def thirds(value):
@@ -159,18 +156,17 @@
     return high, middle, value - high - middle
 
 
-def far_kernel(sel, *refs):
-    own, other, mine, theirs = refs[:2], refs[2:4], refs[4:7], refs[7:10]
-    start, gains = refs[10:13], refs[13]
-    acts, acts_grad = refs[14:16]
-    sums = refs[16:19]
+def far_other_kernel(sel, *refs):
+    other, theirs, start, gains = dict(zip((6, 7), refs)), refs[2:5], refs[5:8], refs[8]
+    acts, acts_grad = refs[9:11]
+    sums = refs[11:14]
 
     @pl.when(pl.program_id(0) == 0)
     def _():
         for ref, before in zip(sums, start):
             ref[...] = before[...]
 
-    accumulate(sums, own, other, mine, theirs, FAR_OWN, FAR_OTHER)
+    multiply(sums, other, theirs, FAR_OTHER, True)
 
     @pl.when(pl.program_id(0) == STEPS - 1)
     def _():
@@ -200,6 +196,7 @@
 
 
 def results_kernel(pieces, sel, acts, acts_other, wg, wu, wd, wall, *outs):
+    half = sel[0]
     blocks = [(p // 2, 2 * (p % 2) + b) for group in pieces for p in group for b in range(2)]
     places = [(at, 64 * row) for at, group in enumerate(pieces) for row in range(2 * len(group))]
     own = joined([acts[32 * (4 * a + b) : 32 * (4 * a + b) + 32, :] for a, b in blocks])
@@ -208,38 +205,32 @@
     grads = pair(own[:, 256:768], other[:, 256:768])
     total = outs[0].shape[1] - 128
     width = total // STEPS
-    k = pl.program_id(0)
-
-    @pl.when(k == STEPS - 1)
-    def _():
-        lane = lax.broadcasted_iota(jnp.int32, (own.shape[0], 128), 1)
-        dots = jnp.zeros((own.shape[0], 128), F32)
-        last = own[:, 768:].astype(F32) + other[:, 768:].astype(F32)
-        for slot in range(2):
-            mine = jnp.sum(jnp.where((lane < 6) & (lane % 2 == slot), last, 0.0), axis=1, keepdims=True)
-            for at, part in enumerate(thirds(mine)):
-                dots = jnp.where(lane == 32 * at + 2 * sel[2] + slot, part, dots)
+    lane = lax.broadcasted_iota(jnp.int32, (own.shape[0], 128), 1)
+    dots = jnp.zeros((own.shape[0], 128), F32)
+    last = own[:, 768:].astype(F32) + other[:, 768:].astype(F32)
+    for slot in range(2):
+        mine = jnp.sum(jnp.where((lane < 6) & (lane % 2 == slot), last, 0.0), axis=1, keepdims=True)
+        for at, part in enumerate(thirds(mine)):
+            dots = jnp.where(lane == 32 * at + 2 * sel[2] + slot, part, dots)
+    for block, (at, row) in enumerate(places):
+        outs[at][row : row + 32, total:] = dots[32 * block : 32 * block + 32].astype(BF)
+        outs[at][row + 32 : row + 64, total:] = jnp.zeros((32, 128), BF)
+    for k in range(STEPS):
+        cols = slice(k * width, k * width + width)
+        down = joined([wall[k, 28 + 2 * q : 30 + 2 * q].reshape(256, 128) for q in range(7)], axis=1)
+        down = joined([down_block(wd, k, half, width), down])
+        up = [up_block(wg, k, half), up_block(wu, k, half)]
+        up += [wall[k, at : at + 7].reshape(width, 128) for at in (0, 7, 14, 21)]
+        out = jnp.dot(hidden, down, preferred_element_type=F32)
+        grad = lax.dot_general(grads, joined(up, axis=1), NT, preferred_element_type=F32)
         for block, (at, row) in enumerate(places):
-            outs[at][row : row + 32, total:] = dots[32 * block : 32 * block + 32].astype(BF)
-            outs[at][row + 32 : row + 64, total:] = jnp.zeros((32, 128), BF)
-
-    tiles = [
-        joined([wall[0, 28 + 2 * q : 30 + 2 * q].reshape(256, 128) for q in range(7)], axis=1)
-    ]
-    gate, up, down = weight_block(wg, wu, wd)
-    down = joined([down, *tiles])
-    ups = [gate, up] + [wall[0, at : at + 7].reshape(width, 128) for at in (0, 7, 14, 21)]
-    out = jnp.dot(hidden, down, preferred_element_type=F32)
-    grad = lax.dot_general(grads, joined(ups, axis=1), NT, preferred_element_type=F32)
-    cols = pl.ds(pl.multiple_of(k * width, 128), width)
-    for block, (at, row) in enumerate(places):
-        here = slice(32 * block, 32 * block + 32)
-        outs[at][row : row + 32, cols] = out[here].astype(BF)
-        outs[at][row + 32 : row + 64, cols] = grad[here].astype(BF)
+            here = slice(32 * block, 32 * block + 32)
+            outs[at][row : row + 32, cols] = out[here].astype(BF)
+            outs[at][row + 32 : row + 64, cols] = grad[here].astype(BF)
 
 
 def grads_kernel(swapped, sel, *refs):
-    rows, acts = refs[:5], refs[5]
+    rows, acts = refs[:8], refs[8]
     grad_gate, grad_up, grad_down = refs[-3:]
     blocks = turned(ALL) if swapped else ALL
     tok, cot = rows_of(rows, blocks, False), rows_of(rows, blocks, True)
@@ -276,30 +267,41 @@
 
 
 def pack(sel, tokens, cotangent):
+    tok, wide = tokens.shape
+    width = wide // (2 * STEPS)
+    spec = pl.BlockSpec((tok, width), lambda k, sel: (0, 2 * k + sel[0]))
     return pl.pallas_call(
         pack_kernel,
-        in_specs=[SM, HB, HB],
-        out_specs=HB,
-        out_shape=shape((2 * tokens.shape[0], tokens.shape[1] // 2)),
-        scratch_shapes=[pltpu.SemaphoreType.DMA((2 * STEPS,))],
+        grid_spec=pltpu.PrefetchScalarGridSpec(
+            num_scalar_prefetch=1,
+            grid=(STEPS,),
+            in_specs=[spec, spec],
+            out_specs=pl.BlockSpec((2 * tok, width), lambda k, sel: (0, k)),
+        ),
+        out_shape=shape((2 * tok, wide // 2)),
         compiler_params=params(60),
         cost_estimate=cost(0, 2),
         name="pack",
     )(sel, tokens, cotangent)
 
 
-def pack_weights(sel, w_gate, w_up, w_down):
-    views = [w.reshape(2, STEPS, 2, 7, 128, 128) for w in (w_gate, w_up)]
+def pack_weights(sel, weights):
+    width = weights[0].shape[3]
+    up_spec = pl.BlockSpec((2, 1, 1, width, 128), lambda k, sel: (0, k, sel[1], 0, 0))
+    down_spec = pl.BlockSpec((2, 128, width), lambda k, sel: (0, 0, 2 * k + sel[1]))
     return pl.pallas_call(
         pack_weights_kernel,
-        in_specs=[SM, HB, HB, HB],
-        out_specs=HB,
+        grid_spec=pltpu.PrefetchScalarGridSpec(
+            num_scalar_prefetch=1,
+            grid=(STEPS,),
+            in_specs=[up_spec, up_spec, down_spec],
+            out_specs=pl.BlockSpec((1, 42, 128, 128), lambda k, sel: (k, 0, 0, 0)),
+        ),
         out_shape=shape((STEPS, 42, 128, 128)),
-        scratch_shapes=[pltpu.SemaphoreType.DMA((72,))],
         compiler_params=params(60),
-        cost_estimate=cost(0, 11),
+        cost_estimate=cost(0, 0.1),
         name="pack_weights",
-    )(sel, *views, w_down)
+    )(sel, *weights)
 
 
 def weight_specs(width, which):
@@ -324,20 +326,36 @@
         ),
         out_shape=[shape((512, 256), F32)] * 3,
         compiler_params=params(58),
-        cost_estimate=cost(4 * 384 * 768 * width * STEPS, 22),
+        cost_estimate=cost(0, 0.1),
         name="near_sums",
     )(sel, *own, *other, *weights, *weights)
 
 
-def activations(sel, own, other, weights, sums, gains):
+def far_sums(sel, own, weights, sums):
     width = own[0].shape[1] // STEPS
     return pl.pallas_call(
-        far_kernel,
+        far_own_kernel,
         grid_spec=pltpu.PrefetchScalarGridSpec(
             num_scalar_prefetch=1,
             grid=(STEPS,),
-            in_specs=row_specs(own + other, width)
-            + weight_specs(width, 0)
+            in_specs=row_specs(own, width) + weight_specs(width, 0) + [whole((512, 256))] * 3,
+            out_specs=[whole((512, 256))] * 3,
+        ),
+        out_shape=[shape((512, 256), F32)] * 3,
+        compiler_params=params(50),
+        cost_estimate=cost(2 * 128 * 768 * width * STEPS, 10),
+        name="far_sums",
+    )(sel, *own, *weights, *sums)
+
+
+def activations(sel, other, weights, sums, gains):
+    width = other[0].shape[1] // STEPS
+    return pl.pallas_call(
+        far_other_kernel,
+        grid_spec=pltpu.PrefetchScalarGridSpec(
+            num_scalar_prefetch=1,
+            grid=(STEPS,),
+            in_specs=row_specs(other, width)
             + weight_specs(width, 1)
             + [whole((512, 256))] * 3
             + [whole((512, 128))],
@@ -345,28 +363,20 @@
             scratch_shapes=[pltpu.VMEM((512, 256), F32)] * 3,
         ),
         out_shape=[shape((512, 896)), shape((512, 768))],
-        compiler_params=params(58),
-        cost_estimate=cost(4 * 128 * 768 * own[0].shape[1], 15),
+        compiler_params=params(50),
+        cost_estimate=cost(2 * 128 * 768 * width * STEPS, 10),
         name="activations",
-    )(sel, *own, *other, *weights, *weights, *sums, gains)
+    )(sel, *other, *weights, *sums, gains)
 
 
 def results(pieces, sel, acts, acts_other, weights, wall, half):
-    width = half // STEPS
-    sizes = [128 * len(group) for group in pieces]
     return pl.pallas_call(
         functools.partial(results_kernel, pieces),
-        grid_spec=pltpu.PrefetchScalarGridSpec(
-            num_scalar_prefetch=1,
-            grid=(STEPS,),
-            in_specs=[whole((512, 896))] * 2
-            + weight_specs(width, 0)
-            + [pl.BlockSpec((1, 42, 128, 128), lambda k, sel: (k, 0, 0, 0))],
-            out_specs=[VM] * len(sizes),
-        ),
-        out_shape=[shape((size, half + 128)) for size in sizes],
-        compiler_params=params(60 - sum(sizes) // 128),
-        cost_estimate=cost(sum(sizes) * 1536 * half, 12 + sum(sizes) // 128),
+        in_specs=[SM] + [VM] * 6,
+        out_specs=[VM] * len(pieces),
+        out_shape=[shape((128 * len(group), half + 128)) for group in pieces],
+        compiler_params=params(12),
+        cost_estimate=cost(2 * 64 * sum(map(len, pieces)) * 1536 * half, 12),
         name="results",
     )(sel, acts, acts_other, *weights, wall)
 
@@ -388,7 +398,7 @@
         ),
         out_shape=[up_shape, up_shape, shape((2, 128, 2 * half))],
         input_output_aliases={2 + len(rows) + i: i for i in range(len(before))},
-        compiler_params=params(56),
+        compiler_params=params(20),
         cost_estimate=cost(2 * 512 * 768 * width * count, 3.5 * count),
         name="weight_grads",
     )(sel, *rows, acts, *before)
@@ -431,14 +441,8 @@
     columns = jnp.stack([2 * lines, 2 * lines + 1, 2 * (lines ^ (NY * NX // 2)) + 1], axis=1)
     pick_slot = columns[:, :, None] == jnp.arange(slots, dtype=jnp.int32)[None, None, :]
     cols = jnp.sum(jnp.where(pick_slot[:, None], gate[None, :, None, :], 0.0), axis=3)
-    stack = joined([own, plus, minus, far])
-    stack, cols = lax.optimization_barrier((stack, cols))
-    from_minus, from_plus = send(stack, outer(1)), send(stack, outer(-1))
-    a_far, b_far = send(from_minus[:128], outer(1)), send(from_plus[128:], outer(-1))
-    rows = [stack, from_plus, from_minus, a_far, b_far]
-    rows_other = [send(piece, other_core()) for piece in rows]
-    wall = send(pack_weights(sel, w_gate, w_up, w_down), other_core())
-
+    a, b = joined([own, plus]), joined([minus, far])
+    a, b, cols = lax.optimization_barrier((a, b, cols))
     cols = lax.all_to_all(cols, ("y", "x"), split_axis=0, concat_axis=0, tiled=True)
     ring = jnp.array(RING, jnp.int32)
     out_y = ((y + ring) % NY)[:, None] * NX + ((x + ring) % NX)[None, :]
@@ -450,8 +454,19 @@
     gains = jnp.stack([cols[:, 0], cols[:, 1], cols[:, 1] + cols[:, 2]], axis=1)
     gains = jnp.pad(gains, ((0, 0), (0, 125)))
 
-    sums = near_sums(sel, rows[:3], rows_other[:3], weights)
-    acts, acts_grad = activations(sel, rows[3:], rows_other[3:], weights, sums, gains)
+    a_minus, b_plus = send(a, outer(1)), send(b, outer(-1))
+    b_minus, a_plus = send(b, outer(1)), send(a, outer(-1))
+    a_far, b_far = send(a_minus, outer(1)), send(b_plus, outer(-1))
+    wall = send(pack_weights(sel, weights), other_core())
+
+    near = [a, b, a_plus, b_plus, a_minus, b_minus]
+    near_other = [send(piece, other_core()) for piece in near]
+    sums = near_sums(sel, near, near_other, weights)
+    (a_on, b_on), sums, gains, wall = lax.optimization_barrier(((a_far, b_far), sums, gains, wall))
+    far_rows, far_other = [a_far, b_far], [send(a_on, other_core()), send(b_on, other_core())]
+    rows, rows_other = near + far_rows, near_other + far_other
+    sums = far_sums(sel, far_rows, weights, sums)
+    acts, acts_grad = activations(sel, far_other, weights, sums, gains)
     acts_other = send(acts, other_core())
     grads = weight_grads(False, 0, 2, sel, rows, acts_grad, [])
     acts_other, grads = lax.optimization_barrier((acts_other, grads))

time: 360 us -> 191 us (0.53)
  Pallas kernels: 249 us -> 65.1 us
  waiting for transfers between devices: 57.3 us -> 68.3 us
    pallas_call x5 -> x6, Pallas kernels: 216 us -> 35.3 us  [the longest x2 13.3 us: results(): pl.pallas_call(functools.partial(results_kernel, pieces), in_specs=[SM] +...]
    unnamed x29 -> x79, local copies, waits for them, and re-layouts: 3.11 us -> 11.4 us
    all_to_all x1, waiting for transfers between devices: 0.01 us -> 8.2 us  [per_device(): lax.all_to_all(cols, ('y', 'x'), split_axis=0, concat_axis=0, tiled=True)]
    slice x2 -> x0, local copies, waits for them, and re-layouts: 4.32 us -> none  [the longest x1 2.16 us: per_device(): from_minus[:128]]
    ppermute x24 -> x29, waiting for transfers between devices: 57.3 us -> 60.1 us  [send(): return lax.ppermute(value, AXES, pairs)]
    ppermute x24 -> x29, starting transfers between devices: 29 us -> 29.9 us  [send(): return lax.ppermute(value, AXES, pairs)]
  transfers between devices with their start and end apart: 25 -> 30, of which waited for: 11 -> 14; matrix products, arithmetic and copies ran while one was open for 3% -> 2% of each run, Pallas kernels for 62% -> 25%
where the time goes in v4:
time: 191 us; the launch traced here: 190 us
  waiting for transfers between devices  68.3 us (36%)
  Pallas kernels  65.1 us (34%)
  starting transfers between devices  34.5 us (18%)
  local copies, waits for them, and re-layouts  12.6 us (7%)
  other arithmetic  8.41 us (4%)
    ppermute x29, waiting for transfers between devices, send(): return lax.ppermute(value, AXES, pairs)  60.1 us
    ppermute x29, starting transfers between devices, send(): return lax.ppermute(value, AXES, pairs)  29.9 us
    pallas_call x3, Pallas kernels, weight_grads(): pl.pallas_call(functools.partial(grads_kernel, swapped), grid_spec=pltpu....  18 us
    pallas_call x2, Pallas kernels, results(): pl.pallas_call(functools.partial(results_kernel, pieces), in_specs=[SM] +...  13.3 us
    pallas_call x1, Pallas kernels, near_sums(): pl.pallas_call(near_kernel, grid_spec=pltpu.PrefetchScalarGridSpec(num_sc...  11.8 us
    unnamed x79, local copies, waits for them, and re-layouts  11.4 us
    all_to_all x1, waiting for transfers between devices, per_device(): lax.all_to_all(cols, ('y', 'x'), split_axis=0, concat_axis=0, tiled=True)  8.2 us
    pallas_call x1, Pallas kernels, activations(): pl.pallas_call(far_other_kernel, grid_spec=pltpu.PrefetchScalarGridSpec(n...  6.65 us
  transfers between devices with their start and end apart: 30, of which 14 were waited for; matrix products, arithmetic and copies ran while one was open for 2% of the time, Pallas kernels for 25%

profile of v4, /device:TPU:0, one launch (start us, length us, event | category | flops | bytes accessed | tf_op | source)
XLA Modules:
  0.0 190.1 jit_solution(8025101523129876854)
XLA Ops:
  1.3 6.3 %pack_weights.1 = bf16[4,42,128,128]{3,2,1,0:T(8,128)(2,1)} custom-call(s32[3]{0:T(128)} %pad_add_fusion.1.sel, bf16[2,4,2,896,128]{4,3,2,1,0:T(8,128)(2,1)} %bitcast.9, bf16[2,4,2,896,128]{4,3,2,1,0:T(8,128)(2,1)} %bitcast.16, bf16[2,128,7168]{2,1,0:T(8,128)(2,1)} %wd.5), custom_call_target="tpu_custom_call" | custom-call | bytes 104857 | tf_op jit(solution)/shard_map/pack_weights/pallas_call | solution.py:292
  7.5 3.7 %pack.1 = bf16[64,3584]{1,0:T(8,128)(2,1)} custom-call(s32[3]{0:T(128)} %pad_add_fusion.1.sel, bf16[32,7168]{1,0:T(8,128)(2,1)} %tok.1, bf16[32,7168]{1,0:T(8,128)(2,1)} %cot.1), custom_call_target="tpu_custom_call" | custom-call | bytes 2097152 | tf_op jit(solution)/shard_map/pack/pallas_call | solution.py:273
  11.2 2.8 %collective-permute-start = (bf16[64,3584]{1,0:T(8,128)(2,1)}, bf16[64,3584]{1,0:T(8,128)(2,1)S(1)}, u32[]{:S(2)}, u32[]{:S(2)}) collective-permute-start(bf16[64,3584]{1,0:T(8,128)(2,1)} %pack.1), channel_id=1, source_target_pairs={{0,3},{1,0},{2,1},{3,2},{4,7},{5,4},{6,5},{7,6},{8,11},{9,8},{10,9... | collective-permute-start | bytes 1376264 | tf_op jit(solution)/shard_map/ppermute | solution.py:51
  17.6 7.7 %collective-permute-done = bf16[64,3584]{1,0:T(8,128)(2,1)S(1)} collective-permute-done((bf16[64,3584]{1,0:T(8,128)(2,1)}, bf16[64,3584]{1,0:T(8,128)(2,1)S(1)}, u32[]{:S(2)}, u32[]{:S(2)}) %collective-permute-start) | collective-permute-done | bytes 458784 | tf_op jit(solution)/shard_map/ppermute | solution.py:51
  34.6 9.4 %collective-permute-done.3.refs_4_ = bf16[128,3584]{1,0:T(8,128)(2,1)} collective-permute-done((bf16[128,3584]{1,0:T(8,128)(2,1)S(1)}, bf16[128,3584]{1,0:T(8,128)(2,1)}, u32[]{:S(2)}, u32[]{:S(2)}) %collective-permute-start.3) | collective-permute-done | bytes 917536 | tf_op jit(solution)/shard_map/ppermute | solution.py:51
  44.6 9.6 %collective-permute-done.7.refs_2_ = bf16[128,3584]{1,0:T(8,128)(2,1)S(1)} collective-permute-done((bf16[128,3584]{1,0:T(8,128)(2,1)S(1)}, bf16[128,3584]{1,0:T(8,128)(2,1)S(1)}, u32[]{:S(2)}, u32[]{:S(2)}) %collective-permute-start.7) | collective-permute-done | bytes 917536 | tf_op jit(solution)/shard_map/ppermute | solution.py:51
  54.7 2.9 %collective-permute-start.6 = (bf16[128,3584]{1,0:T(8,128)(2,1)}, bf16[128,3584]{1,0:T(8,128)(2,1)S(1)}, u32[]{:S(2)}, u32[]{:S(2)}) collective-permute-start(bf16[128,3584]{1,0:T(8,128)(2,1)} %collective-permute-done.5.refs_3_), channel_id=1, source_target_pairs={{0,12},{1,13},{2,14},{3,15},{4,0},{5,1},{6,2},{7,3},{8,4},{9,5},{1... | collective-permute-start | bytes 2752520 | tf_op jit(solution)/shard_map/ppermute | solution.py:51
  60.0 4.6 %all-to-all-start = ((f32[16,32,3]{1,2,0:T(4,128)}), f32[16,32,3]{1,2,0:T(4,128)S(1)}, u32[]{:S(2)}, u32[]{:S(2)}) async-start(f32[16,32,3]{1,2,0:T(4,128)} %select_reduce_fusion), calls=%async_computation | async-start | bytes 65536 | tf_op jit(solution)/shard_map/all_to_all | solution.py:446
  64.7 8.2 %all-to-all-done = f32[16,32,3]{1,2,0:T(4,128)S(1)} async-done(((f32[16,32,3]{1,2,0:T(4,128)}), f32[16,32,3]{1,2,0:T(4,128)S(1)}, u32[]{:S(2)}, u32[]{:S(2)}) %all-to-all-start) | async-done | bytes 6176 | tf_op jit(solution)/shard_map/all_to_all | solution.py:446
  73.4 11.8 %near_sums.1 = (f32[512,256]{1,0:T(8,128)}, f32[512,256]{1,0:T(8,128)}, f32[512,256]{1,0:T(8,128)}) custom-call(s32[3]{0:T(128)} %pad_add_fusion.1.sel, bf16[128,3584]{1,0:T(8,128)(2,1)} %copy-done.3, bf16[128,3584]{1,0:T(8,128)(2,1)} %copy-done.5, bf16[128,3584]{1,0:T(8,128)(2,1)} %copy-done.9, bf16[128,3584]{1,0:T(8,128)(2,1)} %collective-permute-done.5.refs_3_, ...), custom_call_target="tpu_custom_call" | custom-call | bytes 104857 | tf_op jit(solution)/shard_map/near_sums/pallas_call | solution.py:319
  89.3 5.4 %far_sums.1 = (f32[512,256]{1,0:T(8,128)S(1)}, f32[512,256]{1,0:T(8,128)S(1)}, f32[512,256]{1,0:T(8,128)S(1)}) custom-call(s32[3]{0:T(128)S(1)} %copy-done.30, bf16[128,3584]{1,0:T(8,128)(2,1)} %collective-permute-done.4.refs_0_.refs_6_, bf16[128,3584]{1,0:T(8,128)(2,1)} %copy-done.7, bf16[2,4,2,896,128]{4,3,2,1,0:T(8,128)(2,1)} %bitcast.12, ...), custom_call_target="tpu_custom_call" | custom-call | flops 704643072 | bytes 10485760 | tf_op jit(solution)/shard_map/far_sums/pallas_call | solution.py:336
  99.7 6.7 %activations.1 = (bf16[512,896]{1,0:T(8,128)(2,1)S(1)}, bf16[512,768]{1,0:T(8,128)(2,1)S(1)}) custom-call(s32[3]{0:T(128)S(1)} %copy-done.30, bf16[128,3584]{1,0:T(8,128)(2,1)} %copy-done.11, bf16[128,3584]{1,0:T(8,128)(2,1)} %copy-done.13, bf16[2,4,2,896,128]{4,3,2,1,0:T(8,128)(2,1)} %bitcast.13, bf16[2,4,2,896,128]{4,3,2,1,0:T(8,128)(2,1)} %bitcast.20, ...), custom_call_target="tpu_custom_call" | custom-call | flops 704643072 | bytes 10485760 | tf_op jit(solution)/shard_map/activations/pallas_call | solution.py:353
  106.7 5.3 %weight_grads.3 = (bf16[2,4,2,896,128]{4,3,2,1,0:T(8,128)(2,1)}, bf16[2,4,2,896,128]{4,3,2,1,0:T(8,128)(2,1)}, bf16[2,128,7168]{2,1,0:T(8,128)(2,1)}) custom-call(s32[3]{0:T(128)S(1)} %copy-done.30, bf16[128,3584]{1,0:T(8,128)(2,1)S(1)} %copy-done.4, bf16[128,3584]{1,0:T(8,128)(2,1)S(1)} %copy-done.6, bf16[128,3584]{1,0:T(8,128)(2,1)S(1)} %copy-done.10, ...), custom_call_target="tpu_custom_call" | custom-call | flops 1409286144 | bytes 7340032 | tf_op jit(solution)/shard_map/weight_grads/pallas_call | solution.py:391
  112.0 5.6 %results.3 = (bf16[128,3712]{1,0:T(8,128)(2,1)S(1)}, bf16[128,3712]{1,0:T(8,128)(2,1)S(1)}) custom-call(s32[3]{0:T(128)S(1)} %copy-done.30, bf16[512,896]{1,0:T(8,128)(2,1)S(1)} %get-tuple-element.67.acts, bf16[512,896]{1,0:T(8,128)(2,1)S(1)} %collective-permute-done.18.acts_other, bf16[2,4,2,896,128]{4,3,2,1,0:T(8,128)(2,1)S(1)} %bitcast.14, ...), custom_call_target="tpu_custom_call" | custom-call | flops 1409286144 | bytes 12582912 | tf_op jit(solution)/shard_map/results/pallas_call | solution.py:373
  117.7 3.2 %collective-permute-start.21 = (bf16[128,3712]{1,0:T(8,128)(2,1)S(1)}, bf16[128,3712]{1,0:T(8,128)(2,1)S(1)}, u32[]{:S(2)}, u32[]{:S(2)}) collective-permute-start(bf16[128,3712]{1,0:T(8,128)(2,1)S(1)} %get-tuple-element.82), channel_id=1, source_target_pairs={{0,12},{1,13},{2,14},{3,15},{4,0},{5,1},{6,2},{7,3},{8,4},{9,5},{1... | collective-permute-start | bytes 2850824 | tf_op jit(solution)/shard_map/ppermute | solution.py:51
  120.9 7.7 %results.2 = (bf16[128,3712]{1,0:T(8,128)(2,1)S(1)}, bf16[128,3712]{1,0:T(8,128)(2,1)S(1)}, bf16[256,3712]{1,0:T(8,128)(2,1)S(1)}, bf16[256,3712]{1,0:T(8,128)(2,1)S(1)}) custom-call(s32[3]{0:T(128)S(1)} %copy-done.30, bf16[512,896]{1,0:T(8,128)(2,1)S(1)} %get-tuple-element.67.acts, bf16[512,896]{1,0:T(8,128)(2,1)S(1)} %collective-permute-done.18.acts_other, ...), custom_call_target="tpu_custom_call" | custom-call | flops 4227858432 | bytes 12582912 | tf_op jit(solution)/shard_map/results/pallas_call | solution.py:373
  128.6 4.0 %collective-permute-done.19 = bf16[128,3712]{1,0:T(8,128)(2,1)S(1)} collective-permute-done((bf16[128,3712]{1,0:T(8,128)(2,1)S(1)}, bf16[128,3712]{1,0:T(8,128)(2,1)S(1)}, u32[]{:S(2)}, u32[]{:S(2)}) %collective-permute-start.19) | collective-permute-done | bytes 950304 | tf_op jit(solution)/shard_map/ppermute | solution.py:51
  133.4 3.3 %collective-permute-start.22 = (bf16[256,3712]{1,0:T(8,128)(2,1)S(1)}, bf16[256,3712]{1,0:T(8,128)(2,1)S(1)}, u32[]{:S(2)}, u32[]{:S(2)}) collective-permute-start(bf16[256,3712]{1,0:T(8,128)(2,1)S(1)} %fusion.1), channel_id=1, source_target_pairs={{0,12},{1,13},{2,14},{3,15},{4,0},{5,1},{6,2},{7,3},{8,4},{9,5},{1... | collective-permute-start | bytes 5701640 | tf_op jit(solution)/shard_map/ppermute | solution.py:51
  136.8 5.3 %weight_grads.4 = (bf16[2,4,2,896,128]{4,3,2,1,0:T(8,128)(2,1)}, bf16[2,4,2,896,128]{4,3,2,1,0:T(8,128)(2,1)}, bf16[2,128,7168]{2,1,0:T(8,128)(2,1)}) custom-call(s32[3]{0:T(128)S(1)} %copy-done.30, bf16[128,3584]{1,0:T(8,128)(2,1)S(1)} %copy-done.4, bf16[128,3584]{1,0:T(8,128)(2,1)S(1)} %copy-done.6, ...), custom_call_target="tpu_custom_call", output_to_operand_aliasing={{0}: (10, {}), {1}: (11, {}), {2}: (12, {})} | custom-call | flops 1409286144 | bytes 7340032 | tf_op jit(solution)/shard_map/weight_grads/pallas_call | solution.py:391
  142.1 7.4 %weight_grads.5 = (bf16[2,4,2,896,128]{4,3,2,1,0:T(8,128)(2,1)}, bf16[2,4,2,896,128]{4,3,2,1,0:T(8,128)(2,1)}, bf16[2,128,7168]{2,1,0:T(8,128)(2,1)}) custom-call(s32[3]{0:T(128)S(1)} %copy-done.30, bf16[128,3584]{1,0:T(8,128)(2,1)S(1)} %copy-done.16, ...), custom_call_target="tpu_custom_call", output_to_operand_aliasing={{0}: (10, {}), {1}: (11, {}), {2}: (12, {})} | custom-call | flops 2818572288 | bytes 14680064 | tf_op jit(solution)/shard_map/weight_grads/pallas_call | solution.py:391
  149.6 8.6 %collective-permute-done.20 = bf16[256,3712]{1,0:T(8,128)(2,1)S(1)} collective-permute-done((bf16[256,3712]{1,0:T(8,128)(2,1)S(1)}, bf16[256,3712]{1,0:T(8,128)(2,1)S(1)}, u32[]{:S(2)}, u32[]{:S(2)}) %collective-permute-start.20) | collective-permute-done | bytes 1900576 | tf_op jit(solution)/shard_map/ppermute | solution.py:51
  162.8 7.7 %collective-permute-done.25 = bf16[64,3712]{1,0:T(8,128)(2,1)S(1)} collective-permute-done((bf16[64,3712]{1,0:T(8,128)(2,1)}, bf16[64,3712]{1,0:T(8,128)(2,1)S(1)}, u32[]{:S(2)}, u32[]{:S(2)}) %collective-permute-start.25) | collective-permute-done | bytes 475168 | tf_op jit(solution)/shard_map/ppermute | solution.py:51
  170.5 3.3 %collective-permute-done.24 = bf16[64,3712]{1,0:T(8,128)(2,1)} collective-permute-done((bf16[64,3712]{1,0:T(8,128)(2,1)}, bf16[64,3712]{1,0:T(8,128)(2,1)}, u32[]{:S(2)}, u32[]{:S(2)}) %collective-permute-start.24) | collective-permute-done | bytes 475168 | tf_op jit(solution)/shard_map/ppermute | solution.py:51
  177.4 4.0 %collective-permute-start.28 = (bf16[64,1024]{1,0:T(8,128)(2,1)S(1)}, bf16[64,1024]{1,0:T(8,128)(2,1)S(1)}, u32[]{:S(2)}, u32[]{:S(2)}) collective-permute-start(bf16[64,1024]{1,0:T(8,128)(2,1)S(1)} %get-tuple-element.123), channel_id=1, source_target_pairs={{0,64},{1,65},{2,66},{3,67},{4,68},{5,69},{6,70},{7,71},{8,72},{9,... | collective-permute-start | bytes 393224 | tf_op jit(solution)/shard_map/ppermute | solution.py:51
  (166 shorter events, 44.5 us)
Async XLA Ops:
  7.5 77.7 %collective-permute-start.15 = (bf16[4,42,128,128]{3,2,1,0:T(8,128)(2,1)}, bf16[4,42,128,128]{3,2,1,0:T(8,128)(2,1)}, u32[]{:S(2)}, u32[]{:S(2)}) collective-permute-start(bf16[4,42,128,128]{3,2,1,0:T(8,128)(2,1)} %pack_weights.1), channel_id=1, source_target_pairs={{0,16},{1,17},{2,18},{3,19},{4,20},{5,21},{6,22},{7,23},{8,24},{9,... | collective-permute-start | bytes 16515080 | tf_op jit(solution)/shard_map/ppermute | solution.py:51
  11.2 14.1 %collective-permute-start = (bf16[64,3584]{1,0:T(8,128)(2,1)}, bf16[64,3584]{1,0:T(8,128)(2,1)S(1)}, u32[]{:S(2)}, u32[]{:S(2)}) collective-permute-start(bf16[64,3584]{1,0:T(8,128)(2,1)} %pack.1), channel_id=1, source_target_pairs={{0,3},{1,0},{2,1},{3,2},{4,7},{5,4},{6,5},{7,6},{8,11},{9,8},{10,9... | collective-permute-start | bytes 1376264 | tf_op jit(solution)/shard_map/ppermute | solution.py:51
  14.1 12.3 %collective-permute-start.2 = (bf16[64,3584]{1,0:T(8,128)(2,1)}, bf16[64,3584]{1,0:T(8,128)(2,1)S(1)}, u32[]{:S(2)}, u32[]{:S(2)}) collective-permute-start(bf16[64,3584]{1,0:T(8,128)(2,1)} %pack.1), channel_id=1, source_target_pairs={{0,2},{1,3},{2,0},{3,1},{4,6},{5,7},{6,4},{7,5},{8,10},{9,11},{10,... | collective-permute-start | bytes 1376264 | tf_op jit(solution)/shard_map/ppermute | solution.py:51
  14.9 14.3 %collective-permute-start.1 = (bf16[64,3584]{1,0:T(8,128)(2,1)}, bf16[64,3584]{1,0:T(8,128)(2,1)S(1)}, u32[]{:S(2)}, u32[]{:S(2)}) collective-permute-start(bf16[64,3584]{1,0:T(8,128)(2,1)} %pack.1), channel_id=1, source_target_pairs={{0,1},{1,2},{2,3},{3,0},{4,5},{5,6},{6,7},{7,4},{8,9},{9,10},{10,1... | collective-permute-start | bytes 1376264 | tf_op jit(solution)/shard_map/ppermute | solution.py:51
  29.3 14.8 %collective-permute-start.3 = (bf16[128,3584]{1,0:T(8,128)(2,1)S(1)}, bf16[128,3584]{1,0:T(8,128)(2,1)}, u32[]{:S(2)}, u32[]{:S(2)}) collective-permute-start(bf16[128,3584]{1,0:T(8,128)(2,1)S(1)} %pad_maximum_fusion.refs_0_), channel_id=1, source_target_pairs={{0,4},{1,5},{2,6},{3,7},{4,8},{5,9},{6,10},{7,11},{8,12},{9,13},{1... | collective-permute-start | bytes 2752520 | tf_op jit(solution)/shard_map/ppermute | solution.py:51
  30.9 13.5 %collective-permute-start.5 = (bf16[128,3584]{1,0:T(8,128)(2,1)S(1)}, bf16[128,3584]{1,0:T(8,128)(2,1)}, u32[]{:S(2)}, u32[]{:S(2)}) collective-permute-start(bf16[128,3584]{1,0:T(8,128)(2,1)S(1)} %pad_maximum_fusion.1.refs_1_), channel_id=1, source_target_pairs={{0,12},{1,13},{2,14},{3,15},{4,0},{5,1},{6,2},{7,3},{8,4},{9,5},{1... | collective-permute-start | bytes 2752520 | tf_op jit(solution)/shard_map/ppermute | solution.py:51
  32.6 21.6 %collective-permute-start.7 = (bf16[128,3584]{1,0:T(8,128)(2,1)S(1)}, bf16[128,3584]{1,0:T(8,128)(2,1)S(1)}, u32[]{:S(2)}, u32[]{:S(2)}) collective-permute-start(bf16[128,3584]{1,0:T(8,128)(2,1)S(1)} %pad_maximum_fusion.refs_0_), channel_id=1, source_target_pairs={{0,12},{1,13},{2,14},{3,15},{4,0},{5,1},{6,2},{7,3},{8,4},{9,5},{1... | collective-permute-start | bytes 2752520 | tf_op jit(solution)/shard_map/ppermute | solution.py:51
  34.4 19.8 %collective-permute-start.8 = (bf16[128,3584]{1,0:T(8,128)(2,1)S(1)}, bf16[128,3584]{1,0:T(8,128)(2,1)}, u32[]{:S(2)}, u32[]{:S(2)}) collective-permute-start(bf16[128,3584]{1,0:T(8,128)(2,1)S(1)} %pad_maximum_fusion.1.refs_1_), channel_id=1, source_target_pairs={{0,4},{1,5},{2,6},{3,7},{4,8},{5,9},{6,10},{7,11},{8,12},{9,13},{1... | collective-permute-start | bytes 2752520 | tf_op jit(solution)/shard_map/ppermute | solution.py:51
  44.1 10.6 %collective-permute-start.9 = (bf16[128,3584]{1,0:T(8,128)(2,1)S(1)}, bf16[128,3584]{1,0:T(8,128)(2,1)S(1)}, u32[]{:S(2)}, u32[]{:S(2)}) collective-permute-start(bf16[128,3584]{1,0:T(8,128)(2,1)S(1)} %pad_maximum_fusion.refs_0_), channel_id=1, source_target_pairs={{0,16},{1,17},{2,18},{3,19},{4,20},{5,21},{6,22},{7,23},{8,24},{9,... | collective-permute-start | bytes 2752520 | tf_op jit(solution)/shard_map/ppermute | solution.py:51
  44.4 13.1 %collective-permute-start.10 = (bf16[128,3584]{1,0:T(8,128)(2,1)S(1)}, bf16[128,3584]{1,0:T(8,128)(2,1)S(1)}, u32[]{:S(2)}, u32[]{:S(2)}) collective-permute-start(bf16[128,3584]{1,0:T(8,128)(2,1)S(1)} %pad_maximum_fusion.1.refs_1_), channel_id=1, source_target_pairs={{0,16},{1,17},{2,18},{3,19},{4,20},{5,21},{6,22},{7,23},{8,24},{9,... | collective-permute-start | bytes 2752520 | tf_op jit(solution)/shard_map/ppermute | solution.py:51
  54.7 30.5 %collective-permute-start.6 = (bf16[128,3584]{1,0:T(8,128)(2,1)}, bf16[128,3584]{1,0:T(8,128)(2,1)S(1)}, u32[]{:S(2)}, u32[]{:S(2)}) collective-permute-start(bf16[128,3584]{1,0:T(8,128)(2,1)} %collective-permute-done.5.refs_3_), channel_id=1, source_target_pairs={{0,12},{1,13},{2,14},{3,15},{4,0},{5,1},{6,2},{7,3},{8,4},{9,5},{1... | collective-permute-start | bytes 2752520 | tf_op jit(solution)/shard_map/ppermute | solution.py:51
  57.5 27.6 %collective-permute-start.4 = (bf16[128,3584]{1,0:T(8,128)(2,1)}, bf16[128,3584]{1,0:T(8,128)(2,1)}, u32[]{:S(2)}, u32[]{:S(2)}) collective-permute-start(bf16[128,3584]{1,0:T(8,128)(2,1)} %collective-permute-done.3.refs_4_), channel_id=1, source_target_pairs={{0,4},{1,5},{2,6},{3,7},{4,8},{5,9},{6,10},{7,11},{8,12},{9,13},{1... | collective-permute-start | bytes 2752520 | tf_op jit(solution)/shard_map/ppermute | solution.py:51
  57.7 15.7 %collective-permute-start.13 = (bf16[128,3584]{1,0:T(8,128)(2,1)}, bf16[128,3584]{1,0:T(8,128)(2,1)}, u32[]{:S(2)}, u32[]{:S(2)}) collective-permute-start(bf16[128,3584]{1,0:T(8,128)(2,1)} %collective-permute-done.3.refs_4_), channel_id=1, source_target_pairs={{0,16},{1,17},{2,18},{3,19},{4,20},{5,21},{6,22},{7,23},{8,24},{9,... | collective-permute-start | bytes 2752520 | tf_op jit(solution)/shard_map/ppermute | solution.py:51
  59.8 13.6 %collective-permute-start.14 = (bf16[128,3584]{1,0:T(8,128)(2,1)}, bf16[128,3584]{1,0:T(8,128)(2,1)}, u32[]{:S(2)}, u32[]{:S(2)}) collective-permute-start(bf16[128,3584]{1,0:T(8,128)(2,1)} %collective-permute-done.8.refs_5_), channel_id=1, source_target_pairs={{0,16},{1,17},{2,18},{3,19},{4,20},{5,21},{6,22},{7,23},{8,24},{9,... | collective-permute-start | bytes 2752520 | tf_op jit(solution)/shard_map/ppermute | solution.py:51
  60.0 12.9 %all-to-all-start = ((f32[16,32,3]{1,2,0:T(4,128)}), f32[16,32,3]{1,2,0:T(4,128)S(1)}, u32[]{:S(2)}, u32[]{:S(2)}) async-start(f32[16,32,3]{1,2,0:T(4,128)} %select_reduce_fusion), calls=%async_computation | async-start | bytes 65536 | tf_op jit(solution)/shard_map/all_to_all | solution.py:446
  85.2 11.1 %collective-permute-start.16 = (bf16[128,3584]{1,0:T(8,128)(2,1)}, bf16[128,3584]{1,0:T(8,128)(2,1)S(1)}, u32[]{:S(2)}, u32[]{:S(2)}) collective-permute-start(bf16[128,3584]{1,0:T(8,128)(2,1)} %collective-permute-done.4.refs_0_.refs_6_), channel_id=1, source_target_pairs={{0,16},{1,17},{2,18},{3,19},{4,20},{5,21},{6,22},{7,23},{8,24},{9,... | collective-permute-start | bytes 2752520 | tf_op jit(solution)/shard_map/ppermute | solution.py:51
  85.3 11.0 %collective-permute-start.17 = (bf16[128,3584]{1,0:T(8,128)(2,1)S(1)}, bf16[128,3584]{1,0:T(8,128)(2,1)S(1)}, u32[]{:S(2)}, u32[]{:S(2)}) collective-permute-start(bf16[128,3584]{1,0:T(8,128)(2,1)S(1)} %collective-permute-done.6.refs_1_.refs_7_), channel_id=1, source_target_pairs={{0,16},{1,17},{2,18},{3,19},{4,20},{5,21},{6,22},{7,23},{8,24},{9,... | collective-permute-start | bytes 2752520 | tf_op jit(solution)/shard_map/ppermute | solution.py:51
  117.6 15.0 %collective-permute-start.19 = (bf16[128,3712]{1,0:T(8,128)(2,1)S(1)}, bf16[128,3712]{1,0:T(8,128)(2,1)S(1)}, u32[]{:S(2)}, u32[]{:S(2)}) collective-permute-start(bf16[128,3712]{1,0:T(8,128)(2,1)S(1)} %get-tuple-element.80), channel_id=1, source_target_pairs={{0,4},{1,5},{2,6},{3,7},{4,8},{5,9},{6,10},{7,11},{8,12},{9,13},{1... | collective-permute-start | bytes 2850824 | tf_op jit(solution)/shard_map/ppermute | solution.py:51
  117.7 15.4 %collective-permute-start.21 = (bf16[128,3712]{1,0:T(8,128)(2,1)S(1)}, bf16[128,3712]{1,0:T(8,128)(2,1)S(1)}, u32[]{:S(2)}, u32[]{:S(2)}) collective-permute-start(bf16[128,3712]{1,0:T(8,128)(2,1)S(1)} %get-tuple-element.82), channel_id=1, source_target_pairs={{0,12},{1,13},{2,14},{3,15},{4,0},{5,1},{6,2},{7,3},{8,4},{9,5},{1... | collective-permute-start | bytes 2850824 | tf_op jit(solution)/shard_map/ppermute | solution.py:51
  133.0 25.2 %collective-permute-start.20 = (bf16[256,3712]{1,0:T(8,128)(2,1)S(1)}, bf16[256,3712]{1,0:T(8,128)(2,1)S(1)}, u32[]{:S(2)}, u32[]{:S(2)}) collective-permute-start(bf16[256,3712]{1,0:T(8,128)(2,1)S(1)} %fusion), channel_id=1, source_target_pairs={{0,4},{1,5},{2,6},{3,7},{4,8},{5,9},{6,10},{7,11},{8,12},{9,13},{1... | collective-permute-start | bytes 5701640 | tf_op jit(solution)/shard_map/ppermute | solution.py:51
  133.4 24.8 %collective-permute-start.22 = (bf16[256,3712]{1,0:T(8,128)(2,1)S(1)}, bf16[256,3712]{1,0:T(8,128)(2,1)S(1)}, u32[]{:S(2)}, u32[]{:S(2)}) collective-permute-start(bf16[256,3712]{1,0:T(8,128)(2,1)S(1)} %fusion.1), channel_id=1, source_target_pairs={{0,12},{1,13},{2,14},{3,15},{4,0},{5,1},{6,2},{7,3},{8,4},{9,5},{1... | collective-permute-start | bytes 5701640 | tf_op jit(solution)/shard_map/ppermute | solution.py:51
  160.0 10.5 %collective-permute-start.25 = (bf16[64,3712]{1,0:T(8,128)(2,1)}, bf16[64,3712]{1,0:T(8,128)(2,1)S(1)}, u32[]{:S(2)}, u32[]{:S(2)}) collective-permute-start(bf16[64,3712]{1,0:T(8,128)(2,1)} %get-tuple-element.113), channel_id=1, source_target_pairs={{0,2},{1,3},{2,0},{3,1},{4,6},{5,7},{6,4},{7,5},{8,10},{9,11},{10,... | collective-permute-start | bytes 1425416 | tf_op jit(solution)/shard_map/ppermute | solution.py:51
  160.8 13.0 %collective-permute-start.24 = (bf16[64,3712]{1,0:T(8,128)(2,1)}, bf16[64,3712]{1,0:T(8,128)(2,1)}, u32[]{:S(2)}, u32[]{:S(2)}) collective-permute-start(bf16[64,3712]{1,0:T(8,128)(2,1)} %get-tuple-element.112), channel_id=1, source_target_pairs={{0,3},{1,0},{2,1},{3,2},{4,7},{5,4},{6,5},{7,6},{8,11},{9,8},{10,9... | collective-permute-start | bytes 1425416 | tf_op jit(solution)/shard_map/ppermute | solution.py:51
  162.6 13.0 %collective-permute-start.23 = (bf16[64,3712]{1,0:T(8,128)(2,1)}, bf16[64,3712]{1,0:T(8,128)(2,1)}, u32[]{:S(2)}, u32[]{:S(2)}) collective-permute-start(bf16[64,3712]{1,0:T(8,128)(2,1)} %get-tuple-element.114), channel_id=1, source_target_pairs={{0,1},{1,2},{2,3},{3,0},{4,5},{5,6},{6,7},{7,4},{8,9},{9,10},{10,1... | collective-permute-start | bytes 1425416 | tf_op jit(solution)/shard_map/ppermute | solution.py:51
  (44 other events, 350.5 us)

commit v5 on v4

--- a/solution.py
+++ b/solution.py
@@ -9,6 +9,8 @@
 from jax.sharding import PartitionSpec as P
 
 ROUTE_SCALE = 2.5
+TOP = 8
+ROUTE = 3 * 24
 NZ, NC, NY, NX = 4, 2, 4, 4
 AXES = ("z", "c", "y", "x")
 STEPS = 4
@@ -99,10 +101,22 @@
     return first, second, back
 
 
-def pack_kernel(sel, tok, cot, packed):
-    rows = tok.shape[0]
-    packed[:rows] = tok[...]
-    packed[rows:] = cot[...]
+def pack_kernel(sel, tok, cot, extra, packed, sems):
+    rows, half = extra.shape[0], packed.shape[1] - 128
+    width = half // STEPS
+    copies = []
+    for k in range(STEPS):
+        at = pl.multiple_of((2 * k + sel[0]) * width, 128)
+        for base, ref in enumerate((tok, cot)):
+            target = packed.at[pl.ds(base * rows, rows), pl.ds(k * width, width)]
+            copies.append(
+                pltpu.make_async_copy(ref.at[:, pl.ds(at, width)], target, sems.at[len(copies)])
+            )
+            copies[-1].start()
+    packed[:rows, half:] = extra[...]
+    packed[rows:, half:] = jnp.zeros_like(extra)
+    for one in copies:
+        one.wait()
 
 
 def pack_weights_kernel(sel, wg, wu, wd, wall):
@@ -139,33 +153,43 @@
     multiply(sums, other, theirs, NEAR_OTHER, True)
 
 
-def far_own_kernel(sel, *refs):
-    own, mine, start, sums = dict(zip((6, 7), refs)), refs[2:5], refs[5:8], refs[8:11]
+def line_weights(extra, held, sel, gains):
+    rows = rows_of(extra, ALL, False)
+    picked = jnp.dot(rows, held[...], preferred_element_type=F32)
+    lane = lax.broadcasted_iota(jnp.int32, picked.shape, 1)
+    slot = lane.astype(F32)
+    chosen = slot < 0
+    for at in range(TOP):
+        chosen = chosen | (slot == rows[:, ROUTE + at : ROUTE + at + 1].astype(F32))
+    sig = jnp.where(chosen, jax.nn.sigmoid(picked), 0.0)
+    weight = ROUTE_SCALE * sig / jnp.sum(sig, axis=1, keepdims=True)
+
+    def column(at):
+        return jnp.sum(jnp.where(lane == at, weight, 0.0), axis=1, keepdims=True)
+
+    cold, hot, partner = column(2 * sel[2]), column(2 * sel[2] + 1), column(sel[3])
+    gains[...] = jnp.where(lane == 0, cold, jnp.where(lane == 1, hot, hot + partner))
+
+
+def thirds(value):
+    high = value.astype(BF).astype(F32)
+    middle = (value - high).astype(BF).astype(F32)
+    return high, middle, value - high - middle
+
+
+def far_kernel(sel, *refs):
+    own, other = dict(zip((6, 7), refs)), dict(zip((6, 7), refs[2:]))
+    mine, theirs, start, extra, held = refs[4:7], refs[7:10], refs[10:13], refs[13:21], refs[21]
+    acts, acts_grad = refs[22:24]
+    sums, gains = refs[24:27], refs[27]
 
     @pl.when(pl.program_id(0) == 0)
     def _():
         for ref, before in zip(sums, start):
             ref[...] = before[...]
+        line_weights(extra, held, sel, gains)
 
     multiply(sums, own, mine, FAR_OWN, False)
-
-
-def thirds(value):
-    high = value.astype(BF).astype(F32)
-    middle = (value - high).astype(BF).astype(F32)
-    return high, middle, value - high - middle
-
-
-def far_other_kernel(sel, *refs):
-    other, theirs, start, gains = dict(zip((6, 7), refs)), refs[2:5], refs[5:8], refs[8]
-    acts, acts_grad = refs[9:11]
-    sums = refs[11:14]
-
-    @pl.when(pl.program_id(0) == 0)
-    def _():
-        for ref, before in zip(sums, start):
-            ref[...] = before[...]
-
     multiply(sums, other, theirs, FAR_OTHER, True)
 
     @pl.when(pl.program_id(0) == STEPS - 1)
@@ -266,23 +290,18 @@
     return jax.ShapeDtypeStruct(dims, dtype)
 
 
-def pack(sel, tokens, cotangent):
+def pack(sel, tokens, cotangent, extra):
     tok, wide = tokens.shape
-    width = wide // (2 * STEPS)
-    spec = pl.BlockSpec((tok, width), lambda k, sel: (0, 2 * k + sel[0]))
     return pl.pallas_call(
         pack_kernel,
-        grid_spec=pltpu.PrefetchScalarGridSpec(
-            num_scalar_prefetch=1,
-            grid=(STEPS,),
-            in_specs=[spec, spec],
-            out_specs=pl.BlockSpec((2 * tok, width), lambda k, sel: (0, k)),
-        ),
-        out_shape=shape((2 * tok, wide // 2)),
-        compiler_params=params(60),
+        in_specs=[SM, HB, HB, VM],
+        out_specs=VM,
+        out_shape=shape((2 * tok, wide // 2 + 128)),
+        scratch_shapes=[pltpu.SemaphoreType.DMA((2 * STEPS,))],
+        compiler_params=params(56),
         cost_estimate=cost(0, 2),
         name="pack",
-    )(sel, tokens, cotangent)
+    )(sel, tokens, cotangent, extra)
 
 
 def pack_weights(sel, weights):
@@ -298,8 +317,8 @@
             out_specs=pl.BlockSpec((1, 42, 128, 128), lambda k, sel: (k, 0, 0, 0)),
         ),
         out_shape=shape((STEPS, 42, 128, 128)),
-        compiler_params=params(60),
-        cost_estimate=cost(0, 0.1),
+        compiler_params=params(56),
+        cost_estimate=cost(0, 11),
         name="pack_weights",
     )(sel, *weights)
 
@@ -314,59 +333,46 @@
     return [pl.BlockSpec((r.shape[0], width), lambda k, sel: (0, first + k)) for r in rows]
 
 
+WIDTH = 896
+
+
 def near_sums(sel, own, other, weights):
-    width = own[0].shape[1] // STEPS
     return pl.pallas_call(
         near_kernel,
         grid_spec=pltpu.PrefetchScalarGridSpec(
             num_scalar_prefetch=1,
             grid=(STEPS,),
-            in_specs=row_specs(own + other, width) + weight_specs(width, 0) + weight_specs(width, 1),
+            in_specs=row_specs(own + other, WIDTH) + weight_specs(WIDTH, 0) + weight_specs(WIDTH, 1),
             out_specs=[whole((512, 256))] * 3,
         ),
         out_shape=[shape((512, 256), F32)] * 3,
-        compiler_params=params(58),
+        compiler_params=params(56),
         cost_estimate=cost(0, 0.1),
         name="near_sums",
     )(sel, *own, *other, *weights, *weights)
 
 
-def far_sums(sel, own, weights, sums):
-    width = own[0].shape[1] // STEPS
+def activations(sel, own, other, weights, sums, held):
+    extra = pl.BlockSpec((128, 128), lambda k, sel: (0, STEPS * WIDTH // 128))
     return pl.pallas_call(
-        far_own_kernel,
+        far_kernel,
         grid_spec=pltpu.PrefetchScalarGridSpec(
             num_scalar_prefetch=1,
             grid=(STEPS,),
-            in_specs=row_specs(own, width) + weight_specs(width, 0) + [whole((512, 256))] * 3,
-            out_specs=[whole((512, 256))] * 3,
-        ),
-        out_shape=[shape((512, 256), F32)] * 3,
-        compiler_params=params(50),
-        cost_estimate=cost(2 * 128 * 768 * width * STEPS, 10),
-        name="far_sums",
-    )(sel, *own, *weights, *sums)
-
-
-def activations(sel, other, weights, sums, gains):
-    width = other[0].shape[1] // STEPS
-    return pl.pallas_call(
-        far_other_kernel,
-        grid_spec=pltpu.PrefetchScalarGridSpec(
-            num_scalar_prefetch=1,
-            grid=(STEPS,),
-            in_specs=row_specs(other, width)
-            + weight_specs(width, 1)
+            in_specs=row_specs(own[6:] + other, WIDTH)
+            + weight_specs(WIDTH, 0)
+            + weight_specs(WIDTH, 1)
             + [whole((512, 256))] * 3
-            + [whole((512, 128))],
+            + [extra] * 8
+            + [whole((128, 128))],
             out_specs=[whole((512, 896)), whole((512, 768))],
-            scratch_shapes=[pltpu.VMEM((512, 256), F32)] * 3,
+            scratch_shapes=[pltpu.VMEM((512, 256), F32)] * 3 + [pltpu.VMEM((512, 128), F32)],
         ),
         out_shape=[shape((512, 896)), shape((512, 768))],
-        compiler_params=params(50),
-        cost_estimate=cost(2 * 128 * 768 * width * STEPS, 10),
+        compiler_params=params(56),
+        cost_estimate=cost(4 * 128 * 768 * WIDTH * STEPS, 15),
         name="activations",
-    )(sel, *other, *weights, *sums, gains)
+    )(sel, *own[6:], *other, *weights, *weights, *sums, *own, held)
 
 
 def results(pieces, sel, acts, acts_other, weights, wall, half):
@@ -375,15 +381,14 @@
         in_specs=[SM] + [VM] * 6,
         out_specs=[VM] * len(pieces),
         out_shape=[shape((128 * len(group), half + 128)) for group in pieces],
-        compiler_params=params(12),
+        compiler_params=params(18),
         cost_estimate=cost(2 * 64 * sum(map(len, pieces)) * 1536 * half, 12),
         name="results",
     )(sel, acts, acts_other, *weights, wall)
 
 
 def weight_grads(swapped, first, count, sel, rows, acts, before):
-    half = rows[0].shape[1]
-    width = half // STEPS
+    width, half = WIDTH, WIDTH * STEPS
     at = 1 if swapped else 0
     up_spec = pl.BlockSpec((2, 1, 1, width, 128), lambda k, sel: (0, first + k, sel[at], 0, 0))
     down_spec = pl.BlockSpec((2, 128, width), lambda k, sel: (0, 0, 2 * (first + k) + sel[at]))
@@ -425,48 +430,36 @@
     width = half // STEPS
     slots = slot_expert.shape[0]
     z, core, y, x = (lax.axis_index(a) for a in AXES)
-    sel = jnp.stack([core, 1 - core, y * NX + x])
+    line = y * NX + x
+    sel = jnp.stack([core, 1 - core, line, 2 * (line ^ (NY * NX // 2)) + 1])
     weights = (
         w_gate.reshape(2, STEPS, 2, width, 128),
         w_up.reshape(2, STEPS, 2, width, 128),
         w_down,
     )
-    own = pack(sel, tokens, cotangent)
+    high = lax.reduce_precision(gate_logits, 8, 7)
+    middle = lax.reduce_precision(gate_logits - high, 8, 7)
+    extra = joined([high, middle, gate_logits - high - middle, route_slot.astype(F32)], axis=1)
+    extra = jnp.pad(extra, ((0, 0), (0, 128 - extra.shape[1]))).astype(BF)
+    own = pack(sel, tokens, cotangent, extra)
+    own, later = lax.optimization_barrier((own, sel))
     minus, plus, far = send(own, inner(1)), send(own, inner(-1)), send(own, inner(2))
-    chosen = jnp.any(
-        route_slot[:, :, None] == jnp.arange(slots, dtype=jnp.int32)[None, None, :], axis=1
-    )
-    gate, pull_back = jax.vjp(lambda lg: gate_weights(lg, slot_expert, chosen), gate_logits)
-    lines = jnp.arange(NY * NX, dtype=jnp.int32)
-    columns = jnp.stack([2 * lines, 2 * lines + 1, 2 * (lines ^ (NY * NX // 2)) + 1], axis=1)
-    pick_slot = columns[:, :, None] == jnp.arange(slots, dtype=jnp.int32)[None, None, :]
-    cols = jnp.sum(jnp.where(pick_slot[:, None], gate[None, :, None, :], 0.0), axis=3)
     a, b = joined([own, plus]), joined([minus, far])
-    a, b, cols = lax.optimization_barrier((a, b, cols))
-    cols = lax.all_to_all(cols, ("y", "x"), split_axis=0, concat_axis=0, tiled=True)
-    ring = jnp.array(RING, jnp.int32)
-    out_y = ((y + ring) % NY)[:, None] * NX + ((x + ring) % NX)[None, :]
-    out_x = ((y + ring) % NY)[None, :] * NX + ((x + ring) % NX)[:, None]
-    order = jnp.where(core == 0, out_y, out_x).reshape(-1)
-    pick_line = order[:, None] == lines[None, :]
-    cols = jnp.sum(jnp.where(pick_line[:, :, None, None], cols[None], 0.0), axis=1)
-    cols = cols.reshape(NY * NX * tok, 3)
-    gains = jnp.stack([cols[:, 0], cols[:, 1], cols[:, 1] + cols[:, 2]], axis=1)
-    gains = jnp.pad(gains, ((0, 0), (0, 125)))
-
     a_minus, b_plus = send(a, outer(1)), send(b, outer(-1))
     b_minus, a_plus = send(b, outer(1)), send(a, outer(-1))
     a_far, b_far = send(a_minus, outer(1)), send(b_plus, outer(-1))
-    wall = send(pack_weights(sel, weights), other_core())
+    wall = send(pack_weights(later, weights), other_core())
 
     near = [a, b, a_plus, b_plus, a_minus, b_minus]
     near_other = [send(piece, other_core()) for piece in near]
     sums = near_sums(sel, near, near_other, weights)
-    (a_on, b_on), sums, gains, wall = lax.optimization_barrier(((a_far, b_far), sums, gains, wall))
+    (a_on, b_on), sums = lax.optimization_barrier(((a_far, b_far), sums))
     far_rows, far_other = [a_far, b_far], [send(a_on, other_core()), send(b_on, other_core())]
     rows, rows_other = near + far_rows, near_other + far_other
-    sums = far_sums(sel, far_rows, weights, sums)
-    acts, acts_grad = activations(sel, far_other, weights, sums, gains)
+    experts = jnp.tile(jnp.arange(24, dtype=jnp.int32), 3)
+    held = experts[:, None] == slot_expert[None, :]
+    held = jnp.pad(held.astype(F32), ((0, 128 - 72), (0, 128 - slots))).astype(BF)
+    acts, acts_grad = activations(sel, rows, far_other, weights, sums, held)
     acts_other = send(acts, other_core())
     grads = weight_grads(False, 0, 2, sel, rows, acts_grad, [])
     acts_other, grads = lax.optimization_barrier((acts_other, grads))
@@ -500,6 +493,10 @@
         last = last + send(block_for(by), along_z(by)).astype(F32)
     mixed, grad_tokens = last[:tok, :width].astype(BF), last[tok:, :width].astype(BF)
     home = sum(last[:tok, width + at : width + at + slots] for at in (0, slots, 2 * slots))
+    chosen = jnp.any(
+        route_slot[:, :, None] == jnp.arange(slots, dtype=jnp.int32)[None, None, :], axis=1
+    )
+    _, pull_back = jax.vjp(lambda lg: gate_weights(lg, slot_expert, chosen), gate_logits)
     grad_logits = pull_back(home)[0]
     return (
         mixed,

time: 191 us -> 182 us (0.953)
  waiting for transfers between devices: 68.3 us -> 53 us
  other arithmetic: 8.41 us -> 13.8 us
    all_to_all x1 -> x0, waiting for transfers between devices: 8.2 us -> none  [per_device(): lax.all_to_all(cols, ('y', 'x'), split_axis=0, concat_axis=0, tiled=True)]
    ppermute x29, waiting for transfers between devices: 60.1 us -> 53 us  [send(): return lax.ppermute(value, AXES, pairs)]
    all_to_all x1 -> x0, starting transfers between devices: 4.62 us -> none  [per_device(): lax.all_to_all(cols, ('y', 'x'), split_axis=0, concat_axis=0, tiled=True)]
    ppermute x29, starting transfers between devices: 29.9 us -> 34 us  [send(): return lax.ppermute(value, AXES, pairs)]
    dynamic_update_slice x1, other arithmetic: 0.36 us -> 2.42 us  [per_device(): lax.dynamic_update_slice(to_plus, add(to_plus[:128], from_a), (0, 0))]
    dynamic_update_slice x1, other arithmetic: 0.36 us -> 2.37 us  [per_device(): lax.dynamic_update_slice(to_minus, add(to_minus[:128], from_b), (0, 0))]
    pallas_call x3 -> x2, Pallas kernels: 15.7 us -> 14.3 us  [the longest x1 11.7 us: activations(): pl.pallas_call(far_kernel, grid_spec=pltpu.PrefetchScalarGridSpec(num_sca...]
    unnamed x79 -> x85, local copies, waits for them, and re-layouts: 11.4 us -> 10.9 us
  transfers between devices with their start and end apart: 30 -> 29, of which waited for: 14 -> 18; matrix products, arithmetic and copies ran while one was open for 2% -> 3% of each run, Pallas kernels for 25% -> 32%
where the time goes in v5:
time: 182 us; the launch traced here: 180 us
  Pallas kernels  66.1 us (36%)
  waiting for transfers between devices  53 us (29%)
  starting transfers between devices  34 us (19%)
  other arithmetic  13.8 us (8%)
  local copies, waits for them, and re-layouts  11.9 us (7%)
    ppermute x29, waiting for transfers between devices, send(): return lax.ppermute(value, AXES, pairs)  53 us
    ppermute x29, starting transfers between devices, send(): return lax.ppermute(value, AXES, pairs)  34 us
    pallas_call x3, Pallas kernels, weight_grads(): pl.pallas_call(functools.partial(grads_kernel, swapped), grid_spec=pltpu....  18.8 us
    pallas_call x2, Pallas kernels, results(): pl.pallas_call(functools.partial(results_kernel, pieces), in_specs=[SM] +...  15 us
    pallas_call x1, Pallas kernels, near_sums(): pl.pallas_call(near_kernel, grid_spec=pltpu.PrefetchScalarGridSpec(num_sc...  11.8 us
    pallas_call x1, Pallas kernels, activations(): pl.pallas_call(far_kernel, grid_spec=pltpu.PrefetchScalarGridSpec(num_sca...  11.7 us
    unnamed x85, local copies, waits for them, and re-layouts  10.9 us
    pallas_call x1, Pallas kernels, pack_weights(): pl.pallas_call(pack_weights_kernel, grid_spec=pltpu.PrefetchScalarGridSpe...  6.28 us
  transfers between devices with their start and end apart: 29, of which 18 were waited for; matrix products, arithmetic and copies ran while one was open for 3% of the time, Pallas kernels for 32%

profile of v5, /device:TPU:0, one launch (start us, length us, event | category | flops | bytes accessed | tf_op | source)
XLA Modules:
  0.0 180.0 jit_solution(7885940472694222093)
XLA Ops:
  4.3 2.6 %pack.1 = bf16[64,3712]{1,0:T(8,128)(2,1)} custom-call(s32[4]{0:T(128)} %pad_add_fusion.sel, bf16[32,7168]{1,0:T(8,128)(2,1)} %tok.1, bf16[32,7168]{1,0:T(8,128)(2,1)} %cot.1, bf16[32,128]{1,0:T(8,128)(2,1)} %fusion.11.extra), custom_call_target="tpu_custom_call" | custom-call | bytes 2097152 | tf_op jit(solution)/shard_map/pack/pallas_call | solution.py:295
  6.8 2.9 %collective-permute-start = (bf16[64,3712]{1,0:T(8,128)(2,1)}, bf16[64,3712]{1,0:T(8,128)(2,1)S(1)}, u32[]{:S(2)}, u32[]{:S(2)}) collective-permute-start(bf16[64,3712]{1,0:T(8,128)(2,1)} %pack.1), channel_id=1, source_target_pairs={{0,3},{1,0},{2,1},{3,2},{4,7},{5,4},{6,5},{7,6},{8,11},{9,8},{10,9... | collective-permute-start | bytes 1425416 | tf_op jit(solution)/shard_map/ppermute | solution.py:53
  12.0 6.3 %pack_weights.1 = bf16[4,42,128,128]{3,2,1,0:T(8,128)(2,1)} custom-call(s32[4]{0:T(128)} %pad_add_fusion.sel, bf16[2,4,2,896,128]{4,3,2,1,0:T(8,128)(2,1)} %bitcast.8, bf16[2,4,2,896,128]{4,3,2,1,0:T(8,128)(2,1)} %bitcast.15, bf16[2,128,7168]{2,1,0:T(8,128)(2,1)} %wd.5), custom_call_target="tpu_custom_call" | custom-call | bytes 11534336 | tf_op jit(solution)/shard_map/pack_weights/pallas_call | solution.py:311
  18.4 3.0 %collective-permute-done = bf16[64,3712]{1,0:T(8,128)(2,1)S(1)} collective-permute-done((bf16[64,3712]{1,0:T(8,128)(2,1)}, bf16[64,3712]{1,0:T(8,128)(2,1)S(1)}, u32[]{:S(2)}, u32[]{:S(2)}) %collective-permute-start) | collective-permute-done | bytes 475168 | tf_op jit(solution)/shard_map/ppermute | solution.py:53
  25.4 2.7 %collective-permute-start.5 = (bf16[128,3712]{1,0:T(8,128)(2,1)S(1)}, bf16[128,3712]{1,0:T(8,128)(2,1)S(1)}, u32[]{:S(2)}, u32[]{:S(2)}) collective-permute-start(bf16[128,3712]{1,0:T(8,128)(2,1)S(1)} %constant_dynamic-update-slice_fusion.2.refs_1_.refs_14_), channel_id=1, source_target_pairs={{0,12},{1,13},{2,14},{3,15},{4,0},{5,1},{6,2},{7,3},{8,4},{9,5},{1... | collective-permute-start | bytes 2850824 | tf_op jit(solution)/shard_map/ppermute | solution.py:53
  30.1 6.3 %collective-permute-done.1.refs_4_.refs_17_ = bf16[128,3712]{1,0:T(8,128)(2,1)S(1)} collective-permute-done((bf16[128,3712]{1,0:T(8,128)(2,1)S(1)}, bf16[128,3712]{1,0:T(8,128)(2,1)S(1)}, u32[]{:S(2)}, u32[]{:S(2)}) %collective-permute-start.1) | collective-permute-done | bytes 950304 | tf_op jit(solution)/shard_map/ppermute | solution.py:53
  36.4 3.0 %collective-permute-done.5.refs_3_.refs_16_ = bf16[128,3712]{1,0:T(8,128)(2,1)S(1)} collective-permute-done((bf16[128,3712]{1,0:T(8,128)(2,1)S(1)}, bf16[128,3712]{1,0:T(8,128)(2,1)S(1)}, u32[]{:S(2)}, u32[]{:S(2)}) %collective-permute-start.5) | collective-permute-done | bytes 950304 | tf_op jit(solution)/shard_map/ppermute | solution.py:53
  39.4 10.2 %collective-permute-done.7.refs_2_.refs_15_ = bf16[128,3712]{1,0:T(8,128)(2,1)S(1)} collective-permute-done((bf16[128,3712]{1,0:T(8,128)(2,1)S(1)}, bf16[128,3712]{1,0:T(8,128)(2,1)S(1)}, u32[]{:S(2)}, u32[]{:S(2)}) %collective-permute-start.7) | collective-permute-done | bytes 950304 | tf_op jit(solution)/shard_map/ppermute | solution.py:53
  54.8 3.7 %collective-permute-start.6 = (bf16[128,3712]{1,0:T(8,128)(2,1)S(1)}, bf16[128,3712]{1,0:T(8,128)(2,1)}, u32[]{:S(2)}, u32[]{:S(2)}) collective-permute-start(bf16[128,3712]{1,0:T(8,128)(2,1)S(1)} %collective-permute-done.5.refs_3_.refs_16_), channel_id=1, source_target_pairs={{0,12},{1,13},{2,14},{3,15},{4,0},{5,1},{6,2},{7,3},{8,4},{9,5},{1... | collective-permute-start | bytes 2850824 | tf_op jit(solution)/shard_map/ppermute | solution.py:53
  59.5 11.8 %near_sums.1 = (f32[512,256]{1,0:T(8,128)}, f32[512,256]{1,0:T(8,128)}, f32[512,256]{1,0:T(8,128)}) custom-call(s32[4]{0:T(128)} %pad_add_fusion.sel, bf16[128,3712]{1,0:T(8,128)(2,1)} %copy-done.5, bf16[128,3712]{1,0:T(8,128)(2,1)} %copy-done.3, bf16[128,3712]{1,0:T(8,128)(2,1)} %copy-done.12, bf16[128,3712]{1,0:T(8,128)(2,1)} %copy-done.9, ...), custom_call_target="tpu_custom_call" | custom-call | bytes 104857 | tf_op jit(solution)/shard_map/near_sums/pallas_call | solution.py:340
  75.6 11.7 %activations.1 = (bf16[512,896]{1,0:T(8,128)(2,1)}, bf16[512,768]{1,0:T(8,128)(2,1)}) custom-call(s32[4]{0:T(128)} %pad_add_fusion.sel, bf16[128,3712]{1,0:T(8,128)(2,1)} %collective-permute-done.2.refs_0_.refs_19_.refs_6_, bf16[128,3712]{1,0:T(8,128)(2,1)} %collective-permute-done.6.refs_1_.refs_20_.refs_7_, ...), custom_call_target="tpu_custom_call" | custom-call | flops 1409286144 | bytes 15728640 | tf_op jit(solution)/shard_map/activations/pallas_call | solution.py:357
  91.3 5.4 %weight_grads.3 = (bf16[2,4,2,896,128]{4,3,2,1,0:T(8,128)(2,1)}, bf16[2,4,2,896,128]{4,3,2,1,0:T(8,128)(2,1)}, bf16[2,128,7168]{2,1,0:T(8,128)(2,1)}) custom-call(s32[4]{0:T(128)S(1)} %copy-done.36, bf16[128,3712]{1,0:T(8,128)(2,1)S(1)} %copy-done.6, bf16[128,3712]{1,0:T(8,128)(2,1)S(1)} %copy-done.4, bf16[128,3712]{1,0:T(8,128)(2,1)S(1)} %copy-done.13, ...), custom_call_target="tpu_custom_call" | custom-call | flops 1409286144 | bytes 7340032 | tf_op jit(solution)/shard_map/weight_grads/pallas_call | solution.py:396
  96.7 5.5 %results.3 = (bf16[128,3712]{1,0:T(8,128)(2,1)S(1)}, bf16[128,3712]{1,0:T(8,128)(2,1)S(1)}) custom-call(s32[4]{0:T(128)S(1)} %copy-done.36, bf16[512,896]{1,0:T(8,128)(2,1)S(1)} %copy-done.31, bf16[512,896]{1,0:T(8,128)(2,1)S(1)} %collective-permute-done.17.acts_other, bf16[2,4,2,896,128]{4,3,2,1,0:T(8,128)(2,1)S(1)} %bitcast.13, ...), custom_call_target="tpu_custom_call" | custom-call | flops 1409286144 | bytes 12582912 | tf_op jit(solution)/shard_map/results/pallas_call | solution.py:379
  102.3 3.2 %collective-permute-start.21 = (bf16[128,3712]{1,0:T(8,128)(2,1)S(1)}, bf16[128,3712]{1,0:T(8,128)(2,1)S(1)}, u32[]{:S(2)}, u32[]{:S(2)}) collective-permute-start(bf16[128,3712]{1,0:T(8,128)(2,1)S(1)} %get-tuple-element.70), channel_id=1, source_target_pairs={{0,12},{1,13},{2,14},{3,15},{4,0},{5,1},{6,2},{7,3},{8,4},{9,5},{1... | collective-permute-start | bytes 2850824 | tf_op jit(solution)/shard_map/ppermute | solution.py:53
  105.5 9.5 %results.2 = (bf16[128,3712]{1,0:T(8,128)(2,1)S(1)}, bf16[128,3712]{1,0:T(8,128)(2,1)S(1)}, bf16[256,3712]{1,0:T(8,128)(2,1)}, bf16[256,3712]{1,0:T(8,128)(2,1)}) custom-call(s32[4]{0:T(128)S(1)} %copy-done.36, bf16[512,896]{1,0:T(8,128)(2,1)S(1)} %copy-done.31, bf16[512,896]{1,0:T(8,128)(2,1)S(1)} %collective-permute-done.17.acts_other, ...), custom_call_target="tpu_custom_call" | custom-call | flops 4227858432 | bytes 12582912 | tf_op jit(solution)/shard_map/results/pallas_call | solution.py:379
  117.3 2.4 %fusion = bf16[256,3712]{1,0:T(8,128)(2,1)} fusion(bf16[256,3712]{1,0:T(8,128)(2,1)} %get-tuple-element.67, bf16[128,3712]{1,0:T(8,128)(2,1)S(1)} %collective-permute-done.19), kind=kLoop, calls=%fused_computation.2 | loop fusion | flops 1900544 | bytes 2850816 | tf_op jit(solution)/shard_map/dynamic_update_slice | solution.py:473
  119.7 2.4 %fusion.1 = bf16[256,3712]{1,0:T(8,128)(2,1)} fusion(bf16[256,3712]{1,0:T(8,128)(2,1)} %get-tuple-element.69, bf16[128,3712]{1,0:T(8,128)(2,1)S(1)} %collective-permute-done.21), kind=kLoop, calls=%fused_computation.3 | loop fusion | flops 1900544 | bytes 2850816 | tf_op jit(solution)/shard_map/dynamic_update_slice | solution.py:474
  122.1 3.2 %collective-permute-start.22 = (bf16[256,3712]{1,0:T(8,128)(2,1)}, bf16[256,3712]{1,0:T(8,128)(2,1)}, u32[]{:S(2)}, u32[]{:S(2)}) collective-permute-start(bf16[256,3712]{1,0:T(8,128)(2,1)} %fusion.1), channel_id=1, source_target_pairs={{0,12},{1,13},{2,14},{3,15},{4,0},{5,1},{6,2},{7,3},{8,4},{9,5},{1... | collective-permute-start | bytes 5701640 | tf_op jit(solution)/shard_map/ppermute | solution.py:53
  130.1 5.4 %weight_grads.4 = (bf16[2,4,2,896,128]{4,3,2,1,0:T(8,128)(2,1)}, bf16[2,4,2,896,128]{4,3,2,1,0:T(8,128)(2,1)}, bf16[2,128,7168]{2,1,0:T(8,128)(2,1)}) custom-call(s32[4]{0:T(128)S(1)} %copy-done.36, bf16[128,3712]{1,0:T(8,128)(2,1)S(1)} %copy-done.6, bf16[128,3712]{1,0:T(8,128)(2,1)S(1)} %copy-done.4, ...), custom_call_target="tpu_custom_call", output_to_operand_aliasing={{0}: (10, {}), {1}: (11, {}), {2}: (12, {})} | custom-call | flops 1409286144 | bytes 7340032 | tf_op jit(solution)/shard_map/weight_grads/pallas_call | solution.py:396
  135.6 7.9 %weight_grads.5 = (bf16[2,4,2,896,128]{4,3,2,1,0:T(8,128)(2,1)}, bf16[2,4,2,896,128]{4,3,2,1,0:T(8,128)(2,1)}, bf16[2,128,7168]{2,1,0:T(8,128)(2,1)}) custom-call(s32[4]{0:T(128)S(1)} %copy-done.36, bf16[128,3712]{1,0:T(8,128)(2,1)S(1)} %copy-done.22, ...), custom_call_target="tpu_custom_call", output_to_operand_aliasing={{0}: (10, {}), {1}: (11, {}), {2}: (12, {})} | custom-call | flops 2818572288 | bytes 14680064 | tf_op jit(solution)/shard_map/weight_grads/pallas_call | solution.py:396
  147.1 3.1 %add_convert_fusion.4 = (bf16[64,3712]{1,0:T(8,128)(2,1)S(1)}, bf16[64,3712]{1,0:T(8,128)(2,1)}, bf16[64,3712]{1,0:T(8,128)(2,1)S(1)}) fusion(bf16[256,3712]{1,0:T(8,128)(2,1)} %collective-permute-done.22, bf16[256,3712]{1,0:T(8,128)(2,1)} %collective-permute-done.20, bf16[128,3712]{1,0:T(8,128)(2,1)S(1)} %copy-done.33, bf16[128,3712]{1,0:T(8,128)(2,1)S(1)} %copy-done.35), kind=kLoop, calls=%fused_computation.6 | loop fusion | flops 4276224 | bytes 5701632 | tf_op jit(solution)/shard_map/convert_element_type | solution.py:424
  153.0 7.7 %collective-permute-done.25 = bf16[64,3712]{1,0:T(8,128)(2,1)S(1)} collective-permute-done((bf16[64,3712]{1,0:T(8,128)(2,1)}, bf16[64,3712]{1,0:T(8,128)(2,1)S(1)}, u32[]{:S(2)}, u32[]{:S(2)}) %collective-permute-start.25) | collective-permute-done | bytes 475168 | tf_op jit(solution)/shard_map/ppermute | solution.py:53
  160.6 2.7 %collective-permute-done.24 = bf16[64,3712]{1,0:T(8,128)(2,1)S(1)} collective-permute-done((bf16[64,3712]{1,0:T(8,128)(2,1)S(1)}, bf16[64,3712]{1,0:T(8,128)(2,1)S(1)}, u32[]{:S(2)}, u32[]{:S(2)}) %collective-permute-start.24) | collective-permute-done | bytes 475168 | tf_op jit(solution)/shard_map/ppermute | solution.py:53
  167.3 4.0 %collective-permute-start.28 = (bf16[64,1024]{1,0:T(8,128)(2,1)S(1)}, bf16[64,1024]{1,0:T(8,128)(2,1)S(1)}, u32[]{:S(2)}, u32[]{:S(2)}) collective-permute-start(bf16[64,1024]{1,0:T(8,128)(2,1)S(1)} %get-tuple-element.113), channel_id=1, source_target_pairs={{0,64},{1,65},{2,66},{3,67},{4,68},{5,69},{6,70},{7,71},{8,72},{9,... | collective-permute-start | bytes 393224 | tf_op jit(solution)/shard_map/ppermute | solution.py:53
  (159 shorter events, 52.4 us)
Async XLA Ops:
  6.8 14.5 %collective-permute-start = (bf16[64,3712]{1,0:T(8,128)(2,1)}, bf16[64,3712]{1,0:T(8,128)(2,1)S(1)}, u32[]{:S(2)}, u32[]{:S(2)}) collective-permute-start(bf16[64,3712]{1,0:T(8,128)(2,1)} %pack.1), channel_id=1, source_target_pairs={{0,3},{1,0},{2,1},{3,2},{4,7},{5,4},{6,5},{7,6},{8,11},{9,8},{10,9... | collective-permute-start | bytes 1425416 | tf_op jit(solution)/shard_map/ppermute | solution.py:53
  9.7 15.5 %collective-permute-start.3 = (bf16[64,3712]{1,0:T(8,128)(2,1)}, bf16[64,3712]{1,0:T(8,128)(2,1)S(1)}, u32[]{:S(2)}, u32[]{:S(2)}) collective-permute-start(bf16[64,3712]{1,0:T(8,128)(2,1)} %pack.1), channel_id=1, source_target_pairs={{0,1},{1,2},{2,3},{3,0},{4,5},{5,6},{6,7},{7,4},{8,9},{9,10},{10,1... | collective-permute-start | bytes 1425416 | tf_op jit(solution)/shard_map/ppermute | solution.py:53
  9.8 15.6 %collective-permute-start.4 = (bf16[64,3712]{1,0:T(8,128)(2,1)}, bf16[64,3712]{1,0:T(8,128)(2,1)S(1)}, u32[]{:S(2)}, u32[]{:S(2)}) collective-permute-start(bf16[64,3712]{1,0:T(8,128)(2,1)} %pack.1), channel_id=1, source_target_pairs={{0,2},{1,3},{2,0},{3,1},{4,6},{5,7},{6,4},{7,5},{8,10},{9,11},{10,... | collective-permute-start | bytes 1425416 | tf_op jit(solution)/shard_map/ppermute | solution.py:53
  18.3 78.3 %collective-permute-start.18 = (bf16[4,42,128,128]{3,2,1,0:T(8,128)(2,1)}, bf16[4,42,128,128]{3,2,1,0:T(8,128)(2,1)}, u32[]{:S(2)}, u32[]{:S(2)}) collective-permute-start(bf16[4,42,128,128]{3,2,1,0:T(8,128)(2,1)} %pack_weights.1), channel_id=1, source_target_pairs={{0,16},{1,17},{2,18},{3,19},{4,20},{5,21},{6,22},{7,23},{8,24},{9,... | collective-permute-start | bytes 16515080 | tf_op jit(solution)/shard_map/ppermute | solution.py:53
  21.4 15.0 %collective-permute-start.1 = (bf16[128,3712]{1,0:T(8,128)(2,1)S(1)}, bf16[128,3712]{1,0:T(8,128)(2,1)S(1)}, u32[]{:S(2)}, u32[]{:S(2)}) collective-permute-start(bf16[128,3712]{1,0:T(8,128)(2,1)S(1)} %constant_dynamic-update-slice_fusion.refs_0_.refs_13_), channel_id=1, source_target_pairs={{0,4},{1,5},{2,6},{3,7},{4,8},{5,9},{6,10},{7,11},{8,12},{9,13},{1... | collective-permute-start | bytes 2850824 | tf_op jit(solution)/shard_map/ppermute | solution.py:53
  25.4 14.0 %collective-permute-start.5 = (bf16[128,3712]{1,0:T(8,128)(2,1)S(1)}, bf16[128,3712]{1,0:T(8,128)(2,1)S(1)}, u32[]{:S(2)}, u32[]{:S(2)}) collective-permute-start(bf16[128,3712]{1,0:T(8,128)(2,1)S(1)} %constant_dynamic-update-slice_fusion.2.refs_1_.refs_14_), channel_id=1, source_target_pairs={{0,12},{1,13},{2,14},{3,15},{4,0},{5,1},{6,2},{7,3},{8,4},{9,5},{1... | collective-permute-start | bytes 2850824 | tf_op jit(solution)/shard_map/ppermute | solution.py:53
  28.1 21.4 %collective-permute-start.7 = (bf16[128,3712]{1,0:T(8,128)(2,1)S(1)}, bf16[128,3712]{1,0:T(8,128)(2,1)S(1)}, u32[]{:S(2)}, u32[]{:S(2)}) collective-permute-start(bf16[128,3712]{1,0:T(8,128)(2,1)S(1)} %constant_dynamic-update-slice_fusion.refs_0_.refs_13_), channel_id=1, source_target_pairs={{0,12},{1,13},{2,14},{3,15},{4,0},{5,1},{6,2},{7,3},{8,4},{9,5},{1... | collective-permute-start | bytes 2850824 | tf_op jit(solution)/shard_map/ppermute | solution.py:53
  29.7 19.9 %collective-permute-start.8 = (bf16[128,3712]{1,0:T(8,128)(2,1)S(1)}, bf16[128,3712]{1,0:T(8,128)(2,1)S(1)}, u32[]{:S(2)}, u32[]{:S(2)}) collective-permute-start(bf16[128,3712]{1,0:T(8,128)(2,1)S(1)} %constant_dynamic-update-slice_fusion.2.refs_1_.refs_14_), channel_id=1, source_target_pairs={{0,4},{1,5},{2,6},{3,7},{4,8},{5,9},{6,10},{7,11},{8,12},{9,13},{1... | collective-permute-start | bytes 2850824 | tf_op jit(solution)/shard_map/ppermute | solution.py:53
  36.4 13.7 %collective-permute-start.9 = (bf16[128,3712]{1,0:T(8,128)(2,1)S(1)}, bf16[128,3712]{1,0:T(8,128)(2,1)S(1)}, u32[]{:S(2)}, u32[]{:S(2)}) collective-permute-start(bf16[128,3712]{1,0:T(8,128)(2,1)S(1)} %constant_dynamic-update-slice_fusion.refs_0_.refs_13_), channel_id=1, source_target_pairs={{0,16},{1,17},{2,18},{3,19},{4,20},{5,21},{6,22},{7,23},{8,24},{9,... | collective-permute-start | bytes 2850824 | tf_op jit(solution)/shard_map/ppermute | solution.py:53
  39.4 10.8 %collective-permute-start.10 = (bf16[128,3712]{1,0:T(8,128)(2,1)S(1)}, bf16[128,3712]{1,0:T(8,128)(2,1)S(1)}, u32[]{:S(2)}, u32[]{:S(2)}) collective-permute-start(bf16[128,3712]{1,0:T(8,128)(2,1)S(1)} %constant_dynamic-update-slice_fusion.2.refs_1_.refs_14_), channel_id=1, source_target_pairs={{0,16},{1,17},{2,18},{3,19},{4,20},{5,21},{6,22},{7,23},{8,24},{9,... | collective-permute-start | bytes 2850824 | tf_op jit(solution)/shard_map/ppermute | solution.py:53
  50.1 8.4 %collective-permute-start.13 = (bf16[128,3712]{1,0:T(8,128)(2,1)S(1)}, bf16[128,3712]{1,0:T(8,128)(2,1)S(1)}, u32[]{:S(2)}, u32[]{:S(2)}) collective-permute-start(bf16[128,3712]{1,0:T(8,128)(2,1)S(1)} %collective-permute-done.1.refs_4_.refs_17_), channel_id=1, source_target_pairs={{0,16},{1,17},{2,18},{3,19},{4,20},{5,21},{6,22},{7,23},{8,24},{9,... | collective-permute-start | bytes 2850824 | tf_op jit(solution)/shard_map/ppermute | solution.py:53
  50.2 9.3 %collective-permute-start.14 = (bf16[128,3712]{1,0:T(8,128)(2,1)S(1)}, bf16[128,3712]{1,0:T(8,128)(2,1)}, u32[]{:S(2)}, u32[]{:S(2)}) collective-permute-start(bf16[128,3712]{1,0:T(8,128)(2,1)S(1)} %collective-permute-done.8.refs_5_.refs_18_), channel_id=1, source_target_pairs={{0,16},{1,17},{2,18},{3,19},{4,20},{5,21},{6,22},{7,23},{8,24},{9,... | collective-permute-start | bytes 2850824 | tf_op jit(solution)/shard_map/ppermute | solution.py:53
  52.1 19.2 %collective-permute-start.2 = (bf16[128,3712]{1,0:T(8,128)(2,1)S(1)}, bf16[128,3712]{1,0:T(8,128)(2,1)}, u32[]{:S(2)}, u32[]{:S(2)}) collective-permute-start(bf16[128,3712]{1,0:T(8,128)(2,1)S(1)} %collective-permute-done.1.refs_4_.refs_17_), channel_id=1, source_target_pairs={{0,4},{1,5},{2,6},{3,7},{4,8},{5,9},{6,10},{7,11},{8,12},{9,13},{1... | collective-permute-start | bytes 2850824 | tf_op jit(solution)/shard_map/ppermute | solution.py:53
  54.8 16.5 %collective-permute-start.6 = (bf16[128,3712]{1,0:T(8,128)(2,1)S(1)}, bf16[128,3712]{1,0:T(8,128)(2,1)}, u32[]{:S(2)}, u32[]{:S(2)}) collective-permute-start(bf16[128,3712]{1,0:T(8,128)(2,1)S(1)} %collective-permute-done.5.refs_3_.refs_16_), channel_id=1, source_target_pairs={{0,12},{1,13},{2,14},{3,15},{4,0},{5,1},{6,2},{7,3},{8,4},{9,5},{1... | collective-permute-start | bytes 2850824 | tf_op jit(solution)/shard_map/ppermute | solution.py:53
  87.3 9.3 %collective-permute-start.17 = (bf16[512,896]{1,0:T(8,128)(2,1)}, bf16[512,896]{1,0:T(8,128)(2,1)S(1)}, u32[]{:S(2)}, u32[]{:S(2)}) collective-permute-start(bf16[512,896]{1,0:T(8,128)(2,1)} %get-tuple-element.55.acts), channel_id=1, source_target_pairs={{0,16},{1,17},{2,18},{3,19},{4,20},{5,21},{6,22},{7,23},{8,24},{9,... | collective-permute-start | bytes 2752520 | tf_op jit(solution)/shard_map/ppermute | solution.py:53
  102.2 15.0 %collective-permute-start.19 = (bf16[128,3712]{1,0:T(8,128)(2,1)S(1)}, bf16[128,3712]{1,0:T(8,128)(2,1)S(1)}, u32[]{:S(2)}, u32[]{:S(2)}) collective-permute-start(bf16[128,3712]{1,0:T(8,128)(2,1)S(1)} %get-tuple-element.68), channel_id=1, source_target_pairs={{0,4},{1,5},{2,6},{3,7},{4,8},{5,9},{6,10},{7,11},{8,12},{9,13},{1... | collective-permute-start | bytes 2850824 | tf_op jit(solution)/shard_map/ppermute | solution.py:53
  102.3 17.4 %collective-permute-start.21 = (bf16[128,3712]{1,0:T(8,128)(2,1)S(1)}, bf16[128,3712]{1,0:T(8,128)(2,1)S(1)}, u32[]{:S(2)}, u32[]{:S(2)}) collective-permute-start(bf16[128,3712]{1,0:T(8,128)(2,1)S(1)} %get-tuple-element.70), channel_id=1, source_target_pairs={{0,12},{1,13},{2,14},{3,15},{4,0},{5,1},{6,2},{7,3},{8,4},{9,5},{1... | collective-permute-start | bytes 2850824 | tf_op jit(solution)/shard_map/ppermute | solution.py:53
  119.7 25.5 %collective-permute-start.20 = (bf16[256,3712]{1,0:T(8,128)(2,1)}, bf16[256,3712]{1,0:T(8,128)(2,1)}, u32[]{:S(2)}, u32[]{:S(2)}) collective-permute-start(bf16[256,3712]{1,0:T(8,128)(2,1)} %fusion), channel_id=1, source_target_pairs={{0,4},{1,5},{2,6},{3,7},{4,8},{5,9},{6,10},{7,11},{8,12},{9,13},{1... | collective-permute-start | bytes 5701640 | tf_op jit(solution)/shard_map/ppermute | solution.py:53
  122.1 25.0 %collective-permute-start.22 = (bf16[256,3712]{1,0:T(8,128)(2,1)}, bf16[256,3712]{1,0:T(8,128)(2,1)}, u32[]{:S(2)}, u32[]{:S(2)}) collective-permute-start(bf16[256,3712]{1,0:T(8,128)(2,1)} %fusion.1), channel_id=1, source_target_pairs={{0,12},{1,13},{2,14},{3,15},{4,0},{5,1},{6,2},{7,3},{8,4},{9,5},{1... | collective-permute-start | bytes 5701640 | tf_op jit(solution)/shard_map/ppermute | solution.py:53
  150.1 10.5 %collective-permute-start.25 = (bf16[64,3712]{1,0:T(8,128)(2,1)}, bf16[64,3712]{1,0:T(8,128)(2,1)S(1)}, u32[]{:S(2)}, u32[]{:S(2)}) collective-permute-start(bf16[64,3712]{1,0:T(8,128)(2,1)} %get-tuple-element.101), channel_id=1, source_target_pairs={{0,2},{1,3},{2,0},{3,1},{4,6},{5,7},{6,4},{7,5},{8,10},{9,11},{10,... | collective-permute-start | bytes 1425416 | tf_op jit(solution)/shard_map/ppermute | solution.py:53
  150.4 12.9 %collective-permute-start.24 = (bf16[64,3712]{1,0:T(8,128)(2,1)S(1)}, bf16[64,3712]{1,0:T(8,128)(2,1)S(1)}, u32[]{:S(2)}, u32[]{:S(2)}) collective-permute-start(bf16[64,3712]{1,0:T(8,128)(2,1)S(1)} %get-tuple-element.100), channel_id=1, source_target_pairs={{0,3},{1,0},{2,1},{3,2},{4,7},{5,4},{6,5},{7,6},{8,11},{9,8},{10,9... | collective-permute-start | bytes 1425416 | tf_op jit(solution)/shard_map/ppermute | solution.py:53
  151.3 14.3 %collective-permute-start.23 = (bf16[64,3712]{1,0:T(8,128)(2,1)S(1)}, bf16[64,3712]{1,0:T(8,128)(2,1)S(1)}, u32[]{:S(2)}, u32[]{:S(2)}) collective-permute-start(bf16[64,3712]{1,0:T(8,128)(2,1)S(1)} %get-tuple-element.102), channel_id=1, source_target_pairs={{0,1},{1,2},{2,3},{3,0},{4,5},{5,6},{6,7},{7,4},{8,9},{9,10},{10,1... | collective-permute-start | bytes 1425416 | tf_op jit(solution)/shard_map/ppermute | solution.py:53
  167.3 7.7 %collective-permute-start.28 = (bf16[64,1024]{1,0:T(8,128)(2,1)S(1)}, bf16[64,1024]{1,0:T(8,128)(2,1)S(1)}, u32[]{:S(2)}, u32[]{:S(2)}) collective-permute-start(bf16[64,1024]{1,0:T(8,128)(2,1)S(1)} %get-tuple-element.113), channel_id=1, source_target_pairs={{0,64},{1,65},{2,66},{3,67},{4,68},{5,69},{6,70},{7,71},{8,72},{9,... | collective-permute-start | bytes 393224 | tf_op jit(solution)/shard_map/ppermute | solution.py:53
  171.9 6.2 %collective-permute-start.26 = (bf16[64,1024]{1,0:T(8,128)(2,1)S(1)}, bf16[64,1024]{1,0:T(8,128)(2,1)S(1)}, u32[]{:S(2)}, u32[]{:S(2)}) collective-permute-start(bf16[64,1024]{1,0:T(8,128)(2,1)S(1)} %get-tuple-element.111), channel_id=1, source_target_pairs={{0,32},{1,33},{2,34},{3,35},{4,36},{5,37},{6,38},{7,39},{8,40},{9,... | collective-permute-start | bytes 393224 | tf_op jit(solution)/shard_map/ppermute | solution.py:53
  (45 other events, 434.2 us)

commit v6 on v5

--- a/solution.py
+++ b/solution.py
@@ -381,13 +381,13 @@
         in_specs=[SM] + [VM] * 6,
         out_specs=[VM] * len(pieces),
         out_shape=[shape((128 * len(group), half + 128)) for group in pieces],
-        compiler_params=params(18),
+        compiler_params=params(14),
         cost_estimate=cost(2 * 64 * sum(map(len, pieces)) * 1536 * half, 12),
         name="results",
     )(sel, acts, acts_other, *weights, wall)
 
 
-def weight_grads(swapped, first, count, sel, rows, acts, before):
+def weight_grads(swapped, first, count, sel, rows, acts, before, room):
     width, half = WIDTH, WIDTH * STEPS
     at = 1 if swapped else 0
     up_spec = pl.BlockSpec((2, 1, 1, width, 128), lambda k, sel: (0, first + k, sel[at], 0, 0))
@@ -403,7 +403,7 @@
         ),
         out_shape=[up_shape, up_shape, shape((2, 128, 2 * half))],
         input_output_aliases={2 + len(rows) + i: i for i in range(len(before))},
-        compiler_params=params(20),
+        compiler_params=params(room),
         cost_estimate=cost(2 * 512 * 768 * width * count, 3.5 * count),
         name="weight_grads",
     )(sel, *rows, acts, *before)
@@ -439,8 +439,11 @@
     )
     high = lax.reduce_precision(gate_logits, 8, 7)
     middle = lax.reduce_precision(gate_logits - high, 8, 7)
-    extra = joined([high, middle, gate_logits - high - middle, route_slot.astype(F32)], axis=1)
-    extra = jnp.pad(extra, ((0, 0), (0, 128 - extra.shape[1]))).astype(BF)
+    parts = (high, middle, gate_logits - high - middle, route_slot.astype(F32))
+    extra = sum(
+        lax.pad(part, 0.0, ((0, 0, 0), (24 * at, 128 - 24 * at - part.shape[1], 0)))
+        for at, part in enumerate(parts)
+    ).astype(BF)
     own = pack(sel, tokens, cotangent, extra)
     own, later = lax.optimization_barrier((own, sel))
     minus, plus, far = send(own, inner(1)), send(own, inner(-1)), send(own, inner(2))
@@ -461,25 +464,23 @@
     held = jnp.pad(held.astype(F32), ((0, 128 - 72), (0, 128 - slots))).astype(BF)
     acts, acts_grad = activations(sel, rows, far_other, weights, sums, held)
     acts_other = send(acts, other_core())
-    grads = weight_grads(False, 0, 2, sel, rows, acts_grad, [])
-    acts_other, grads = lax.optimization_barrier((acts_other, grads))
 
     far_a, far_b = results(((6,), (7,)), sel, acts, acts_other, weights, wall, half)
-    own_a, own_b, to_plus, to_minus = results(
-        ((0,), (1,), (2, 3), (5, 4)), sel, acts, acts_other, weights, wall, half
-    )
-    own_a, grads = lax.optimization_barrier((own_a, grads))
+    own_a, own_b, plus_a, plus_b, minus_b, minus_a = results(
+        ((0,), (1,), (2,), (3,), (5,), (4,)), sel, acts, acts_other, weights, wall, half
+    )
+    own_a, acts_grad = lax.optimization_barrier((own_a, acts_grad))
     from_a, from_b = send(far_a, outer(1)), send(far_b, outer(-1))
-    to_plus = lax.dynamic_update_slice(to_plus, add(to_plus[:128], from_a), (0, 0))
-    to_minus = lax.dynamic_update_slice(to_minus, add(to_minus[:128], from_b), (0, 0))
-    got_p, got_m = send(to_plus, outer(1)), send(to_minus, outer(-1))
-    grads = weight_grads(False, 2, 2, sel, rows, acts_grad, grads)
-    grads = weight_grads(True, 0, 4, sel, rows_other, acts_grad, grads)
-    (got_p, got_m), grads = lax.optimization_barrier(((got_p, got_m), grads))
-    keep = (own_a[:64], got_p[:64], got_m[128:192])
-    to_plus = add(own_a[64:], got_p[64:128], got_m[192:])
-    to_minus = add(own_b[:64], got_p[128:192], got_m[:64])
-    to_far = add(own_b[64:], got_p[192:], got_m[64:128])
+    b_early, a_early = send(plus_b, outer(1)), send(minus_a, outer(-1))
+    a_late = send(add(plus_a, from_a), outer(1))
+    b_late = send(add(minus_b, from_b), outer(-1))
+    grads = weight_grads(False, 0, 4, sel, rows, acts_grad, [], 52)
+    grads = weight_grads(True, 0, 4, sel, rows_other, acts_grad, grads, 52)
+    (a_late, b_late), grads = lax.optimization_barrier(((a_late, b_late), grads))
+    keep = (own_a[:64], a_late[:64], a_early[:64])
+    to_plus = add(own_a[64:], a_late[64:], a_early[64:])
+    to_minus = add(own_b[:64], b_late[:64], b_early[:64])
+    to_far = add(own_b[64:], b_late[64:], b_early[64:])
     total = add(
         *keep, send(to_plus, inner(1)), send(to_minus, inner(-1)), send(to_far, inner(2))
     )

time: 182 us -> 173 us (0.951)
  local copies, waits for them, and re-layouts: 11.9 us -> 6.81 us
  Pallas kernels: 66.1 us -> 62.6 us
  starting transfers between devices: 34 us -> 37.3 us
  other arithmetic: 13.8 us -> 11.6 us
    unnamed x85 -> x57, local copies, waits for them, and re-layouts: 10.9 us -> 5.85 us
    dynamic_update_slice x2 -> x0, other arithmetic: 4.79 us -> none  [the longest x1 2.42 us: per_device(): lax.dynamic_update_slice(to_plus, add(to_plus[:128], from_a), (0, 0))]
    ppermute x29 -> x31, starting transfers between devices: 34 us -> 37.3 us  [send(): return lax.ppermute(value, AXES, pairs)]
    convert_element_type x2 -> x5, other arithmetic: 4.62 us -> 7.87 us  [add(): return total.astype(BF)]
    pallas_call x3 -> x2, Pallas kernels: 18.8 us -> 16.4 us  [weight_grads(): pl.pallas_call(functools.partial(grads_kernel, swapped), grid_spec=pltpu....]
    ppermute x29 -> x31, waiting for transfers between devices: 53 us -> 52.8 us  [send(): return lax.ppermute(value, AXES, pairs)]
  transfers between devices with their start and end apart: 29 -> 31, of which waited for: 18 -> 18; matrix products, arithmetic and copies ran while one was open for 3% -> 5% of each run, Pallas kernels for 32% -> 32%
where the time goes in v6:
time: 173 us; the launch traced here: 172 us
  Pallas kernels  62.6 us (36%)
  waiting for transfers between devices  52.8 us (31%)
  starting transfers between devices  37.3 us (22%)
  other arithmetic  11.6 us (7%)
  local copies, waits for them, and re-layouts  6.81 us (4%)
    ppermute x31, waiting for transfers between devices, send(): return lax.ppermute(value, AXES, pairs)  52.8 us
    ppermute x31, starting transfers between devices, send(): return lax.ppermute(value, AXES, pairs)  37.3 us
    pallas_call x2, Pallas kernels, weight_grads(): pl.pallas_call(functools.partial(grads_kernel, swapped), grid_spec=pltpu....  16.4 us
    pallas_call x2, Pallas kernels, results(): pl.pallas_call(functools.partial(results_kernel, pieces), in_specs=[SM] +...  14.3 us
    pallas_call x1, Pallas kernels, near_sums(): pl.pallas_call(near_kernel, grid_spec=pltpu.PrefetchScalarGridSpec(num_sc...  11.8 us
    pallas_call x1, Pallas kernels, activations(): pl.pallas_call(far_kernel, grid_spec=pltpu.PrefetchScalarGridSpec(num_sca...  11.3 us
    convert_element_type x5, other arithmetic, add(): return total.astype(BF)  7.87 us
    pallas_call x1, Pallas kernels, pack_weights(): pl.pallas_call(pack_weights_kernel, grid_spec=pltpu.PrefetchScalarGridSpe...  6.27 us
  transfers between devices with their start and end apart: 31, of which 18 were waited for; matrix products, arithmetic and copies ran while one was open for 5% of the time, Pallas kernels for 32%

profile of v6, /device:TPU:0, one launch (start us, length us, event | category | flops | bytes accessed | tf_op | source)
XLA Modules:
  0.0 172.1 jit_solution(12878634417442257087)
XLA Ops:
  3.5 2.6 %pack.1 = bf16[64,3712]{1,0:T(8,128)(2,1)} custom-call(s32[4]{0:T(128)} %pad_add_fusion.sel, bf16[32,7168]{1,0:T(8,128)(2,1)} %tok.1, bf16[32,7168]{1,0:T(8,128)(2,1)} %cot.1, bf16[32,128]{1,0:T(8,128)(2,1)} %add_convert_fusion.6.extra), custom_call_target="tpu_custom_call" | custom-call | bytes 2097152 | tf_op jit(solution)/shard_map/pack/pallas_call | solution.py:295
  6.1 2.9 %collective-permute-start = (bf16[64,3712]{1,0:T(8,128)(2,1)}, bf16[64,3712]{1,0:T(8,128)(2,1)S(1)}, u32[]{:S(2)}, u32[]{:S(2)}) collective-permute-start(bf16[64,3712]{1,0:T(8,128)(2,1)} %pack.1), channel_id=1, source_target_pairs={{0,3},{1,0},{2,1},{3,2},{4,7},{5,4},{6,5},{7,6},{8,11},{9,8},{10,9... | collective-permute-start | bytes 1425416 | tf_op jit(solution)/shard_map/ppermute | solution.py:53
  11.3 6.3 %pack_weights.1 = bf16[4,42,128,128]{3,2,1,0:T(8,128)(2,1)} custom-call(s32[4]{0:T(128)} %pad_add_fusion.sel, bf16[2,4,2,896,128]{4,3,2,1,0:T(8,128)(2,1)} %bitcast.8, bf16[2,4,2,896,128]{4,3,2,1,0:T(8,128)(2,1)} %bitcast.15, bf16[2,128,7168]{2,1,0:T(8,128)(2,1)} %wd.5), custom_call_target="tpu_custom_call" | custom-call | bytes 11534336 | tf_op jit(solution)/shard_map/pack_weights/pallas_call | solution.py:311
  17.6 3.0 %collective-permute-done = bf16[64,3712]{1,0:T(8,128)(2,1)S(1)} collective-permute-done((bf16[64,3712]{1,0:T(8,128)(2,1)}, bf16[64,3712]{1,0:T(8,128)(2,1)S(1)}, u32[]{:S(2)}, u32[]{:S(2)}) %collective-permute-start) | collective-permute-done | bytes 475168 | tf_op jit(solution)/shard_map/ppermute | solution.py:53
  24.6 2.7 %collective-permute-start.5 = (bf16[128,3712]{1,0:T(8,128)(2,1)S(1)}, bf16[128,3712]{1,0:T(8,128)(2,1)S(1)}, u32[]{:S(2)}, u32[]{:S(2)}) collective-permute-start(bf16[128,3712]{1,0:T(8,128)(2,1)S(1)} %constant_dynamic-update-slice_fusion.2.refs_1_.refs_14_), channel_id=1, source_target_pairs={{0,12},{1,13},{2,14},{3,15},{4,0},{5,1},{6,2},{7,3},{8,4},{9,5},{1... | collective-permute-start | bytes 2850824 | tf_op jit(solution)/shard_map/ppermute | solution.py:53
  29.4 6.3 %collective-permute-done.1.refs_4_.refs_17_ = bf16[128,3712]{1,0:T(8,128)(2,1)S(1)} collective-permute-done((bf16[128,3712]{1,0:T(8,128)(2,1)S(1)}, bf16[128,3712]{1,0:T(8,128)(2,1)S(1)}, u32[]{:S(2)}, u32[]{:S(2)}) %collective-permute-start.1) | collective-permute-done | bytes 950304 | tf_op jit(solution)/shard_map/ppermute | solution.py:53
  35.6 3.0 %collective-permute-done.5.refs_3_.refs_16_ = bf16[128,3712]{1,0:T(8,128)(2,1)S(1)} collective-permute-done((bf16[128,3712]{1,0:T(8,128)(2,1)S(1)}, bf16[128,3712]{1,0:T(8,128)(2,1)S(1)}, u32[]{:S(2)}, u32[]{:S(2)}) %collective-permute-start.5) | collective-permute-done | bytes 950304 | tf_op jit(solution)/shard_map/ppermute | solution.py:53
  38.6 10.2 %collective-permute-done.7.refs_2_.refs_15_ = bf16[128,3712]{1,0:T(8,128)(2,1)S(1)} collective-permute-done((bf16[128,3712]{1,0:T(8,128)(2,1)S(1)}, bf16[128,3712]{1,0:T(8,128)(2,1)S(1)}, u32[]{:S(2)}, u32[]{:S(2)}) %collective-permute-start.7) | collective-permute-done | bytes 950304 | tf_op jit(solution)/shard_map/ppermute | solution.py:53
  54.0 3.7 %collective-permute-start.6 = (bf16[128,3712]{1,0:T(8,128)(2,1)S(1)}, bf16[128,3712]{1,0:T(8,128)(2,1)}, u32[]{:S(2)}, u32[]{:S(2)}) collective-permute-start(bf16[128,3712]{1,0:T(8,128)(2,1)S(1)} %collective-permute-done.5.refs_3_.refs_16_), channel_id=1, source_target_pairs={{0,12},{1,13},{2,14},{3,15},{4,0},{5,1},{6,2},{7,3},{8,4},{9,5},{1... | collective-permute-start | bytes 2850824 | tf_op jit(solution)/shard_map/ppermute | solution.py:53
  58.8 11.8 %near_sums.1 = (f32[512,256]{1,0:T(8,128)}, f32[512,256]{1,0:T(8,128)}, f32[512,256]{1,0:T(8,128)}) custom-call(s32[4]{0:T(128)} %pad_add_fusion.sel, bf16[128,3712]{1,0:T(8,128)(2,1)} %copy-done.3, bf16[128,3712]{1,0:T(8,128)(2,1)} %copy-done.13, bf16[128,3712]{1,0:T(8,128)(2,1)} %copy-done.16, bf16[128,3712]{1,0:T(8,128)(2,1)} %copy-done.15, ...), custom_call_target="tpu_custom_call" | custom-call | bytes 104857 | tf_op jit(solution)/shard_map/near_sums/pallas_call | solution.py:340
  74.9 11.3 %activations.1 = (bf16[512,896]{1,0:T(8,128)(2,1)}, bf16[512,768]{1,0:T(8,128)(2,1)}) custom-call(s32[4]{0:T(128)} %pad_add_fusion.sel, bf16[128,3712]{1,0:T(8,128)(2,1)} %collective-permute-done.2.refs_0_.refs_19_.refs_6_, bf16[128,3712]{1,0:T(8,128)(2,1)} %collective-permute-done.6.refs_1_.refs_20_.refs_7_, bf16[128,3712]{1,0:T(8,128)(2,1)} %copy-done.22, ...), custom_call_target="tpu_custom_call" | custom-call | flops 1409286144 | bytes 15728640 | tf_op jit(solution)/shard_map/activations/pallas_call | solution.py:357
  86.6 2.5 %collective-permute-done.17.acts_other = bf16[512,896]{1,0:T(8,128)(2,1)S(1)} collective-permute-done((bf16[512,896]{1,0:T(8,128)(2,1)}, bf16[512,896]{1,0:T(8,128)(2,1)S(1)}, u32[]{:S(2)}, u32[]{:S(2)}) %collective-permute-start.17) | collective-permute-done | bytes 917536 | tf_op jit(solution)/shard_map/ppermute | solution.py:53
  92.4 5.6 %results.3 = (bf16[128,3712]{1,0:T(8,128)(2,1)S(1)}, bf16[128,3712]{1,0:T(8,128)(2,1)S(1)}) custom-call(s32[4]{0:T(128)S(1)} %copy-done.11, bf16[512,896]{1,0:T(8,128)(2,1)S(1)} %copy-done.7, bf16[512,896]{1,0:T(8,128)(2,1)S(1)} %collective-permute-done.17.acts_other, bf16[2,4,2,896,128]{4,3,2,1,0:T(8,128)(2,1)S(1)} %bitcast.13, ...), custom_call_target="tpu_custom_call" | custom-call | flops 1409286144 | bytes 12582912 | tf_op jit(solution)/shard_map/results/pallas_call | solution.py:379
  98.0 3.2 %collective-permute-start.21 = (bf16[128,3712]{1,0:T(8,128)(2,1)S(1)}, bf16[128,3712]{1,0:T(8,128)(2,1)S(1)}, u32[]{:S(2)}, u32[]{:S(2)}) collective-permute-start(bf16[128,3712]{1,0:T(8,128)(2,1)S(1)} %get-tuple-element.56), channel_id=1, source_target_pairs={{0,12},{1,13},{2,14},{3,15},{4,0},{5,1},{6,2},{7,3},{8,4},{9,5},{1... | collective-permute-start | bytes 2850824 | tf_op jit(solution)/shard_map/ppermute | solution.py:53
  101.3 8.7 %results.2 = (bf16[128,3712]{1,0:T(8,128)(2,1)S(1)}, bf16[128,3712]{1,0:T(8,128)(2,1)S(1)}, bf16[128,3712]{1,0:T(8,128)(2,1)S(1)}, bf16[128,3712]{1,0:T(8,128)(2...) custom-call(s32[4]{0:T(128)S(1)} %copy-done.11, bf16[512,896]{1,0:T(8,128)(2,1)S(1)} %copy-done.7, ...), custom_call_target="tpu_custom_call" | custom-call | flops 4227858432 | bytes 12582912 | tf_op jit(solution)/shard_map/results/pallas_call | solution.py:379
  109.9 3.0 %collective-permute-done.19 = bf16[128,3712]{1,0:T(8,128)(2,1)S(1)} collective-permute-done((bf16[128,3712]{1,0:T(8,128)(2,1)S(1)}, bf16[128,3712]{1,0:T(8,128)(2,1)S(1)}, u32[]{:S(2)}, u32[]{:S(2)}) %collective-permute-start.19) | collective-permute-done | bytes 950304 | tf_op jit(solution)/shard_map/ppermute | solution.py:53
  115.4 3.2 %collective-permute-start.22 = (bf16[128,3712]{1,0:T(8,128)(2,1)}, bf16[128,3712]{1,0:T(8,128)(2,1)}, u32[]{:S(2)}, u32[]{:S(2)}) collective-permute-start(bf16[128,3712]{1,0:T(8,128)(2,1)} %add_convert_fusion), channel_id=1, source_target_pairs={{0,12},{1,13},{2,14},{3,15},{4,0},{5,1},{6,2},{7,3},{8,4},{9,5},{1... | collective-permute-start | bytes 2850824 | tf_op jit(solution)/shard_map/ppermute | solution.py:53
  118.7 3.2 %collective-permute-start.23 = (bf16[128,3712]{1,0:T(8,128)(2,1)}, bf16[128,3712]{1,0:T(8,128)(2,1)}, u32[]{:S(2)}, u32[]{:S(2)}) collective-permute-start(bf16[128,3712]{1,0:T(8,128)(2,1)} %copy-done.12), channel_id=1, source_target_pairs={{0,12},{1,13},{2,14},{3,15},{4,0},{5,1},{6,2},{7,3},{8,4},{9,5},{1... | collective-permute-start | bytes 2850824 | tf_op jit(solution)/shard_map/ppermute | solution.py:53
  121.9 8.2 %weight_grads.2 = (bf16[2,4,2,896,128]{4,3,2,1,0:T(8,128)(2,1)}, bf16[2,4,2,896,128]{4,3,2,1,0:T(8,128)(2,1)}, bf16[2,128,7168]{2,1,0:T(8,128)(2,1)}) custom-call(s32[4]{0:T(128)S(1)} %copy-done.11, bf16[128,3712]{1,0:T(8,128)(2,1)S(1)} %copy-done.4, bf16[128,3712]{1,0:T(8,128)(2,1)} %copy-done.13, bf16[128,3712]{1,0:T(8,128)(2,1)} %copy-done.16, ...), custom_call_target="tpu_custom_call" | custom-call | flops 2818572288 | bytes 14680064 | tf_op jit(solution)/shard_map/weight_grads/pallas_call | solution.py:396
  130.2 8.2 %weight_grads.3 = (bf16[2,4,2,896,128]{4,3,2,1,0:T(8,128)(2,1)}, bf16[2,4,2,896,128]{4,3,2,1,0:T(8,128)(2,1)}, bf16[2,128,7168]{2,1,0:T(8,128)(2,1)}) custom-call(s32[4]{0:T(128)S(1)} %copy-done.11, bf16[128,3712]{1,0:T(8,128)(2,1)S(1)} %copy-done.6, bf16[128,3712]{1,0:T(8,128)(2,1)} %copy-done.18, ...), custom_call_target="tpu_custom_call", output_to_operand_aliasing={{0}: (10, {}), {1}: (11, {}), {2}: (12, {})} | custom-call | flops 2818572288 | bytes 14680064 | tf_op jit(solution)/shard_map/weight_grads/pallas_call | solution.py:396
  139.7 2.6 %add_convert_fusion.4 = (bf16[64,3712]{1,0:T(8,128)(2,1)S(1)}, bf16[64,3712]{1,0:T(8,128)(2,1)}) fusion(bf16[128,3712]{1,0:T(8,128)(2,1)} %collective-permute-done.25, bf16[128,3712]{1,0:T(8,128)(2,1)} %collective-permute-done.22, bf16[128,3712]{1,0:T(8,128)(2,1)S(1)} %copy-done.9), kind=kLoop, calls=%fused_computation.4 | loop fusion | flops 2850816 | bytes 3801088 | tf_op jit(solution)/shard_map/convert_element_type | solution.py:424
  146.5 6.2 %collective-permute-done.27 = bf16[64,3712]{1,0:T(8,128)(2,1)S(1)} collective-permute-done((bf16[64,3712]{1,0:T(8,128)(2,1)}, bf16[64,3712]{1,0:T(8,128)(2,1)S(1)}, u32[]{:S(2)}, u32[]{:S(2)}) %collective-permute-start.27) | collective-permute-done | bytes 475168 | tf_op jit(solution)/shard_map/ppermute | solution.py:53
  152.8 2.7 %collective-permute-done.26 = bf16[64,3712]{1,0:T(8,128)(2,1)S(1)} collective-permute-done((bf16[64,3712]{1,0:T(8,128)(2,1)S(1)}, bf16[64,3712]{1,0:T(8,128)(2,1)S(1)}, u32[]{:S(2)}, u32[]{:S(2)}) %collective-permute-start.26) | collective-permute-done | bytes 475168 | tf_op jit(solution)/shard_map/ppermute | solution.py:53
  159.4 4.0 %collective-permute-start.30 = (bf16[64,1024]{1,0:T(8,128)(2,1)S(1)}, bf16[64,1024]{1,0:T(8,128)(2,1)S(1)}, u32[]{:S(2)}, u32[]{:S(2)}) collective-permute-start(bf16[64,1024]{1,0:T(8,128)(2,1)S(1)} %get-tuple-element.96), channel_id=1, source_target_pairs={{0,64},{1,65},{2,66},{3,67},{4,68},{5,69},{6,70},{7,71},{8,72},{9,... | collective-permute-start | bytes 393224 | tf_op jit(solution)/shard_map/ppermute | solution.py:53
  (133 shorter events, 45.9 us)
Async XLA Ops:
  6.1 14.5 %collective-permute-start = (bf16[64,3712]{1,0:T(8,128)(2,1)}, bf16[64,3712]{1,0:T(8,128)(2,1)S(1)}, u32[]{:S(2)}, u32[]{:S(2)}) collective-permute-start(bf16[64,3712]{1,0:T(8,128)(2,1)} %pack.1), channel_id=1, source_target_pairs={{0,3},{1,0},{2,1},{3,2},{4,7},{5,4},{6,5},{7,6},{8,11},{9,8},{10,9... | collective-permute-start | bytes 1425416 | tf_op jit(solution)/shard_map/ppermute | solution.py:53
  9.0 15.5 %collective-permute-start.3 = (bf16[64,3712]{1,0:T(8,128)(2,1)}, bf16[64,3712]{1,0:T(8,128)(2,1)S(1)}, u32[]{:S(2)}, u32[]{:S(2)}) collective-permute-start(bf16[64,3712]{1,0:T(8,128)(2,1)} %pack.1), channel_id=1, source_target_pairs={{0,1},{1,2},{2,3},{3,0},{4,5},{5,6},{6,7},{7,4},{8,9},{9,10},{10,1... | collective-permute-start | bytes 1425416 | tf_op jit(solution)/shard_map/ppermute | solution.py:53
  9.0 15.6 %collective-permute-start.4 = (bf16[64,3712]{1,0:T(8,128)(2,1)}, bf16[64,3712]{1,0:T(8,128)(2,1)S(1)}, u32[]{:S(2)}, u32[]{:S(2)}) collective-permute-start(bf16[64,3712]{1,0:T(8,128)(2,1)} %pack.1), channel_id=1, source_target_pairs={{0,2},{1,3},{2,0},{3,1},{4,6},{5,7},{6,4},{7,5},{8,10},{9,11},{10,... | collective-permute-start | bytes 1425416 | tf_op jit(solution)/shard_map/ppermute | solution.py:53
  17.5 71.6 %collective-permute-start.18 = (bf16[4,42,128,128]{3,2,1,0:T(8,128)(2,1)}, bf16[4,42,128,128]{3,2,1,0:T(8,128)(2,1)}, u32[]{:S(2)}, u32[]{:S(2)}) collective-permute-start(bf16[4,42,128,128]{3,2,1,0:T(8,128)(2,1)} %pack_weights.1), channel_id=1, source_target_pairs={{0,16},{1,17},{2,18},{3,19},{4,20},{5,21},{6,22},{7,23},{8,24},{9,... | collective-permute-start | bytes 16515080 | tf_op jit(solution)/shard_map/ppermute | solution.py:53
  20.6 15.0 %collective-permute-start.1 = (bf16[128,3712]{1,0:T(8,128)(2,1)S(1)}, bf16[128,3712]{1,0:T(8,128)(2,1)S(1)}, u32[]{:S(2)}, u32[]{:S(2)}) collective-permute-start(bf16[128,3712]{1,0:T(8,128)(2,1)S(1)} %constant_dynamic-update-slice_fusion.refs_0_.refs_13_), channel_id=1, source_target_pairs={{0,4},{1,5},{2,6},{3,7},{4,8},{5,9},{6,10},{7,11},{8,12},{9,13},{1... | collective-permute-start | bytes 2850824 | tf_op jit(solution)/shard_map/ppermute | solution.py:53
  24.6 14.0 %collective-permute-start.5 = (bf16[128,3712]{1,0:T(8,128)(2,1)S(1)}, bf16[128,3712]{1,0:T(8,128)(2,1)S(1)}, u32[]{:S(2)}, u32[]{:S(2)}) collective-permute-start(bf16[128,3712]{1,0:T(8,128)(2,1)S(1)} %constant_dynamic-update-slice_fusion.2.refs_1_.refs_14_), channel_id=1, source_target_pairs={{0,12},{1,13},{2,14},{3,15},{4,0},{5,1},{6,2},{7,3},{8,4},{9,5},{1... | collective-permute-start | bytes 2850824 | tf_op jit(solution)/shard_map/ppermute | solution.py:53
  27.3 21.4 %collective-permute-start.7 = (bf16[128,3712]{1,0:T(8,128)(2,1)S(1)}, bf16[128,3712]{1,0:T(8,128)(2,1)S(1)}, u32[]{:S(2)}, u32[]{:S(2)}) collective-permute-start(bf16[128,3712]{1,0:T(8,128)(2,1)S(1)} %constant_dynamic-update-slice_fusion.refs_0_.refs_13_), channel_id=1, source_target_pairs={{0,12},{1,13},{2,14},{3,15},{4,0},{5,1},{6,2},{7,3},{8,4},{9,5},{1... | collective-permute-start | bytes 2850824 | tf_op jit(solution)/shard_map/ppermute | solution.py:53
  28.9 19.9 %collective-permute-start.8 = (bf16[128,3712]{1,0:T(8,128)(2,1)S(1)}, bf16[128,3712]{1,0:T(8,128)(2,1)S(1)}, u32[]{:S(2)}, u32[]{:S(2)}) collective-permute-start(bf16[128,3712]{1,0:T(8,128)(2,1)S(1)} %constant_dynamic-update-slice_fusion.2.refs_1_.refs_14_), channel_id=1, source_target_pairs={{0,4},{1,5},{2,6},{3,7},{4,8},{5,9},{6,10},{7,11},{8,12},{9,13},{1... | collective-permute-start | bytes 2850824 | tf_op jit(solution)/shard_map/ppermute | solution.py:53
  35.6 13.7 %collective-permute-start.9 = (bf16[128,3712]{1,0:T(8,128)(2,1)S(1)}, bf16[128,3712]{1,0:T(8,128)(2,1)S(1)}, u32[]{:S(2)}, u32[]{:S(2)}) collective-permute-start(bf16[128,3712]{1,0:T(8,128)(2,1)S(1)} %constant_dynamic-update-slice_fusion.refs_0_.refs_13_), channel_id=1, source_target_pairs={{0,16},{1,17},{2,18},{3,19},{4,20},{5,21},{6,22},{7,23},{8,24},{9,... | collective-permute-start | bytes 2850824 | tf_op jit(solution)/shard_map/ppermute | solution.py:53
  38.6 10.8 %collective-permute-start.10 = (bf16[128,3712]{1,0:T(8,128)(2,1)S(1)}, bf16[128,3712]{1,0:T(8,128)(2,1)S(1)}, u32[]{:S(2)}, u32[]{:S(2)}) collective-permute-start(bf16[128,3712]{1,0:T(8,128)(2,1)S(1)} %constant_dynamic-update-slice_fusion.2.refs_1_.refs_14_), channel_id=1, source_target_pairs={{0,16},{1,17},{2,18},{3,19},{4,20},{5,21},{6,22},{7,23},{8,24},{9,... | collective-permute-start | bytes 2850824 | tf_op jit(solution)/shard_map/ppermute | solution.py:53
  49.3 8.4 %collective-permute-start.13 = (bf16[128,3712]{1,0:T(8,128)(2,1)S(1)}, bf16[128,3712]{1,0:T(8,128)(2,1)S(1)}, u32[]{:S(2)}, u32[]{:S(2)}) collective-permute-start(bf16[128,3712]{1,0:T(8,128)(2,1)S(1)} %collective-permute-done.1.refs_4_.refs_17_), channel_id=1, source_target_pairs={{0,16},{1,17},{2,18},{3,19},{4,20},{5,21},{6,22},{7,23},{8,24},{9,... | collective-permute-start | bytes 2850824 | tf_op jit(solution)/shard_map/ppermute | solution.py:53
  49.4 9.3 %collective-permute-start.14 = (bf16[128,3712]{1,0:T(8,128)(2,1)S(1)}, bf16[128,3712]{1,0:T(8,128)(2,1)}, u32[]{:S(2)}, u32[]{:S(2)}) collective-permute-start(bf16[128,3712]{1,0:T(8,128)(2,1)S(1)} %collective-permute-done.8.refs_5_.refs_18_), channel_id=1, source_target_pairs={{0,16},{1,17},{2,18},{3,19},{4,20},{5,21},{6,22},{7,23},{8,24},{9,... | collective-permute-start | bytes 2850824 | tf_op jit(solution)/shard_map/ppermute | solution.py:53
  51.3 19.2 %collective-permute-start.2 = (bf16[128,3712]{1,0:T(8,128)(2,1)S(1)}, bf16[128,3712]{1,0:T(8,128)(2,1)}, u32[]{:S(2)}, u32[]{:S(2)}) collective-permute-start(bf16[128,3712]{1,0:T(8,128)(2,1)S(1)} %collective-permute-done.1.refs_4_.refs_17_), channel_id=1, source_target_pairs={{0,4},{1,5},{2,6},{3,7},{4,8},{5,9},{6,10},{7,11},{8,12},{9,13},{1... | collective-permute-start | bytes 2850824 | tf_op jit(solution)/shard_map/ppermute | solution.py:53
  54.0 16.5 %collective-permute-start.6 = (bf16[128,3712]{1,0:T(8,128)(2,1)S(1)}, bf16[128,3712]{1,0:T(8,128)(2,1)}, u32[]{:S(2)}, u32[]{:S(2)}) collective-permute-start(bf16[128,3712]{1,0:T(8,128)(2,1)S(1)} %collective-permute-done.5.refs_3_.refs_16_), channel_id=1, source_target_pairs={{0,12},{1,13},{2,14},{3,15},{4,0},{5,1},{6,2},{7,3},{8,4},{9,5},{1... | collective-permute-start | bytes 2850824 | tf_op jit(solution)/shard_map/ppermute | solution.py:53
  98.0 15.0 %collective-permute-start.19 = (bf16[128,3712]{1,0:T(8,128)(2,1)S(1)}, bf16[128,3712]{1,0:T(8,128)(2,1)S(1)}, u32[]{:S(2)}, u32[]{:S(2)}) collective-permute-start(bf16[128,3712]{1,0:T(8,128)(2,1)S(1)} %get-tuple-element.54), channel_id=1, source_target_pairs={{0,4},{1,5},{2,6},{3,7},{4,8},{5,9},{6,10},{7,11},{8,12},{9,13},{1... | collective-permute-start | bytes 2850824 | tf_op jit(solution)/shard_map/ppermute | solution.py:53
  98.0 16.2 %collective-permute-start.21 = (bf16[128,3712]{1,0:T(8,128)(2,1)S(1)}, bf16[128,3712]{1,0:T(8,128)(2,1)S(1)}, u32[]{:S(2)}, u32[]{:S(2)}) collective-permute-start(bf16[128,3712]{1,0:T(8,128)(2,1)S(1)} %get-tuple-element.56), channel_id=1, source_target_pairs={{0,12},{1,13},{2,14},{3,15},{4,0},{5,1},{6,2},{7,3},{8,4},{9,5},{1... | collective-permute-start | bytes 2850824 | tf_op jit(solution)/shard_map/ppermute | solution.py:53
  114.2 24.2 %collective-permute-start.20 = (bf16[128,3712]{1,0:T(8,128)(2,1)}, bf16[128,3712]{1,0:T(8,128)(2,1)}, u32[]{:S(2)}, u32[]{:S(2)}) collective-permute-start(bf16[128,3712]{1,0:T(8,128)(2,1)} %add_convert_fusion.1), channel_id=1, source_target_pairs={{0,4},{1,5},{2,6},{3,7},{4,8},{5,9},{6,10},{7,11},{8,12},{9,13},{1... | collective-permute-start | bytes 2850824 | tf_op jit(solution)/shard_map/ppermute | solution.py:53
  115.4 23.0 %collective-permute-start.22 = (bf16[128,3712]{1,0:T(8,128)(2,1)}, bf16[128,3712]{1,0:T(8,128)(2,1)}, u32[]{:S(2)}, u32[]{:S(2)}) collective-permute-start(bf16[128,3712]{1,0:T(8,128)(2,1)} %add_convert_fusion), channel_id=1, source_target_pairs={{0,12},{1,13},{2,14},{3,15},{4,0},{5,1},{6,2},{7,3},{8,4},{9,5},{1... | collective-permute-start | bytes 2850824 | tf_op jit(solution)/shard_map/ppermute | solution.py:53
  118.6 21.1 %collective-permute-start.25 = (bf16[128,3712]{1,0:T(8,128)(2,1)}, bf16[128,3712]{1,0:T(8,128)(2,1)}, u32[]{:S(2)}, u32[]{:S(2)}) collective-permute-start(bf16[128,3712]{1,0:T(8,128)(2,1)} %get-tuple-element.68), channel_id=1, source_target_pairs={{0,4},{1,5},{2,6},{3,7},{4,8},{5,9},{6,10},{7,11},{8,12},{9,13},{1... | collective-permute-start | bytes 2850824 | tf_op jit(solution)/shard_map/ppermute | solution.py:53
  118.7 24.7 %collective-permute-start.23 = (bf16[128,3712]{1,0:T(8,128)(2,1)}, bf16[128,3712]{1,0:T(8,128)(2,1)}, u32[]{:S(2)}, u32[]{:S(2)}) collective-permute-start(bf16[128,3712]{1,0:T(8,128)(2,1)} %copy-done.12), channel_id=1, source_target_pairs={{0,12},{1,13},{2,14},{3,15},{4,0},{5,1},{6,2},{7,3},{8,4},{9,5},{1... | collective-permute-start | bytes 2850824 | tf_op jit(solution)/shard_map/ppermute | solution.py:53
  142.3 10.5 %collective-permute-start.27 = (bf16[64,3712]{1,0:T(8,128)(2,1)}, bf16[64,3712]{1,0:T(8,128)(2,1)S(1)}, u32[]{:S(2)}, u32[]{:S(2)}) collective-permute-start(bf16[64,3712]{1,0:T(8,128)(2,1)} %get-tuple-element.87), channel_id=1, source_target_pairs={{0,2},{1,3},{2,0},{3,1},{4,6},{5,7},{6,4},{7,5},{8,10},{9,11},{10,... | collective-permute-start | bytes 1425416 | tf_op jit(solution)/shard_map/ppermute | solution.py:53
  142.6 12.9 %collective-permute-start.26 = (bf16[64,3712]{1,0:T(8,128)(2,1)S(1)}, bf16[64,3712]{1,0:T(8,128)(2,1)S(1)}, u32[]{:S(2)}, u32[]{:S(2)}) collective-permute-start(bf16[64,3712]{1,0:T(8,128)(2,1)S(1)} %get-tuple-element.86), channel_id=1, source_target_pairs={{0,3},{1,0},{2,1},{3,2},{4,7},{5,4},{6,5},{7,6},{8,11},{9,8},{10,9... | collective-permute-start | bytes 1425416 | tf_op jit(solution)/shard_map/ppermute | solution.py:53
  144.7 13.0 %collective-permute-start.24 = (bf16[64,3712]{1,0:T(8,128)(2,1)S(1)}, bf16[64,3712]{1,0:T(8,128)(2,1)S(1)}, u32[]{:S(2)}, u32[]{:S(2)}) collective-permute-start(bf16[64,3712]{1,0:T(8,128)(2,1)S(1)} %add_convert_fusion.5), channel_id=1, source_target_pairs={{0,1},{1,2},{2,3},{3,0},{4,5},{5,6},{6,7},{7,4},{8,9},{9,10},{10,1... | collective-permute-start | bytes 1425416 | tf_op jit(solution)/shard_map/ppermute | solution.py:53
  159.4 8.1 %collective-permute-start.30 = (bf16[64,1024]{1,0:T(8,128)(2,1)S(1)}, bf16[64,1024]{1,0:T(8,128)(2,1)S(1)}, u32[]{:S(2)}, u32[]{:S(2)}) collective-permute-start(bf16[64,1024]{1,0:T(8,128)(2,1)S(1)} %get-tuple-element.96), channel_id=1, source_target_pairs={{0,64},{1,65},{2,66},{3,67},{4,68},{5,69},{6,70},{7,71},{8,72},{9,... | collective-permute-start | bytes 393224 | tf_op jit(solution)/shard_map/ppermute | solution.py:53
  (33 other events, 371.3 us)

commit v7 on v6

--- a/solution.py
+++ b/solution.py
@@ -153,6 +153,24 @@
     multiply(sums, other, theirs, NEAR_OTHER, True)
 
 
+def sums_kernel(numbers, blocks, swapped, has_start, with_gains, sel, *refs):
+    count = len(numbers)
+    rows, weights, refs = dict(zip(numbers, refs)), refs[count : count + 3], refs[count + 3 :]
+    start, refs = (refs[:3], refs[3:]) if has_start else (None, refs)
+    if with_gains:
+        extra, held, refs = refs[:8], refs[8], refs[9:]
+    sums = refs[:3]
+
+    @pl.when(pl.program_id(0) == 0)
+    def _():
+        for at, ref in enumerate(sums):
+            ref[...] = start[at][...] if has_start else jnp.zeros_like(ref)
+        if with_gains:
+            line_weights(extra, held, sel, refs[3])
+
+    multiply(sums, rows, weights, blocks, swapped)
+
+
 def line_weights(extra, held, sel, gains):
     rows = rows_of(extra, ALL, False)
     picked = jnp.dot(rows, held[...], preferred_element_type=F32)
@@ -177,19 +195,16 @@
     return high, middle, value - high - middle
 
 
-def far_kernel(sel, *refs):
-    own, other = dict(zip((6, 7), refs)), dict(zip((6, 7), refs[2:]))
-    mine, theirs, start, extra, held = refs[4:7], refs[7:10], refs[10:13], refs[13:21], refs[21]
-    acts, acts_grad = refs[22:24]
-    sums, gains = refs[24:27], refs[27]
+def last_kernel(sel, *refs):
+    other, theirs, start, gains = dict(zip((6, 7), refs)), refs[2:5], refs[5:8], refs[8]
+    acts, acts_grad = refs[9:11]
+    sums = refs[11:14]
 
     @pl.when(pl.program_id(0) == 0)
     def _():
         for ref, before in zip(sums, start):
             ref[...] = before[...]
-        line_weights(extra, held, sel, gains)
-
-    multiply(sums, own, mine, FAR_OWN, False)
+
     multiply(sums, other, theirs, FAR_OTHER, True)
 
     @pl.when(pl.program_id(0) == STEPS - 1)
@@ -352,27 +367,45 @@
     )(sel, *own, *other, *weights, *weights)
 
 
-def activations(sel, own, other, weights, sums, held):
+def add_sums(name, numbers, blocks, swapped, sel, rows, weights, start=(), gains=()):
     extra = pl.BlockSpec((128, 128), lambda k, sel: (0, STEPS * WIDTH // 128))
-    return pl.pallas_call(
-        far_kernel,
+    shapes = [shape((512, 256), F32)] * 3 + [shape((512, 128), F32)] * bool(gains)
+    return pl.pallas_call(
+        functools.partial(sums_kernel, numbers, blocks, swapped, bool(start), bool(gains)),
         grid_spec=pltpu.PrefetchScalarGridSpec(
             num_scalar_prefetch=1,
             grid=(STEPS,),
-            in_specs=row_specs(own[6:] + other, WIDTH)
-            + weight_specs(WIDTH, 0)
+            in_specs=row_specs(rows, WIDTH)
+            + weight_specs(WIDTH, int(swapped))
+            + [whole((512, 256))] * len(start)
+            + ([extra] * 8 + [whole((128, 128))] if gains else []),
+            out_specs=[whole(s.shape) for s in shapes],
+        ),
+        out_shape=shapes,
+        compiler_params=params(56),
+        cost_estimate=cost(0, 0.1),
+        name=name,
+    )(sel, *rows, *weights, *start, *gains)
+
+
+def activations(sel, other, weights, sums, gains):
+    return pl.pallas_call(
+        last_kernel,
+        grid_spec=pltpu.PrefetchScalarGridSpec(
+            num_scalar_prefetch=1,
+            grid=(STEPS,),
+            in_specs=row_specs(other, WIDTH)
             + weight_specs(WIDTH, 1)
             + [whole((512, 256))] * 3
-            + [extra] * 8
-            + [whole((128, 128))],
+            + [whole((512, 128))],
             out_specs=[whole((512, 896)), whole((512, 768))],
-            scratch_shapes=[pltpu.VMEM((512, 256), F32)] * 3 + [pltpu.VMEM((512, 128), F32)],
+            scratch_shapes=[pltpu.VMEM((512, 256), F32)] * 3,
         ),
         out_shape=[shape((512, 896)), shape((512, 768))],
         compiler_params=params(56),
-        cost_estimate=cost(4 * 128 * 768 * WIDTH * STEPS, 15),
+        cost_estimate=cost(2 * 128 * 768 * WIDTH * STEPS, 10),
         name="activations",
-    )(sel, *own[6:], *other, *weights, *weights, *sums, *own, held)
+    )(sel, *other, *weights, *sums, gains)
 
 
 def results(pieces, sel, acts, acts_other, weights, wall, half):
@@ -462,7 +495,10 @@
     experts = jnp.tile(jnp.arange(24, dtype=jnp.int32), 3)
     held = experts[:, None] == slot_expert[None, :]
     held = jnp.pad(held.astype(F32), ((0, 128 - 72), (0, 128 - slots))).astype(BF)
-    acts, acts_grad = activations(sel, rows, far_other, weights, sums, held)
+    *sums, gains = add_sums(
+        "far_own", (6, 7), FAR_OWN, False, sel, far_rows, weights, sums, (*rows, held)
+    )
+    acts, acts_grad = activations(sel, far_other, weights, sums, gains)
     acts_other = send(acts, other_core())
 
     far_a, far_b = results(((6,), (7,)), sel, acts, acts_other, weights, wall, half)

time: 173 us -> 176 us (1.017)
  Pallas kernels: 62.6 us -> 67.9 us
  waiting for transfers between devices: 52.8 us -> 49.9 us
    pallas_call x1 -> x2, Pallas kernels: 11.3 us -> 16.6 us  [the longest x1 8.45 us: activations(): pl.pallas_call(last_kernel, grid_spec=pltpu.PrefetchScalarGridSpec(num_sc...]
    ppermute x31, waiting for transfers between devices: 52.8 us -> 49.9 us  [send(): return lax.ppermute(value, AXES, pairs)]
    unnamed x57 -> x59, local copies, waits for them, and re-layouts: 5.85 us -> 7.11 us
  transfers between devices with their start and end apart: 31 -> 31, of which waited for: 18 -> 16; matrix products, arithmetic and copies ran while one was open for 5% -> 4% of each run, Pallas kernels for 32% -> 34%
where the time goes in v7:
time: 176 us
  Pallas kernels  67.9 us (39%)
  waiting for transfers between devices  49.9 us (28%)
  starting transfers between devices  37 us (21%)
  other arithmetic  11.6 us (7%)
  local copies, waits for them, and re-layouts  8.07 us (5%)
    ppermute x31, waiting for transfers between devices, send(): return lax.ppermute(value, AXES, pairs)  49.9 us
    ppermute x31, starting transfers between devices, send(): return lax.ppermute(value, AXES, pairs)  37 us
    pallas_call x2, Pallas kernels, weight_grads(): pl.pallas_call(functools.partial(grads_kernel, swapped), grid_spec=pltpu....  16.4 us
    pallas_call x2, Pallas kernels, results(): pl.pallas_call(functools.partial(results_kernel, pieces), in_specs=[SM] +...  14.3 us
    pallas_call x1, Pallas kernels, near_sums(): pl.pallas_call(near_kernel, grid_spec=pltpu.PrefetchScalarGridSpec(num_sc...  11.7 us
    pallas_call x1, Pallas kernels, activations(): pl.pallas_call(last_kernel, grid_spec=pltpu.PrefetchScalarGridSpec(num_sc...  8.45 us
    pallas_call x1, Pallas kernels, add_sums(): pl.pallas_call(functools.partial(sums_kernel, numbers, blocks, swapped, b...  8.18 us
    convert_element_type x5, other arithmetic, add(): return total.astype(BF)  7.88 us
  transfers between devices with their start and end apart: 31, of which 16 were waited for; matrix products, arithmetic and copies ran while one was open for 4% of the time, Pallas kernels for 34%

profile of v7, /device:TPU:0, one launch (start us, length us, event | category | flops | bytes accessed | tf_op | source)
XLA Modules:
  0.0 175.6 jit_solution(11590560974571989201)
XLA Ops:
  6.1 2.9 %collective-permute-start = (bf16[64,3712]{1,0:T(8,128)(2,1)}, bf16[64,3712]{1,0:T(8,128)(2,1)S(1)}, u32[]{:S(2)}, u32[]{:S(2)}) collective-permute-start(bf16[64,3712]{1,0:T(8,128)(2,1)} %pack.1), channel_id=1, source_target_pairs={{0,3},{1,0},{2,1},{3,2},{4,7},{5,4},{6,5},{7,6},{8,11},{9,8},{10,9... | collective-permute-start | bytes 1425416 | tf_op jit(solution)/shard_map/ppermute | solution.py:53
  11.3 6.3 %pack_weights.1 = bf16[4,42,128,128]{3,2,1,0:T(8,128)(2,1)} custom-call(s32[4]{0:T(128)} %pad_add_fusion.sel, bf16[2,4,2,896,128]{4,3,2,1,0:T(8,128)(2,1)} %bitcast.8, bf16[2,4,2,896,128]{4,3,2,1,0:T(8,128)(2,1)} %bitcast.15, bf16[2,128,7168]{2,1,0:T(8,128)(2,1)} %wd.5), custom_call_target="tpu_custom_call" | custom-call | bytes 11534336 | tf_op jit(solution)/shard_map/pack_weights/pallas_call | solution.py:326
  17.6 3.0 %collective-permute-done = bf16[64,3712]{1,0:T(8,128)(2,1)S(1)} collective-permute-done((bf16[64,3712]{1,0:T(8,128)(2,1)}, bf16[64,3712]{1,0:T(8,128)(2,1)S(1)}, u32[]{:S(2)}, u32[]{:S(2)}) %collective-permute-start) | collective-permute-done | bytes 475168 | tf_op jit(solution)/shard_map/ppermute | solution.py:53
  24.6 2.7 %collective-permute-start.5 = (bf16[128,3712]{1,0:T(8,128)(2,1)S(1)}, bf16[128,3712]{1,0:T(8,128)(2,1)S(1)}, u32[]{:S(2)}, u32[]{:S(2)}) collective-permute-start(bf16[128,3712]{1,0:T(8,128)(2,1)S(1)} %constant_dynamic-update-slice_fusion.2.refs_1_.refs_9_), channel_id=1, source_target_pairs={{0,12},{1,13},{2,14},{3,15},{4,0},{5,1},{6,2},{7,3},{8,4},{9,5},{1... | collective-permute-start | bytes 2850824 | tf_op jit(solution)/shard_map/ppermute | solution.py:53
  29.4 6.3 %collective-permute-done.1.refs_4_.refs_12_ = bf16[128,3712]{1,0:T(8,128)(2,1)S(1)} collective-permute-done((bf16[128,3712]{1,0:T(8,128)(2,1)S(1)}, bf16[128,3712]{1,0:T(8,128)(2,1)S(1)}, u32[]{:S(2)}, u32[]{:S(2)}) %collective-permute-start.1) | collective-permute-done | bytes 950304 | tf_op jit(solution)/shard_map/ppermute | solution.py:53
  35.7 3.0 %collective-permute-done.5.refs_3_.refs_11_ = bf16[128,3712]{1,0:T(8,128)(2,1)S(1)} collective-permute-done((bf16[128,3712]{1,0:T(8,128)(2,1)S(1)}, bf16[128,3712]{1,0:T(8,128)(2,1)S(1)}, u32[]{:S(2)}, u32[]{:S(2)}) %collective-permute-start.5) | collective-permute-done | bytes 950304 | tf_op jit(solution)/shard_map/ppermute | solution.py:53
  38.6 10.2 %collective-permute-done.7.refs_2_.refs_10_ = bf16[128,3712]{1,0:T(8,128)(2,1)S(1)} collective-permute-done((bf16[128,3712]{1,0:T(8,128)(2,1)S(1)}, bf16[128,3712]{1,0:T(8,128)(2,1)S(1)}, u32[]{:S(2)}, u32[]{:S(2)}) %collective-permute-start.7) | collective-permute-done | bytes 950304 | tf_op jit(solution)/shard_map/ppermute | solution.py:53
  54.1 3.7 %collective-permute-start.6 = (bf16[128,3712]{1,0:T(8,128)(2,1)S(1)}, bf16[128,3712]{1,0:T(8,128)(2,1)}, u32[]{:S(2)}, u32[]{:S(2)}) collective-permute-start(bf16[128,3712]{1,0:T(8,128)(2,1)S(1)} %collective-permute-done.5.refs_3_.refs_11_), channel_id=1, source_target_pairs={{0,12},{1,13},{2,14},{3,15},{4,0},{5,1},{6,2},{7,3},{8,4},{9,5},{1... | collective-permute-start | bytes 2850824 | tf_op jit(solution)/shard_map/ppermute | solution.py:53
  58.8 11.7 %near_sums.1 = (f32[512,256]{1,0:T(8,128)}, f32[512,256]{1,0:T(8,128)}, f32[512,256]{1,0:T(8,128)}) custom-call(s32[4]{0:T(128)} %pad_add_fusion.sel, bf16[128,3712]{1,0:T(8,128)(2,1)} %copy-done.3, bf16[128,3712]{1,0:T(8,128)(2,1)} %copy-done.13, bf16[128,3712]{1,0:T(8,128)(2,1)} %copy-done.16, bf16[128,3712]{1,0:T(8,128)(2,1)} %copy-done.15, ...), custom_call_target="tpu_custom_call" | custom-call | bytes 104857 | tf_op jit(solution)/shard_map/near_sums/pallas_call | solution.py:355
  71.9 8.2 %far_own.1 = (f32[512,256]{1,0:T(8,128)}, f32[512,256]{1,0:T(8,128)}, f32[512,256]{1,0:T(8,128)}, f32[512,128]{1,0:T(8,128)}) custom-call(s32[4]{0:T(128)} %pad_add_fusion.sel, bf16[128,3712]{1,0:T(8,128)(2,1)} %collective-permute-done.2.refs_0_.refs_14_.refs_6_, bf16[128,3712]{1,0:T(8,128)(2,1)} %collective-permute-done.6.refs_1_.refs_15_.refs_7_, ...), custom_call_target="tpu_custom_call" | custom-call | bytes 104857 | tf_op jit(solution)/shard_map/far_own/pallas_call | solution.py:373
  81.4 8.5 %activations.1 = (bf16[512,896]{1,0:T(8,128)(2,1)}, bf16[512,768]{1,0:T(8,128)(2,1)}) custom-call(s32[4]{0:T(128)} %pad_add_fusion.sel, bf16[128,3712]{1,0:T(8,128)(2,1)} %copy-done.22, bf16[128,3712]{1,0:T(8,128)(2,1)} %copy-done.23, bf16[2,4,2,896,128]{4,3,2,1,0:T(8,128)(2,1)} %bitcast.12, bf16[2,4,2,896,128]{4,3,2,1,0:T(8,128)(2,1)} %bitcast.19, ...), custom_call_target="tpu_custom_call" | custom-call | flops 704643072 | bytes 10485760 | tf_op jit(solution)/shard_map/activations/pallas_call | solution.py:392
  90.0 2.6 %collective-permute-done.17.acts_other = bf16[512,896]{1,0:T(8,128)(2,1)S(1)} collective-permute-done((bf16[512,896]{1,0:T(8,128)(2,1)}, bf16[512,896]{1,0:T(8,128)(2,1)S(1)}, u32[]{:S(2)}, u32[]{:S(2)}) %collective-permute-start.17) | collective-permute-done | bytes 917536 | tf_op jit(solution)/shard_map/ppermute | solution.py:53
  95.8 5.6 %results.3 = (bf16[128,3712]{1,0:T(8,128)(2,1)S(1)}, bf16[128,3712]{1,0:T(8,128)(2,1)S(1)}) custom-call(s32[4]{0:T(128)S(1)} %copy-done.11, bf16[512,896]{1,0:T(8,128)(2,1)S(1)} %copy-done.7, bf16[512,896]{1,0:T(8,128)(2,1)S(1)} %collective-permute-done.17.acts_other, bf16[2,4,2,896,128]{4,3,2,1,0:T(8,128)(2,1)S(1)} %bitcast.13, ...), custom_call_target="tpu_custom_call" | custom-call | flops 1409286144 | bytes 12582912 | tf_op jit(solution)/shard_map/results/pallas_call | solution.py:412
  101.5 3.2 %collective-permute-start.21 = (bf16[128,3712]{1,0:T(8,128)(2,1)S(1)}, bf16[128,3712]{1,0:T(8,128)(2,1)S(1)}, u32[]{:S(2)}, u32[]{:S(2)}) collective-permute-start(bf16[128,3712]{1,0:T(8,128)(2,1)S(1)} %get-tuple-element.64), channel_id=1, source_target_pairs={{0,12},{1,13},{2,14},{3,15},{4,0},{5,1},{6,2},{7,3},{8,4},{9,5},{1... | collective-permute-start | bytes 2850824 | tf_op jit(solution)/shard_map/ppermute | solution.py:53
  104.7 8.7 %results.2 = (bf16[128,3712]{1,0:T(8,128)(2,1)S(1)}, bf16[128,3712]{1,0:T(8,128)(2,1)S(1)}, bf16[128,3712]{1,0:T(8,128)(2,1)S(1)}, bf16[128,3712]{1,0:T(8,128)(2...) custom-call(s32[4]{0:T(128)S(1)} %copy-done.11, bf16[512,896]{1,0:T(8,128)(2,1)S(1)} %copy-done.7, ...), custom_call_target="tpu_custom_call" | custom-call | flops 4227858432 | bytes 12582912 | tf_op jit(solution)/shard_map/results/pallas_call | solution.py:412
  113.4 3.0 %collective-permute-done.19 = bf16[128,3712]{1,0:T(8,128)(2,1)S(1)} collective-permute-done((bf16[128,3712]{1,0:T(8,128)(2,1)S(1)}, bf16[128,3712]{1,0:T(8,128)(2,1)S(1)}, u32[]{:S(2)}, u32[]{:S(2)}) %collective-permute-start.19) | collective-permute-done | bytes 950304 | tf_op jit(solution)/shard_map/ppermute | solution.py:53
  118.8 3.2 %collective-permute-start.22 = (bf16[128,3712]{1,0:T(8,128)(2,1)}, bf16[128,3712]{1,0:T(8,128)(2,1)}, u32[]{:S(2)}, u32[]{:S(2)}) collective-permute-start(bf16[128,3712]{1,0:T(8,128)(2,1)} %add_convert_fusion), channel_id=1, source_target_pairs={{0,12},{1,13},{2,14},{3,15},{4,0},{5,1},{6,2},{7,3},{8,4},{9,5},{1... | collective-permute-start | bytes 2850824 | tf_op jit(solution)/shard_map/ppermute | solution.py:53
  122.2 3.2 %collective-permute-start.23 = (bf16[128,3712]{1,0:T(8,128)(2,1)}, bf16[128,3712]{1,0:T(8,128)(2,1)}, u32[]{:S(2)}, u32[]{:S(2)}) collective-permute-start(bf16[128,3712]{1,0:T(8,128)(2,1)} %copy-done.12), channel_id=1, source_target_pairs={{0,12},{1,13},{2,14},{3,15},{4,0},{5,1},{6,2},{7,3},{8,4},{9,5},{1... | collective-permute-start | bytes 2850824 | tf_op jit(solution)/shard_map/ppermute | solution.py:53
  125.4 8.2 %weight_grads.2 = (bf16[2,4,2,896,128]{4,3,2,1,0:T(8,128)(2,1)}, bf16[2,4,2,896,128]{4,3,2,1,0:T(8,128)(2,1)}, bf16[2,128,7168]{2,1,0:T(8,128)(2,1)}) custom-call(s32[4]{0:T(128)S(1)} %copy-done.11, bf16[128,3712]{1,0:T(8,128)(2,1)S(1)} %copy-done.4, bf16[128,3712]{1,0:T(8,128)(2,1)} %copy-done.13, bf16[128,3712]{1,0:T(8,128)(2,1)} %copy-done.16, ...), custom_call_target="tpu_custom_call" | custom-call | flops 2818572288 | bytes 14680064 | tf_op jit(solution)/shard_map/weight_grads/pallas_call | solution.py:429
  133.6 8.2 %weight_grads.3 = (bf16[2,4,2,896,128]{4,3,2,1,0:T(8,128)(2,1)}, bf16[2,4,2,896,128]{4,3,2,1,0:T(8,128)(2,1)}, bf16[2,128,7168]{2,1,0:T(8,128)(2,1)}) custom-call(s32[4]{0:T(128)S(1)} %copy-done.11, bf16[128,3712]{1,0:T(8,128)(2,1)S(1)} %copy-done.6, bf16[128,3712]{1,0:T(8,128)(2,1)} %copy-done.18, ...), custom_call_target="tpu_custom_call", output_to_operand_aliasing={{0}: (10, {}), {1}: (11, {}), {2}: (12, {})} | custom-call | flops 2818572288 | bytes 14680064 | tf_op jit(solution)/shard_map/weight_grads/pallas_call | solution.py:429
  143.1 2.6 %add_convert_fusion.4 = (bf16[64,3712]{1,0:T(8,128)(2,1)S(1)}, bf16[64,3712]{1,0:T(8,128)(2,1)}) fusion(bf16[128,3712]{1,0:T(8,128)(2,1)} %collective-permute-done.25, bf16[128,3712]{1,0:T(8,128)(2,1)} %collective-permute-done.22, bf16[128,3712]{1,0:T(8,128)(2,1)S(1)} %copy-done.9), kind=kLoop, calls=%fused_computation.4 | loop fusion | flops 2850816 | bytes 3801088 | tf_op jit(solution)/shard_map/convert_element_type | solution.py:457
  150.0 6.3 %collective-permute-done.27 = bf16[64,3712]{1,0:T(8,128)(2,1)S(1)} collective-permute-done((bf16[64,3712]{1,0:T(8,128)(2,1)}, bf16[64,3712]{1,0:T(8,128)(2,1)S(1)}, u32[]{:S(2)}, u32[]{:S(2)}) %collective-permute-start.27) | collective-permute-done | bytes 475168 | tf_op jit(solution)/shard_map/ppermute | solution.py:53
  156.2 2.7 %collective-permute-done.26 = bf16[64,3712]{1,0:T(8,128)(2,1)S(1)} collective-permute-done((bf16[64,3712]{1,0:T(8,128)(2,1)S(1)}, bf16[64,3712]{1,0:T(8,128)(2,1)S(1)}, u32[]{:S(2)}, u32[]{:S(2)}) %collective-permute-start.26) | collective-permute-done | bytes 475168 | tf_op jit(solution)/shard_map/ppermute | solution.py:53
  162.9 4.0 %collective-permute-start.30 = (bf16[64,1024]{1,0:T(8,128)(2,1)S(1)}, bf16[64,1024]{1,0:T(8,128)(2,1)S(1)}, u32[]{:S(2)}, u32[]{:S(2)}) collective-permute-start(bf16[64,1024]{1,0:T(8,128)(2,1)S(1)} %get-tuple-element.104), channel_id=1, source_target_pairs={{0,64},{1,65},{2,66},{3,67},{4,68},{5,69},{6,70},{7,71},{8,72},{9,... | collective-permute-start | bytes 393224 | tf_op jit(solution)/shard_map/ppermute | solution.py:53
  (136 shorter events, 46.6 us)
Async XLA Ops:
  6.1 14.5 %collective-permute-start = (bf16[64,3712]{1,0:T(8,128)(2,1)}, bf16[64,3712]{1,0:T(8,128)(2,1)S(1)}, u32[]{:S(2)}, u32[]{:S(2)}) collective-permute-start(bf16[64,3712]{1,0:T(8,128)(2,1)} %pack.1), channel_id=1, source_target_pairs={{0,3},{1,0},{2,1},{3,2},{4,7},{5,4},{6,5},{7,6},{8,11},{9,8},{10,9... | collective-permute-start | bytes 1425416 | tf_op jit(solution)/shard_map/ppermute | solution.py:53
  9.0 15.5 %collective-permute-start.3 = (bf16[64,3712]{1,0:T(8,128)(2,1)}, bf16[64,3712]{1,0:T(8,128)(2,1)S(1)}, u32[]{:S(2)}, u32[]{:S(2)}) collective-permute-start(bf16[64,3712]{1,0:T(8,128)(2,1)} %pack.1), channel_id=1, source_target_pairs={{0,1},{1,2},{2,3},{3,0},{4,5},{5,6},{6,7},{7,4},{8,9},{9,10},{10,1... | collective-permute-start | bytes 1425416 | tf_op jit(solution)/shard_map/ppermute | solution.py:53
  9.0 15.6 %collective-permute-start.4 = (bf16[64,3712]{1,0:T(8,128)(2,1)}, bf16[64,3712]{1,0:T(8,128)(2,1)S(1)}, u32[]{:S(2)}, u32[]{:S(2)}) collective-permute-start(bf16[64,3712]{1,0:T(8,128)(2,1)} %pack.1), channel_id=1, source_target_pairs={{0,2},{1,3},{2,0},{3,1},{4,6},{5,7},{6,4},{7,5},{8,10},{9,11},{10,... | collective-permute-start | bytes 1425416 | tf_op jit(solution)/shard_map/ppermute | solution.py:53
  17.6 75.0 %collective-permute-start.18 = (bf16[4,42,128,128]{3,2,1,0:T(8,128)(2,1)}, bf16[4,42,128,128]{3,2,1,0:T(8,128)(2,1)}, u32[]{:S(2)}, u32[]{:S(2)}) collective-permute-start(bf16[4,42,128,128]{3,2,1,0:T(8,128)(2,1)} %pack_weights.1), channel_id=1, source_target_pairs={{0,16},{1,17},{2,18},{3,19},{4,20},{5,21},{6,22},{7,23},{8,24},{9,... | collective-permute-start | bytes 16515080 | tf_op jit(solution)/shard_map/ppermute | solution.py:53
  20.6 15.0 %collective-permute-start.1 = (bf16[128,3712]{1,0:T(8,128)(2,1)S(1)}, bf16[128,3712]{1,0:T(8,128)(2,1)S(1)}, u32[]{:S(2)}, u32[]{:S(2)}) collective-permute-start(bf16[128,3712]{1,0:T(8,128)(2,1)S(1)} %constant_dynamic-update-slice_fusion.refs_0_.refs_8_), channel_id=1, source_target_pairs={{0,4},{1,5},{2,6},{3,7},{4,8},{5,9},{6,10},{7,11},{8,12},{9,13},{1... | collective-permute-start | bytes 2850824 | tf_op jit(solution)/shard_map/ppermute | solution.py:53
  24.6 14.0 %collective-permute-start.5 = (bf16[128,3712]{1,0:T(8,128)(2,1)S(1)}, bf16[128,3712]{1,0:T(8,128)(2,1)S(1)}, u32[]{:S(2)}, u32[]{:S(2)}) collective-permute-start(bf16[128,3712]{1,0:T(8,128)(2,1)S(1)} %constant_dynamic-update-slice_fusion.2.refs_1_.refs_9_), channel_id=1, source_target_pairs={{0,12},{1,13},{2,14},{3,15},{4,0},{5,1},{6,2},{7,3},{8,4},{9,5},{1... | collective-permute-start | bytes 2850824 | tf_op jit(solution)/shard_map/ppermute | solution.py:53
  27.4 21.4 %collective-permute-start.7 = (bf16[128,3712]{1,0:T(8,128)(2,1)S(1)}, bf16[128,3712]{1,0:T(8,128)(2,1)S(1)}, u32[]{:S(2)}, u32[]{:S(2)}) collective-permute-start(bf16[128,3712]{1,0:T(8,128)(2,1)S(1)} %constant_dynamic-update-slice_fusion.refs_0_.refs_8_), channel_id=1, source_target_pairs={{0,12},{1,13},{2,14},{3,15},{4,0},{5,1},{6,2},{7,3},{8,4},{9,5},{1... | collective-permute-start | bytes 2850824 | tf_op jit(solution)/shard_map/ppermute | solution.py:53
  28.9 19.9 %collective-permute-start.8 = (bf16[128,3712]{1,0:T(8,128)(2,1)S(1)}, bf16[128,3712]{1,0:T(8,128)(2,1)S(1)}, u32[]{:S(2)}, u32[]{:S(2)}) collective-permute-start(bf16[128,3712]{1,0:T(8,128)(2,1)S(1)} %constant_dynamic-update-slice_fusion.2.refs_1_.refs_9_), channel_id=1, source_target_pairs={{0,4},{1,5},{2,6},{3,7},{4,8},{5,9},{6,10},{7,11},{8,12},{9,13},{1... | collective-permute-start | bytes 2850824 | tf_op jit(solution)/shard_map/ppermute | solution.py:53
  35.7 13.7 %collective-permute-start.9 = (bf16[128,3712]{1,0:T(8,128)(2,1)S(1)}, bf16[128,3712]{1,0:T(8,128)(2,1)S(1)}, u32[]{:S(2)}, u32[]{:S(2)}) collective-permute-start(bf16[128,3712]{1,0:T(8,128)(2,1)S(1)} %constant_dynamic-update-slice_fusion.refs_0_.refs_8_), channel_id=1, source_target_pairs={{0,16},{1,17},{2,18},{3,19},{4,20},{5,21},{6,22},{7,23},{8,24},{9,... | collective-permute-start | bytes 2850824 | tf_op jit(solution)/shard_map/ppermute | solution.py:53
  38.6 10.8 %collective-permute-start.10 = (bf16[128,3712]{1,0:T(8,128)(2,1)S(1)}, bf16[128,3712]{1,0:T(8,128)(2,1)S(1)}, u32[]{:S(2)}, u32[]{:S(2)}) collective-permute-start(bf16[128,3712]{1,0:T(8,128)(2,1)S(1)} %constant_dynamic-update-slice_fusion.2.refs_1_.refs_9_), channel_id=1, source_target_pairs={{0,16},{1,17},{2,18},{3,19},{4,20},{5,21},{6,22},{7,23},{8,24},{9,... | collective-permute-start | bytes 2850824 | tf_op jit(solution)/shard_map/ppermute | solution.py:53
  49.4 9.3 %collective-permute-start.14 = (bf16[128,3712]{1,0:T(8,128)(2,1)S(1)}, bf16[128,3712]{1,0:T(8,128)(2,1)}, u32[]{:S(2)}, u32[]{:S(2)}) collective-permute-start(bf16[128,3712]{1,0:T(8,128)(2,1)S(1)} %collective-permute-done.8.refs_5_.refs_13_), channel_id=1, source_target_pairs={{0,16},{1,17},{2,18},{3,19},{4,20},{5,21},{6,22},{7,23},{8,24},{9,... | collective-permute-start | bytes 2850824 | tf_op jit(solution)/shard_map/ppermute | solution.py:53
  51.3 19.2 %collective-permute-start.2 = (bf16[128,3712]{1,0:T(8,128)(2,1)S(1)}, bf16[128,3712]{1,0:T(8,128)(2,1)}, u32[]{:S(2)}, u32[]{:S(2)}) collective-permute-start(bf16[128,3712]{1,0:T(8,128)(2,1)S(1)} %collective-permute-done.1.refs_4_.refs_12_), channel_id=1, source_target_pairs={{0,4},{1,5},{2,6},{3,7},{4,8},{5,9},{6,10},{7,11},{8,12},{9,13},{1... | collective-permute-start | bytes 2850824 | tf_op jit(solution)/shard_map/ppermute | solution.py:53
  54.1 16.5 %collective-permute-start.6 = (bf16[128,3712]{1,0:T(8,128)(2,1)S(1)}, bf16[128,3712]{1,0:T(8,128)(2,1)}, u32[]{:S(2)}, u32[]{:S(2)}) collective-permute-start(bf16[128,3712]{1,0:T(8,128)(2,1)S(1)} %collective-permute-done.5.refs_3_.refs_11_), channel_id=1, source_target_pairs={{0,12},{1,13},{2,14},{3,15},{4,0},{5,1},{6,2},{7,3},{8,4},{9,5},{1... | collective-permute-start | bytes 2850824 | tf_op jit(solution)/shard_map/ppermute | solution.py:53
  70.5 9.6 %collective-permute-start.15 = (bf16[128,3712]{1,0:T(8,128)(2,1)}, bf16[128,3712]{1,0:T(8,128)(2,1)S(1)}, u32[]{:S(2)}, u32[]{:S(2)}) collective-permute-start(bf16[128,3712]{1,0:T(8,128)(2,1)} %collective-permute-done.2.refs_0_.refs_14_.refs_6_), channel_id=1, source_target_pairs={{0,16},{1,17},{2,18},{3,19},{4,20},{5,21},{6,22},{7,23},{8,24},{9,... | collective-permute-start | bytes 2850824 | tf_op jit(solution)/shard_map/ppermute | solution.py:53
  70.6 9.5 %collective-permute-start.16 = (bf16[128,3712]{1,0:T(8,128)(2,1)}, bf16[128,3712]{1,0:T(8,128)(2,1)S(1)}, u32[]{:S(2)}, u32[]{:S(2)}) collective-permute-start(bf16[128,3712]{1,0:T(8,128)(2,1)} %collective-permute-done.6.refs_1_.refs_15_.refs_7_), channel_id=1, source_target_pairs={{0,16},{1,17},{2,18},{3,19},{4,20},{5,21},{6,22},{7,23},{8,24},{9,... | collective-permute-start | bytes 2850824 | tf_op jit(solution)/shard_map/ppermute | solution.py:53
  101.4 15.0 %collective-permute-start.19 = (bf16[128,3712]{1,0:T(8,128)(2,1)S(1)}, bf16[128,3712]{1,0:T(8,128)(2,1)S(1)}, u32[]{:S(2)}, u32[]{:S(2)}) collective-permute-start(bf16[128,3712]{1,0:T(8,128)(2,1)S(1)} %get-tuple-element.62), channel_id=1, source_target_pairs={{0,4},{1,5},{2,6},{3,7},{4,8},{5,9},{6,10},{7,11},{8,12},{9,13},{1... | collective-permute-start | bytes 2850824 | tf_op jit(solution)/shard_map/ppermute | solution.py:53
  101.5 16.2 %collective-permute-start.21 = (bf16[128,3712]{1,0:T(8,128)(2,1)S(1)}, bf16[128,3712]{1,0:T(8,128)(2,1)S(1)}, u32[]{:S(2)}, u32[]{:S(2)}) collective-permute-start(bf16[128,3712]{1,0:T(8,128)(2,1)S(1)} %get-tuple-element.64), channel_id=1, source_target_pairs={{0,12},{1,13},{2,14},{3,15},{4,0},{5,1},{6,2},{7,3},{8,4},{9,5},{1... | collective-permute-start | bytes 2850824 | tf_op jit(solution)/shard_map/ppermute | solution.py:53
  117.7 24.2 %collective-permute-start.20 = (bf16[128,3712]{1,0:T(8,128)(2,1)}, bf16[128,3712]{1,0:T(8,128)(2,1)}, u32[]{:S(2)}, u32[]{:S(2)}) collective-permute-start(bf16[128,3712]{1,0:T(8,128)(2,1)} %add_convert_fusion.1), channel_id=1, source_target_pairs={{0,4},{1,5},{2,6},{3,7},{4,8},{5,9},{6,10},{7,11},{8,12},{9,13},{1... | collective-permute-start | bytes 2850824 | tf_op jit(solution)/shard_map/ppermute | solution.py:53
  118.8 23.0 %collective-permute-start.22 = (bf16[128,3712]{1,0:T(8,128)(2,1)}, bf16[128,3712]{1,0:T(8,128)(2,1)}, u32[]{:S(2)}, u32[]{:S(2)}) collective-permute-start(bf16[128,3712]{1,0:T(8,128)(2,1)} %add_convert_fusion), channel_id=1, source_target_pairs={{0,12},{1,13},{2,14},{3,15},{4,0},{5,1},{6,2},{7,3},{8,4},{9,5},{1... | collective-permute-start | bytes 2850824 | tf_op jit(solution)/shard_map/ppermute | solution.py:53
  122.1 21.0 %collective-permute-start.25 = (bf16[128,3712]{1,0:T(8,128)(2,1)}, bf16[128,3712]{1,0:T(8,128)(2,1)}, u32[]{:S(2)}, u32[]{:S(2)}) collective-permute-start(bf16[128,3712]{1,0:T(8,128)(2,1)} %get-tuple-element.76), channel_id=1, source_target_pairs={{0,4},{1,5},{2,6},{3,7},{4,8},{5,9},{6,10},{7,11},{8,12},{9,13},{1... | collective-permute-start | bytes 2850824 | tf_op jit(solution)/shard_map/ppermute | solution.py:53
  122.2 24.6 %collective-permute-start.23 = (bf16[128,3712]{1,0:T(8,128)(2,1)}, bf16[128,3712]{1,0:T(8,128)(2,1)}, u32[]{:S(2)}, u32[]{:S(2)}) collective-permute-start(bf16[128,3712]{1,0:T(8,128)(2,1)} %copy-done.12), channel_id=1, source_target_pairs={{0,12},{1,13},{2,14},{3,15},{4,0},{5,1},{6,2},{7,3},{8,4},{9,5},{1... | collective-permute-start | bytes 2850824 | tf_op jit(solution)/shard_map/ppermute | solution.py:53
  145.7 10.5 %collective-permute-start.27 = (bf16[64,3712]{1,0:T(8,128)(2,1)}, bf16[64,3712]{1,0:T(8,128)(2,1)S(1)}, u32[]{:S(2)}, u32[]{:S(2)}) collective-permute-start(bf16[64,3712]{1,0:T(8,128)(2,1)} %get-tuple-element.95), channel_id=1, source_target_pairs={{0,2},{1,3},{2,0},{3,1},{4,6},{5,7},{6,4},{7,5},{8,10},{9,11},{10,... | collective-permute-start | bytes 1425416 | tf_op jit(solution)/shard_map/ppermute | solution.py:53
  146.0 12.9 %collective-permute-start.26 = (bf16[64,3712]{1,0:T(8,128)(2,1)S(1)}, bf16[64,3712]{1,0:T(8,128)(2,1)S(1)}, u32[]{:S(2)}, u32[]{:S(2)}) collective-permute-start(bf16[64,3712]{1,0:T(8,128)(2,1)S(1)} %get-tuple-element.94), channel_id=1, source_target_pairs={{0,3},{1,0},{2,1},{3,2},{4,7},{5,4},{6,5},{7,6},{8,11},{9,8},{10,9... | collective-permute-start | bytes 1425416 | tf_op jit(solution)/shard_map/ppermute | solution.py:53
  148.1 13.0 %collective-permute-start.24 = (bf16[64,3712]{1,0:T(8,128)(2,1)S(1)}, bf16[64,3712]{1,0:T(8,128)(2,1)S(1)}, u32[]{:S(2)}, u32[]{:S(2)}) collective-permute-start(bf16[64,3712]{1,0:T(8,128)(2,1)S(1)} %add_convert_fusion.5), channel_id=1, source_target_pairs={{0,1},{1,2},{2,3},{3,0},{4,5},{5,6},{6,7},{7,4},{8,9},{9,10},{10,1... | collective-permute-start | bytes 1425416 | tf_op jit(solution)/shard_map/ppermute | solution.py:53
  (34 other events, 363.0 us)

commit v8 on v6

--- a/solution.py
+++ b/solution.py
@@ -101,8 +101,8 @@
     return first, second, back
 
 
-def pack_kernel(sel, tok, cot, extra, packed, sems):
-    rows, half = extra.shape[0], packed.shape[1] - 128
+def pack_kernel(sel, tok, cot, logits, routes, packed, sems):
+    rows, half = tok.shape[0], packed.shape[1] - 128
     width = half // STEPS
     copies = []
     for k in range(STEPS):
@@ -113,8 +113,16 @@
                 pltpu.make_async_copy(ref.at[:, pl.ds(at, width)], target, sems.at[len(copies)])
             )
             copies[-1].start()
-    packed[:rows, half:] = extra[...]
-    packed[rows:, half:] = jnp.zeros_like(extra)
+    experts = logits.shape[0]
+    high, middle, low = thirds(logits[...])
+    extra = jnp.zeros((rows, 128), F32)
+    for at, part in enumerate((high, middle, low, routes[...].astype(F32))):
+        lane = lax.broadcasted_iota(jnp.int32, (part.shape[0], 128), 1)
+        row = lax.broadcasted_iota(jnp.int32, (part.shape[0], 128), 0)
+        here = jnp.where(lane == row + experts * at, 1.0, 0.0).astype(BF)
+        extra += lax.dot_general(part.astype(BF), here, TN, preferred_element_type=F32)
+    packed[:rows, half:] = extra.astype(BF)
+    packed[rows:, half:] = jnp.zeros((rows, 128), BF)
     for one in copies:
         one.wait()
 
@@ -290,18 +298,18 @@
     return jax.ShapeDtypeStruct(dims, dtype)
 
 
-def pack(sel, tokens, cotangent, extra):
+def pack(sel, tokens, cotangent, logits, routes):
     tok, wide = tokens.shape
     return pl.pallas_call(
         pack_kernel,
-        in_specs=[SM, HB, HB, VM],
+        in_specs=[SM, HB, HB, VM, VM],
         out_specs=VM,
         out_shape=shape((2 * tok, wide // 2 + 128)),
         scratch_shapes=[pltpu.SemaphoreType.DMA((2 * STEPS,))],
         compiler_params=params(56),
         cost_estimate=cost(0, 2),
         name="pack",
-    )(sel, tokens, cotangent, extra)
+    )(sel, tokens, cotangent, logits.T, routes.T)
 
 
 def pack_weights(sel, weights):
@@ -437,14 +445,7 @@
         w_up.reshape(2, STEPS, 2, width, 128),
         w_down,
     )
-    high = lax.reduce_precision(gate_logits, 8, 7)
-    middle = lax.reduce_precision(gate_logits - high, 8, 7)
-    parts = (high, middle, gate_logits - high - middle, route_slot.astype(F32))
-    extra = sum(
-        lax.pad(part, 0.0, ((0, 0, 0), (24 * at, 128 - 24 * at - part.shape[1], 0)))
-        for at, part in enumerate(parts)
-    ).astype(BF)
-    own = pack(sel, tokens, cotangent, extra)
+    own = pack(sel, tokens, cotangent, gate_logits, route_slot)
     own, later = lax.optimization_barrier((own, sel))
     minus, plus, far = send(own, inner(1)), send(own, inner(-1)), send(own, inner(2))
     a, b = joined([own, plus]), joined([minus, far])

time: 173 us -> 171 us (0.988)
    unnamed x57 -> x59, local copies, waits for them, and re-layouts: 5.85 us -> 5.15 us
where the time goes in v8:
time: 171 us; the launch traced here: 170 us
  Pallas kernels  62.6 us (37%)
  waiting for transfers between devices  52.7 us (31%)
  starting transfers between devices  37.3 us (22%)
  other arithmetic  10.2 us (6%)
  local copies, waits for them, and re-layouts  6.03 us (4%)
    ppermute x31, waiting for transfers between devices, send(): return lax.ppermute(value, AXES, pairs)  52.7 us
    ppermute x31, starting transfers between devices, send(): return lax.ppermute(value, AXES, pairs)  37.3 us
    pallas_call x2, Pallas kernels, weight_grads(): pl.pallas_call(functools.partial(grads_kernel, swapped), grid_spec=pltpu....  16.4 us
    pallas_call x2, Pallas kernels, results(): pl.pallas_call(functools.partial(results_kernel, pieces), in_specs=[SM] +...  14.3 us
    pallas_call x1, Pallas kernels, near_sums(): pl.pallas_call(near_kernel, grid_spec=pltpu.PrefetchScalarGridSpec(num_sc...  11.8 us
    pallas_call x1, Pallas kernels, activations(): pl.pallas_call(far_kernel, grid_spec=pltpu.PrefetchScalarGridSpec(num_sca...  11.3 us
    convert_element_type x5, other arithmetic, add(): return total.astype(BF)  7.87 us
    pallas_call x1, Pallas kernels, pack_weights(): pl.pallas_call(pack_weights_kernel, grid_spec=pltpu.PrefetchScalarGridSpe...  6.27 us
  transfers between devices with their start and end apart: 31, of which 18 were waited for; matrix products, arithmetic and copies ran while one was open for 5% of the time, Pallas kernels for 32%

profile of v8, /device:TPU:0, one launch (start us, length us, event | category | flops | bytes accessed | tf_op | source)
XLA Modules:
  0.0 169.9 jit_solution(5841262756291436792)
XLA Ops:
  1.2 2.6 %pack.1 = bf16[64,3712]{1,0:T(8,128)(2,1)} custom-call(s32[4]{0:T(128)} %pad_add_fusion.sel, bf16[32,7168]{1,0:T(8,128)(2,1)} %tok.1, bf16[32,7168]{1,0:T(8,128)(2,1)} %cot.1, f32[24,32]{1,0:T(8,128)} %bitcast.26, s32[8,32]{1,0:T(8,128)} %bitcast.27), custom_call_target="tpu_custom_call" | custom-call | bytes 2097152 | tf_op jit(solution)/shard_map/pack/pallas_call | solution.py:303
  3.8 2.9 %collective-permute-start = (bf16[64,3712]{1,0:T(8,128)(2,1)}, bf16[64,3712]{1,0:T(8,128)(2,1)S(1)}, u32[]{:S(2)}, u32[]{:S(2)}) collective-permute-start(bf16[64,3712]{1,0:T(8,128)(2,1)} %pack.1), channel_id=1, source_target_pairs={{0,3},{1,0},{2,1},{3,2},{4,7},{5,4},{6,5},{7,6},{8,11},{9,8},{10,9... | collective-permute-start | bytes 1425416 | tf_op jit(solution)/shard_map/ppermute | solution.py:53
  9.0 6.3 %pack_weights.1 = bf16[4,42,128,128]{3,2,1,0:T(8,128)(2,1)} custom-call(s32[4]{0:T(128)} %pad_add_fusion.sel, bf16[2,4,2,896,128]{4,3,2,1,0:T(8,128)(2,1)} %bitcast.10, bf16[2,4,2,896,128]{4,3,2,1,0:T(8,128)(2,1)} %bitcast.17, bf16[2,128,7168]{2,1,0:T(8,128)(2,1)} %wd.5), custom_call_target="tpu_custom_call" | custom-call | bytes 11534336 | tf_op jit(solution)/shard_map/pack_weights/pallas_call | solution.py:319
  15.4 3.0 %collective-permute-done = bf16[64,3712]{1,0:T(8,128)(2,1)S(1)} collective-permute-done((bf16[64,3712]{1,0:T(8,128)(2,1)}, bf16[64,3712]{1,0:T(8,128)(2,1)S(1)}, u32[]{:S(2)}, u32[]{:S(2)}) %collective-permute-start) | collective-permute-done | bytes 475168 | tf_op jit(solution)/shard_map/ppermute | solution.py:53
  22.4 2.7 %collective-permute-start.5 = (bf16[128,3712]{1,0:T(8,128)(2,1)S(1)}, bf16[128,3712]{1,0:T(8,128)(2,1)S(1)}, u32[]{:S(2)}, u32[]{:S(2)}) collective-permute-start(bf16[128,3712]{1,0:T(8,128)(2,1)S(1)} %constant_dynamic-update-slice_fusion.2.refs_1_.refs_14_), channel_id=1, source_target_pairs={{0,12},{1,13},{2,14},{3,15},{4,0},{5,1},{6,2},{7,3},{8,4},{9,5},{1... | collective-permute-start | bytes 2850824 | tf_op jit(solution)/shard_map/ppermute | solution.py:53
  27.1 6.3 %collective-permute-done.1.refs_4_.refs_17_ = bf16[128,3712]{1,0:T(8,128)(2,1)S(1)} collective-permute-done((bf16[128,3712]{1,0:T(8,128)(2,1)S(1)}, bf16[128,3712]{1,0:T(8,128)(2,1)S(1)}, u32[]{:S(2)}, u32[]{:S(2)}) %collective-permute-start.1) | collective-permute-done | bytes 950304 | tf_op jit(solution)/shard_map/ppermute | solution.py:53
  33.4 3.0 %collective-permute-done.5.refs_3_.refs_16_ = bf16[128,3712]{1,0:T(8,128)(2,1)S(1)} collective-permute-done((bf16[128,3712]{1,0:T(8,128)(2,1)S(1)}, bf16[128,3712]{1,0:T(8,128)(2,1)S(1)}, u32[]{:S(2)}, u32[]{:S(2)}) %collective-permute-start.5) | collective-permute-done | bytes 950304 | tf_op jit(solution)/shard_map/ppermute | solution.py:53
  36.4 10.2 %collective-permute-done.7.refs_2_.refs_15_ = bf16[128,3712]{1,0:T(8,128)(2,1)S(1)} collective-permute-done((bf16[128,3712]{1,0:T(8,128)(2,1)S(1)}, bf16[128,3712]{1,0:T(8,128)(2,1)S(1)}, u32[]{:S(2)}, u32[]{:S(2)}) %collective-permute-start.7) | collective-permute-done | bytes 950304 | tf_op jit(solution)/shard_map/ppermute | solution.py:53
  51.8 3.7 %collective-permute-start.6 = (bf16[128,3712]{1,0:T(8,128)(2,1)S(1)}, bf16[128,3712]{1,0:T(8,128)(2,1)}, u32[]{:S(2)}, u32[]{:S(2)}) collective-permute-start(bf16[128,3712]{1,0:T(8,128)(2,1)S(1)} %collective-permute-done.5.refs_3_.refs_16_), channel_id=1, source_target_pairs={{0,12},{1,13},{2,14},{3,15},{4,0},{5,1},{6,2},{7,3},{8,4},{9,5},{1... | collective-permute-start | bytes 2850824 | tf_op jit(solution)/shard_map/ppermute | solution.py:53
  56.5 11.8 %near_sums.1 = (f32[512,256]{1,0:T(8,128)}, f32[512,256]{1,0:T(8,128)}, f32[512,256]{1,0:T(8,128)}) custom-call(s32[4]{0:T(128)} %pad_add_fusion.sel, bf16[128,3712]{1,0:T(8,128)(2,1)} %copy-done.3, bf16[128,3712]{1,0:T(8,128)(2,1)} %copy-done.13, bf16[128,3712]{1,0:T(8,128)(2,1)} %copy-done.16, bf16[128,3712]{1,0:T(8,128)(2,1)} %copy-done.15, ...), custom_call_target="tpu_custom_call" | custom-call | bytes 104857 | tf_op jit(solution)/shard_map/near_sums/pallas_call | solution.py:348
  72.6 11.3 %activations.1 = (bf16[512,896]{1,0:T(8,128)(2,1)}, bf16[512,768]{1,0:T(8,128)(2,1)}) custom-call(s32[4]{0:T(128)} %pad_add_fusion.sel, bf16[128,3712]{1,0:T(8,128)(2,1)} %collective-permute-done.2.refs_0_.refs_19_.refs_6_, bf16[128,3712]{1,0:T(8,128)(2,1)} %collective-permute-done.6.refs_1_.refs_20_.refs_7_, bf16[128,3712]{1,0:T(8,128)(2,1)} %copy-done.22, ...), custom_call_target="tpu_custom_call" | custom-call | flops 1409286144 | bytes 15728640 | tf_op jit(solution)/shard_map/activations/pallas_call | solution.py:365
  84.3 2.5 %collective-permute-done.17.acts_other = bf16[512,896]{1,0:T(8,128)(2,1)S(1)} collective-permute-done((bf16[512,896]{1,0:T(8,128)(2,1)}, bf16[512,896]{1,0:T(8,128)(2,1)S(1)}, u32[]{:S(2)}, u32[]{:S(2)}) %collective-permute-start.17) | collective-permute-done | bytes 917536 | tf_op jit(solution)/shard_map/ppermute | solution.py:53
  90.1 5.6 %results.3 = (bf16[128,3712]{1,0:T(8,128)(2,1)S(1)}, bf16[128,3712]{1,0:T(8,128)(2,1)S(1)}) custom-call(s32[4]{0:T(128)S(1)} %copy-done.11, bf16[512,896]{1,0:T(8,128)(2,1)S(1)} %copy-done.7, bf16[512,896]{1,0:T(8,128)(2,1)S(1)} %collective-permute-done.17.acts_other, bf16[2,4,2,896,128]{4,3,2,1,0:T(8,128)(2,1)S(1)} %bitcast.15, ...), custom_call_target="tpu_custom_call" | custom-call | flops 1409286144 | bytes 12582912 | tf_op jit(solution)/shard_map/results/pallas_call | solution.py:387
  95.8 3.2 %collective-permute-start.21 = (bf16[128,3712]{1,0:T(8,128)(2,1)S(1)}, bf16[128,3712]{1,0:T(8,128)(2,1)S(1)}, u32[]{:S(2)}, u32[]{:S(2)}) collective-permute-start(bf16[128,3712]{1,0:T(8,128)(2,1)S(1)} %get-tuple-element.56), channel_id=1, source_target_pairs={{0,12},{1,13},{2,14},{3,15},{4,0},{5,1},{6,2},{7,3},{8,4},{9,5},{1... | collective-permute-start | bytes 2850824 | tf_op jit(solution)/shard_map/ppermute | solution.py:53
  99.0 8.7 %results.2 = (bf16[128,3712]{1,0:T(8,128)(2,1)S(1)}, bf16[128,3712]{1,0:T(8,128)(2,1)S(1)}, bf16[128,3712]{1,0:T(8,128)(2,1)S(1)}, bf16[128,3712]{1,0:T(8,128)(2...) custom-call(s32[4]{0:T(128)S(1)} %copy-done.11, bf16[512,896]{1,0:T(8,128)(2,1)S(1)} %copy-done.7, ...), custom_call_target="tpu_custom_call" | custom-call | flops 4227858432 | bytes 12582912 | tf_op jit(solution)/shard_map/results/pallas_call | solution.py:387
  107.7 3.0 %collective-permute-done.19 = bf16[128,3712]{1,0:T(8,128)(2,1)S(1)} collective-permute-done((bf16[128,3712]{1,0:T(8,128)(2,1)S(1)}, bf16[128,3712]{1,0:T(8,128)(2,1)S(1)}, u32[]{:S(2)}, u32[]{:S(2)}) %collective-permute-start.19) | collective-permute-done | bytes 950304 | tf_op jit(solution)/shard_map/ppermute | solution.py:53
  113.1 3.2 %collective-permute-start.22 = (bf16[128,3712]{1,0:T(8,128)(2,1)}, bf16[128,3712]{1,0:T(8,128)(2,1)}, u32[]{:S(2)}, u32[]{:S(2)}) collective-permute-start(bf16[128,3712]{1,0:T(8,128)(2,1)} %add_convert_fusion), channel_id=1, source_target_pairs={{0,12},{1,13},{2,14},{3,15},{4,0},{5,1},{6,2},{7,3},{8,4},{9,5},{1... | collective-permute-start | bytes 2850824 | tf_op jit(solution)/shard_map/ppermute | solution.py:53
  116.5 3.2 %collective-permute-start.23 = (bf16[128,3712]{1,0:T(8,128)(2,1)}, bf16[128,3712]{1,0:T(8,128)(2,1)}, u32[]{:S(2)}, u32[]{:S(2)}) collective-permute-start(bf16[128,3712]{1,0:T(8,128)(2,1)} %copy-done.12), channel_id=1, source_target_pairs={{0,12},{1,13},{2,14},{3,15},{4,0},{5,1},{6,2},{7,3},{8,4},{9,5},{1... | collective-permute-start | bytes 2850824 | tf_op jit(solution)/shard_map/ppermute | solution.py:53
  119.7 8.2 %weight_grads.2 = (bf16[2,4,2,896,128]{4,3,2,1,0:T(8,128)(2,1)}, bf16[2,4,2,896,128]{4,3,2,1,0:T(8,128)(2,1)}, bf16[2,128,7168]{2,1,0:T(8,128)(2,1)}) custom-call(s32[4]{0:T(128)S(1)} %copy-done.11, bf16[128,3712]{1,0:T(8,128)(2,1)S(1)} %copy-done.4, bf16[128,3712]{1,0:T(8,128)(2,1)} %copy-done.13, bf16[128,3712]{1,0:T(8,128)(2,1)} %copy-done.16, ...), custom_call_target="tpu_custom_call" | custom-call | flops 2818572288 | bytes 14680064 | tf_op jit(solution)/shard_map/weight_grads/pallas_call | solution.py:404
  127.9 8.2 %weight_grads.3 = (bf16[2,4,2,896,128]{4,3,2,1,0:T(8,128)(2,1)}, bf16[2,4,2,896,128]{4,3,2,1,0:T(8,128)(2,1)}, bf16[2,128,7168]{2,1,0:T(8,128)(2,1)}) custom-call(s32[4]{0:T(128)S(1)} %copy-done.11, bf16[128,3712]{1,0:T(8,128)(2,1)S(1)} %copy-done.6, bf16[128,3712]{1,0:T(8,128)(2,1)} %copy-done.18, ...), custom_call_target="tpu_custom_call", output_to_operand_aliasing={{0}: (10, {}), {1}: (11, {}), {2}: (12, {})} | custom-call | flops 2818572288 | bytes 14680064 | tf_op jit(solution)/shard_map/weight_grads/pallas_call | solution.py:404
  137.4 2.6 %add_convert_fusion.4 = (bf16[64,3712]{1,0:T(8,128)(2,1)S(1)}, bf16[64,3712]{1,0:T(8,128)(2,1)}) fusion(bf16[128,3712]{1,0:T(8,128)(2,1)} %collective-permute-done.25, bf16[128,3712]{1,0:T(8,128)(2,1)} %collective-permute-done.22, bf16[128,3712]{1,0:T(8,128)(2,1)S(1)} %copy-done.9), kind=kLoop, calls=%fused_computation.4 | loop fusion | flops 2850816 | bytes 3801088 | tf_op jit(solution)/shard_map/convert_element_type | solution.py:432
  144.4 6.2 %collective-permute-done.27 = bf16[64,3712]{1,0:T(8,128)(2,1)S(1)} collective-permute-done((bf16[64,3712]{1,0:T(8,128)(2,1)}, bf16[64,3712]{1,0:T(8,128)(2,1)S(1)}, u32[]{:S(2)}, u32[]{:S(2)}) %collective-permute-start.27) | collective-permute-done | bytes 475168 | tf_op jit(solution)/shard_map/ppermute | solution.py:53
  150.5 2.7 %collective-permute-done.26 = bf16[64,3712]{1,0:T(8,128)(2,1)S(1)} collective-permute-done((bf16[64,3712]{1,0:T(8,128)(2,1)S(1)}, bf16[64,3712]{1,0:T(8,128)(2,1)S(1)}, u32[]{:S(2)}, u32[]{:S(2)}) %collective-permute-start.26) | collective-permute-done | bytes 475168 | tf_op jit(solution)/shard_map/ppermute | solution.py:53
  157.2 4.0 %collective-permute-start.30 = (bf16[64,1024]{1,0:T(8,128)(2,1)S(1)}, bf16[64,1024]{1,0:T(8,128)(2,1)S(1)}, u32[]{:S(2)}, u32[]{:S(2)}) collective-permute-start(bf16[64,1024]{1,0:T(8,128)(2,1)S(1)} %get-tuple-element.90), channel_id=1, source_target_pairs={{0,64},{1,65},{2,66},{3,67},{4,68},{5,69},{6,70},{7,71},{8,72},{9,... | collective-permute-start | bytes 393224 | tf_op jit(solution)/shard_map/ppermute | solution.py:53
  (131 shorter events, 43.8 us)
Async XLA Ops:
  3.8 14.5 %collective-permute-start = (bf16[64,3712]{1,0:T(8,128)(2,1)}, bf16[64,3712]{1,0:T(8,128)(2,1)S(1)}, u32[]{:S(2)}, u32[]{:S(2)}) collective-permute-start(bf16[64,3712]{1,0:T(8,128)(2,1)} %pack.1), channel_id=1, source_target_pairs={{0,3},{1,0},{2,1},{3,2},{4,7},{5,4},{6,5},{7,6},{8,11},{9,8},{10,9... | collective-permute-start | bytes 1425416 | tf_op jit(solution)/shard_map/ppermute | solution.py:53
  6.7 15.5 %collective-permute-start.3 = (bf16[64,3712]{1,0:T(8,128)(2,1)}, bf16[64,3712]{1,0:T(8,128)(2,1)S(1)}, u32[]{:S(2)}, u32[]{:S(2)}) collective-permute-start(bf16[64,3712]{1,0:T(8,128)(2,1)} %pack.1), channel_id=1, source_target_pairs={{0,1},{1,2},{2,3},{3,0},{4,5},{5,6},{6,7},{7,4},{8,9},{9,10},{10,1... | collective-permute-start | bytes 1425416 | tf_op jit(solution)/shard_map/ppermute | solution.py:53
  6.7 15.6 %collective-permute-start.4 = (bf16[64,3712]{1,0:T(8,128)(2,1)}, bf16[64,3712]{1,0:T(8,128)(2,1)S(1)}, u32[]{:S(2)}, u32[]{:S(2)}) collective-permute-start(bf16[64,3712]{1,0:T(8,128)(2,1)} %pack.1), channel_id=1, source_target_pairs={{0,2},{1,3},{2,0},{3,1},{4,6},{5,7},{6,4},{7,5},{8,10},{9,11},{10,... | collective-permute-start | bytes 1425416 | tf_op jit(solution)/shard_map/ppermute | solution.py:53
  15.3 71.6 %collective-permute-start.18 = (bf16[4,42,128,128]{3,2,1,0:T(8,128)(2,1)}, bf16[4,42,128,128]{3,2,1,0:T(8,128)(2,1)}, u32[]{:S(2)}, u32[]{:S(2)}) collective-permute-start(bf16[4,42,128,128]{3,2,1,0:T(8,128)(2,1)} %pack_weights.1), channel_id=1, source_target_pairs={{0,16},{1,17},{2,18},{3,19},{4,20},{5,21},{6,22},{7,23},{8,24},{9,... | collective-permute-start | bytes 16515080 | tf_op jit(solution)/shard_map/ppermute | solution.py:53
  18.4 15.0 %collective-permute-start.1 = (bf16[128,3712]{1,0:T(8,128)(2,1)S(1)}, bf16[128,3712]{1,0:T(8,128)(2,1)S(1)}, u32[]{:S(2)}, u32[]{:S(2)}) collective-permute-start(bf16[128,3712]{1,0:T(8,128)(2,1)S(1)} %constant_dynamic-update-slice_fusion.refs_0_.refs_13_), channel_id=1, source_target_pairs={{0,4},{1,5},{2,6},{3,7},{4,8},{5,9},{6,10},{7,11},{8,12},{9,13},{1... | collective-permute-start | bytes 2850824 | tf_op jit(solution)/shard_map/ppermute | solution.py:53
  22.4 14.0 %collective-permute-start.5 = (bf16[128,3712]{1,0:T(8,128)(2,1)S(1)}, bf16[128,3712]{1,0:T(8,128)(2,1)S(1)}, u32[]{:S(2)}, u32[]{:S(2)}) collective-permute-start(bf16[128,3712]{1,0:T(8,128)(2,1)S(1)} %constant_dynamic-update-slice_fusion.2.refs_1_.refs_14_), channel_id=1, source_target_pairs={{0,12},{1,13},{2,14},{3,15},{4,0},{5,1},{6,2},{7,3},{8,4},{9,5},{1... | collective-permute-start | bytes 2850824 | tf_op jit(solution)/shard_map/ppermute | solution.py:53
  25.1 21.4 %collective-permute-start.7 = (bf16[128,3712]{1,0:T(8,128)(2,1)S(1)}, bf16[128,3712]{1,0:T(8,128)(2,1)S(1)}, u32[]{:S(2)}, u32[]{:S(2)}) collective-permute-start(bf16[128,3712]{1,0:T(8,128)(2,1)S(1)} %constant_dynamic-update-slice_fusion.refs_0_.refs_13_), channel_id=1, source_target_pairs={{0,12},{1,13},{2,14},{3,15},{4,0},{5,1},{6,2},{7,3},{8,4},{9,5},{1... | collective-permute-start | bytes 2850824 | tf_op jit(solution)/shard_map/ppermute | solution.py:53
  26.7 19.9 %collective-permute-start.8 = (bf16[128,3712]{1,0:T(8,128)(2,1)S(1)}, bf16[128,3712]{1,0:T(8,128)(2,1)S(1)}, u32[]{:S(2)}, u32[]{:S(2)}) collective-permute-start(bf16[128,3712]{1,0:T(8,128)(2,1)S(1)} %constant_dynamic-update-slice_fusion.2.refs_1_.refs_14_), channel_id=1, source_target_pairs={{0,4},{1,5},{2,6},{3,7},{4,8},{5,9},{6,10},{7,11},{8,12},{9,13},{1... | collective-permute-start | bytes 2850824 | tf_op jit(solution)/shard_map/ppermute | solution.py:53
  33.4 13.7 %collective-permute-start.9 = (bf16[128,3712]{1,0:T(8,128)(2,1)S(1)}, bf16[128,3712]{1,0:T(8,128)(2,1)S(1)}, u32[]{:S(2)}, u32[]{:S(2)}) collective-permute-start(bf16[128,3712]{1,0:T(8,128)(2,1)S(1)} %constant_dynamic-update-slice_fusion.refs_0_.refs_13_), channel_id=1, source_target_pairs={{0,16},{1,17},{2,18},{3,19},{4,20},{5,21},{6,22},{7,23},{8,24},{9,... | collective-permute-start | bytes 2850824 | tf_op jit(solution)/shard_map/ppermute | solution.py:53
  36.4 10.8 %collective-permute-start.10 = (bf16[128,3712]{1,0:T(8,128)(2,1)S(1)}, bf16[128,3712]{1,0:T(8,128)(2,1)S(1)}, u32[]{:S(2)}, u32[]{:S(2)}) collective-permute-start(bf16[128,3712]{1,0:T(8,128)(2,1)S(1)} %constant_dynamic-update-slice_fusion.2.refs_1_.refs_14_), channel_id=1, source_target_pairs={{0,16},{1,17},{2,18},{3,19},{4,20},{5,21},{6,22},{7,23},{8,24},{9,... | collective-permute-start | bytes 2850824 | tf_op jit(solution)/shard_map/ppermute | solution.py:53
  47.1 8.4 %collective-permute-start.13 = (bf16[128,3712]{1,0:T(8,128)(2,1)S(1)}, bf16[128,3712]{1,0:T(8,128)(2,1)S(1)}, u32[]{:S(2)}, u32[]{:S(2)}) collective-permute-start(bf16[128,3712]{1,0:T(8,128)(2,1)S(1)} %collective-permute-done.1.refs_4_.refs_17_), channel_id=1, source_target_pairs={{0,16},{1,17},{2,18},{3,19},{4,20},{5,21},{6,22},{7,23},{8,24},{9,... | collective-permute-start | bytes 2850824 | tf_op jit(solution)/shard_map/ppermute | solution.py:53
  47.2 9.3 %collective-permute-start.14 = (bf16[128,3712]{1,0:T(8,128)(2,1)S(1)}, bf16[128,3712]{1,0:T(8,128)(2,1)}, u32[]{:S(2)}, u32[]{:S(2)}) collective-permute-start(bf16[128,3712]{1,0:T(8,128)(2,1)S(1)} %collective-permute-done.8.refs_5_.refs_18_), channel_id=1, source_target_pairs={{0,16},{1,17},{2,18},{3,19},{4,20},{5,21},{6,22},{7,23},{8,24},{9,... | collective-permute-start | bytes 2850824 | tf_op jit(solution)/shard_map/ppermute | solution.py:53
  49.1 19.2 %collective-permute-start.2 = (bf16[128,3712]{1,0:T(8,128)(2,1)S(1)}, bf16[128,3712]{1,0:T(8,128)(2,1)}, u32[]{:S(2)}, u32[]{:S(2)}) collective-permute-start(bf16[128,3712]{1,0:T(8,128)(2,1)S(1)} %collective-permute-done.1.refs_4_.refs_17_), channel_id=1, source_target_pairs={{0,4},{1,5},{2,6},{3,7},{4,8},{5,9},{6,10},{7,11},{8,12},{9,13},{1... | collective-permute-start | bytes 2850824 | tf_op jit(solution)/shard_map/ppermute | solution.py:53
  51.8 16.5 %collective-permute-start.6 = (bf16[128,3712]{1,0:T(8,128)(2,1)S(1)}, bf16[128,3712]{1,0:T(8,128)(2,1)}, u32[]{:S(2)}, u32[]{:S(2)}) collective-permute-start(bf16[128,3712]{1,0:T(8,128)(2,1)S(1)} %collective-permute-done.5.refs_3_.refs_16_), channel_id=1, source_target_pairs={{0,12},{1,13},{2,14},{3,15},{4,0},{5,1},{6,2},{7,3},{8,4},{9,5},{1... | collective-permute-start | bytes 2850824 | tf_op jit(solution)/shard_map/ppermute | solution.py:53
  95.7 15.0 %collective-permute-start.19 = (bf16[128,3712]{1,0:T(8,128)(2,1)S(1)}, bf16[128,3712]{1,0:T(8,128)(2,1)S(1)}, u32[]{:S(2)}, u32[]{:S(2)}) collective-permute-start(bf16[128,3712]{1,0:T(8,128)(2,1)S(1)} %get-tuple-element.54), channel_id=1, source_target_pairs={{0,4},{1,5},{2,6},{3,7},{4,8},{5,9},{6,10},{7,11},{8,12},{9,13},{1... | collective-permute-start | bytes 2850824 | tf_op jit(solution)/shard_map/ppermute | solution.py:53
  95.8 16.2 %collective-permute-start.21 = (bf16[128,3712]{1,0:T(8,128)(2,1)S(1)}, bf16[128,3712]{1,0:T(8,128)(2,1)S(1)}, u32[]{:S(2)}, u32[]{:S(2)}) collective-permute-start(bf16[128,3712]{1,0:T(8,128)(2,1)S(1)} %get-tuple-element.56), channel_id=1, source_target_pairs={{0,12},{1,13},{2,14},{3,15},{4,0},{5,1},{6,2},{7,3},{8,4},{9,5},{1... | collective-permute-start | bytes 2850824 | tf_op jit(solution)/shard_map/ppermute | solution.py:53
  112.0 24.2 %collective-permute-start.20 = (bf16[128,3712]{1,0:T(8,128)(2,1)}, bf16[128,3712]{1,0:T(8,128)(2,1)}, u32[]{:S(2)}, u32[]{:S(2)}) collective-permute-start(bf16[128,3712]{1,0:T(8,128)(2,1)} %add_convert_fusion.1), channel_id=1, source_target_pairs={{0,4},{1,5},{2,6},{3,7},{4,8},{5,9},{6,10},{7,11},{8,12},{9,13},{1... | collective-permute-start | bytes 2850824 | tf_op jit(solution)/shard_map/ppermute | solution.py:53
  113.1 23.0 %collective-permute-start.22 = (bf16[128,3712]{1,0:T(8,128)(2,1)}, bf16[128,3712]{1,0:T(8,128)(2,1)}, u32[]{:S(2)}, u32[]{:S(2)}) collective-permute-start(bf16[128,3712]{1,0:T(8,128)(2,1)} %add_convert_fusion), channel_id=1, source_target_pairs={{0,12},{1,13},{2,14},{3,15},{4,0},{5,1},{6,2},{7,3},{8,4},{9,5},{1... | collective-permute-start | bytes 2850824 | tf_op jit(solution)/shard_map/ppermute | solution.py:53
  116.4 21.1 %collective-permute-start.25 = (bf16[128,3712]{1,0:T(8,128)(2,1)}, bf16[128,3712]{1,0:T(8,128)(2,1)}, u32[]{:S(2)}, u32[]{:S(2)}) collective-permute-start(bf16[128,3712]{1,0:T(8,128)(2,1)} %get-tuple-element.68), channel_id=1, source_target_pairs={{0,4},{1,5},{2,6},{3,7},{4,8},{5,9},{6,10},{7,11},{8,12},{9,13},{1... | collective-permute-start | bytes 2850824 | tf_op jit(solution)/shard_map/ppermute | solution.py:53
  116.5 24.7 %collective-permute-start.23 = (bf16[128,3712]{1,0:T(8,128)(2,1)}, bf16[128,3712]{1,0:T(8,128)(2,1)}, u32[]{:S(2)}, u32[]{:S(2)}) collective-permute-start(bf16[128,3712]{1,0:T(8,128)(2,1)} %copy-done.12), channel_id=1, source_target_pairs={{0,12},{1,13},{2,14},{3,15},{4,0},{5,1},{6,2},{7,3},{8,4},{9,5},{1... | collective-permute-start | bytes 2850824 | tf_op jit(solution)/shard_map/ppermute | solution.py:53
  140.0 10.5 %collective-permute-start.27 = (bf16[64,3712]{1,0:T(8,128)(2,1)}, bf16[64,3712]{1,0:T(8,128)(2,1)S(1)}, u32[]{:S(2)}, u32[]{:S(2)}) collective-permute-start(bf16[64,3712]{1,0:T(8,128)(2,1)} %get-tuple-element.81), channel_id=1, source_target_pairs={{0,2},{1,3},{2,0},{3,1},{4,6},{5,7},{6,4},{7,5},{8,10},{9,11},{10,... | collective-permute-start | bytes 1425416 | tf_op jit(solution)/shard_map/ppermute | solution.py:53
  140.3 12.9 %collective-permute-start.26 = (bf16[64,3712]{1,0:T(8,128)(2,1)S(1)}, bf16[64,3712]{1,0:T(8,128)(2,1)S(1)}, u32[]{:S(2)}, u32[]{:S(2)}) collective-permute-start(bf16[64,3712]{1,0:T(8,128)(2,1)S(1)} %get-tuple-element.80), channel_id=1, source_target_pairs={{0,3},{1,0},{2,1},{3,2},{4,7},{5,4},{6,5},{7,6},{8,11},{9,8},{10,9... | collective-permute-start | bytes 1425416 | tf_op jit(solution)/shard_map/ppermute | solution.py:53
  142.5 13.0 %collective-permute-start.24 = (bf16[64,3712]{1,0:T(8,128)(2,1)S(1)}, bf16[64,3712]{1,0:T(8,128)(2,1)S(1)}, u32[]{:S(2)}, u32[]{:S(2)}) collective-permute-start(bf16[64,3712]{1,0:T(8,128)(2,1)S(1)} %add_convert_fusion.5), channel_id=1, source_target_pairs={{0,1},{1,2},{2,3},{3,0},{4,5},{5,6},{6,7},{7,4},{8,9},{9,10},{10,1... | collective-permute-start | bytes 1425416 | tf_op jit(solution)/shard_map/ppermute | solution.py:53
  157.2 8.1 %collective-permute-start.30 = (bf16[64,1024]{1,0:T(8,128)(2,1)S(1)}, bf16[64,1024]{1,0:T(8,128)(2,1)S(1)}, u32[]{:S(2)}, u32[]{:S(2)}) collective-permute-start(bf16[64,1024]{1,0:T(8,128)(2,1)S(1)} %get-tuple-element.90), channel_id=1, source_target_pairs={{0,64},{1,65},{2,66},{3,67},{4,68},{5,69},{6,70},{7,71},{8,72},{9,... | collective-permute-start | bytes 393224 | tf_op jit(solution)/shard_map/ppermute | solution.py:53
  (34 other events, 379.0 us)

commit v9 on v8

--- a/solution.py
+++ b/solution.py
@@ -476,6 +476,7 @@
     a_late = send(add(plus_a, from_a), outer(1))
     b_late = send(add(minus_b, from_b), outer(-1))
     grads = weight_grads(False, 0, 4, sel, rows, acts_grad, [], 52)
+    (a_early, b_early), grads = lax.optimization_barrier(((a_early, b_early), grads))
     grads = weight_grads(True, 0, 4, sel, rows_other, acts_grad, grads, 52)
     (a_late, b_late), grads = lax.optimization_barrier(((a_late, b_late), grads))
     keep = (own_a[:64], a_late[:64], a_early[:64])

time: 171 us -> 168 us (0.982)
  waiting for transfers between devices: 52.7 us -> 45.1 us
  starting transfers between devices: 37.3 us -> 39.9 us
    ppermute x31, waiting for transfers between devices: 52.7 us -> 45.1 us  [send(): return lax.ppermute(value, AXES, pairs)]
    ppermute x31, starting transfers between devices: 37.3 us -> 39.9 us  [send(): return lax.ppermute(value, AXES, pairs)]
    unnamed x59 -> x55, local copies, waits for them, and re-layouts: 5.15 us -> 5.13 us
  transfers between devices with their start and end apart: 31 -> 31, of which waited for: 18 -> 17; matrix products, arithmetic and copies ran while one was open for 5% -> 4% of each run, Pallas kernels for 32% -> 33%
where the time goes in v9:
time: 168 us; the launch traced here: 165 us
  Pallas kernels  63 us (38%)
  waiting for transfers between devices  45.1 us (27%)
  starting transfers between devices  39.9 us (24%)
  other arithmetic  10.2 us (6%)
  local copies, waits for them, and re-layouts  6.01 us (4%)
    ppermute x31, waiting for transfers between devices, send(): return lax.ppermute(value, AXES, pairs)  45.1 us
    ppermute x31, starting transfers between devices, send(): return lax.ppermute(value, AXES, pairs)  39.9 us
    pallas_call x2, Pallas kernels, weight_grads(): pl.pallas_call(functools.partial(grads_kernel, swapped), grid_spec=pltpu....  16.4 us
    pallas_call x2, Pallas kernels, results(): pl.pallas_call(functools.partial(results_kernel, pieces), in_specs=[SM] +...  14.6 us
    pallas_call x1, Pallas kernels, near_sums(): pl.pallas_call(near_kernel, grid_spec=pltpu.PrefetchScalarGridSpec(num_sc...  11.8 us
    pallas_call x1, Pallas kernels, activations(): pl.pallas_call(far_kernel, grid_spec=pltpu.PrefetchScalarGridSpec(num_sca...  11.3 us
    convert_element_type x5, other arithmetic, add(): return total.astype(BF)  7.86 us
    pallas_call x1, Pallas kernels, pack_weights(): pl.pallas_call(pack_weights_kernel, grid_spec=pltpu.PrefetchScalarGridSpe...  6.28 us
  transfers between devices with their start and end apart: 31, of which 17 were waited for; matrix products, arithmetic and copies ran while one was open for 4% of the time, Pallas kernels for 33%

profile of v9, /device:TPU:0, one launch (start us, length us, event | category | flops | bytes accessed | tf_op | source)
XLA Modules:
  0.0 165.3 jit_solution(8337674311681630058)
XLA Ops:
  1.3 2.6 %pack.1 = bf16[64,3712]{1,0:T(8,128)(2,1)} custom-call(s32[4]{0:T(128)} %pad_add_fusion.sel, bf16[32,7168]{1,0:T(8,128)(2,1)} %tok.1, bf16[32,7168]{1,0:T(8,128)(2,1)} %cot.1, f32[24,32]{1,0:T(8,128)} %bitcast.26, s32[8,32]{1,0:T(8,128)} %bitcast.27), custom_call_target="tpu_custom_call" | custom-call | bytes 2097152 | tf_op jit(solution)/shard_map/pack/pallas_call | solution.py:303
  3.9 2.9 %collective-permute-start = (bf16[64,3712]{1,0:T(8,128)(2,1)}, bf16[64,3712]{1,0:T(8,128)(2,1)S(1)}, u32[]{:S(2)}, u32[]{:S(2)}) collective-permute-start(bf16[64,3712]{1,0:T(8,128)(2,1)} %pack.1), channel_id=1, source_target_pairs={{0,3},{1,0},{2,1},{3,2},{4,7},{5,4},{6,5},{7,6},{8,11},{9,8},{10,9... | collective-permute-start | bytes 1425416 | tf_op jit(solution)/shard_map/ppermute | solution.py:53
  8.5 6.3 %pack_weights.1 = bf16[4,42,128,128]{3,2,1,0:T(8,128)(2,1)} custom-call(s32[4]{0:T(128)} %pad_add_fusion.sel, bf16[2,4,2,896,128]{4,3,2,1,0:T(8,128)(2,1)} %bitcast.10, bf16[2,4,2,896,128]{4,3,2,1,0:T(8,128)(2,1)} %bitcast.17, bf16[2,128,7168]{2,1,0:T(8,128)(2,1)} %wd.5), custom_call_target="tpu_custom_call" | custom-call | bytes 11534336 | tf_op jit(solution)/shard_map/pack_weights/pallas_call | solution.py:319
  14.8 3.6 %collective-permute-done = bf16[64,3712]{1,0:T(8,128)(2,1)S(1)} collective-permute-done((bf16[64,3712]{1,0:T(8,128)(2,1)}, bf16[64,3712]{1,0:T(8,128)(2,1)S(1)}, u32[]{:S(2)}, u32[]{:S(2)}) %collective-permute-start) | collective-permute-done | bytes 475168 | tf_op jit(solution)/shard_map/ppermute | solution.py:53
  18.5 3.1 %collective-permute-start.7 = (bf16[128,3712]{1,0:T(8,128)(2,1)S(1)}, bf16[128,3712]{1,0:T(8,128)(2,1)S(1)}, u32[]{:S(2)}, u32[]{:S(2)}) collective-permute-start(bf16[128,3712]{1,0:T(8,128)(2,1)S(1)} %constant_dynamic-update-slice_fusion.refs_0_.refs_13_), channel_id=1, source_target_pairs={{0,12},{1,13},{2,14},{3,15},{4,0},{5,1},{6,2},{7,3},{8,4},{9,5},{1... | collective-permute-start | bytes 2850824 | tf_op jit(solution)/shard_map/ppermute | solution.py:53
  26.8 6.2 %collective-permute-done.7.refs_2_.refs_15_ = bf16[128,3712]{1,0:T(8,128)(2,1)S(1)} collective-permute-done((bf16[128,3712]{1,0:T(8,128)(2,1)S(1)}, bf16[128,3712]{1,0:T(8,128)(2,1)S(1)}, u32[]{:S(2)}, u32[]{:S(2)}) %collective-permute-start.7) | collective-permute-done | bytes 950304 | tf_op jit(solution)/shard_map/ppermute | solution.py:53
  32.9 3.7 %collective-permute-start.5 = (bf16[128,3712]{1,0:T(8,128)(2,1)S(1)}, bf16[128,3712]{1,0:T(8,128)(2,1)}, u32[]{:S(2)}, u32[]{:S(2)}) collective-permute-start(bf16[128,3712]{1,0:T(8,128)(2,1)S(1)} %constant_dynamic-update-slice_fusion.2.refs_1_.refs_14_), channel_id=1, source_target_pairs={{0,12},{1,13},{2,14},{3,15},{4,0},{5,1},{6,2},{7,3},{8,4},{9,5},{1... | collective-permute-start | bytes 2850824 | tf_op jit(solution)/shard_map/ppermute | solution.py:53
  37.7 9.7 %collective-permute-done.8.refs_5_.refs_18_ = bf16[128,3712]{1,0:T(8,128)(2,1)S(1)} collective-permute-done((bf16[128,3712]{1,0:T(8,128)(2,1)S(1)}, bf16[128,3712]{1,0:T(8,128)(2,1)S(1)}, u32[]{:S(2)}, u32[]{:S(2)}) %collective-permute-start.8) | collective-permute-done | bytes 950304 | tf_op jit(solution)/shard_map/ppermute | solution.py:53
  48.4 3.4 %collective-permute-start.6 = (bf16[128,3712]{1,0:T(8,128)(2,1)}, bf16[128,3712]{1,0:T(8,128)(2,1)}, u32[]{:S(2)}, u32[]{:S(2)}) collective-permute-start(bf16[128,3712]{1,0:T(8,128)(2,1)} %collective-permute-done.5.refs_3_.refs_16_), channel_id=1, source_target_pairs={{0,12},{1,13},{2,14},{3,15},{4,0},{5,1},{6,2},{7,3},{8,4},{9,5},{1... | collective-permute-start | bytes 2850824 | tf_op jit(solution)/shard_map/ppermute | solution.py:53
  52.9 11.8 %near_sums.1 = (f32[512,256]{1,0:T(8,128)}, f32[512,256]{1,0:T(8,128)}, f32[512,256]{1,0:T(8,128)}) custom-call(s32[4]{0:T(128)} %pad_add_fusion.sel, bf16[128,3712]{1,0:T(8,128)(2,1)} %copy-done.3, bf16[128,3712]{1,0:T(8,128)(2,1)} %copy-done.12, bf16[128,3712]{1,0:T(8,128)(2,1)} %copy-done.14, bf16[128,3712]{1,0:T(8,128)(2,1)} %collective-permute-done.5.refs_3_.refs_16_, ...), custom_call_target="tpu_custom_call" | custom-call | bytes 104857 | tf_op jit(solution)/shard_map/near_sums/pallas_call | solution.py:348
  69.0 11.3 %activations.1 = (bf16[512,896]{1,0:T(8,128)(2,1)}, bf16[512,768]{1,0:T(8,128)(2,1)}) custom-call(s32[4]{0:T(128)} %pad_add_fusion.sel, bf16[128,3712]{1,0:T(8,128)(2,1)} %collective-permute-done.2.refs_0_.refs_19_.refs_6_, bf16[128,3712]{1,0:T(8,128)(2,1)} %collective-permute-done.6.refs_1_.refs_20_.refs_7_, bf16[128,3712]{1,0:T(8,128)(2,1)} %copy-done.20, ...), custom_call_target="tpu_custom_call" | custom-call | flops 1409286144 | bytes 15728640 | tf_op jit(solution)/shard_map/activations/pallas_call | solution.py:365
  80.7 2.5 %collective-permute-done.17.acts_other = bf16[512,896]{1,0:T(8,128)(2,1)S(1)} collective-permute-done((bf16[512,896]{1,0:T(8,128)(2,1)}, bf16[512,896]{1,0:T(8,128)(2,1)S(1)}, u32[]{:S(2)}, u32[]{:S(2)}) %collective-permute-start.17) | collective-permute-done | bytes 917536 | tf_op jit(solution)/shard_map/ppermute | solution.py:53
  86.5 5.6 %results.3 = (bf16[128,3712]{1,0:T(8,128)(2,1)S(1)}, bf16[128,3712]{1,0:T(8,128)(2,1)S(1)}) custom-call(s32[4]{0:T(128)S(1)} %copy-done.11, bf16[512,896]{1,0:T(8,128)(2,1)S(1)} %copy-done.7, bf16[512,896]{1,0:T(8,128)(2,1)S(1)} %collective-permute-done.17.acts_other, bf16[2,4,2,896,128]{4,3,2,1,0:T(8,128)(2,1)S(1)} %bitcast.15, ...), custom_call_target="tpu_custom_call" | custom-call | flops 1409286144 | bytes 12582912 | tf_op jit(solution)/shard_map/results/pallas_call | solution.py:387
  93.4 2.1 %collective-permute-start.21 = (bf16[128,3712]{1,0:T(8,128)(2,1)S(1)}, bf16[128,3712]{1,0:T(8,128)(2,1)S(1)}, u32[]{:S(2)}, u32[]{:S(2)}) collective-permute-start(bf16[128,3712]{1,0:T(8,128)(2,1)S(1)} %get-tuple-element.61), channel_id=1, source_target_pairs={{0,12},{1,13},{2,14},{3,15},{4,0},{5,1},{6,2},{7,3},{8,4},{9,5},{1... | collective-permute-start | bytes 2850824 | tf_op jit(solution)/shard_map/ppermute | solution.py:53
  95.5 9.0 %results.2 = (bf16[128,3712]{1,0:T(8,128)(2,1)S(1)}, bf16[128,3712]{1,0:T(8,128)(2,1)S(1)}, bf16[128,3712]{1,0:T(8,128)(2,1)S(1)}, bf16[128,3712]{1,0:T(8,128)(2...) custom-call(s32[4]{0:T(128)S(1)} %copy-done.11, bf16[512,896]{1,0:T(8,128)(2,1)S(1)} %copy-done.7, ...), custom_call_target="tpu_custom_call" | custom-call | flops 4227858432 | bytes 12582912 | tf_op jit(solution)/shard_map/results/pallas_call | solution.py:387
  109.6 3.2 %collective-permute-start.22 = (bf16[128,3712]{1,0:T(8,128)(2,1)}, bf16[128,3712]{1,0:T(8,128)(2,1)}, u32[]{:S(2)}, u32[]{:S(2)}) collective-permute-start(bf16[128,3712]{1,0:T(8,128)(2,1)} %add_convert_fusion), channel_id=1, source_target_pairs={{0,12},{1,13},{2,14},{3,15},{4,0},{5,1},{6,2},{7,3},{8,4},{9,5},{1... | collective-permute-start | bytes 2850824 | tf_op jit(solution)/shard_map/ppermute | solution.py:53
  112.9 8.2 %weight_grads.2 = (bf16[2,4,2,896,128]{4,3,2,1,0:T(8,128)(2,1)}, bf16[2,4,2,896,128]{4,3,2,1,0:T(8,128)(2,1)}, bf16[2,128,7168]{2,1,0:T(8,128)(2,1)}) custom-call(s32[4]{0:T(128)S(1)} %copy-done.11, bf16[128,3712]{1,0:T(8,128)(2,1)S(1)} %copy-done.4, bf16[128,3712]{1,0:T(8,128)(2,1)} %copy-done.12, bf16[128,3712]{1,0:T(8,128)(2,1)} %copy-done.14, ...), custom_call_target="tpu_custom_call" | custom-call | flops 2818572288 | bytes 14680064 | tf_op jit(solution)/shard_map/weight_grads/pallas_call | solution.py:404
  121.9 8.2 %weight_grads.3 = (bf16[2,4,2,896,128]{4,3,2,1,0:T(8,128)(2,1)}, bf16[2,4,2,896,128]{4,3,2,1,0:T(8,128)(2,1)}, bf16[2,128,7168]{2,1,0:T(8,128)(2,1)}) custom-call(s32[4]{0:T(128)S(1)} %copy-done.11, bf16[128,3712]{1,0:T(8,128)(2,1)S(1)} %copy-done.6, bf16[128,3712]{1,0:T(8,128)(2,1)} %copy-done.13, ...), custom_call_target="tpu_custom_call", output_to_operand_aliasing={{0}: (10, {}), {1}: (11, {}), {2}: (12, {})} | custom-call | flops 2818572288 | bytes 14680064 | tf_op jit(solution)/shard_map/weight_grads/pallas_call | solution.py:404
  133.6 2.6 %add_convert_fusion.4 = (bf16[64,3712]{1,0:T(8,128)(2,1)}, bf16[64,3712]{1,0:T(8,128)(2,1)S(1)}) fusion(bf16[128,3712]{1,0:T(8,128)(2,1)} %collective-permute-done.24, bf16[128,3712]{1,0:T(8,128)(2,1)} %collective-permute-done.22, bf16[128,3712]{1,0:T(8,128)(2,1)S(1)} %copy-done.9), kind=kLoop, calls=%fused_computation.4 | loop fusion | flops 2850816 | bytes 3801088 | tf_op jit(solution)/shard_map/convert_element_type | solution.py:432
  136.2 3.3 %collective-permute-start.26 = (bf16[64,3712]{1,0:T(8,128)(2,1)}, bf16[64,3712]{1,0:T(8,128)(2,1)S(1)}, u32[]{:S(2)}, u32[]{:S(2)}) collective-permute-start(bf16[64,3712]{1,0:T(8,128)(2,1)} %get-tuple-element.90), channel_id=1, source_target_pairs={{0,3},{1,0},{2,1},{3,2},{4,7},{5,4},{6,5},{7,6},{8,11},{9,8},{10,9... | collective-permute-start | bytes 1425416 | tf_op jit(solution)/shard_map/ppermute | solution.py:53
  143.5 7.6 %collective-permute-done.26 = bf16[64,3712]{1,0:T(8,128)(2,1)S(1)} collective-permute-done((bf16[64,3712]{1,0:T(8,128)(2,1)}, bf16[64,3712]{1,0:T(8,128)(2,1)S(1)}, u32[]{:S(2)}, u32[]{:S(2)}) %collective-permute-start.26) | collective-permute-done | bytes 475168 | tf_op jit(solution)/shard_map/ppermute | solution.py:53
  154.8 2.2 %collective-permute-start.29 = (bf16[64,1024]{1,0:T(8,128)(2,1)S(1)}, bf16[64,1024]{1,0:T(8,128)(2,1)S(1)}, u32[]{:S(2)}, u32[]{:S(2)}) collective-permute-start(bf16[64,1024]{1,0:T(8,128)(2,1)S(1)} %get-tuple-element.99), channel_id=1, source_target_pairs={{0,96},{1,97},{2,98},{3,99},{4,100},{5,101},{6,102},{7,103},{8,104... | collective-permute-start | bytes 393224 | tf_op jit(solution)/shard_map/ppermute | solution.py:53
  158.8 2.2 %collective-permute-done.28 = bf16[64,1024]{1,0:T(8,128)(2,1)S(1)} collective-permute-done((bf16[64,1024]{1,0:T(8,128)(2,1)S(1)}, bf16[64,1024]{1,0:T(8,128)(2,1)S(1)}, u32[]{:S(2)}, u32[]{:S(2)}) %collective-permute-start.28) | collective-permute-done | bytes 131104 | tf_op jit(solution)/shard_map/ppermute | solution.py:53
  161.0 2.5 %collective-permute-done.30 = bf16[64,1024]{1,0:T(8,128)(2,1)S(1)} collective-permute-done((bf16[64,1024]{1,0:T(8,128)(2,1)S(1)}, bf16[64,1024]{1,0:T(8,128)(2,1)S(1)}, u32[]{:S(2)}, u32[]{:S(2)}) %collective-permute-start.30) | collective-permute-done | bytes 131104 | tf_op jit(solution)/shard_map/ppermute | solution.py:53
  (127 shorter events, 40.4 us)
Async XLA Ops:
  3.9 14.5 %collective-permute-start = (bf16[64,3712]{1,0:T(8,128)(2,1)}, bf16[64,3712]{1,0:T(8,128)(2,1)S(1)}, u32[]{:S(2)}, u32[]{:S(2)}) collective-permute-start(bf16[64,3712]{1,0:T(8,128)(2,1)} %pack.1), channel_id=1, source_target_pairs={{0,3},{1,0},{2,1},{3,2},{4,7},{5,4},{6,5},{7,6},{8,11},{9,8},{10,9... | collective-permute-start | bytes 1425416 | tf_op jit(solution)/shard_map/ppermute | solution.py:53
  6.8 17.1 %collective-permute-start.4 = (bf16[64,3712]{1,0:T(8,128)(2,1)}, bf16[64,3712]{1,0:T(8,128)(2,1)S(1)}, u32[]{:S(2)}, u32[]{:S(2)}) collective-permute-start(bf16[64,3712]{1,0:T(8,128)(2,1)} %pack.1), channel_id=1, source_target_pairs={{0,2},{1,3},{2,0},{3,1},{4,6},{5,7},{6,4},{7,5},{8,10},{9,11},{10,... | collective-permute-start | bytes 1425416 | tf_op jit(solution)/shard_map/ppermute | solution.py:53
  7.6 14.7 %collective-permute-start.3 = (bf16[64,3712]{1,0:T(8,128)(2,1)}, bf16[64,3712]{1,0:T(8,128)(2,1)S(1)}, u32[]{:S(2)}, u32[]{:S(2)}) collective-permute-start(bf16[64,3712]{1,0:T(8,128)(2,1)} %pack.1), channel_id=1, source_target_pairs={{0,1},{1,2},{2,3},{3,0},{4,5},{5,6},{6,7},{7,4},{8,9},{9,10},{10,1... | collective-permute-start | bytes 1425416 | tf_op jit(solution)/shard_map/ppermute | solution.py:53
  14.8 68.4 %collective-permute-start.18 = (bf16[4,42,128,128]{3,2,1,0:T(8,128)(2,1)}, bf16[4,42,128,128]{3,2,1,0:T(8,128)(2,1)}, u32[]{:S(2)}, u32[]{:S(2)}) collective-permute-start(bf16[4,42,128,128]{3,2,1,0:T(8,128)(2,1)} %pack_weights.1), channel_id=1, source_target_pairs={{0,16},{1,17},{2,18},{3,19},{4,20},{5,21},{6,22},{7,23},{8,24},{9,... | collective-permute-start | bytes 16515080 | tf_op jit(solution)/shard_map/ppermute | solution.py:53
  18.4 6.7 %collective-permute-start.9 = (bf16[128,3712]{1,0:T(8,128)(2,1)S(1)}, bf16[128,3712]{1,0:T(8,128)(2,1)S(1)}, u32[]{:S(2)}, u32[]{:S(2)}) collective-permute-start(bf16[128,3712]{1,0:T(8,128)(2,1)S(1)} %constant_dynamic-update-slice_fusion.refs_0_.refs_13_), channel_id=1, source_target_pairs={{0,16},{1,17},{2,18},{3,19},{4,20},{5,21},{6,22},{7,23},{8,24},{9,... | collective-permute-start | bytes 2850824 | tf_op jit(solution)/shard_map/ppermute | solution.py:53
  18.5 14.4 %collective-permute-start.7 = (bf16[128,3712]{1,0:T(8,128)(2,1)S(1)}, bf16[128,3712]{1,0:T(8,128)(2,1)S(1)}, u32[]{:S(2)}, u32[]{:S(2)}) collective-permute-start(bf16[128,3712]{1,0:T(8,128)(2,1)S(1)} %constant_dynamic-update-slice_fusion.refs_0_.refs_13_), channel_id=1, source_target_pairs={{0,12},{1,13},{2,14},{3,15},{4,0},{5,1},{6,2},{7,3},{8,4},{9,5},{1... | collective-permute-start | bytes 2850824 | tf_op jit(solution)/shard_map/ppermute | solution.py:53
  22.3 15.0 %collective-permute-start.1 = (bf16[128,3712]{1,0:T(8,128)(2,1)S(1)}, bf16[128,3712]{1,0:T(8,128)(2,1)S(1)}, u32[]{:S(2)}, u32[]{:S(2)}) collective-permute-start(bf16[128,3712]{1,0:T(8,128)(2,1)S(1)} %constant_dynamic-update-slice_fusion.refs_0_.refs_13_), channel_id=1, source_target_pairs={{0,4},{1,5},{2,6},{3,7},{4,8},{5,9},{6,10},{7,11},{8,12},{9,13},{1... | collective-permute-start | bytes 2850824 | tf_op jit(solution)/shard_map/ppermute | solution.py:53
  24.0 13.3 %collective-permute-start.10 = (bf16[128,3712]{1,0:T(8,128)(2,1)S(1)}, bf16[128,3712]{1,0:T(8,128)(2,1)S(1)}, u32[]{:S(2)}, u32[]{:S(2)}) collective-permute-start(bf16[128,3712]{1,0:T(8,128)(2,1)S(1)} %constant_dynamic-update-slice_fusion.2.refs_1_.refs_14_), channel_id=1, source_target_pairs={{0,16},{1,17},{2,18},{3,19},{4,20},{5,21},{6,22},{7,23},{8,24},{9,... | collective-permute-start | bytes 2850824 | tf_op jit(solution)/shard_map/ppermute | solution.py:53
  25.2 22.2 %collective-permute-start.8 = (bf16[128,3712]{1,0:T(8,128)(2,1)S(1)}, bf16[128,3712]{1,0:T(8,128)(2,1)S(1)}, u32[]{:S(2)}, u32[]{:S(2)}) collective-permute-start(bf16[128,3712]{1,0:T(8,128)(2,1)S(1)} %constant_dynamic-update-slice_fusion.2.refs_1_.refs_14_), channel_id=1, source_target_pairs={{0,4},{1,5},{2,6},{3,7},{4,8},{5,9},{6,10},{7,11},{8,12},{9,13},{1... | collective-permute-start | bytes 2850824 | tf_op jit(solution)/shard_map/ppermute | solution.py:53
  32.9 15.0 %collective-permute-start.5 = (bf16[128,3712]{1,0:T(8,128)(2,1)S(1)}, bf16[128,3712]{1,0:T(8,128)(2,1)}, u32[]{:S(2)}, u32[]{:S(2)}) collective-permute-start(bf16[128,3712]{1,0:T(8,128)(2,1)S(1)} %constant_dynamic-update-slice_fusion.2.refs_1_.refs_14_), channel_id=1, source_target_pairs={{0,12},{1,13},{2,14},{3,15},{4,0},{5,1},{6,2},{7,3},{8,4},{9,5},{1... | collective-permute-start | bytes 2850824 | tf_op jit(solution)/shard_map/ppermute | solution.py:53
  37.2 10.7 %collective-permute-start.11 = (bf16[128,3712]{1,0:T(8,128)(2,1)S(1)}, bf16[128,3712]{1,0:T(8,128)(2,1)S(1)}, u32[]{:S(2)}, u32[]{:S(2)}) collective-permute-start(bf16[128,3712]{1,0:T(8,128)(2,1)S(1)} %collective-permute-done.7.refs_2_.refs_15_), channel_id=1, source_target_pairs={{0,16},{1,17},{2,18},{3,19},{4,20},{5,21},{6,22},{7,23},{8,24},{9,... | collective-permute-start | bytes 2850824 | tf_op jit(solution)/shard_map/ppermute | solution.py:53
  37.2 11.2 %collective-permute-start.13 = (bf16[128,3712]{1,0:T(8,128)(2,1)S(1)}, bf16[128,3712]{1,0:T(8,128)(2,1)S(1)}, u32[]{:S(2)}, u32[]{:S(2)}) collective-permute-start(bf16[128,3712]{1,0:T(8,128)(2,1)S(1)} %collective-permute-done.1.refs_4_.refs_17_), channel_id=1, source_target_pairs={{0,16},{1,17},{2,18},{3,19},{4,20},{5,21},{6,22},{7,23},{8,24},{9,... | collective-permute-start | bytes 2850824 | tf_op jit(solution)/shard_map/ppermute | solution.py:53
  47.9 16.7 %collective-permute-start.2 = (bf16[128,3712]{1,0:T(8,128)(2,1)S(1)}, bf16[128,3712]{1,0:T(8,128)(2,1)}, u32[]{:S(2)}, u32[]{:S(2)}) collective-permute-start(bf16[128,3712]{1,0:T(8,128)(2,1)S(1)} %collective-permute-done.1.refs_4_.refs_17_), channel_id=1, source_target_pairs={{0,4},{1,5},{2,6},{3,7},{4,8},{5,9},{6,10},{7,11},{8,12},{9,13},{1... | collective-permute-start | bytes 2850824 | tf_op jit(solution)/shard_map/ppermute | solution.py:53
  48.4 16.2 %collective-permute-start.6 = (bf16[128,3712]{1,0:T(8,128)(2,1)}, bf16[128,3712]{1,0:T(8,128)(2,1)}, u32[]{:S(2)}, u32[]{:S(2)}) collective-permute-start(bf16[128,3712]{1,0:T(8,128)(2,1)} %collective-permute-done.5.refs_3_.refs_16_), channel_id=1, source_target_pairs={{0,12},{1,13},{2,14},{3,15},{4,0},{5,1},{6,2},{7,3},{8,4},{9,5},{1... | collective-permute-start | bytes 2850824 | tf_op jit(solution)/shard_map/ppermute | solution.py:53
  92.1 15.1 %collective-permute-start.19 = (bf16[128,3712]{1,0:T(8,128)(2,1)S(1)}, bf16[128,3712]{1,0:T(8,128)(2,1)S(1)}, u32[]{:S(2)}, u32[]{:S(2)}) collective-permute-start(bf16[128,3712]{1,0:T(8,128)(2,1)S(1)} %get-tuple-element.59), channel_id=1, source_target_pairs={{0,4},{1,5},{2,6},{3,7},{4,8},{5,9},{6,10},{7,11},{8,12},{9,13},{1... | collective-permute-start | bytes 2850824 | tf_op jit(solution)/shard_map/ppermute | solution.py:53
  93.4 15.0 %collective-permute-start.21 = (bf16[128,3712]{1,0:T(8,128)(2,1)S(1)}, bf16[128,3712]{1,0:T(8,128)(2,1)S(1)}, u32[]{:S(2)}, u32[]{:S(2)}) collective-permute-start(bf16[128,3712]{1,0:T(8,128)(2,1)S(1)} %get-tuple-element.61), channel_id=1, source_target_pairs={{0,12},{1,13},{2,14},{3,15},{4,0},{5,1},{6,2},{7,3},{8,4},{9,5},{1... | collective-permute-start | bytes 2850824 | tf_op jit(solution)/shard_map/ppermute | solution.py:53
  104.6 16.5 %collective-permute-start.23 = (bf16[128,3712]{1,0:T(8,128)(2,1)}, bf16[128,3712]{1,0:T(8,128)(2,1)}, u32[]{:S(2)}, u32[]{:S(2)}) collective-permute-start(bf16[128,3712]{1,0:T(8,128)(2,1)} %get-tuple-element.63), channel_id=1, source_target_pairs={{0,12},{1,13},{2,14},{3,15},{4,0},{5,1},{6,2},{7,3},{8,4},{9,5},{1... | collective-permute-start | bytes 2850824 | tf_op jit(solution)/shard_map/ppermute | solution.py:53
  106.6 15.3 %collective-permute-start.24 = (bf16[128,3712]{1,0:T(8,128)(2,1)}, bf16[128,3712]{1,0:T(8,128)(2,1)}, u32[]{:S(2)}, u32[]{:S(2)}) collective-permute-start(bf16[128,3712]{1,0:T(8,128)(2,1)} %get-tuple-element.64), channel_id=1, source_target_pairs={{0,4},{1,5},{2,6},{3,7},{4,8},{5,9},{6,10},{7,11},{8,12},{9,13},{1... | collective-permute-start | bytes 2850824 | tf_op jit(solution)/shard_map/ppermute | solution.py:53
  108.4 23.7 %collective-permute-start.20 = (bf16[128,3712]{1,0:T(8,128)(2,1)}, bf16[128,3712]{1,0:T(8,128)(2,1)}, u32[]{:S(2)}, u32[]{:S(2)}) collective-permute-start(bf16[128,3712]{1,0:T(8,128)(2,1)} %add_convert_fusion.1), channel_id=1, source_target_pairs={{0,4},{1,5},{2,6},{3,7},{4,8},{5,9},{6,10},{7,11},{8,12},{9,13},{1... | collective-permute-start | bytes 2850824 | tf_op jit(solution)/shard_map/ppermute | solution.py:53
  109.6 22.5 %collective-permute-start.22 = (bf16[128,3712]{1,0:T(8,128)(2,1)}, bf16[128,3712]{1,0:T(8,128)(2,1)}, u32[]{:S(2)}, u32[]{:S(2)}) collective-permute-start(bf16[128,3712]{1,0:T(8,128)(2,1)} %add_convert_fusion), channel_id=1, source_target_pairs={{0,12},{1,13},{2,14},{3,15},{4,0},{5,1},{6,2},{7,3},{8,4},{9,5},{1... | collective-permute-start | bytes 2850824 | tf_op jit(solution)/shard_map/ppermute | solution.py:53
  133.4 10.1 %collective-permute-start.25 = (bf16[64,3712]{1,0:T(8,128)(2,1)S(1)}, bf16[64,3712]{1,0:T(8,128)(2,1)S(1)}, u32[]{:S(2)}, u32[]{:S(2)}) collective-permute-start(bf16[64,3712]{1,0:T(8,128)(2,1)S(1)} %add_convert_fusion.5), channel_id=1, source_target_pairs={{0,1},{1,2},{2,3},{3,0},{4,5},{5,6},{6,7},{7,4},{8,9},{9,10},{10,1... | collective-permute-start | bytes 1425416 | tf_op jit(solution)/shard_map/ppermute | solution.py:53
  136.2 14.9 %collective-permute-start.26 = (bf16[64,3712]{1,0:T(8,128)(2,1)}, bf16[64,3712]{1,0:T(8,128)(2,1)S(1)}, u32[]{:S(2)}, u32[]{:S(2)}) collective-permute-start(bf16[64,3712]{1,0:T(8,128)(2,1)} %get-tuple-element.90), channel_id=1, source_target_pairs={{0,3},{1,0},{2,1},{3,2},{4,7},{5,4},{6,5},{7,6},{8,11},{9,8},{10,9... | collective-permute-start | bytes 1425416 | tf_op jit(solution)/shard_map/ppermute | solution.py:53
  139.5 11.6 %collective-permute-start.27 = (bf16[64,3712]{1,0:T(8,128)(2,1)S(1)}, bf16[64,3712]{1,0:T(8,128)(2,1)S(1)}, u32[]{:S(2)}, u32[]{:S(2)}) collective-permute-start(bf16[64,3712]{1,0:T(8,128)(2,1)S(1)} %get-tuple-element.91), channel_id=1, source_target_pairs={{0,2},{1,3},{2,0},{3,1},{4,6},{5,7},{6,4},{7,5},{8,10},{9,11},{10,... | collective-permute-start | bytes 1425416 | tf_op jit(solution)/shard_map/ppermute | solution.py:53
  152.8 8.2 %collective-permute-start.28 = (bf16[64,1024]{1,0:T(8,128)(2,1)S(1)}, bf16[64,1024]{1,0:T(8,128)(2,1)S(1)}, u32[]{:S(2)}, u32[]{:S(2)}) collective-permute-start(bf16[64,1024]{1,0:T(8,128)(2,1)S(1)} %get-tuple-element.98), channel_id=1, source_target_pairs={{0,32},{1,33},{2,34},{3,35},{4,36},{5,37},{6,38},{7,39},{8,40},{9,... | collective-permute-start | bytes 393224 | tf_op jit(solution)/shard_map/ppermute | solution.py:53
  (32 other events, 354.3 us)
